TPU v7x, 32 devices: a whole 2x2x4 slice. The times are simulated.
32 devices in a mesh: shard: 4 (over z), context: 2 (over x), tensor: 4 (over y, core).
Axes of the slice: x: 2, y: 2, z: 4, core: 2. Of those that a mesh axis runs over, the one named last changes fastest.
Arguments:
- frames: bfloat16 [8, 1024, 1536], P('shard', ('context', 'tensor')), may hold values from -12 to 12
- text_states: bfloat16 [8, 64, 1536], P('shard'), may hold values from -6 to 6
- cotangent: bfloat16 [8, 1024, 1536], P('shard', ('context', 'tensor')), may hold values from -6 to 6
- norm_gain: float32 [3, 1536], replicated, may hold values from 0.1 to 1.9
- norm_bias: float32 [3, 1536], replicated, may hold values from -1.5 to 1.5
- self_qkv: bfloat16 [3, 1536, 1536], P(None, 'shard', 'tensor'), may hold values from -0.15625 to 0.15625
- self_out: bfloat16 [1536, 1536], P('shard', 'tensor'), may hold values from -1.75 to 1.75
- cross_qkv: bfloat16 [3, 1536, 1536], P(None, 'shard', 'tensor'), may hold values from -0.15625 to 0.15625
- cross_out: bfloat16 [1536, 1536], P('shard', 'tensor'), may hold values from -0.875 to 0.875
- mlp_up: bfloat16 [1536, 6144], P('shard', 'tensor'), may hold values from -0.20412415 to 0.20412415
- mlp_down: bfloat16 [1536, 6144], P('shard', 'tensor'), may hold values from -0.15625 to 0.15625
Outputs:
- layer_out: bfloat16 [8, 1024, 1536], P('shard', ('context', 'tensor'))
- grad_frames: float32 [8, 1024, 1536], P('shard', ('context', 'tensor'))
- grad_text: float32 [8, 64, 1536], P('shard', ('context', 'tensor'))
- grad_norm_gain: float32 [3, 1536], P(None, 'shard')
- grad_norm_bias: float32 [3, 1536], P(None, 'shard')
- grad_self_qkv: float32 [3, 1536, 1536], P(None, 'shard', 'tensor')
- grad_self_out: float32 [1536, 1536], P('shard', 'tensor')
- grad_cross_qkv: float32 [3, 1536, 1536], P(None, 'shard', 'tensor')
- grad_cross_out: float32 [1536, 1536], P('shard', 'tensor')
- grad_mlp_up: float32 [1536, 6144], P('shard', 'tensor')
- grad_mlp_down: float32 [1536, 6144], P('shard', 'tensor')
- rms: float32 [4], replicated
All inputs are finite; a program needn't handle non-finite values.
Results may differ from a plain program's by a relative error of at most 0.019.
Values may be sent and summed in bfloat16 or wider, within the bound.
A program may use at most 192 MiB of HBM per device.

v0:
```python
from functools import partial

import jax
import jax.numpy as jnp
from jax import lax
from jax.sharding import PartitionSpec as P

D = 1536
HEAD_DIM = 64


epsilon = 1e-05
highest = lax.Precision.HIGHEST
masked_value = -1e30


def layer_norm(inputs, scaling, offset):
    average = jnp.mean(inputs, axis=-1, keepdims=True)
    centred = inputs - average
    variance = jnp.mean(centred * centred, axis=-1, keepdims=True)
    return centred * lax.rsqrt(variance + epsilon) * scaling + offset


def split_heads(tensor):
    return tensor.reshape(tensor.shape[0], tensor.shape[1], -1, HEAD_DIM)


def join_heads(tensor):
    return tensor.reshape(tensor.shape[0], tensor.shape[1], -1)


def gather_rows(values):
    return lax.all_gather(values, "tensor", axis=1, tiled=True)


def sum_rows(terms):
    return lax.psum_scatter(terms, "tensor", scatter_dimension=1, tiled=True)


def finish_branch(mixture, out_columns):
    return sum_rows(
        jnp.einsum("cfe,de->cfd", mixture, out_columns, preferred_element_type=jnp.float32)
    )


def score_block(query_heads, key_heads, query_start):
    scaled = jnp.einsum(
        "qhd,khd->hqk", query_heads, key_heads, preferred_element_type=jnp.float32
    ) * HEAD_DIM ** (-0.5)
    if query_start is None:
        return scaled
    query_place = query_start + jnp.arange(query_heads.shape[0], dtype=jnp.int32)
    key_place = jnp.arange(key_heads.shape[0], dtype=jnp.int32)
    allowed = key_place[None, :] <= query_place[:, None]
    return jnp.where(allowed[None], scaled, masked_value)


def attend_forward(query_heads, key_heads, value_heads, query_start):
    scores = score_block(query_heads, key_heads, query_start)
    row_max = jnp.max(scores, axis=-1, keepdims=True)
    exponent = jnp.exp(scores - row_max)
    row_total = jnp.sum(exponent, axis=-1, keepdims=True)
    soft_weights = (exponent / row_total).astype(jnp.bfloat16)
    mixture = jnp.einsum(
        "hqk,khd->qhd", soft_weights, value_heads, preferred_element_type=jnp.float32
    )
    return (mixture.astype(jnp.bfloat16), (row_max + jnp.log(row_total))[..., 0])


def attend_backward(query_heads, key_heads, value_heads, grad_mixture, log_total, query_start):
    scores = score_block(query_heads, key_heads, query_start)
    soft_weights = jnp.exp(scores - log_total[..., None])
    grad_weights = jnp.einsum(
        "qhd,khd->hqk", grad_mixture, value_heads, preferred_element_type=jnp.float32
    )
    row_inner = jnp.sum(soft_weights * grad_weights, axis=-1, keepdims=True)
    grad_scores = (soft_weights * (grad_weights - row_inner)).astype(jnp.bfloat16)
    factor = HEAD_DIM ** (-0.5)
    grad_query = (
        jnp.einsum("hqk,khd->qhd", grad_scores, key_heads, preferred_element_type=jnp.float32)
        * factor
    )
    grad_key = (
        jnp.einsum("hqk,qhd->khd", grad_scores, query_heads, preferred_element_type=jnp.float32)
        * factor
    )
    grad_value = jnp.einsum(
        "hqk,qhd->khd",
        soft_weights.astype(jnp.bfloat16),
        grad_mixture,
        preferred_element_type=jnp.float32,
    )
    return (grad_query, grad_key, grad_value)


def on_device(
    frames,
    text_states,
    cotangent,
    norm_gain,
    norm_bias,
    self_qkv,
    self_out,
    cross_qkv,
    cross_out,
    mlp_up,
    mlp_down,
):
    frame_count = frames.shape[1] * lax.axis_size("tensor")
    query_start = lax.axis_index("context") * frame_count
    self_inputs_full, self_output_full = (
        lax.all_gather(self_qkv, "shard", axis=1, tiled=True),
        lax.all_gather(self_out, "shard", axis=0, tiled=True),
    )
    stream_zero = frames.astype(jnp.float32)
    norm_one, norm_one_back = jax.vjp(layer_norm, stream_zero, norm_gain[0], norm_bias[0])
    normed_one = gather_rows(norm_one.astype(jnp.bfloat16))
    self_proj = jnp.einsum(
        "cfd,tde->tcfe", normed_one, self_inputs_full, preferred_element_type=jnp.float32
    ).astype(jnp.bfloat16)
    self_query = self_proj[0]
    keys_all, values_all = (
        lax.all_gather(self_proj[1], "context", axis=1, tiled=True),
        lax.all_gather(self_proj[2], "context", axis=1, tiled=True),
    )

    def self_clip(pieces):
        return attend_forward(pieces[0], pieces[1], pieces[2], query_start)

    self_mix, self_log = lax.map(
        self_clip, (split_heads(self_query), split_heads(keys_all), split_heads(values_all))
    )
    self_mix = join_heads(self_mix)
    branch_one = finish_branch(self_mix, self_output_full)
    stream_one = stream_zero + branch_one
    cross_inputs_full, cross_output_full = (
        lax.all_gather(cross_qkv, "shard", axis=1, tiled=True),
        lax.all_gather(cross_out, "shard", axis=0, tiled=True),
    )
    norm_two, norm_two_back = jax.vjp(layer_norm, stream_one, norm_gain[1], norm_bias[1])
    normed_two = gather_rows(norm_two.astype(jnp.bfloat16))
    cross_query = jnp.einsum(
        "cfd,de->cfe", normed_two, cross_inputs_full[0], preferred_element_type=jnp.float32
    ).astype(jnp.bfloat16)
    text_pair = jnp.einsum(
        "cnd,tde->tcne", text_states, cross_inputs_full[1:], preferred_element_type=jnp.float32
    ).astype(jnp.bfloat16)

    def cross_clip(pieces):
        return attend_forward(pieces[0], pieces[1], pieces[2], None)

    cross_mix, cross_log = lax.map(
        cross_clip, (split_heads(cross_query), split_heads(text_pair[0]), split_heads(text_pair[1]))
    )
    cross_mix = join_heads(cross_mix)
    branch_two = finish_branch(cross_mix, cross_output_full)
    stream_two = stream_one + branch_two
    up_full, down_full = (
        lax.all_gather(mlp_up, "shard", axis=0, tiled=True),
        lax.all_gather(mlp_down, "shard", axis=0, tiled=True),
    )
    norm_three, norm_three_back = jax.vjp(layer_norm, stream_two, norm_gain[2], norm_bias[2])
    normed_three = gather_rows(norm_three.astype(jnp.bfloat16))
    pre_act = jnp.einsum("cfd,dh->cfh", normed_three, up_full, preferred_element_type=jnp.float32)
    hidden, gelu_back = jax.vjp(partial(jax.nn.gelu, approximate=False), pre_act)
    hidden_low = hidden.astype(jnp.bfloat16)
    branch_three = sum_rows(
        jnp.einsum("cfh,dh->cfd", hidden_low, down_full, preferred_element_type=jnp.float32)
    )
    stream_out = stream_two + branch_three
    squares = jnp.stack(
        [
            jnp.sum(stream_out * stream_out),
            jnp.sum(branch_one * branch_one),
            jnp.sum(branch_two * branch_two),
            jnp.sum(branch_three * branch_three),
        ]
    )
    grad_stream = cotangent.astype(jnp.float32)
    grad_branch = gather_rows(grad_stream.astype(jnp.bfloat16))
    grad_hidden = jnp.einsum(
        "cfd,dh->cfh", grad_branch, down_full, preferred_element_type=jnp.float32
    )
    grad_down = jnp.einsum(
        "cfd,cfh->dh", grad_branch, hidden_low, preferred_element_type=jnp.float32
    )
    grad_pre = gelu_back(grad_hidden)[0].astype(jnp.bfloat16)
    grad_up = jnp.einsum("cfd,cfh->dh", normed_three, grad_pre, preferred_element_type=jnp.float32)
    grad_normed = sum_rows(
        jnp.einsum("cfh,dh->cfd", grad_pre, up_full, preferred_element_type=jnp.float32)
    )
    grad_inner, gain_three, shift_three = norm_three_back(grad_normed)
    grad_stream = grad_stream + grad_inner
    grad_branch = gather_rows(grad_stream.astype(jnp.bfloat16))
    grad_cross_mix = jnp.einsum(
        "cfd,de->cfe", grad_branch, cross_output_full, preferred_element_type=jnp.float32
    ).astype(jnp.bfloat16)
    grad_cross_output = jnp.einsum(
        "cfd,cfe->de", grad_branch, cross_mix, preferred_element_type=jnp.float32
    )

    def cross_back(pieces):
        return attend_backward(pieces[0], pieces[1], pieces[2], pieces[3], pieces[4], None)

    grad_cq, grad_ck, grad_cv = lax.map(
        cross_back,
        (
            split_heads(cross_query),
            split_heads(text_pair[0]),
            split_heads(text_pair[1]),
            split_heads(grad_cross_mix),
            cross_log,
        ),
    )
    grad_cq = join_heads(grad_cq).astype(jnp.bfloat16)
    text_grads = jnp.stack([join_heads(grad_ck), join_heads(grad_cv)])
    text_float = text_states.astype(jnp.float32)
    grad_cross_query_w = jnp.einsum(
        "cfd,cfe->de", normed_two, grad_cq, preferred_element_type=jnp.float32
    )
    grad_cross_text_w = jnp.einsum("cnd,tcne->tde", text_float, text_grads, precision=highest)
    grad_cross_inputs = jnp.concatenate([grad_cross_query_w[None], grad_cross_text_w], axis=0)
    text_part = jnp.einsum(
        "tcne,tde->cnd", text_grads, cross_inputs_full[1:].astype(jnp.float32), precision=highest
    )
    grad_text = lax.psum_scatter(text_part, ("context", "tensor"), scatter_dimension=1, tiled=True)
    grad_normed = sum_rows(
        jnp.einsum("cfe,de->cfd", grad_cq, cross_inputs_full[0], preferred_element_type=jnp.float32)
    )
    grad_inner, gain_two, shift_two = norm_two_back(grad_normed)
    grad_stream = grad_stream + grad_inner
    grad_branch = gather_rows(grad_stream.astype(jnp.bfloat16))
    grad_self_mix = jnp.einsum(
        "cfd,de->cfe", grad_branch, self_output_full, preferred_element_type=jnp.float32
    ).astype(jnp.bfloat16)
    grad_self_output = jnp.einsum(
        "cfd,cfe->de", grad_branch, self_mix, preferred_element_type=jnp.float32
    )

    def self_back(pieces):
        return attend_backward(pieces[0], pieces[1], pieces[2], pieces[3], pieces[4], query_start)

    grad_sq, grad_sk, grad_sv = lax.map(
        self_back,
        (
            split_heads(self_query),
            split_heads(keys_all),
            split_heads(values_all),
            split_heads(grad_self_mix),
            self_log,
        ),
    )
    grad_keys, grad_values = (
        lax.psum_scatter(join_heads(grad_sk), "context", scatter_dimension=1, tiled=True),
        lax.psum_scatter(join_heads(grad_sv), "context", scatter_dimension=1, tiled=True),
    )
    stacked = jnp.stack(
        [
            join_heads(grad_sq).astype(jnp.bfloat16),
            grad_keys.astype(jnp.bfloat16),
            grad_values.astype(jnp.bfloat16),
        ]
    )
    grad_self_inputs = jnp.einsum(
        "cfd,tcfe->tde", normed_one, stacked, preferred_element_type=jnp.float32
    )
    grad_normed = sum_rows(
        jnp.einsum("tcfe,tde->cfd", stacked, self_inputs_full, preferred_element_type=jnp.float32)
    )
    grad_inner, gain_one, shift_one = norm_one_back(grad_normed)
    grad_frames = grad_stream + grad_inner
    part_sqkv, part_sout, part_cqkv, part_cout, part_up, part_down = (
        lax.psum_scatter(grad_self_inputs, "shard", scatter_dimension=1, tiled=True),
        lax.psum_scatter(grad_self_output, "shard", scatter_dimension=0, tiled=True),
        lax.psum_scatter(grad_cross_inputs, "shard", scatter_dimension=1, tiled=True),
        lax.psum_scatter(grad_cross_output, "shard", scatter_dimension=0, tiled=True),
        lax.psum_scatter(grad_up, "shard", scatter_dimension=0, tiled=True),
        lax.psum_scatter(grad_down, "shard", scatter_dimension=0, tiled=True),
    )
    sum_sqkv, sum_sout, sum_cqkv, sum_cout, sum_up, sum_down = lax.psum(
        (part_sqkv, part_sout, part_cqkv, part_cout, part_up, part_down), "context"
    )
    gain_rows = jnp.stack([gain_one, gain_two, gain_three])
    shift_rows = jnp.stack([shift_one, shift_two, shift_three])
    gain_total, shift_total, square_total = lax.psum(
        (gain_rows, shift_rows, squares), ("shard", "context", "tensor")
    )
    width = D // lax.axis_size("shard")
    start = lax.axis_index("shard") * width
    grad_gain = lax.dynamic_slice_in_dim(gain_total, start, width, 1)
    grad_shift = lax.dynamic_slice_in_dim(shift_total, start, width, 1)
    entries = float(
        frames.shape[0]
        * lax.axis_size("shard")
        * frames.shape[1]
        * lax.axis_size("context")
        * lax.axis_size("tensor")
        * frames.shape[2]
    )
    stats = jnp.sqrt(square_total / entries)
    return (
        stream_out.astype(jnp.bfloat16),
        grad_frames,
        grad_text,
        grad_gain,
        grad_shift,
        sum_sqkv,
        sum_sout,
        sum_cqkv,
        sum_cout,
        sum_up,
        sum_down,
        stats,
    )


def solution(mesh):
    in_specs = (
        P("shard", ("context", "tensor"), None),
        P("shard", None, None),
        P("shard", ("context", "tensor"), None),
        P(),
        P(),
        P(None, "shard", "tensor"),
        P("shard", "tensor"),
        P(None, "shard", "tensor"),
        P("shard", "tensor"),
        P("shard", "tensor"),
        P("shard", "tensor"),
    )
    out_specs = (
        P("shard", ("context", "tensor"), None),
        P("shard", ("context", "tensor"), None),
        P("shard", ("context", "tensor"), None),
        P(None, "shard"),
        P(None, "shard"),
        P(None, "shard", "tensor"),
        P("shard", "tensor"),
        P(None, "shard", "tensor"),
        P("shard", "tensor"),
        P("shard", "tensor"),
        P("shard", "tensor"),
        P(),
    )
    return jax.shard_map(
        on_device, mesh=mesh, in_specs=in_specs, out_specs=out_specs, check_vma=False
    )
```

profile of v0, /device:TPU:0, one launch (start us, length us, event | category | flops | bytes accessed | tf_op | source)
XLA Modules:
  0.0 2162.9 jit_solution(3474178771869646374)
XLA Ops:
  18.4 29.1 %all-gather.17.cloned.1.call-done = bf16[2,512,1536]{2,1,0:T(8,128)(2,1)} async-done(((bf16[2,128,1536]{2,1,0:T(8,128)(2,1)}), bf16[2,512,1536]{2,1,0:T(8,128)(2,1)}) %all-gather.17.cloned.1.call-update) | async-done | bytes 3145744 | tf_op jit(solution)/shard_map/all_gather | solution.py:33
  47.5 72.1 %all-gather.19.cloned.1.call-done = bf16[3,1536,384]{1,2,0:T(8,128)(2,1)} async-done(((bf16[3,384,384]{1,2,0:T(8,128)(2,1)}), bf16[3,1536,384]{1,2,0:T(8,128)(2,1)}) %all-gather.19.cloned.1.call-update) | async-done | bytes 3538960 | tf_op jit(solution)/shard_map/all_gather | solution.py:112
  119.6 6.8 convert_bitcast_fusion
  129.0 24.8 %all-gather.43.cloned.1.call-done = bf16[1,2,1024,384]{2,3,0,1:T(8,128)(2,1)} async-done(((bf16[1,2,512,384]{2,3,0,1:T(8,128)(2,1)}), bf16[1,2,1024,384]{2,3,0,1:T(8,128)(2,1)}) %all-gather.43.cloned.1.call-update) | async-done | bytes 1572880 | tf_op jit(solution)/shard_map/all_gather | solution.py:123
  153.8 29.2 %all-gather.41.cloned.1.call-done = bf16[1,2,1024,384]{2,3,0,1:T(8,128)(2,1)} async-done(((bf16[1,2,512,384]{2,3,0,1:T(8,128)(2,1)}), bf16[1,2,1024,384]{2,3,0,1:T(8,128)(2,1)}) %all-gather.41.cloned.1.call-update) | async-done | bytes 1572880 | tf_op jit(solution)/shard_map/all_gather | solution.py:124
  183.1 23.0 %while.52 = (s32[]{:T(128)}, bf16[2,512,6,64]{1,3,2,0:T(8,128)(2,1)S(1)}, f32[2,6,512]{2,1,0:T(8,128)S(1)}, bf16[2,1024,6,64]{1,3,2,0:T(8,128)(2,1)}, s32[]{:T(1...) while((s32[]{:T(128)}, bf16[2,512,6,64]{1,3,2,0:T(8,128)(2,1)S(1)}, ...), condition=%wide.region_5.6_spmd, body=%wide.region_2.5_spmd.sunk | while | flops 843773440 | bytes 48621696 | solution.py:130
  206.2 8.3 all-gather.21.cloned.1.call-done
  221.1 57.3 %reduce-scatter.16.cloned.1.call-done = f32[2,128,1536]{2,1,0:T(8,128)} async-done(((f32[2,512,1536]{2,1,0:T(8,128)}), f32[2,128,1536]{2,1,0:T(8,128)}) %reduce-scatter.16.cloned.1.call-update) | async-done | bytes 1572880 | tf_op jit(solution)/shard_map/reduce_scatter | solution.py:37
  283.2 66.8 %all-gather.23.cloned.1.call-done = bf16[3,1536,384]{2,1,0:T(8,128)(2,1)} async-done(((bf16[3,384,384]{2,1,0:T(8,128)(2,1)}), bf16[3,1536,384]{2,1,0:T(8,128)(2,1)}) %all-gather.23.cloned.1.call-update) | async-done | bytes 3538960 | tf_op jit(solution)/shard_map/all_gather | solution.py:137
  354.1 25.3 %all-gather.25.cloned.1.call-done = bf16[2,512,1536]{2,1,0:T(8,128)(2,1)} async-done(((bf16[2,128,1536]{2,1,0:T(8,128)(2,1)}), bf16[2,512,1536]{2,1,0:T(8,128)(2,1)}) %all-gather.25.cloned.1.call-update) | async-done | bytes 3145744 | tf_op jit(solution)/shard_map/all_gather | solution.py:33
  384.6 7.7 while.53
  392.4 19.2 all-gather.27.cloned.1.call-done
  418.4 56.8 %reduce-scatter.18.cloned.1.call-done = f32[2,128,1536]{2,1,0:T(8,128)} async-done(((f32[2,512,1536]{2,1,0:T(8,128)}), f32[2,128,1536]{2,1,0:T(8,128)}) %reduce-scatter.18.cloned.1.call-update) | async-done | bytes 1572880 | tf_op jit(solution)/shard_map/reduce_scatter | solution.py:37
  482.2 84.0 %all-gather.31.cloned.1.call-done = bf16[1536,1536]{1,0:T(8,128)(2,1)} async-done(((bf16[384,1536]{1,0:T(8,128)(2,1)}), bf16[1536,1536]{1,0:T(8,128)(2,1)}) %all-gather.31.cloned.1.call-update) | async-done | bytes 4718608 | tf_op jit(solution)/shard_map/all_gather | solution.py:159
  566.2 29.0 %all-gather.29.cloned.1.call-done = bf16[2,512,1536]{2,1,0:T(8,128)(2,1)} async-done(((bf16[2,128,1536]{2,1,0:T(8,128)(2,1)}), bf16[2,512,1536]{2,1,0:T(8,128)(2,1)}) %all-gather.29.cloned.1.call-update) | async-done | bytes 3145744 | tf_op jit(solution)/shard_map/all_gather | solution.py:33
  595.2 9.9 fusion.128
  607.7 15.3 multiply_convert_fusion.2
  623.0 63.3 %all-gather.33.cloned.1.call-done = bf16[1536,1536]{1,0:T(8,128)(2,1)} async-done(((bf16[384,1536]{1,0:T(8,128)(2,1)}), bf16[1536,1536]{1,0:T(8,128)(2,1)}) %all-gather.33.cloned.1.call-update) | async-done | bytes 4718608 | tf_op jit(solution)/shard_map/all_gather | solution.py:160
  686.2 9.8 fusion.96
  696.1 18.6 all-gather.35.cloned.1.call-done
  714.7 11.3 add_convert_fusion
  727.8 9.6 fusion.98
  737.9 37.6 %reduce-scatter.20.cloned.1.call-done = f32[2,128,1536]{2,1,0:T(8,128)} async-done(((f32[2,512,1536]{2,1,0:T(8,128)}), f32[2,128,1536]{2,1,0:T(8,128)}) %reduce-scatter.20.cloned.1.call-update) | async-done | bytes 1572880 | tf_op jit(solution)/shard_map/reduce_scatter | solution.py:37
  775.5 60.9 %reduce-scatter.22.cloned.1.call-done = f32[2,128,1536]{2,1,0:T(8,128)} async-done(((f32[2,512,1536]{2,1,0:T(8,128)}), f32[2,128,1536]{2,1,0:T(8,128)}) %reduce-scatter.22.cloned.1.call-update) | async-done | bytes 1572880 | tf_op jit(solution)/shard_map/reduce_scatter | solution.py:37
  846.2 27.0 %all-gather.37.cloned.1.call-done = bf16[2,512,1536]{2,1,0:T(8,128)(2,1)} async-done(((bf16[2,128,1536]{2,1,0:T(8,128)(2,1)}), bf16[2,512,1536]{2,1,0:T(8,128)(2,1)}) %all-gather.37.cloned.1.call-update) | async-done | bytes 3145744 | tf_op jit(solution)/shard_map/all_gather | solution.py:33
  878.6 11.8 while.54
  896.5 58.5 %reduce-scatter.24.cloned.1.call-done = f32[2,128,1536]{2,1,0:T(8,128)} async-done(((f32[2,512,1536]{2,1,0:T(8,128)}), f32[2,128,1536]{2,1,0:T(8,128)}) %reduce-scatter.24.cloned.1.call-update) | async-done | bytes 1572880 | tf_op jit(solution)/shard_map/reduce_scatter | solution.py:37
  962.2 28.6 %all-gather.39.cloned.1.call-done = bf16[2,512,1536]{2,1,0:T(8,128)(2,1)} async-done(((bf16[2,128,1536]{2,1,0:T(8,128)(2,1)}), bf16[2,512,1536]{2,1,0:T(8,128)(2,1)}) %all-gather.39.cloned.1.call-update) | async-done | bytes 3145744 | tf_op jit(solution)/shard_map/all_gather | solution.py:33
  995.4 52.9 %while.55 = (s32[]{:T(128)}, bf16[2,512,6,64]{1,3,2,0:T(8,128)(2,1)}, f32[2,1024,6,64]{1,3,2,0:T(8,128)}, f32[2,1024,6,64]{1,3,2,0:T(8,128)}, bf16[2,1024,6,64]{...) while((s32[]{:T(128)}, ...), condition=%wide.region_28.29_spmd, body=%wide.region_26.28_spmd.sunk | while | flops 2061563392 | bytes 142185744 | solution.py:243
  1003.0 7.2 multiply_reduce_fusion.15
  1010.1 6.9 multiply_convert_fusion.6
  1029.4 7.2 multiply_reduce_fusion.15
  1036.5 6.9 multiply_convert_fusion.6
  1055.6 10.4 convolution_bitcast_fusion.2
  1066.1 9.9 convolution_bitcast_fusion.1
  1098.8 42.3 %reduce-scatter.26.cloned.1.call-done = f32[2,512,384]{2,1,0:T(8,128)} async-done(((f32[2,1024,384]{2,1,0:T(8,128)}), f32[2,512,384]{2,1,0:T(8,128)}) %reduce-scatter.26.cloned.1.call-update) | async-done | bytes 1572880 | tf_op jit(solution)/shard_map/reduce_scatter | solution.py:254
  1142.6 7.7 convolution_bitcast_fusion.3
  1150.4 8.1 convolution_bitcast_fusion.4
  1158.6 146.3 %reduce-scatter.42.cloned.1.call-done = f32[384,1536]{1,0:T(8,128)} async-done(((f32[1536,1536]{1,0:T(8,128)}), f32[384,1536]{1,0:T(8,128)}) %reduce-scatter.42.cloned.1.call-update) | async-done | bytes 2359312 | tf_op jit(solution)/shard_map/reduce_scatter | solution.py:277
  1304.9 164.7 %reduce-scatter.44.cloned.1.call-done = f32[384,1536]{0,1:T(8,128)} async-done(((f32[1536,1536]{0,1:T(8,128)}), f32[384,1536]{0,1:T(8,128)}) %reduce-scatter.44.cloned.1.call-update) | async-done | bytes 2359312 | tf_op jit(solution)/shard_map/reduce_scatter | solution.py:278
  1469.6 51.7 %reduce-scatter.40.cloned.1.call-done = f32[384,384]{1,0:T(8,128)} async-done(((f32[1536,384]{1,0:T(8,128)}), f32[384,384]{1,0:T(8,128)}) %reduce-scatter.40.cloned.1.call-update) | async-done | bytes 589840 | tf_op jit(solution)/shard_map/reduce_scatter | solution.py:276
  1521.3 125.4 %reduce-scatter.38.cloned.1.call-done = f32[3,384,384]{1,2,0:T(8,128)} async-done(((f32[3,1536,384]{1,2,0:T(8,128)}), f32[3,384,384]{1,2,0:T(8,128)}) %reduce-scatter.38.cloned.1.call-update) | async-done | bytes 1769488 | tf_op jit(solution)/shard_map/reduce_scatter | solution.py:275
  1646.7 51.4 %reduce-scatter.36.cloned.1.call-done = f32[384,384]{1,0:T(8,128)} async-done(((f32[1536,384]{1,0:T(8,128)}), f32[384,384]{1,0:T(8,128)}) %reduce-scatter.36.cloned.1.call-update) | async-done | bytes 589840 | tf_op jit(solution)/shard_map/reduce_scatter | solution.py:274
  1698.2 125.3 %reduce-scatter.34.cloned.1.call-done = f32[3,384,384]{1,2,0:T(8,128)} async-done(((f32[3,1536,384]{1,2,0:T(8,128)}), f32[3,384,384]{1,2,0:T(8,128)}) %reduce-scatter.34.cloned.1.call-update) | async-done | bytes 1769488 | tf_op jit(solution)/shard_map/reduce_scatter | solution.py:273
  1831.7 53.3 %reduce-scatter.30.cloned.1.call-done = f32[2,128,1536]{2,1,0:T(8,128)} async-done(((f32[2,512,1536]{2,1,0:T(8,128)}), f32[2,128,1536]{2,1,0:T(8,128)}) %reduce-scatter.30.cloned.1.call-update) | async-done | bytes 1572880 | tf_op jit(solution)/shard_map/reduce_scatter | solution.py:37
  1887.9 40.6 %all-reduce = (f32[3,1536]{1,0:T(4,128)S(1)}, f32[3,1536]{1,0:T(4,128)S(1)}, f32[4]{0:T(128)S(1)}) all-reduce(f32[3,1536]{1,0:T(4,128)S(1)} %pad_maximum_fusion.7, f32[3,1536]{1,0:T(4,128)S(1)} %pad_maximum_fusion.8, f32[4]{0:T(128)S(1)} %pad_maximum_fusion.9), channel_id=1, replica_groups=mesh['shard'=4,'context'=2,'tensor'=4] {'shard','context','tensor'}, use_global_device_ids=true, to_apply=%region_38.39 | all-reduce | flops 9220 | bytes 73760 | tf_op jit(solution)/shard_map/psum | solution.py:285
  1932.7 179.6 %all-reduce.4.cloned.1.call-done = (f32[3,384,384]{1,2,0:T(8,128)}, f32[384,384]{1,0:T(8,128)}, f32[3,384,384]{1,2,0:T(8,128)}, f32[384,384]{1,0:T(8,128)}, f32[384,1536]{1,0:T(8,128)}, /*index=5*/f32[384,1536]{0,1:T(8,128)}) async-done(((f32[3,384,384]{1,2,0:T(8,128)}, f32[384,384]{1,0:T(8,128)}, f32[3,384,384]{1,2,0:T(8,128)}, f32[384,384]{1,0:T(8,128)}, f32[384,1536]{1,0:T(8,128)}, ...) | async-done | bytes 9437200 | tf_op jit(solution)/shard_map/psum | solution.py:280
  2120.3 31.2 %reduce-scatter.32.cloned.1.call-done = f32[2,8,1536]{2,1,0:T(8,128)} async-done(((f32[2,64,1536]{2,1,0:T(8,128)}), f32[2,8,1536]{2,1,0:T(8,128)}) %reduce-scatter.32.cloned.1.call-update) | async-done | bytes 98320 | tf_op jit(solution)/shard_map/reduce_scatter | solution.py:226
  (370 shorter events, 211.3 us)
Async XLA Ops:
  7.2 342.8 %copy-start = (bf16[2,64,1536]{2,1,0:T(8,128)(2,1)S(1)}, bf16[2,64,1536]{2,1,0:T(8,128)(2,1)}, u32[]{:S(2)}) copy-start(bf16[2,64,1536]{2,1,0:T(8,128)(2,1)} %param.20) | copy-start | bytes 1179652
  7.2 40.3 %all-gather.17.cloned.1.call-start = ((), (), s32[]{:S(2)}) async-start(), calls=%async_computation.15 | async-start | bytes 3932160 | tf_op jit(solution)/shard_map/all_gather | solution.py:33
  8.7 111.0 %copy-start.46 = (f32[2,128]{1,0:T(2,128)}, f32[2,128]{1,0:T(2,128)S(1)}, u32[]{:S(2)}) copy-start(f32[2,128]{1,0:T(2,128)S(1)} %broadcast_multiply_fusion.2) | copy-start | bytes 3076
  10.7 108.9 %copy-start.57 = (f32[2,128]{1,0:T(2,128)}, f32[2,128]{1,0:T(2,128)S(1)}, u32[]{:S(2)}) copy-start(f32[2,128]{1,0:T(2,128)S(1)} %fusion.147) | copy-start | bytes 3076
  12.2 107.4 %copy-start.43 = (f32[1536]{0:T(1024)}, f32[1536]{0:T(1024)S(1)}, u32[]{:S(2)}) copy-start(f32[1536]{0:T(1024)S(1)} %get-tuple-element.268) | copy-start | bytes 18436
  16.1 103.5 %all-gather.19.cloned.1.call-start = ((), (), s32[]{:S(2)}) async-start(), calls=%async_computation.16 | async-start | bytes 4423680 | tf_op jit(solution)/shard_map/all_gather | solution.py:112
  18.4 135.4 %all-gather.43.cloned.1.call-start = ((), (), s32[]{:S(2)}) async-start(), calls=%async_computation.43 | async-start | bytes 2359296 | tf_op jit(solution)/shard_map/all_gather | solution.py:123
  127.8 55.3 %all-gather.41.cloned.1.call-start = ((), (), s32[]{:S(2)}) async-start(), calls=%async_computation.42 | async-start | bytes 2359296 | tf_op jit(solution)/shard_map/all_gather | solution.py:124
  128.4 86.1 %all-gather.21.cloned.1.call-start = ((), (), s32[]{:S(2)}) async-start(), calls=%async_computation.17 | async-start | bytes 1474560 | tf_op jit(solution)/shard_map/all_gather | solution.py:113
  129.0 149.4 %reduce-scatter.16.cloned.1.call-start = ((), (), s32[]{:S(2)}) async-start(), calls=%async_computation.18 | async-start | bytes 7864320 | tf_op jit(solution)/shard_map/reduce_scatter | solution.py:37
  206.1 14.1 copy-start.27
  220.2 58.2 %copy-start.4 = (bf16[2,128,1536]{2,1,0:T(8,128)(2,1)S(1)}, bf16[2,128,1536]{2,1,0:T(8,128)(2,1)}, u32[]{:S(2)}) copy-start(bf16[2,128,1536]{2,1,0:T(8,128)(2,1)} %param.19) | copy-start | bytes 2359300
  220.3 129.7 %all-gather.23.cloned.1.call-start = ((), (), s32[]{:S(2)}) async-start(), calls=%async_computation.19 | async-start | bytes 4423680 | tf_op jit(solution)/shard_map/all_gather | solution.py:137
  221.0 158.4 %all-gather.25.cloned.1.call-start = ((), (), s32[]{:S(2)}) async-start(), calls=%async_computation.20 | async-start | bytes 3932160 | tf_op jit(solution)/shard_map/all_gather | solution.py:33
  282.4 129.1 %all-gather.27.cloned.1.call-start = ((), (), s32[]{:S(2)}) async-start(), calls=%async_computation.21 | async-start | bytes 1474560 | tf_op jit(solution)/shard_map/all_gather | solution.py:138
  283.2 192.0 %reduce-scatter.18.cloned.1.call-start = ((), (), s32[]{:S(2)}) async-start(), calls=%async_computation.22 | async-start | bytes 7864320 | tf_op jit(solution)/shard_map/reduce_scatter | solution.py:37
  417.6 148.7 %all-gather.31.cloned.1.call-start = ((), (), s32[]{:S(2)}) async-start(), calls=%async_computation.24 | async-start | bytes 5898240 | tf_op jit(solution)/shard_map/all_gather | solution.py:159
  418.3 61.1 %copy-start.45 = (f32[1536]{0:T(1024)S(1)}, f32[1536]{0:T(1024)}, u32[]{:S(2)}) copy-start(f32[1536]{0:T(1024)} %get-tuple-element.267) | copy-start | bytes 18436
  418.3 176.9 %all-gather.29.cloned.1.call-start = ((), (), s32[]{:S(2)}) async-start(), calls=%async_computation.23 | async-start | bytes 3932160 | tf_op jit(solution)/shard_map/all_gather | solution.py:33
  480.6 205.6 %all-gather.33.cloned.1.call-start = ((), (), s32[]{:S(2)}) async-start(), calls=%async_computation.25 | async-start | bytes 5898240 | tf_op jit(solution)/shard_map/all_gather | solution.py:160
  481.4 233.3 %all-gather.35.cloned.1.call-start = ((), (), s32[]{:S(2)}) async-start(), calls=%async_computation.27 | async-start | bytes 3932160 | tf_op jit(solution)/shard_map/all_gather | solution.py:33
  481.9 293.5 %reduce-scatter.20.cloned.1.call-start = ((), (), s32[]{:S(2)}) async-start(), calls=%async_computation.26 | async-start | bytes 7864320 | tf_op jit(solution)/shard_map/reduce_scatter | solution.py:37
  696.1 140.3 %reduce-scatter.22.cloned.1.call-start = ((), (), s32[]{:S(2)}) async-start(), calls=%async_computation.28 | async-start | bytes 7864320 | tf_op jit(solution)/shard_map/reduce_scatter | solution.py:37
  737.4 135.7 %all-gather.37.cloned.1.call-start = ((), (), s32[]{:S(2)}) async-start(), calls=%async_computation.29 | async-start | bytes 3932160 | tf_op jit(solution)/shard_map/all_gather | solution.py:33
  844.5 110.5 %reduce-scatter.24.cloned.1.call-start = ((), (), s32[]{:S(2)}) async-start(), calls=%async_computation.30 | async-start | bytes 7864320 | tf_op jit(solution)/shard_map/reduce_scatter | solution.py:37
  896.4 58.5 %copy-start.49 = (f32[2,128]{1,0:T(2,128)S(1)}, f32[2,128]{1,0:T(2,128)}, u32[]{:S(2)}) copy-start(f32[2,128]{1,0:T(2,128)} %copy-done.48) | copy-start | bytes 3076
  896.4 62.9 %copy-start.15 = (bf16[2,128,1536]{2,1,0:T(8,128)(2,1)S(1)}, bf16[2,128,1536]{2,1,0:T(8,128)(2,1)}, u32[]{:S(2)}) copy-start(bf16[2,128,1536]{2,1,0:T(8,128)(2,1)} %param.21) | copy-start | bytes 2359300
  896.4 61.7 %copy-start.60 = (f32[2,128]{1,0:T(2,128)S(1)}, f32[2,128]{1,0:T(2,128)}, u32[]{:S(2)}) copy-start(f32[2,128]{1,0:T(2,128)} %copy-done.59) | copy-start | bytes 3076
  896.4 94.4 %all-gather.39.cloned.1.call-start = ((), (), s32[]{:S(2)}) async-start(), calls=%async_computation.31 | async-start | bytes 3932160 | tf_op jit(solution)/shard_map/all_gather | solution.py:33
  962.1 135.1 %reduce-scatter.28.cloned.1.call-start = ((), (), s32[]{:S(2)}) async-start(), calls=%async_computation.33 | async-start | bytes 4718592 | tf_op jit(solution)/shard_map/reduce_scatter | solution.py:255
  962.2 33.2 %copy-start.1 = (bf16[2,1024,6,64]{1,3,2,0:T(8,128)(2,1)S(1)}, bf16[2,1024,6,64]{1,3,2,0:T(8,128)(2,1)}, u32[]{:S(2)}) copy-start(bf16[2,1024,6,64]{1,3,2,0:T(8,128)(2,1)} %get-tuple-element.749) | copy-start | bytes 4718596
  1052.0 89.1 %reduce-scatter.26.cloned.1.call-start = ((), (), s32[]{:S(2)}) async-start(), calls=%async_computation.32 | async-start | bytes 4718592 | tf_op jit(solution)/shard_map/reduce_scatter | solution.py:254
  1055.6 249.3 %reduce-scatter.42.cloned.1.call-start = ((), (), s32[]{:S(2)}) async-start(), calls=%async_computation.40 | async-start | bytes 11796480 | tf_op jit(solution)/shard_map/reduce_scatter | solution.py:277
  1066.1 403.5 %reduce-scatter.44.cloned.1.call-start = ((), (), s32[]{:S(2)}) async-start(), calls=%async_computation.41 | async-start | bytes 11796480 | tf_op jit(solution)/shard_map/reduce_scatter | solution.py:278
  1076.1 445.2 %reduce-scatter.40.cloned.1.call-start = ((), (), s32[]{:S(2)}) async-start(), calls=%async_computation.39 | async-start | bytes 2949120 | tf_op jit(solution)/shard_map/reduce_scatter | solution.py:276
  1082.4 564.3 %reduce-scatter.38.cloned.1.call-start = ((), (), s32[]{:S(2)}) async-start(), calls=%async_computation.38 | async-start | bytes 8847360 | tf_op jit(solution)/shard_map/reduce_scatter | solution.py:275
  1090.6 607.6 %reduce-scatter.36.cloned.1.call-start = ((), (), s32[]{:S(2)}) async-start(), calls=%async_computation.37 | async-start | bytes 2949120 | tf_op jit(solution)/shard_map/reduce_scatter | solution.py:274
  1096.8 726.6 %reduce-scatter.34.cloned.1.call-start = ((), (), s32[]{:S(2)}) async-start(), calls=%async_computation.36 | async-start | bytes 8847360 | tf_op jit(solution)/shard_map/reduce_scatter | solution.py:273
  1150.3 734.7 %reduce-scatter.30.cloned.1.call-start = ((), (), s32[]{:S(2)}) async-start(), calls=%async_computation.34 | async-start | bytes 7864320 | tf_op jit(solution)/shard_map/reduce_scatter | solution.py:37
  1158.5 953.7 %all-reduce.4.cloned.1.call-start = ((), (), s32[]{:S(2)}) async-start(), calls=%async_computation.44 | async-start | bytes 18874368 | tf_op jit(solution)/shard_map/psum | solution.py:280
  1823.5 61.6 %copy-start.5 = (bf16[2,128,1536]{2,1,0:T(8,128)(2,1)S(1)}, bf16[2,128,1536]{2,1,0:T(8,128)(2,1)}, u32[]{:S(2)}) copy-start(bf16[2,128,1536]{2,1,0:T(8,128)(2,1)} %param.19) | copy-start | bytes 2359300
  1823.5 61.6 %copy-start.44 = (f32[1536]{0:T(1024)S(1)}, f32[1536]{0:T(1024)}, u32[]{:S(2)}) copy-start(f32[1536]{0:T(1024)} %copy-done.43) | copy-start | bytes 18436
  1823.5 61.5 %copy-start.47 = (f32[2,128]{1,0:T(2,128)S(1)}, f32[2,128]{1,0:T(2,128)}, u32[]{:S(2)}) copy-start(f32[2,128]{1,0:T(2,128)} %copy-done.46) | copy-start | bytes 3076
  1823.5 327.9 %reduce-scatter.32.cloned.1.call-start = ((), (), s32[]{:S(2)}) async-start(), calls=%async_computation.35 | async-start | bytes 884736 | tf_op jit(solution)/shard_map/reduce_scatter | solution.py:226
  1826.7 60.3 %copy-start.65 = (f32[2,128]{1,0:T(2,128)S(1)}, f32[2,128]{1,0:T(2,128)}, u32[]{:S(2)}) copy-start(f32[2,128]{1,0:T(2,128)} %copy-done.64) | copy-start | bytes 3076
  1826.7 60.4 %copy-start.58 = (f32[2,128]{1,0:T(2,128)S(1)}, f32[2,128]{1,0:T(2,128)}, u32[]{:S(2)}) copy-start(f32[2,128]{1,0:T(2,128)} %copy-done.57) | copy-start | bytes 3076
  2117.1 36.3 %copy-start.33 = (f32[384,384]{1,0:T(8,128)S(1)}, f32[384,384]{1,0:T(8,128)}, u32[]{:S(2)}) copy-start(f32[384,384]{1,0:T(8,128)} %get-tuple-element.703) | copy-start | bytes 1769476
  2117.1 37.1 %copy-start.30 = (f32[384,1536]{1,0:T(8,128)S(1)}, f32[384,1536]{1,0:T(8,128)}, u32[]{:S(2)}) copy-start(f32[384,1536]{1,0:T(8,128)} %get-tuple-element.704) | copy-start | bytes 7077892
  (69 other events, 206.5 us)
Sparse Core Ops, SparseCore 0:
  16.3 31.2 all-gather.16
  49.7 69.8 all-gather.18
  127.9 25.8 all-gather.42
  155.8 27.1 all-gather.40
  184.5 29.9 all-gather.20
  220.4 57.9 reduce-scatter.15
  280.0 69.9 all-gather.22
  352.2 27.1 all-gather.24
  381.1 30.4 all-gather.26
  417.7 57.4 reduce-scatter.17
  476.8 89.3 all-gather.30
  568.2 26.9 all-gather.28
  596.8 89.4 all-gather.32
  687.7 26.9 all-gather.34
  717.1 58.3 reduce-scatter.19
  778.0 58.3 reduce-scatter.21
  844.6 28.5 all-gather.36
  896.6 58.3 reduce-scatter.23
  962.3 28.5 all-gather.38
  1052.1 43.3 reduce-scatter.27
  1097.7 43.3 reduce-scatter.25
  1143.6 161.2 reduce-scatter.41
  1307.4 162.1 reduce-scatter.43
  1472.4 48.8 reduce-scatter.39
  1523.7 122.9 reduce-scatter.37
  1649.6 48.5 reduce-scatter.35
  1700.4 122.9 reduce-scatter.33
  1826.1 58.8 reduce-scatter.29
  1887.9 224.2 all-reduce.3
  2116.4 34.9 reduce-scatter.31
where the time goes:
time: 2170 us; the launch traced here: 2160 us
  waiting for transfers between devices  1770 us (82%)
  matrix products  195 us (9%)
  other arithmetic  81.1 us (4%)
  local copies, waits for them, and re-layouts  55.1 us (3%)
  blocking collectives  40.6 us (2%)
    reduce_scatter x6, waiting for transfers between devices, sum_rows(): return lax.psum_scatter(terms, 'tensor', scatter_dimension=1, tiled=True)  324 us
    psum x1, waiting for transfers between devices, on_device(): lax.psum((part_sqkv, part_sout, part_cqkv, part_cout, part_up, part_down)...  180 us
    reduce_scatter x1, waiting for transfers between devices, on_device(): lax.psum_scatter(grad_down, 'shard', scatter_dimension=0, tiled=True)  165 us
    all_gather x6, waiting for transfers between devices, gather_rows(): return lax.all_gather(values, 'tensor', axis=1, tiled=True)  158 us
    reduce_scatter x1, waiting for transfers between devices, on_device(): lax.psum_scatter(grad_up, 'shard', scatter_dimension=0, tiled=True)  146 us
    reduce_scatter x1, waiting for transfers between devices, on_device(): lax.psum_scatter(grad_cross_inputs, 'shard', scatter_dimension=1, tiled=T...  125 us
    reduce_scatter x1, waiting for transfers between devices, on_device(): lax.psum_scatter(grad_self_inputs, 'shard', scatter_dimension=1, tiled=True)  125 us
    all_gather x1, waiting for transfers between devices, on_device(): lax.all_gather(mlp_up, 'shard', axis=0, tiled=True)  84 us
  transfers between devices with their start and end apart: 30, of which 29 were waited for; matrix products, arithmetic and copies ran while one was open for 9% of the time, Pallas kernels for 0%

commit v1 on v0

v1 whole, which is shorter than its diff:
```python
from functools import partial

import jax
import jax.numpy as jnp
from jax import lax
from jax.experimental import pallas as pl
from jax.experimental.pallas import tpu as pltpu
from jax.sharding import PartitionSpec as P

HEAD_DIM = 64
EPS = 1e-05
MASKED = -1e30
MESH = pl.DeviceIdType.MESH
BF = jnp.bfloat16
F32 = jnp.float32
PLANE = ("context", "tensor")
VMEM_LIMIT = 60 * 2**20


def place():
    return (
        lax.axis_index("shard"),
        lax.axis_index("context"),
        lax.axis_index("tensor") // 2,
        lax.axis_index("tensor") % 2,
    )


def device(z, x, y, c):
    return (z, x, 2 * y + c)


def slot(x, y, c):
    return 4 * x + 2 * y + c


def enter(targets):
    barrier = pltpu.get_barrier_semaphore()
    for target in targets:
        pl.semaphore_signal(barrier, inc=1, device_id=target, device_id_type=MESH)
    pl.semaphore_wait(barrier, len(targets))


def gather_kernel(in_ref, out_ref, local_sem, send, recv):
    z, x, y, c = place()
    rows = in_ref.shape[0]
    half = rows // 2
    to_x, to_y, to_c = device(z, 1 - x, y, c), device(z, x, 1 - y, c), device(z, x, y, 1 - c)
    enter((to_x, to_y, to_c))
    me = slot(x, y, c)

    def remote(index, source, place_in, start, size, target):
        return pltpu.make_async_remote_copy(
            src_ref=source,
            dst_ref=out_ref.at[place_in, pl.ds(start, size)],
            send_sem=send.at[index],
            recv_sem=recv.at[index],
            device_id=target,
            device_id_type=MESH,
        )

    def part(index, owner, start, size, target):
        return remote(index, out_ref.at[owner, pl.ds(start, size)], owner, start, size, target)

    own = pltpu.make_async_copy(in_ref, out_ref.at[me], local_sem)
    own.start()
    from_x, from_y, from_d = slot(1 - x, y, c), slot(x, 1 - y, c), slot(1 - x, 1 - y, c)
    sends = [
        remote(0, in_ref, me, 0, rows, to_x),
        remote(1, in_ref, me, 0, rows, to_y),
        remote(2, in_ref, me, 0, rows, to_c),
    ]
    for copy in sends:
        copy.start()

    def arrived(index, owner, start, size):
        remote(index, in_ref.at[pl.ds(0, size)], owner, start, size, to_x).wait_recv()

    arrived(1, from_y, 0, rows)
    later = [part(3, from_y, 0, half, to_x), part(5, from_y, 0, rows, to_c)]
    for copy in later:
        copy.start()
    sends += later
    arrived(0, from_x, 0, rows)
    later = [part(4, from_x, half, half, to_y), part(6, from_x, 0, rows, to_c)]
    for copy in later:
        copy.start()
    sends += later
    arrived(3, from_d, 0, half)
    later = [part(7, from_d, 0, half, to_c)]
    later[0].start()
    sends += later
    arrived(4, from_d, half, half)
    later = [part(8, from_d, half, half, to_c)]
    later[0].start()
    sends += later
    arrived(2, slot(x, y, 1 - c), 0, rows)
    arrived(5, slot(x, 1 - y, 1 - c), 0, rows)
    arrived(6, slot(1 - x, y, 1 - c), 0, rows)
    arrived(7, slot(1 - x, 1 - y, 1 - c), 0, half)
    arrived(8, slot(1 - x, 1 - y, 1 - c), half, half)
    own.wait()
    for copy in sends:
        copy.wait_send()


def plane_gather(values, ident):
    rows, columns = values.shape
    return pl.pallas_call(
        gather_kernel,
        out_shape=jax.ShapeDtypeStruct((8, rows, columns), values.dtype),
        in_specs=[pl.BlockSpec(memory_space=pl.ANY)],
        out_specs=pl.BlockSpec(memory_space=pl.ANY),
        scratch_shapes=[
            pltpu.SemaphoreType.DMA,
            pltpu.SemaphoreType.DMA((9,)),
            pltpu.SemaphoreType.DMA((9,)),
        ],
        name="plane_gather",
        compiler_params=pltpu.CompilerParams(collective_id=ident, has_side_effects=True),
    )(values)


def scatter_kernel(in_ref, out_ref, mine, core, sums, relay, final, local_sem, send, recv):
    z, x, y, c = place()
    rows = out_ref.shape[0]
    half = rows // 2
    to_x, to_y, to_c = device(z, 1 - x, y, c), device(z, x, 1 - y, c), device(z, x, y, 1 - c)
    enter((to_x, to_y, to_c))
    chips = ((1 - x, 1 - y), (1 - x, y), (x, 1 - y), (x, y))

    def remote(index, source, target_ref, target):
        return pltpu.make_async_remote_copy(
            src_ref=source,
            dst_ref=target_ref,
            send_sem=send.at[index],
            recv_sem=recv.at[index],
            device_id=target,
            device_id_type=MESH,
        )

    sends = []
    loads = []
    for index, (cx, cy) in enumerate(chips):
        copy = remote(index, in_ref.at[slot(cx, cy, 1 - c)], core.at[index], to_c)
        copy.start()
        sends.append(copy)
        load = pltpu.make_async_copy(in_ref.at[slot(cx, cy, c)], mine.at[index], local_sem.at[index])
        load.start()
        loads.append(load)

    low, high = pl.ds(0, half), pl.ds(half, half)

    def pair(index, part):
        return mine[index, part].astype(F32) + core[index, part].astype(F32)

    def forward(index, source, target_ref, target):
        copy = remote(index, source, target_ref, target)
        copy.start()
        sends.append(copy)

    loads[0].wait()
    sends[0].wait_recv()
    sums[0, low] = pair(0, low).astype(BF)
    forward(4, sums.at[0, low], relay.at[0], to_x)
    sums[0, high] = pair(0, high).astype(BF)
    forward(5, sums.at[0, high], relay.at[1], to_y)
    loads[1].wait()
    sends[1].wait_recv()
    sums[1, low] = pair(1, low).astype(BF)
    forward(6, sums.at[1, low], final.at[0, low], to_x)
    loads[2].wait()
    sends[2].wait_recv()
    sums[2, high] = pair(2, high).astype(BF)
    forward(7, sums.at[2, high], final.at[1, high], to_y)
    loads[3].wait()
    sends[3].wait_recv()
    sends[5].wait_recv()
    sums[1, high] = (pair(1, high) + relay[1].astype(F32)).astype(BF)
    forward(8, sums.at[1, high], final.at[0, high], to_x)
    sends[4].wait_recv()
    sums[2, low] = (pair(2, low) + relay[0].astype(F32)).astype(BF)
    forward(9, sums.at[2, low], final.at[1, low], to_y)
    sends[6].wait_recv()
    sends[7].wait_recv()
    sends[8].wait_recv()
    sends[9].wait_recv()
    out_ref[...] = (
        mine[3].astype(F32) + core[3].astype(F32) + final[0].astype(F32) + final[1].astype(F32)
    )
    for copy in sends:
        copy.wait_send()


def plane_scatter(values, ident):
    _, rows, columns = values.shape
    return pl.pallas_call(
        scatter_kernel,
        out_shape=jax.ShapeDtypeStruct((rows, columns), F32),
        in_specs=[pl.BlockSpec(memory_space=pl.ANY)],
        out_specs=pl.BlockSpec(memory_space=pltpu.VMEM),
        scratch_shapes=[
            pltpu.VMEM((4, rows, columns), BF),
            pltpu.VMEM((4, rows, columns), BF),
            pltpu.VMEM((3, rows, columns), BF),
            pltpu.VMEM((2, rows // 2, columns), BF),
            pltpu.VMEM((2, rows, columns), BF),
            pltpu.SemaphoreType.DMA((4,)),
            pltpu.SemaphoreType.DMA((10,)),
            pltpu.SemaphoreType.DMA((10,)),
        ],
        name="plane_scatter",
        compiler_params=pltpu.CompilerParams(
            collective_id=ident, has_side_effects=True, vmem_limit_bytes=VMEM_LIMIT
        ),
    )(values)


def exchange_kernel(in_ref, out_ref, local_sem, send, recv):
    z, x, y, c = place()
    others = [
        (dx, dy, dc) for dx in range(2) for dy in range(2) for dc in range(2) if dx + dy + dc > 0
    ]
    spots = [((x + dx) % 2, (y + dy) % 2, (c + dc) % 2) for dx, dy, dc in others]
    enter([device(z, *spot) for spot in spots])
    me = slot(x, y, c)
    own = pltpu.make_async_copy(in_ref.at[me], out_ref.at[me], local_sem)
    own.start()
    sends = []
    for index, spot in enumerate(spots):
        copy = pltpu.make_async_remote_copy(
            src_ref=in_ref.at[slot(*spot)],
            dst_ref=out_ref.at[me],
            send_sem=send.at[index],
            recv_sem=recv.at[index],
            device_id=device(z, *spot),
            device_id_type=MESH,
        )
        copy.start()
        sends.append(copy)
    own.wait()
    for copy in sends:
        copy.wait()


def plane_exchange(values, ident):
    return pl.pallas_call(
        exchange_kernel,
        out_shape=jax.ShapeDtypeStruct(values.shape, values.dtype),
        in_specs=[pl.BlockSpec(memory_space=pl.ANY)],
        out_specs=pl.BlockSpec(memory_space=pl.ANY),
        scratch_shapes=[
            pltpu.SemaphoreType.DMA,
            pltpu.SemaphoreType.DMA((7,)),
            pltpu.SemaphoreType.DMA((7,)),
        ],
        name="plane_exchange",
        compiler_params=pltpu.CompilerParams(collective_id=ident, has_side_effects=True),
    )(values)


def dots(spec, *operands):
    return jnp.einsum(spec, *operands, preferred_element_type=F32)


def layer_norm(inputs, scaling, offset):
    average = jnp.mean(inputs, axis=-1, keepdims=True)
    centred = inputs - average
    variance = jnp.mean(centred * centred, axis=-1, keepdims=True)
    return centred * lax.rsqrt(variance + EPS) * scaling + offset


def self_forward(query, key, value):
    length = query.shape[0]
    scores = dots("qhd,khd->hqk", query, key) * HEAD_DIM ** (-0.5)
    spots = jnp.arange(length)
    scores = jnp.where((spots[None, :] <= spots[:, None])[None], scores, MASKED)
    top = jnp.max(scores, axis=-1, keepdims=True)
    weights = jnp.exp(scores - top)
    total = jnp.sum(weights, axis=-1, keepdims=True)
    mix = dots("hqk,khd->qhd", (weights / total).astype(BF), value)
    return mix.astype(BF), (top + jnp.log(total))[..., 0]


def self_backward(query, key, value, grad_mix, log_total):
    length = query.shape[0]
    scores = dots("qhd,khd->hqk", query, key) * HEAD_DIM ** (-0.5)
    spots = jnp.arange(length)
    scores = jnp.where((spots[None, :] <= spots[:, None])[None], scores, MASKED)
    weights = jnp.exp(scores - log_total[..., None])
    grad_weights = dots("qhd,khd->hqk", grad_mix, value)
    inner = jnp.sum(weights * grad_weights, axis=-1, keepdims=True)
    grad_scores = (weights * (grad_weights - inner)).astype(BF)
    grad_query = dots("hqk,khd->qhd", grad_scores, key) * HEAD_DIM ** (-0.5)
    grad_key = dots("hqk,qhd->khd", grad_scores, query) * HEAD_DIM ** (-0.5)
    grad_value = dots("hqk,qhd->khd", weights.astype(BF), grad_mix)
    return grad_query.astype(BF), grad_key.astype(BF), grad_value.astype(BF)


def on_device(
    frames,
    text_states,
    cotangent,
    norm_gain,
    norm_bias,
    self_qkv,
    self_out,
    cross_qkv,
    cross_out,
    mlp_up,
    mlp_down,
):
    clips, rows, width = frames.shape
    context = lax.axis_index("context")
    depth = self_qkv.shape[1]
    slices = width // depth
    columns = self_qkv.shape[2] // 2
    heads = columns // HEAD_DIM
    block = clips * rows
    texts = text_states.shape[1]

    def half(weight):
        size = weight.shape[-1] // 2
        return lax.dynamic_slice_in_dim(weight, context * size, size, weight.ndim - 1)

    def over_shard(weight, tiled=True):
        return lax.all_gather(weight, "shard", axis=0, tiled=tiled)

    qkv_part = half(self_qkv)
    w_qkv = over_shard(jnp.concatenate([qkv_part[0], qkv_part[1], qkv_part[2]], axis=-1))
    cross_part = half(cross_qkv)
    side = jnp.stack(
        [half(self_out), cross_part[0], half(cross_out), cross_part[1], cross_part[2]]
    )
    w_side = over_shard(side.transpose(0, 2, 1), tiled=False).transpose(1, 2, 0, 3)
    w_side = w_side.reshape(5, columns, width)
    w_up = over_shard(half(mlp_up))
    w_down = over_shard(half(mlp_down))

    stream_zero = frames.astype(F32)
    norm_one, norm_one_back = jax.vjp(layer_norm, stream_zero, norm_gain[0], norm_bias[0])
    all_one = plane_gather(norm_one.astype(BF).reshape(block, width), 0)
    flat_one = all_one.reshape(8 * block, width)
    qkv = dots("rd,de->re", flat_one, w_qkv).astype(BF)

    def by_clip(values):
        values = values.reshape(8, clips, rows, columns).transpose(1, 0, 2, 3)
        return values.reshape(clips, 8 * rows, heads, HEAD_DIM)

    def by_owner(values):
        values = values.reshape(clips, 8, rows, columns).transpose(1, 0, 2, 3)
        return values.reshape(8, block, columns)

    query, key, value = (by_clip(qkv[:, j * columns : (j + 1) * columns]) for j in range(3))
    mix, self_log = lax.map(lambda a: self_forward(*a), (query, key, value))
    mix = by_owner(mix)
    my_mix = plane_exchange(mix, 1)

    plane_w = plane_gather(w_side[:3].reshape(3 * columns, width), 2)
    plane_w = plane_w.reshape(8, 3, columns, width)
    w_out, w_query, w_cross = plane_w[:, 0], plane_w[:, 1], plane_w[:, 2]
    branch_one = dots("bre,bed->rd", my_mix, w_out).reshape(clips, rows, width)
    stream_one = stream_zero + branch_one
    norm_two, norm_two_back = jax.vjp(layer_norm, stream_one, norm_gain[1], norm_bias[1])
    low_two = norm_two.astype(BF)
    cross_q = dots("cfd,bed->cfbe", low_two, w_query).astype(BF)
    text_part = dots("cnd,ted->tcne", text_states, w_side[3:]).astype(BF)
    text_all = plane_gather(text_part.reshape(2 * clips * texts, columns), 3)
    text_all = text_all.reshape(8, 2, clips, texts, heads, HEAD_DIM)
    text_k, text_v = text_all[:, 0], text_all[:, 1]
    cross_q = cross_q.reshape(clips, rows, 8, heads, HEAD_DIM)
    scale = HEAD_DIM ** (-0.5)
    scores = dots("cfbhd,bcnhd->cbhfn", cross_q, text_k) * scale
    top = jnp.max(scores, axis=-1, keepdims=True)
    cross_full = jnp.exp(scores - top)
    cross_full = cross_full / jnp.sum(cross_full, axis=-1, keepdims=True)
    cross_probs = cross_full.astype(BF)
    cross_mix = dots("cbhfn,bcnhd->cfbhd", cross_probs, text_v).astype(BF)
    cross_mix = cross_mix.reshape(clips, rows, 8, columns)
    branch_two = dots("cfbe,bed->cfd", cross_mix, w_cross)
    stream_two = stream_one + branch_two

    norm_three, norm_three_back = jax.vjp(layer_norm, stream_two, norm_gain[2], norm_bias[2])
    all_three = plane_gather(norm_three.astype(BF).reshape(block, width), 4)
    flat_three = all_three.reshape(8 * block, width)
    pre_act = dots("rd,dh->rh", flat_three, w_up)
    hidden, gelu_back = jax.vjp(partial(jax.nn.gelu, approximate=False), pre_act)
    hidden_low = hidden.astype(BF)
    part_three = dots("rh,dh->rd", hidden_low, w_down).astype(BF)
    branch_three = plane_scatter(part_three.reshape(8, block, width), 5)
    branch_three = branch_three.reshape(clips, rows, width)
    stream_out = stream_two + branch_three
    squares = jnp.stack(
        [
            jnp.sum(stream_out * stream_out),
            jnp.sum(branch_one * branch_one),
            jnp.sum(branch_two * branch_two),
            jnp.sum(branch_three * branch_three),
        ]
    )

    flat_grad = plane_gather(cotangent.reshape(block, width), 6).reshape(8 * block, width)
    grad_hidden = dots("rd,dh->rh", flat_grad, w_down)
    grad_pre = gelu_back(grad_hidden)[0].astype(BF)
    part_norm = dots("rh,dh->rd", grad_pre, w_up).astype(BF)
    grad_normed = plane_scatter(part_norm.reshape(8, block, width), 7)

    def to_shard(part):
        return lax.psum_scatter(part.astype(BF), "shard", scatter_dimension=0, tiled=True)

    grad_down = to_shard(dots("rd,rh->dh", flat_grad, hidden_low))
    grad_up = to_shard(dots("rd,rh->dh", flat_three, grad_pre))
    grad_inner, gain_three, shift_three = norm_three_back(grad_normed.reshape(clips, rows, width))
    grad_two = cotangent.astype(F32) + grad_inner

    grad_low = grad_two.astype(BF)
    grad_cross_mix = dots("cfd,bed->cfbe", grad_low, w_cross).astype(BF)
    w_grad_cross = dots("cfd,cfbe->bed", grad_low, cross_mix)
    grad_heads = grad_cross_mix.reshape(clips, rows, 8, heads, HEAD_DIM)
    cross_dp = dots("cfbhd,bcnhd->cbhfn", grad_heads, text_v)
    inner = jnp.sum(cross_full * cross_dp, axis=-1, keepdims=True)
    grad_scores = (cross_full * (cross_dp - inner)).astype(BF)
    grad_cq = (dots("cbhfn,bcnhd->cfbhd", grad_scores, text_k) * scale).astype(BF)
    grad_text_k = dots("cbhfn,cfbhd->bcnhd", grad_scores, cross_q) * scale
    grad_text_v = dots("cbhfn,cfbhd->bcnhd", cross_probs, grad_heads)
    grad_cq = grad_cq.reshape(clips, rows, 8, columns)
    w_grad_query = dots("cfd,cfbe->bed", low_two, grad_cq)
    grad_normed = dots("cfbe,bed->cfd", grad_cq, w_query)
    grad_inner, gain_two, shift_two = norm_two_back(grad_normed)
    grad_one = grad_two + grad_inner

    grad_low = grad_one.astype(BF).reshape(block, width)
    grad_mix = dots("rd,bed->bre", grad_low, w_out).astype(BF)
    w_grad_out = dots("rd,bre->bed", grad_low, my_mix)
    grad_mix = by_clip(plane_exchange(grad_mix, 8))

    text_grads = jnp.stack([grad_text_k, grad_text_v], axis=1).astype(BF)
    text_grads = plane_scatter(text_grads.reshape(8, 2 * clips * texts, columns), 9)
    text_grads = text_grads.reshape(2, clips, texts, columns)
    text_grads_low = text_grads.astype(BF)
    w_grad_text = dots("cnd,tcne->ted", text_states, text_grads_low)
    grad_text = dots("tcne,ted->cnd", text_grads_low, w_side[3:])
    grad_text = grad_text.reshape(clips, 8, texts // 8, width).transpose(1, 0, 2, 3).astype(BF)
    grad_text = plane_scatter(grad_text.reshape(8, clips * texts // 8, width), 10)
    grad_text = grad_text.reshape(clips, texts // 8, width)

    grads = lax.map(lambda a: self_backward(*a), (query, key, value, grad_mix, self_log))
    grad_qkv = jnp.concatenate([by_owner(g) for g in grads], axis=-1).reshape(8 * block, -1)
    part_norm = dots("re,de->rd", grad_qkv, w_qkv).astype(BF)
    grad_w_qkv = to_shard(dots("rd,re->de", flat_one, grad_qkv))
    grad_normed = plane_scatter(part_norm.reshape(8, block, width), 11)
    grad_inner, gain_one, shift_one = norm_one_back(grad_normed.reshape(clips, rows, width))
    grad_frames = grad_one + grad_inner

    part_side = jnp.stack([w_grad_out, w_grad_query, w_grad_cross], axis=1).astype(BF)
    part_side = plane_scatter(part_side.reshape(8, 3 * columns, width), 12)
    part_side = jnp.concatenate([part_side.reshape(3, columns, width), w_grad_text], axis=0)
    part_side = part_side.reshape(5, columns, slices, depth).transpose(2, 0, 1, 3)
    grad_side = to_shard(part_side)[0]

    def whole(values):
        return lax.all_gather(values, "context", axis=values.ndim - 1, tiled=True).astype(F32)

    grad_up, grad_down = whole(grad_up), whole(grad_down)
    grad_self = jnp.stack([grad_w_qkv[:, j * columns : (j + 1) * columns] for j in range(3)])
    grad_side = grad_side.transpose(0, 2, 1)
    grad_all = whole(jnp.concatenate([grad_self, grad_side], axis=0))

    gains = jnp.stack([gain_one, gain_two, gain_three])
    shifts = jnp.stack([shift_one, shift_two, shift_three])
    gains, shifts, squares = lax.psum((gains, shifts, squares), ("shard",) + PLANE)
    start = lax.axis_index("shard") * depth
    grad_gain = lax.dynamic_slice_in_dim(gains, start, depth, 1)
    grad_shift = lax.dynamic_slice_in_dim(shifts, start, depth, 1)
    entries = float(clips * rows * width * lax.axis_size(("shard",) + PLANE))
    return (
        stream_out.astype(BF),
        grad_frames,
        grad_text,
        grad_gain,
        grad_shift,
        grad_all[:3],
        grad_all[3],
        jnp.stack([grad_all[4], grad_all[6], grad_all[7]]),
        grad_all[5],
        grad_up,
        grad_down,
        jnp.sqrt(squares / entries),
    )


def solution(mesh):
    rows = P("shard", PLANE, None)
    stack = P(None, "shard", "tensor")
    flat = P("shard", "tensor")
    return jax.shard_map(
        on_device,
        mesh=mesh,
        in_specs=(rows, P("shard"), rows, P(), P(), stack, flat, stack, flat, flat, flat),
        out_specs=(
            (rows, rows, rows, P(None, "shard"), P(None, "shard"))
            + (stack, flat, stack, flat, flat, flat, P())
        ),
        check_vma=False,
    )
```

time: 2170 us -> 893 us (0.41)
  waiting for transfers between devices: 1770 us -> 45.8 us
  Pallas kernels: 0 us -> 390 us
  local copies, waits for them, and re-layouts: 55.1 us -> 123 us
    reduce_scatter x15 -> x2, waiting for transfers between devices: 1060 us -> 17.1 us  [to_shard(): lax.psum_scatter(part.astype(BF), 'shard', scatter_dimension=0, tiled=True)]
    all_gather x14 -> x7, waiting for transfers between devices: 525 us -> 27.9 us  [the longest x3 27.9 us: whole(): lax.all_gather(values, 'context', axis=values.ndim - 1, tiled=True)]
    pallas_call x0 -> x13, Pallas kernels: none -> 390 us  [the longest x6 182 us: plane_scatter(): pl.pallas_call(scatter_kernel, out_shape=jax.ShapeDtypeStruct((rows, colu...]
    psum x1 -> x0, waiting for transfers between devices: 180 us -> none  [on_device(): lax.psum((part_sqkv, part_sout, part_cqkv, part_cout, part_up, part_down)...]
    unnamed x117 -> x216, local copies, waits for them, and re-layouts: 25 us -> 45.6 us
    dot_general x49 -> x40, matrix products: 195 us -> 187 us  [dots(): return jnp.einsum(spec, *operands, preferred_element_type=F32)]
  transfers between devices with their start and end apart: 30 -> 11, of which waited for: 29 -> 2; matrix products, arithmetic and copies ran while one was open for 9% -> 37% of each run, Pallas kernels for 0% -> 44%
where the time goes in v1:
time: 893 us; the launch traced here: 885 us
  Pallas kernels  390 us (44%)
  matrix products  188 us (21%)
  local copies, waits for them, and re-layouts  123 us (14%)
  other arithmetic  78.2 us (9%)
  waiting for transfers between devices  45.8 us (5%)
  blocking collectives  42.1 us (5%)
  between operations  15.8 us (2%)
    dot_general x40, matrix products, dots(): return jnp.einsum(spec, *operands, preferred_element_type=F32)  187 us
    pallas_call x6, Pallas kernels, plane_scatter(): pl.pallas_call(scatter_kernel, out_shape=jax.ShapeDtypeStruct((rows, colu...  182 us
    pallas_call x5, Pallas kernels, plane_gather(): pl.pallas_call(gather_kernel, out_shape=jax.ShapeDtypeStruct((8, rows, co...  177 us
    unnamed x216, local copies, waits for them, and re-layouts  45.6 us
    psum x1, blocking collectives, on_device(): lax.psum((gains, shifts, squares), ('shard',) + PLANE)  42.1 us
    pallas_call x2, Pallas kernels, plane_exchange(): pl.pallas_call(exchange_kernel, out_shape=jax.ShapeDtypeStruct(values.sha...  30.4 us
    all_gather x3, waiting for transfers between devices, whole(): lax.all_gather(values, 'context', axis=values.ndim - 1, tiled=True)  27.9 us
  transfers between devices with their start and end apart: 11, of which 2 were waited for; matrix products, arithmetic and copies ran while one was open for 37% of the time, Pallas kernels for 44%

profile of v1, /device:TPU:0, one launch (start us, length us, event | category | flops | bytes accessed | tf_op | source)
XLA Modules:
  0.0 885.0 jit_solution(8958909180434445639)
XLA Ops:
  17.7 34.4 %plane_gather.5 = bf16[8,256,1536]{2,1,0:T(8,128)(2,1)} custom-call(bf16[256,1536]{1,0:T(8,128)(2,1)} %bitcast.496), custom_call_target="tpu_custom_call" | custom-call | tf_op jit(solution)/shard_map/plane_gather/pallas_call | solution.py:109
  52.2 32.4 %plane_gather.9 = bf16[8,256,1536]{2,1,0:T(8,128)(2,1)} custom-call(bf16[256,1536]{1,0:T(8,128)(2,1)} %bitcast.472), custom_call_target="tpu_custom_call" | custom-call | tf_op jit(solution)/shard_map/plane_gather/pallas_call | solution.py:109
  84.6 7.3 convolution_convert_fusion.5
  101.3 41.1 %while.26 = (s32[]{:T(128)}, bf16[2,1024,3,64]{1,3,2,0:T(8,128)(2,1)S(1)}, f32[2,3,1024]{2,1,0:T(4,128)S(1)}, bf16[2,1024,3,64]{1,3,2,0:T(8,128)(2,1)S(1)}, bf16...) while((s32[]{:T(128)}, bf16[2,1024,3,64]{1,3,2,0:T(8,128)(2,1)S(1)}, ...), condition=%wide.region_5.6_spmd, body=%wide.region_2.5_spmd.sunk | while | flops 844297216 | bytes 43636824 | solution.py:355
  101.7 6.0 fusion.221
  107.6 7.3 fusion.222
  114.9 6.8 fusion.223
  122.1 6.1 fusion.221
  128.3 7.3 fusion.222
  135.6 6.9 fusion.223
  146.5 15.2 %plane_exchange.2 = bf16[8,256,192]{2,1,0:T(8,128)(2,1)} custom-call(bf16[8,256,192]{2,1,0:T(8,128)(2,1)} %bitcast.491), custom_call_target="tpu_custom_call" | custom-call | tf_op jit(solution)/shard_map/plane_exchange/pallas_call | solution.py:247
  161.8 4.1 copy.289
  170.1 11.9 %plane_gather.7 = bf16[8,256,192]{2,1,0:T(8,128)(2,1)} custom-call(bf16[256,192]{1,0:T(8,128)(2,1)} %bitcast.531), custom_call_target="tpu_custom_call" | custom-call | tf_op jit(solution)/shard_map/plane_gather/pallas_call | solution.py:109
  188.0 65.4 %plane_gather.6 = bf16[8,576,1536]{2,1,0:T(8,128)(2,1)} custom-call(bf16[576,1536]{1,0:T(8,128)(2,1)} %bitcast.479), custom_call_target="tpu_custom_call" | custom-call | tf_op jit(solution)/shard_map/plane_gather/pallas_call | solution.py:109
  253.4 4.8 fusion.162
  258.6 4.1 fusion.115
  266.6 4.9 fusion.161
  273.8 33.2 %plane_gather.8 = bf16[8,256,1536]{2,1,0:T(8,128)(2,1)} custom-call(bf16[256,1536]{1,0:T(8,128)(2,1)} %bitcast.508), custom_call_target="tpu_custom_call" | custom-call | tf_op jit(solution)/shard_map/plane_gather/pallas_call | solution.py:109
  307.0 21.6 %multiply_convert_fusion.1 = (bf16[2048,768]{1,0:T(8,128)(2,1)S(1)}, f32[2048,768]{1,0:T(8,128)}, f32[2048,768]{1,0:T(8,128)}) fusion(bf16[2048,1536]{1,0:T(8,128)(2,1)} %bitcast.485, bf16[1536,768]{1,0:T(8,128)(2,1)} %all-gather.11.cloned.1.call-done), kind=kOutput, calls=%fused_computation.82 | convolution fusion | flops 4934074368 | bytes 24379392 | tf_op jit(solution)/shard_map/rd,dh->rh/dot_general | solution.py:263
  330.3 6.6 fusion.85
  336.9 11.7 %fusion.66 = bf16[2048,768]{1,0:T(8,128)(2,1)S(1)} fusion(f32[2048,768]{1,0:T(8,128)} %get-tuple-element.198, f32[2048,768]{1,0:T(8,128)} %get-tuple-element.227, bf16[2048,1536]{1,0:T(8,128)(2,1)} %bitcast.481, bf16[1536,768]{1,0:T(8,128)(2,1)} %all-gather.13.cloned.1.call-done), kind=kOutput, calls=%fused_computation.80 | convolution fusion | flops 4853858304 | bytes 24379392 | tf_op jit(solution)/shard_map/rd,dh->rh/dot_general | solution.py:263
  350.3 9.4 %convolution_convert_fusion.4 = bf16[1536,768]{1,0:T(8,128)(2,1)} fusion(bf16[2048,1536]{1,0:T(8,128)(2,1)} %bitcast.486, bf16[2048,768]{1,0:T(8,128)(2,1)S(1)} %fusion.66), kind=kOutput, calls=%fused_computation.114 | convolution fusion | flops 4833017856 | bytes 11796480 | tf_op jit(solution)/shard_map/rd,rh->dh/dot_general | solution.py:263
  363.7 9.0 %convolution_convert_fusion = bf16[2048,1536]{1,0:T(8,128)(2,1)} fusion(bf16[2048,768]{1,0:T(8,128)(2,1)} %copy-done.100, bf16[1536,768]{1,0:T(8,128)(2,1)S(1)} %copy-done.96), kind=kOutput, calls=%fused_computation.69 | convolution fusion | flops 4834983936 | bytes 11796480 | tf_op jit(solution)/shard_map/rh,dh->rd/dot_general | solution.py:263
  372.7 32.6 %plane_scatter.7 = f32[256,1536]{1,0:T(8,128)} custom-call(bf16[8,256,1536]{2,1,0:T(8,128)(2,1)} %bitcast.488), custom_call_target="tpu_custom_call" | custom-call | tf_op jit(solution)/shard_map/plane_scatter/pallas_call | solution.py:197
  405.3 9.2 %convolution_convert_fusion.1 = bf16[2048,1536]{1,0:T(8,128)(2,1)} fusion(bf16[2048,768]{1,0:T(8,128)(2,1)} %copy-done.101, bf16[1536,768]{1,0:T(8,128)(2,1)S(1)} %copy-done.97), kind=kOutput, calls=%fused_computation.70 | convolution fusion | flops 4834983936 | bytes 11796480 | tf_op jit(solution)/shard_map/rh,dh->rd/dot_general | solution.py:263
  414.5 32.3 %plane_scatter.6 = f32[256,1536]{1,0:T(8,128)} custom-call(bf16[8,256,1536]{2,1,0:T(8,128)(2,1)} %bitcast.489), custom_call_target="tpu_custom_call" | custom-call | tf_op jit(solution)/shard_map/plane_scatter/pallas_call | solution.py:197
  454.4 4.1 fusion.114
  461.5 4.8 fusion.158
  470.2 3.8 fusion.116
  475.3 15.1 %plane_exchange.3 = bf16[8,256,192]{2,1,0:T(8,128)(2,1)} custom-call(bf16[8,256,192]{2,1,0:T(8,128)(2,1)} %bitcast.492), custom_call_target="tpu_custom_call" | custom-call | tf_op jit(solution)/shard_map/plane_exchange/pallas_call | solution.py:247
  495.5 49.3 %while.27 = (s32[]{:T(128)}, bf16[2,1024,3,64]{1,3,2,0:T(8,128)(2,1)}, bf16[2,1024,3,64]{1,3,2,0:T(8,128)(2,1)}, bf16[2,1024,3,64]{1,3,2,0:T(8,128)(2,1)}, bf16[...) while((s32[]{:T(128)}, ...), condition=%wide.region_19.20_spmd, body=%wide.region_17.19_spmd.sunk | while | flops 2062480384 | bytes 121472288 | solution.py:447
  501.8 7.1 multiply_reduce_fusion.13
  509.0 7.0 multiply_convert_fusion.6
  526.1 7.1 multiply_reduce_fusion.13
  533.3 7.1 multiply_convert_fusion.6
  554.6 8.1 bitcast_convert_fusion.2
  562.6 4.0 copy.236
  576.6 10.3 %plane_scatter.9 = f32[256,192]{1,0:T(8,128)} custom-call(bf16[8,256,192]{2,1,0:T(8,128)(2,1)} %reshape.387.in_ref), custom_call_target="tpu_custom_call" | custom-call | tf_op jit(solution)/shard_map/plane_scatter/pallas_call | solution.py:197
  599.1 5.6 copy.198
  604.7 66.3 %plane_scatter.11 = f32[576,1536]{1,0:T(8,128)} custom-call(bf16[8,576,1536]{2,1,0:T(8,128)(2,1)} %bitcast.458), custom_call_target="tpu_custom_call" | custom-call | tf_op jit(solution)/shard_map/plane_scatter/pallas_call | solution.py:197
  679.1 4.7 maximum_bitcast_fusion
  696.3 7.2 convolution_convert_fusion.2
  706.7 8.5 plane_scatter.10
  715.4 32.3 %plane_scatter.8 = f32[256,1536]{1,0:T(8,128)} custom-call(bf16[8,256,1536]{2,1,0:T(8,128)(2,1)} %bitcast.487), custom_call_target="tpu_custom_call" | custom-call | tf_op jit(solution)/shard_map/plane_scatter/pallas_call | solution.py:197
  752.4 17.1 %reduce-scatter.9.cloned.1.call-done = bf16[1,5,192,384]{3,1,2,0:T(8,128)(2,1)} async-done(((bf16[4,5,192,384]{3,1,2,0:T(8,128)(2,1)}), bf16[1,5,192,384]{3,1,2,0:T(8,128)(2,1)}) %reduce-scatter.9.cloned.1.call-update) | async-done | bytes 737296 | tf_op jit(solution)/shard_map/reduce_scatter | solution.py:409
  778.2 42.1 %all-reduce = (f32[3,1536]{1,0:T(4,128)S(1)}, f32[3,1536]{1,0:T(4,128)S(1)}, f32[4]{0:T(128)S(1)}) all-reduce(f32[3,1536]{1,0:T(4,128)S(1)} %pad_maximum_fusion.5, f32[3,1536]{1,0:T(4,128)S(1)} %pad_maximum_fusion.6, f32[4]{0:T(128)S(1)} %pad_maximum_fusion.7), channel_id=1, replica_groups=mesh['shard'=4,'context'=2,'tensor'=4] {'shard','context','tensor'}, use_global_device_ids=true, to_apply=%region_25.26 | all-reduce | flops 9220 | bytes 73760 | tf_op jit(solution)/shard_map/psum | solution.py:471
  830.8 27.8 %all-gather.15.cloned.1.call-done = bf16[8,384,384]{1,0,2:T(8,128)(2,1)} async-done(((bf16[8,384,192]{1,0,2:T(8,128)(2,1)}), bf16[8,384,384]{1,0,2:T(8,128)(2,1)}) %all-gather.15.cloned.1.call-update) | async-done | bytes 2359312 | tf_op jit(solution)/shard_map/all_gather | solution.py:462
  862.1 4.1 copy.205
  (412 shorter events, 183.7 us)
Async XLA Ops:
  7.2 77.4 %all-gather.9.cloned.1.call-start = ((), (), s32[]{:S(2)}) async-start(), calls=%async_computation.4 | async-start | bytes 2457600 | tf_op jit(solution)/shard_map/all_gather | solution.py:327
  9.8 152.0 %all-gather.21.cloned.1.call-start = ((), (), s32[]{:S(2)}) async-start(), calls=%async_computation.12 | async-start | bytes 3686400 | tf_op jit(solution)/shard_map/all_gather | solution.py:327
  12.1 295.0 %all-gather.11.cloned.1.call-start = ((), (), s32[]{:S(2)}) async-start(), calls=%async_computation.5 | async-start | bytes 2949120 | tf_op jit(solution)/shard_map/all_gather | solution.py:327
  13.0 323.9 %all-gather.13.cloned.1.call-start = ((), (), s32[]{:S(2)}) async-start(), calls=%async_computation.6 | async-start | bytes 2949120 | tf_op jit(solution)/shard_map/all_gather | solution.py:327
  14.0 669.9 %reduce-scatter.11.cloned.1.call-start = ((), (), s32[]{:S(2)}) async-start(), calls=%async_computation.9 | async-start | bytes 2949120 | tf_op jit(solution)/shard_map/reduce_scatter | solution.py:409
  14.2 37.9 %copy-start.78 = (f32[2,128]{1,0:T(2,128)}, f32[2,128]{1,0:T(2,128)S(1)}, u32[]{:S(2)}) copy-start(f32[2,128]{1,0:T(2,128)S(1)} %broadcast_multiply_fusion.2) | copy-start | bytes 3076
  15.2 37.0 %copy-start.83 = (f32[2,128]{1,0:T(2,128)}, f32[2,128]{1,0:T(2,128)S(1)}, u32[]{:S(2)}) copy-start(f32[2,128]{1,0:T(2,128)S(1)} %fusion.144) | copy-start | bytes 3076
  15.8 36.3 %copy-start.69 = (f32[1536]{0:T(1024)}, f32[1536]{0:T(1024)S(1)}, u32[]{:S(2)}) copy-start(f32[1536]{0:T(1024)S(1)} %get-tuple-element.157) | copy-start | bytes 18436
  142.5 19.3 %copy-start.8 = (bf16[2,1024,3,64]{1,3,2,0:T(8,128)(2,1)}, bf16[2,1024,3,64]{1,3,2,0:T(8,128)(2,1)S(1)}, u32[]{:S(2)}) copy-start(bf16[2,1024,3,64]{1,3,2,0:T(8,128)(2,1)S(1)} %get-tuple-element.419) | copy-start | bytes 2359300
  142.5 19.3 %copy-start.10 = (bf16[2,1024,3,64]{1,3,2,0:T(8,128)(2,1)}, bf16[2,1024,3,64]{1,3,2,0:T(8,128)(2,1)S(1)}, u32[]{:S(2)}) copy-start(bf16[2,1024,3,64]{1,3,2,0:T(8,128)(2,1)S(1)} %get-tuple-element.420) | copy-start | bytes 2359300
  142.5 19.3 %copy-start.23 = (bf16[2,1024,3,64]{1,3,2,0:T(8,128)(2,1)}, bf16[2,1024,3,64]{1,3,2,0:T(8,128)(2,1)S(1)}, u32[]{:S(2)}) copy-start(bf16[2,1024,3,64]{1,3,2,0:T(8,128)(2,1)S(1)} %get-tuple-element.424) | copy-start | bytes 2359300
  142.5 19.3 %copy-start.71 = (f32[2,3,1024]{2,1,0:T(4,128)}, f32[2,3,1024]{2,1,0:T(4,128)S(1)}, u32[]{:S(2)}) copy-start(f32[2,3,1024]{2,1,0:T(4,128)S(1)} %get-tuple-element.360) | copy-start | bytes 73732
  187.9 74.7 %copy-start.46 = (bf16[8,1,2,64,3,64]{5,3,4,0,2,1:T(8,128)(2,1)}, bf16[8,1,2,64,3,64]{5,3,4,0,2,1:T(8,128)(2,1)S(1)}, u32[]{:S(2)}) copy-start(bf16[8,1,2,64,3,64]{5,3,4,0,2,1:T(8,128)(2,1)S(1)} %copy.246) | copy-start | bytes 1179652
  188.0 65.5 %copy-start.6 = (bf16[2,128,1536]{2,1,0:T(8,128)(2,1)S(1)}, bf16[2,128,1536]{2,1,0:T(8,128)(2,1)}, u32[]{:S(2)}) copy-start(bf16[2,128,1536]{2,1,0:T(8,128)(2,1)} %param.15) | copy-start | bytes 2359300
  253.4 5.1 copy-start.76
  253.4 5.1 copy-start.94
  258.2 8.3 copy-start.17
  258.2 209.2 %copy-start.85 = (f32[2,128]{1,0:T(2,128)}, f32[2,128]{1,0:T(2,128)S(1)}, u32[]{:S(2)}) copy-start(f32[2,128]{1,0:T(2,128)S(1)} %broadcast_multiply_fusion.1) | copy-start | bytes 3076
  258.6 208.9 %copy-start.89 = (f32[2,128]{1,0:T(2,128)}, f32[2,128]{1,0:T(2,128)S(1)}, u32[]{:S(2)}) copy-start(f32[2,128]{1,0:T(2,128)S(1)} %fusion.145) | copy-start | bytes 3076
  266.1 5.3 copy-start.31
  266.5 4.9 copy-start.57
  266.6 6.1 copy-start.73
  266.6 6.1 copy-start.82
  273.8 56.5 %slice-start = ((s8[6291456]{0:T(1024)(128)(4,1)}), s8[2097152]{0:T(1024)(128)(4,1)S(1)}, s32[]{:S(2)}) async-start(s8[6291456]{0:T(1024)(128)(4,1)} %bitcast.482), calls=%async_computation.15 | async-start | bytes 4194304
  307.0 23.3 %slice-start.1 = ((s8[6291456]{0:T(1024)(128)(4,1)}), s8[4194304]{0:T(1024)(128)(4,1)S(1)}, s32[]{:S(2)}) async-start(s8[6291456]{0:T(1024)(128)(4,1)} %bitcast.482), calls=%async_computation.16 | async-start | bytes 8388608
  350.3 9.4 %copy-start.52 = (bf16[1536,768]{0,1:T(8,128)(2,1)S(1)}, bf16[1536,768]{0,1:T(8,128)(2,1)}, u32[]{:S(2)}) copy-start(bf16[1536,768]{0,1:T(8,128)(2,1)} %fusion.85) | copy-start | bytes 7077892
  362.1 341.5 %reduce-scatter.15.cloned.1.call-start = ((), (), s32[]{:S(2)}) async-start(), calls=%async_computation.14 | async-start | bytes 2949120
  372.7 32.6 %copy-start.97 = (bf16[1536,768]{1,0:T(8,128)(2,1)S(1)}, bf16[1536,768]{1,0:T(8,128)(2,1)}, u32[]{:S(2)}) copy-start(bf16[1536,768]{1,0:T(8,128)(2,1)} %all-gather.13.cloned.1.call-done) | copy-start | bytes 7077892
  414.5 32.4 %copy-start.3 = (f32[256,1536]{1,0:T(8,128)S(1)}, f32[256,1536]{1,0:T(8,128)}, u32[]{:S(2)}) copy-start(f32[256,1536]{1,0:T(8,128)} %plane_scatter.7) | copy-start | bytes 4718596
  492.4 257.5 %reduce-scatter.13.cloned.1.call-start = ((), (), s32[]{:S(2)}) async-start(), calls=%async_computation.13 | async-start | bytes 2457600
  501.8 7.2 copy-start.39
  509.0 7.0 copy-start.40
  526.1 7.2 copy-start.39
  533.3 7.1 copy-start.40
  552.3 10.3 %copy-start.29 = (bf16[48,8,8,128]{3,2,1,0:T(8,128)(2,1)}, bf16[48,8,8,128]{3,2,1,0:T(8,128)(2,1)S(1)}, u32[]{:S(2)}) copy-start(bf16[48,8,8,128]{3,2,1,0:T(8,128)(2,1)S(1)} %copy.256) | copy-start | bytes 2359300
  566.7 202.8 %reduce-scatter.9.cloned.1.call-start = ((), (), s32[]{:S(2)}) async-start(), calls=%async_computation.7 | async-start | bytes 5898240 | tf_op jit(solution)/shard_map/reduce_scatter | solution.py:409
  586.8 5.5 copy-start.58
  586.8 5.5 copy-start.60
  683.8 141.2 %all-gather.17.cloned.1.call-start = ((), (), s32[]{:S(2)}) async-start(), calls=%async_computation.10 | async-start | bytes 1769472 | tf_op jit(solution)/shard_map/all_gather | solution.py:462
  684.6 143.5 %all-gather.19.cloned.1.call-start = ((), (), s32[]{:S(2)}) async-start(), calls=%async_computation.11 | async-start | bytes 1769472 | tf_op jit(solution)/shard_map/all_gather | solution.py:462
  703.6 11.7 %copy-start.93 = (f32[1536]{0:T(1024)S(1)}, f32[1536]{0:T(1024)}, u32[]{:S(2)}) copy-start(f32[1536]{0:T(1024)} %get-tuple-element.152) | copy-start | bytes 18436
  703.6 11.7 %copy-start.81 = (f32[1536]{0:T(1024)S(1)}, f32[1536]{0:T(1024)}, u32[]{:S(2)}) copy-start(f32[1536]{0:T(1024)} %get-tuple-element.147) | copy-start | bytes 18436
  705.7 152.9 %all-gather.15.cloned.1.call-start = ((), (), s32[]{:S(2)}) async-start(), calls=%async_computation.8 | async-start | bytes 3538944 | tf_op jit(solution)/shard_map/all_gather | solution.py:462
  715.3 34.0 %copy-start.7 = (bf16[2,128,1536]{2,1,0:T(8,128)(2,1)S(1)}, bf16[2,128,1536]{2,1,0:T(8,128)(2,1)}, u32[]{:S(2)}) copy-start(bf16[2,128,1536]{2,1,0:T(8,128)(2,1)} %param.15) | copy-start | bytes 2359300
  715.3 34.0 %copy-start.70 = (f32[1536]{0:T(1024)S(1)}, f32[1536]{0:T(1024)}, u32[]{:S(2)}) copy-start(f32[1536]{0:T(1024)} %copy-done.69) | copy-start | bytes 18436
  715.4 34.0 %copy-start.79 = (f32[2,128]{1,0:T(2,128)S(1)}, f32[2,128]{1,0:T(2,128)}, u32[]{:S(2)}) copy-start(f32[2,128]{1,0:T(2,128)} %copy-done.78) | copy-start | bytes 3076
  752.1 21.0 %copy-start.84 = (f32[2,128]{1,0:T(2,128)S(1)}, f32[2,128]{1,0:T(2,128)}, u32[]{:S(2)}) copy-start(f32[2,128]{1,0:T(2,128)} %copy-done.83) | copy-start | bytes 3076
  873.3 5.0 copy-start.1
  (73 other events, 168.3 us)
Sparse Core Ops, SparseCore 0:
  10.2 46.2 all-gather.8
  58.6 59.0 all-gather.20
  119.9 49.1 all-gather.10
  171.1 49.2 all-gather.12
  362.2 48.2 reduce-scatter.10
  492.6 48.2 reduce-scatter.14
  566.8 41.5 reduce-scatter.12
  683.9 85.4 reduce-scatter.8
  771.0 23.8 all-gather.16
  796.9 23.5 all-gather.18
  822.6 35.9 all-gather.14

commit v2 on v1

v2 whole, which is shorter than its diff:
```python
from functools import partial

import jax
import jax.numpy as jnp
from jax import lax
from jax.experimental import pallas as pl
from jax.experimental.pallas import tpu as pltpu
from jax.sharding import PartitionSpec as P

HEAD_DIM = 64
EPS = 1e-05
MASKED = -1e30
MESH = pl.DeviceIdType.MESH
BF = jnp.bfloat16
F32 = jnp.float32
PLANE = ("context", "tensor")
VMEM_LIMIT = 60 * 2**20


def place():
    return (
        lax.axis_index("shard"),
        lax.axis_index("context"),
        lax.axis_index("tensor") // 2,
        lax.axis_index("tensor") % 2,
    )


def device(z, x, y, c):
    return (z, x, 2 * y + c)


def slot(x, y, c):
    return 4 * x + 2 * y + c


def neighbours():
    z, x, y, c = place()
    return [device(z, 1 - x, y, c), device(z, x, 1 - y, c), device(z, x, y, 1 - c)]


def plane_spots():
    z, x, y, c = place()
    steps = [(a, b, d) for a in range(2) for b in range(2) for d in range(2) if a + b + d]
    return [((x + a) % 2, (y + b) % 2, (c + d) % 2) for a, b, d in steps]


def plane_others():
    z = lax.axis_index("shard")
    return [device(z, *spot) for spot in plane_spots()]


def enter(targets):
    barrier = pltpu.get_barrier_semaphore()
    for target in targets:
        pl.semaphore_signal(barrier, inc=1, device_id=target, device_id_type=MESH)
    pl.semaphore_wait(barrier, len(targets))


def remote_copy(source, target_ref, send, recv, target):
    return pltpu.make_async_remote_copy(
        src_ref=source,
        dst_ref=target_ref,
        send_sem=send,
        recv_sem=recv,
        device_id=target,
        device_id_type=MESH,
    )


class Gather:
    semaphores = 9

    def __init__(self, in_ref, out_ref, local_sem, send, recv):
        z, x, y, c = place()
        self.in_ref, self.out_ref, self.local_sem = in_ref, out_ref, local_sem
        self.send, self.recv = send, recv
        self.spot = (x, y, c)
        self.to_x, self.to_y, self.to_c = neighbours()
        self.rows = in_ref.shape[0]
        self.sends = []

    def go(self, index, owner, start, size, target, source=None):
        there = self.out_ref.at[owner, pl.ds(start, size)]
        copy = remote_copy(
            there if source is None else source,
            there,
            self.send.at[index],
            self.recv.at[index],
            target,
        )
        copy.start()
        self.sends.append(copy)

    def arrived(self, index, owner, start, size):
        there = self.out_ref.at[owner, pl.ds(start, size)]
        remote_copy(
            there, there, self.send.at[index], self.recv.at[index], self.to_x
        ).wait_recv()

    def start(self):
        me = slot(*self.spot)
        self.own = pltpu.make_async_copy(self.in_ref, self.out_ref.at[me], self.local_sem)
        self.own.start()
        for index, target in enumerate((self.to_x, self.to_y, self.to_c)):
            self.go(index, me, 0, self.rows, target, self.in_ref)

    def relay_y(self):
        x, y, c = self.spot
        owner = slot(x, 1 - y, c)
        self.arrived(1, owner, 0, self.rows)
        self.go(3, owner, 0, self.rows // 2, self.to_x)
        self.go(5, owner, 0, self.rows, self.to_c)

    def relay_x(self):
        x, y, c = self.spot
        half = self.rows // 2
        owner = slot(1 - x, y, c)
        self.arrived(0, owner, 0, self.rows)
        self.go(4, owner, half, half, self.to_y)
        self.go(6, owner, 0, self.rows, self.to_c)

    def relay_far(self):
        x, y, c = self.spot
        half = self.rows // 2
        owner = slot(1 - x, 1 - y, c)
        self.arrived(3, owner, 0, half)
        self.go(7, owner, 0, half, self.to_c)
        self.arrived(4, owner, half, half)
        self.go(8, owner, half, half, self.to_c)

    def finish(self):
        x, y, c = self.spot
        half = self.rows // 2
        self.arrived(2, slot(x, y, 1 - c), 0, self.rows)
        self.arrived(5, slot(x, 1 - y, 1 - c), 0, self.rows)
        self.arrived(6, slot(1 - x, y, 1 - c), 0, self.rows)
        self.arrived(7, slot(1 - x, 1 - y, 1 - c), 0, half)
        self.arrived(8, slot(1 - x, 1 - y, 1 - c), half, half)
        self.own.wait()
        for copy in self.sends:
            copy.wait_send()

    def rest(self):
        self.relay_y()
        self.relay_x()
        self.relay_far()
        self.finish()


class Scatter:
    semaphores = 10

    @staticmethod
    def scratch(rows, columns):
        return [
            pltpu.VMEM((4, rows, columns), BF),
            pltpu.VMEM((4, rows, columns), BF),
            pltpu.VMEM((3, rows, columns), BF),
            pltpu.VMEM((2, rows // 2, columns), BF),
            pltpu.VMEM((2, rows, columns), BF),
            pltpu.SemaphoreType.DMA((4,)),
            pltpu.SemaphoreType.DMA((10,)),
            pltpu.SemaphoreType.DMA((10,)),
        ]

    def __init__(self, in_ref, out_ref, mine, core, sums, relay, final, local_sem, send, recv):
        self.in_ref, self.out_ref = in_ref, out_ref
        self.mine, self.core, self.sums = mine, core, sums
        self.relay, self.final = relay, final
        self.local_sem, self.send, self.recv = local_sem, send, recv
        self.to_x, self.to_y, self.to_c = neighbours()
        rows = out_ref.shape[0]
        self.low, self.high = pl.ds(0, rows // 2), pl.ds(rows // 2, rows // 2)

    def forward(self, index, source, target_ref, target):
        copy = remote_copy(
            source, target_ref, self.send.at[index], self.recv.at[index], target
        )
        copy.start()
        self.sends.append(copy)

    def pair(self, index, part):
        return self.mine[index, part].astype(F32) + self.core[index, part].astype(F32)

    def start(self):
        z, x, y, c = place()
        self.sends, self.loads = [], []
        chips = ((1 - x, 1 - y), (1 - x, y), (x, 1 - y), (x, y))
        for index, (cx, cy) in enumerate(chips):
            self.forward(
                index, self.in_ref.at[slot(cx, cy, 1 - c)], self.core.at[index], self.to_c
            )
            load = pltpu.make_async_copy(
                self.in_ref.at[slot(cx, cy, c)], self.mine.at[index], self.local_sem.at[index]
            )
            load.start()
            self.loads.append(load)

    def ready(self, index):
        self.loads[index].wait()
        self.sends[index].wait_recv()

    def first(self):
        low, high, sums = self.low, self.high, self.sums
        self.ready(0)
        sums[0, low] = self.pair(0, low).astype(BF)
        self.forward(4, sums.at[0, low], self.relay.at[0], self.to_x)
        sums[0, high] = self.pair(0, high).astype(BF)
        self.forward(5, sums.at[0, high], self.relay.at[1], self.to_y)
        self.ready(1)
        sums[1, low] = self.pair(1, low).astype(BF)
        self.forward(6, sums.at[1, low], self.final.at[0, low], self.to_x)
        self.ready(2)
        sums[2, high] = self.pair(2, high).astype(BF)
        self.forward(7, sums.at[2, high], self.final.at[1, high], self.to_y)
        self.ready(3)

    def second(self):
        low, high, sums = self.low, self.high, self.sums
        self.sends[5].wait_recv()
        sums[1, high] = (self.pair(1, high) + self.relay[1].astype(F32)).astype(BF)
        self.forward(8, sums.at[1, high], self.final.at[0, high], self.to_x)
        self.sends[4].wait_recv()
        sums[2, low] = (self.pair(2, low) + self.relay[0].astype(F32)).astype(BF)
        self.forward(9, sums.at[2, low], self.final.at[1, low], self.to_y)

    def total(self):
        for index in (6, 7, 8, 9):
            self.sends[index].wait_recv()
        everything = self.pair(3, slice(None))
        return everything + self.final[0].astype(F32) + self.final[1].astype(F32)

    def finish(self):
        for copy in self.sends:
            copy.wait_send()


class Exchange:
    def __init__(self, in_ref, out_ref, local_sem, send, recv):
        self.in_ref, self.out_ref, self.local_sem = in_ref, out_ref, local_sem
        self.send, self.recv = send, recv
        z, x, y, c = place()
        self.me = slot(x, y, c)
        self.copies = []

    def start(self, piece, part):
        z = lax.axis_index("shard")
        own = pltpu.make_async_copy(
            self.in_ref.at[self.me, part], self.out_ref.at[self.me, part], self.local_sem.at[piece]
        )
        own.start()
        self.copies.append(own)
        for index, spot in enumerate(plane_spots()):
            copy = remote_copy(
                self.in_ref.at[slot(*spot), part],
                self.out_ref.at[self.me, part],
                self.send.at[piece, index],
                self.recv.at[piece, index],
                device(z, *spot),
            )
            copy.start()
            self.copies.append(copy)

    def finish(self, piece=None):
        copies = self.copies if piece is None else self.copies[8 * piece : 8 * piece + 8]
        for copy in copies:
            copy.wait()


ANY = pl.BlockSpec(memory_space=pl.ANY)
IN_VMEM = pl.BlockSpec(memory_space=pltpu.VMEM)


def call(kernel, name, outs, out_specs, in_specs, scratch, ident=None):
    return pl.pallas_call(
        kernel,
        out_shape=outs,
        in_specs=in_specs,
        out_specs=out_specs,
        scratch_shapes=scratch,
        name=name,
        compiler_params=pltpu.CompilerParams(
            collective_id=ident,
            has_side_effects=ident is not None,
            vmem_limit_bytes=VMEM_LIMIT,
        ),
    )


def shape(*dims, dtype=BF):
    return jax.ShapeDtypeStruct(dims, dtype)


def gather_scratch():
    return [
        pltpu.SemaphoreType.DMA,
        pltpu.SemaphoreType.DMA((9,)),
        pltpu.SemaphoreType.DMA((9,)),
    ]


def gather_kernel(*refs):
    enter(neighbours())
    job = Gather(*refs)
    job.start()
    job.rest()


def plane_gather(values, ident):
    rows, columns = values.shape
    outs = shape(8, rows, columns, dtype=values.dtype)
    return call(gather_kernel, "plane_gather", outs, ANY, [ANY], gather_scratch(), ident)(values)


def scatter_kernel(in_ref, out_ref, *scratch):
    enter(neighbours())
    job = Scatter(in_ref, out_ref, *scratch)
    job.start()
    job.first()
    job.second()
    out_ref[...] = job.total()
    job.finish()


def plane_scatter(values, ident):
    _, rows, columns = values.shape
    outs = shape(rows, columns, dtype=F32)
    scratch = Scatter.scratch(rows, columns)
    return call(scatter_kernel, "plane_scatter", outs, IN_VMEM, [ANY], scratch, ident)(values)


SIDE = 256


def nt(left, right):
    return lax.dot_general(left, right, (((1,), (1,)), ((), ())), preferred_element_type=F32)


def nn(left, right):
    return lax.dot_general(left, right, (((1,), (0,)), ((), ())), preferred_element_type=F32)


def turn(values):
    return jnp.transpose(values.astype(F32))


def causal(scores):
    keys = lax.broadcasted_iota(jnp.int32, scores.shape, 0)
    queries = lax.broadcasted_iota(jnp.int32, scores.shape, 1)
    return jnp.where(keys <= queries, scores, MASKED)


def forward_kernel(
    rows_ref, w_ref, cot_ref,
    qkv_ref, log_ref, mix_ref, mine_ref, cot_out,
    ex_local, ex_send, ex_recv, g_local, g_send, g_recv,
):
    enter(plane_others())
    side = Gather(cot_ref, cot_out, g_local, g_send, g_recv)
    side.start()
    blocks, both, _ = rows_ref.shape
    rows = both // 2
    width = mix_ref.shape[2]
    heads = width // HEAD_DIM
    length = blocks * rows
    step = SIDE // rows

    def project(block, carry):
        qkv_ref[block] = nn(rows_ref[block], w_ref[...]).astype(BF)
        return carry

    lax.fori_loop(0, blocks, project, 0)
    exchange = Exchange(mix_ref, mine_ref, ex_local, ex_send, ex_recv)
    for clip in range(2):
        part = pl.ds(clip * rows, rows)
        for head in range(heads):
            lanes = [pl.ds(j * width + head * HEAD_DIM, HEAD_DIM) for j in range(3)]
            key = qkv_ref[:, part, lanes[1]].reshape(length, HEAD_DIM)
            value = turn(qkv_ref[:, part, lanes[2]].reshape(length, HEAD_DIM)).astype(BF)
            for index in range(length // SIDE):
                spots = pl.ds(index * step, step)
                query = qkv_ref[spots, part, lanes[0]].reshape(SIDE, HEAD_DIM)
                query = query * jnp.asarray(HEAD_DIM ** (-0.5), BF)
                start = index * SIDE
                last = causal(nt(key[start : start + SIDE], query))
                top = jnp.max(last, axis=0, keepdims=True)
                if index:
                    early = nt(key[:start], query)
                    top = jnp.maximum(top, jnp.max(early, axis=0, keepdims=True))
                last = jnp.exp(last - top)
                total = jnp.sum(last, axis=0, keepdims=True)
                mix = nn(value[:, start : start + SIDE], last.astype(BF))
                if index:
                    early = jnp.exp(early - top)
                    total += jnp.sum(early, axis=0, keepdims=True)
                    mix += nn(value[:, :start], early.astype(BF))
                mix = jnp.transpose(mix / total).astype(BF).reshape(step, rows, HEAD_DIM)
                mix_ref[spots, part, pl.ds(head * HEAD_DIM, HEAD_DIM)] = mix
                log_ref[pl.ds(clip * heads + head, 1), pl.ds(start, SIDE)] = top + jnp.log(total)
        exchange.start(clip, part)
        if clip == 0:
            side.relay_y()
            side.relay_x()
    side.relay_far()
    exchange.finish()
    side.finish()


def attend_forward(rows, weights, cotangent, ident):
    blocks, block, width = rows.shape
    columns = weights.shape[1] // 3
    heads = columns // HEAD_DIM
    return call(
        forward_kernel,
        "attend_forward",
        (
            shape(blocks, block, 3 * columns),
            shape(2 * heads, blocks * block // 2, dtype=F32),
            shape(blocks, block, columns),
            shape(blocks, block, columns),
            shape(blocks, block, width),
        ),
        (IN_VMEM, IN_VMEM, IN_VMEM, ANY, ANY),
        [IN_VMEM, IN_VMEM, ANY],
        [
            pltpu.SemaphoreType.DMA((2,)),
            pltpu.SemaphoreType.DMA((2, 7)),
            pltpu.SemaphoreType.DMA((2, 7)),
        ]
        + gather_scratch(),
        ident,
    )(rows, weights, cotangent)


def backward_kernel(
    grad_ref, qkv_ref, mix_ref, log_ref, side_ref,
    out_ref, side_out,
    grad_all, query_turned, ex_local, ex_send, ex_recv, *scratch,
):
    enter(plane_others())
    exchange = Exchange(grad_ref, grad_all, ex_local, ex_send, ex_recv)
    blocks, both, width = mix_ref.shape
    rows = both // 2
    heads = width // HEAD_DIM
    length = blocks * rows
    step = SIDE // rows
    for clip in range(2):
        exchange.start(clip, pl.ds(clip * rows, rows))
    side = Scatter(side_ref, side_out, *scratch)
    side.start()
    side.first()
    for clip in range(2):
        exchange.finish(clip)
        part = pl.ds(clip * rows, rows)
        for head in range(heads):
            lanes = [pl.ds(j * width + head * HEAD_DIM, HEAD_DIM) for j in range(3)]
            query = qkv_ref[:, part, lanes[0]].reshape(length, HEAD_DIM)
            query = query * jnp.asarray(HEAD_DIM ** (-0.5), BF)
            key = qkv_ref[:, part, lanes[1]].reshape(length, HEAD_DIM)
            value = qkv_ref[:, part, lanes[2]].reshape(length, HEAD_DIM)
            key_turned = turn(key).astype(BF)
            here = pl.ds(head * HEAD_DIM, HEAD_DIM)
            grad = grad_all[:, part, here].reshape(length, HEAD_DIM)
            mixed = mix_ref[:, part, here].reshape(length, HEAD_DIM)
            inner = jnp.transpose(grad.astype(F32) * mixed.astype(F32))
            inner = jnp.sum(inner, axis=0, keepdims=True)
            logs = log_ref[pl.ds(clip * heads + head, 1), :]
            for index in range(length // SIDE):
                start = index * SIDE
                spots = pl.ds(index * step, step)
                k_part, v_part = key[start : start + SIDE], value[start : start + SIDE]
                scores = nt(k_part, query[start:])
                first = causal(scores[:, :SIDE])
                if start + SIDE < length:
                    scores = jnp.concatenate([first, scores[:, SIDE:]], axis=1)
                else:
                    scores = first
                weights = jnp.exp(scores - logs[:, start:])
                slopes = nt(v_part, grad[start:])
                slopes = (weights * (slopes - inner[:, start:])).astype(BF)
                grad_key = nn(slopes, query[start:]).astype(BF).reshape(step, rows, HEAD_DIM)
                grad_value = nn(weights.astype(BF), grad[start:]).astype(BF)
                out_ref[spots, part, lanes[1]] = grad_key
                out_ref[spots, part, lanes[2]] = grad_value.reshape(step, rows, HEAD_DIM)
                grad_query = nn(key_turned[:, start : start + SIDE], slopes)
                if index:
                    query_turned[:, start:] += grad_query
                else:
                    query_turned[...] = grad_query
            grad_query = jnp.transpose(query_turned[...]) * HEAD_DIM ** (-0.5)
            grad_query = grad_query.astype(BF).reshape(blocks, rows, HEAD_DIM)
            out_ref[:, part, lanes[0]] = grad_query
        if clip == 0:
            side.second()
    side_out[...] = side.total().astype(BF)
    side.finish()


def attend_backward(grad_mix, qkv, mix, logs, side, ident):
    blocks, block, columns = mix.shape
    _, rows, width = side.shape
    return call(
        backward_kernel,
        "attend_backward",
        (shape(blocks, block, 3 * columns), shape(rows, width)),
        (IN_VMEM, IN_VMEM),
        [ANY, IN_VMEM, IN_VMEM, IN_VMEM, ANY],
        [
            pltpu.VMEM((blocks, block, columns), BF),
            pltpu.VMEM((HEAD_DIM, blocks * block // 2), F32),
            pltpu.SemaphoreType.DMA((2,)),
            pltpu.SemaphoreType.DMA((2, 7)),
            pltpu.SemaphoreType.DMA((2, 7)),
        ]
        + Scatter.scratch(rows, width),
        ident,
    )(grad_mix, qkv, mix, logs, side)


def last_kernel(
    part_ref, frames_ref, gain_ref, grad_ref, stats_ref,
    out_ref, total_ref,
    mine, came, all_ref, st_send, st_recv, z_send, z_recv, *scratch,
):
    z = lax.axis_index("shard")
    shards = lax.axis_size("shard")
    others = [lax.rem(z + i, shards) for i in range(1, shards)]
    spot = place()[1:]
    enter(neighbours() + [device(other, *spot) for other in others])
    job = Scatter(part_ref, out_ref, *scratch)
    job.start()
    inputs = frames_ref[...].astype(F32)
    average = jnp.mean(inputs, axis=-1, keepdims=True)
    centred = inputs - average
    rate = lax.rsqrt(jnp.mean(centred * centred, axis=-1, keepdims=True) + EPS)
    job.first()
    job.second()
    grads = job.total()
    normed = centred * rate
    mine[0] = stats_ref[...]
    mine[0, 0:1] = jnp.sum(grads * normed, axis=0, keepdims=True)
    mine[0, 1:2] = jnp.sum(grads, axis=0, keepdims=True)
    sends = []
    for index, target in enumerate(reversed(neighbours())):
        copy = remote_copy(
            mine.at[index], came.at[index], st_send.at[index], st_recv.at[index], target
        )
        copy.start()
        sends.append(copy)
        if index == 0:
            scaled = grads * gain_ref[...]
            inner = jnp.mean(scaled * normed, axis=-1, keepdims=True)
            scaled = scaled - jnp.mean(scaled, axis=-1, keepdims=True) - normed * inner
            out_ref[...] = grad_ref[...] + rate * scaled
        copy.wait_recv()
        mine[index + 1] = mine[index] + came[index]
    for index, other in enumerate(others):
        copy = remote_copy(
            mine.at[3], all_ref.at[z], z_send.at[index], z_recv.at[index], device(other, *spot)
        )
        copy.start()
        sends.append(copy)
    all_ref[z] = mine[3]
    for copy in sends[3:]:
        copy.wait_recv()
    total = all_ref[0]
    for index in range(1, shards):
        total += all_ref[index]
    total_ref[...] = total
    for copy in sends:
        copy.wait_send()
    job.finish()


def last_step(part, frames, gain, grad, stats, shards, ident):
    _, rows, width = part.shape
    return call(
        last_kernel,
        "last_step",
        (shape(rows, width, dtype=F32), shape(8, width, dtype=F32)),
        (IN_VMEM, IN_VMEM),
        [ANY, IN_VMEM, IN_VMEM, IN_VMEM, IN_VMEM],
        [
            pltpu.VMEM((4, 8, width), F32),
            pltpu.VMEM((3, 8, width), F32),
            pltpu.VMEM((shards, 8, width), F32),
            pltpu.SemaphoreType.DMA((3,)),
            pltpu.SemaphoreType.DMA((3,)),
            pltpu.SemaphoreType.DMA((shards - 1,)),
            pltpu.SemaphoreType.DMA((shards - 1,)),
        ]
        + Scatter.scratch(rows, width),
        ident,
    )(part, frames, gain, grad, stats)


def dots(spec, *operands):
    return jnp.einsum(spec, *operands, preferred_element_type=F32)


def layer_norm(inputs, scaling, offset):
    average = jnp.mean(inputs, axis=-1, keepdims=True)
    centred = inputs - average
    variance = jnp.mean(centred * centred, axis=-1, keepdims=True)
    return centred * lax.rsqrt(variance + EPS) * scaling + offset


def on_device(
    frames,
    text_states,
    cotangent,
    norm_gain,
    norm_bias,
    self_qkv,
    self_out,
    cross_qkv,
    cross_out,
    mlp_up,
    mlp_down,
):
    clips, rows, width = frames.shape
    context = lax.axis_index("context")
    depth = self_qkv.shape[1]
    slices = width // depth
    columns = self_qkv.shape[2] // 2
    heads = columns // HEAD_DIM
    block = clips * rows
    texts = text_states.shape[1]

    def half(weight):
        size = weight.shape[-1] // 2
        return lax.dynamic_slice_in_dim(weight, context * size, size, weight.ndim - 1)

    def over_shard(weight, tiled=True):
        return lax.all_gather(weight, "shard", axis=0, tiled=tiled)

    qkv_part = half(self_qkv)
    w_qkv = over_shard(jnp.concatenate([qkv_part[0], qkv_part[1], qkv_part[2]], axis=-1))
    cross_part = half(cross_qkv)
    side = jnp.stack(
        [half(self_out), cross_part[0], half(cross_out), cross_part[1], cross_part[2]]
    )
    w_side = over_shard(side.transpose(0, 2, 1), tiled=False).transpose(1, 2, 0, 3)
    w_side = w_side.reshape(5, columns, width)
    w_up = over_shard(half(mlp_up))
    w_down = over_shard(half(mlp_down))

    stream_zero = frames.astype(F32)
    norm_one = layer_norm(stream_zero, norm_gain[0], norm_bias[0])
    all_one = plane_gather(norm_one.astype(BF).reshape(block, width), 0)
    flat_one = all_one.reshape(8 * block, width)
    qkv, self_log, mix, my_mix, all_grad = attend_forward(
        all_one, w_qkv, cotangent.reshape(block, width), 1
    )

    plane_w = plane_gather(w_side[:3].reshape(3 * columns, width), 2)
    plane_w = plane_w.reshape(8, 3, columns, width)
    w_out, w_query, w_cross = plane_w[:, 0], plane_w[:, 1], plane_w[:, 2]
    branch_one = dots("bre,bed->rd", my_mix, w_out).reshape(clips, rows, width)
    stream_one = stream_zero + branch_one
    norm_two, norm_two_back = jax.vjp(layer_norm, stream_one, norm_gain[1], norm_bias[1])
    low_two = norm_two.astype(BF)
    cross_q = dots("cfd,bed->cfbe", low_two, w_query).astype(BF)
    text_part = dots("cnd,ted->tcne", text_states, w_side[3:]).astype(BF)
    text_all = plane_gather(text_part.reshape(2 * clips * texts, columns), 3)
    text_all = text_all.reshape(8, 2, clips, texts, heads, HEAD_DIM)
    text_k, text_v = text_all[:, 0], text_all[:, 1]
    cross_q = cross_q.reshape(clips, rows, 8, heads, HEAD_DIM)
    scale = HEAD_DIM ** (-0.5)
    scores = dots("cfbhd,bcnhd->cbhfn", cross_q, text_k) * scale
    top = jnp.max(scores, axis=-1, keepdims=True)
    cross_full = jnp.exp(scores - top)
    cross_full = cross_full / jnp.sum(cross_full, axis=-1, keepdims=True)
    cross_probs = cross_full.astype(BF)
    cross_mix = dots("cbhfn,bcnhd->cfbhd", cross_probs, text_v).astype(BF)
    cross_mix = cross_mix.reshape(clips, rows, 8, columns)
    branch_two = dots("cfbe,bed->cfd", cross_mix, w_cross)
    stream_two = stream_one + branch_two

    norm_three, norm_three_back = jax.vjp(layer_norm, stream_two, norm_gain[2], norm_bias[2])
    all_three = plane_gather(norm_three.astype(BF).reshape(block, width), 4)
    flat_three = all_three.reshape(8 * block, width)
    pre_act = dots("rd,dh->rh", flat_three, w_up)
    hidden, gelu_back = jax.vjp(partial(jax.nn.gelu, approximate=False), pre_act)
    hidden_low = hidden.astype(BF)
    part_three = dots("rh,dh->rd", hidden_low, w_down).astype(BF)
    branch_three = plane_scatter(part_three.reshape(8, block, width), 5)
    branch_three = branch_three.reshape(clips, rows, width)
    stream_out = stream_two + branch_three
    squares = jnp.stack(
        [
            jnp.sum(stream_out * stream_out),
            jnp.sum(branch_one * branch_one),
            jnp.sum(branch_two * branch_two),
            jnp.sum(branch_three * branch_three),
        ]
    )

    flat_grad = all_grad.reshape(8 * block, width)
    grad_hidden = dots("rd,dh->rh", flat_grad, w_down)
    grad_pre = gelu_back(grad_hidden)[0].astype(BF)
    part_norm = dots("rh,dh->rd", grad_pre, w_up).astype(BF)
    grad_normed = plane_scatter(part_norm.reshape(8, block, width), 7)

    def to_shard(part):
        return lax.psum_scatter(part.astype(BF), "shard", scatter_dimension=0, tiled=True)

    grad_down = to_shard(dots("rd,rh->dh", flat_grad, hidden_low))
    grad_up = to_shard(dots("rd,rh->dh", flat_three, grad_pre))
    grad_inner, gain_three, shift_three = norm_three_back(grad_normed.reshape(clips, rows, width))
    grad_two = cotangent.astype(F32) + grad_inner

    grad_low = grad_two.astype(BF)
    grad_cross_mix = dots("cfd,bed->cfbe", grad_low, w_cross).astype(BF)
    w_grad_cross = dots("cfd,cfbe->bed", grad_low, cross_mix)
    grad_heads = grad_cross_mix.reshape(clips, rows, 8, heads, HEAD_DIM)
    cross_dp = dots("cfbhd,bcnhd->cbhfn", grad_heads, text_v)
    inner = jnp.sum(cross_full * cross_dp, axis=-1, keepdims=True)
    grad_scores = (cross_full * (cross_dp - inner)).astype(BF)
    grad_cq = (dots("cbhfn,bcnhd->cfbhd", grad_scores, text_k) * scale).astype(BF)
    grad_text_k = dots("cbhfn,cfbhd->bcnhd", grad_scores, cross_q) * scale
    grad_text_v = dots("cbhfn,cfbhd->bcnhd", cross_probs, grad_heads)
    grad_cq = grad_cq.reshape(clips, rows, 8, columns)
    w_grad_query = dots("cfd,cfbe->bed", low_two, grad_cq)
    grad_normed = dots("cfbe,bed->cfd", grad_cq, w_query)
    grad_inner, gain_two, shift_two = norm_two_back(grad_normed)
    grad_one = grad_two + grad_inner

    grad_low = grad_one.astype(BF).reshape(block, width)
    grad_mix = dots("rd,bed->bre", grad_low, w_out).astype(BF)
    w_grad_out = dots("rd,bre->bed", grad_low, my_mix)

    text_grads = jnp.stack([grad_text_k, grad_text_v], axis=1).astype(BF)
    text_grads = plane_scatter(text_grads.reshape(8, 2 * clips * texts, columns), 9)
    text_grads = text_grads.reshape(2, clips, texts, columns)
    text_grads_low = text_grads.astype(BF)
    w_grad_text = dots("cnd,tcne->ted", text_states, text_grads_low)
    grad_text = dots("tcne,ted->cnd", text_grads_low, w_side[3:])
    grad_text = grad_text.reshape(clips, 8, texts // 8, width).transpose(1, 0, 2, 3).astype(BF)
    grad_text = plane_scatter(grad_text.reshape(8, clips * texts // 8, width), 10)
    grad_text = grad_text.reshape(clips, texts // 8, width)

    part_side = jnp.stack([w_grad_out, w_grad_query, w_grad_cross], axis=1).astype(BF)
    part_side = part_side.reshape(8, 3 * columns, width)
    grad_qkv, part_side = attend_backward(grad_mix, qkv, mix, self_log, part_side, 8)
    grad_qkv = grad_qkv.reshape(8 * block, 3 * columns)
    part_norm = dots("re,de->rd", grad_qkv, w_qkv).astype(BF)
    grad_w_qkv = to_shard(dots("rd,re->de", flat_one, grad_qkv))
    nothing = jnp.zeros((1, width), F32)
    stats = [nothing, nothing] + [
        v[None] for v in (gain_two, shift_two, gain_three, shift_three)
    ]
    stats.append(jnp.pad(squares, (0, width - 4))[None])
    grad_frames, totals = last_step(
        part_norm.reshape(8, block, width),
        frames.reshape(block, width),
        norm_gain[0][None],
        grad_one.reshape(block, width),
        jnp.concatenate(stats + [nothing], axis=0),
        lax.axis_size("shard"),
        11,
    )
    grad_frames = grad_frames.reshape(clips, rows, width)

    part_side = part_side.reshape(3, columns, width)
    part_side = jnp.concatenate([part_side, w_grad_text.astype(BF)], axis=0)
    part_side = part_side.reshape(5, columns, slices, depth).transpose(2, 0, 1, 3)
    grad_side = to_shard(part_side)[0]

    def whole(values):
        return lax.all_gather(values, "context", axis=values.ndim - 1, tiled=True).astype(F32)

    grad_up, grad_down = whole(grad_up), whole(grad_down)
    grad_self = jnp.stack([grad_w_qkv[:, j * columns : (j + 1) * columns] for j in range(3)])
    grad_side = grad_side.transpose(0, 2, 1)
    grad_all = whole(jnp.concatenate([grad_self, grad_side], axis=0))

    gains = jnp.stack([totals[0], totals[2], totals[4]])
    shifts = jnp.stack([totals[1], totals[3], totals[5]])
    squares = totals[6, :4]
    start = lax.axis_index("shard") * depth
    grad_gain = lax.dynamic_slice_in_dim(gains, start, depth, 1)
    grad_shift = lax.dynamic_slice_in_dim(shifts, start, depth, 1)
    entries = float(clips * rows * width * lax.axis_size(("shard",) + PLANE))
    return (
        stream_out.astype(BF),
        grad_frames,
        grad_text,
        grad_gain,
        grad_shift,
        grad_all[:3],
        grad_all[3],
        jnp.stack([grad_all[4], grad_all[6], grad_all[7]]),
        grad_all[5],
        grad_up,
        grad_down,
        jnp.sqrt(squares / entries),
    )


def solution(mesh):
    rows = P("shard", PLANE, None)
    stack = P(None, "shard", "tensor")
    flat = P("shard", "tensor")
    return jax.shard_map(
        on_device,
        mesh=mesh,
        in_specs=(rows, P("shard"), rows, P(), P(), stack, flat, stack, flat, flat, flat),
        out_specs=(
            (rows, rows, rows, P(None, "shard"), P(None, "shard"))
            + (stack, flat, stack, flat, flat, flat, P())
        ),
        check_vma=False,
    )
```

time: 893 us -> 804 us (0.900)
  matrix products: 188 us -> 126 us
  waiting for transfers between devices: 45.8 us -> 96.6 us
  blocking collectives: 42.1 us -> 0 us
  local copies, waits for them, and re-layouts: 123 us -> 87.6 us
  Pallas kernels: 390 us -> 416 us
  other arithmetic: 78.2 us -> 56.7 us
    dot_general x40 -> x25, matrix products: 187 us -> 123 us  [dots(): return jnp.einsum(spec, *operands, preferred_element_type=F32)]
    reduce_scatter x2 -> x3, waiting for transfers between devices: 17.1 us -> 72.4 us  [to_shard(): lax.psum_scatter(part.astype(BF), 'shard', scatter_dimension=0, tiled=True)]
    psum x1 -> x0, blocking collectives: 42.1 us -> none  [on_device(): lax.psum((gains, shifts, squares), ('shard',) + PLANE)]
    pallas_call x13 -> x11, Pallas kernels: 390 us -> 416 us  [the longest x4 145 us: plane_gather(): call(gather_kernel, 'plane_gather', outs, ANY, [ANY], gather_scratch(), i...]
    all_gather x3, waiting for transfers between devices: 27.9 us -> 3.76 us  [whole(): lax.all_gather(values, 'context', axis=values.ndim - 1, tiled=True)]
    all_gather x4, waiting for transfers between devices: 0.06 us -> 19.2 us  [over_shard(): return lax.all_gather(weight, 'shard', axis=0, tiled=tiled)]
    reshape x14 -> x0, local copies, waits for them, and re-layouts: 16.2 us -> none  [the longest x4 6.46 us: by_owner(): values = values.reshape(clips, 8, rows, columns).transpose(1, 0, 2, 3)]
    unnamed x216 -> x118, local copies, waits for them, and re-layouts: 45.6 us -> 30.1 us
  transfers between devices with their start and end apart: 11 -> 11, of which waited for: 2 -> 4; matrix products, arithmetic and copies ran while one was open for 37% -> 25% of each run, Pallas kernels for 44% -> 52%
where the time goes in v2:
time: 804 us; the launch traced here: 799 us
  Pallas kernels  416 us (52%)
  matrix products  126 us (16%)
  waiting for transfers between devices  96.6 us (12%)
  local copies, waits for them, and re-layouts  87.6 us (11%)
  other arithmetic  56.7 us (7%)
  between operations  15.1 us (2%)
    pallas_call x4, Pallas kernels, plane_gather(): call(gather_kernel, 'plane_gather', outs, ANY, [ANY], gather_scratch(), i...  145 us
    dot_general x25, matrix products, dots(): return jnp.einsum(spec, *operands, preferred_element_type=F32)  123 us
    pallas_call x4, Pallas kernels, plane_scatter(): call(scatter_kernel, 'plane_scatter', outs, IN_VMEM, [ANY], scratch, ident)  85 us
    pallas_call x1, Pallas kernels, attend_backward(): call(backward_kernel, 'attend_backward', (shape(blocks, block, 3 * column...  77.7 us
    reduce_scatter x3, waiting for transfers between devices, to_shard(): lax.psum_scatter(part.astype(BF), 'shard', scatter_dimension=0, tiled=True)  72.4 us
    pallas_call x1, Pallas kernels, last_step(): call(last_kernel, 'last_step', (shape(rows, width, dtype=F32), shape(8, w...  62.9 us
    pallas_call x1, Pallas kernels, attend_forward(): call(forward_kernel, 'attend_forward', (shape(blocks, block, 3 * columns)...  46 us
    unnamed x118, local copies, waits for them, and re-layouts  30.1 us
  transfers between devices with their start and end apart: 11, of which 4 were waited for; matrix products, arithmetic and copies ran while one was open for 25% of the time, Pallas kernels for 52%

profile of v2, /device:TPU:0, one launch (start us, length us, event | category | flops | bytes accessed | tf_op | source)
XLA Modules:
  0.0 799.0 jit_solution(18444752924148540548)
XLA Ops:
  18.1 34.4 %plane_gather.4.rows_ref = bf16[8,256,1536]{2,1,0:T(8,128)(2,1)} custom-call(bf16[256,1536]{1,0:T(8,128)(2,1)} %bitcast.266), custom_call_target="tpu_custom_call" | custom-call | tf_op jit(solution)/shard_map/plane_gather/pallas_call | solution.py:313
  52.6 3.9 all-gather.9.cloned.1.call-done.w_ref
  56.5 46.0 %attend_forward.1 = (bf16[8,256,576]{2,1,0:T(8,128)(2,1)}, f32[6,1024]{1,0:T(8,128)}, bf16[8,256,192]{2,1,0:T(8,128)(2,1)}, bf16[8,256,192]{2,1,0:T(8,128)(2,1)}, bf16[8,256,1536]{2,1,0:T(8,128)(2,1)}) custom-call(bf16[8,256,1536]{2,1,0:T(8,128)(2,1)} %plane_gather.4.rows_ref, bf16[1536,576]{1,0:T(8,128)(2,1)} %all-gather.9.cloned.1.call-done.w_ref, ...), custom_call_target="tpu_custom_call" | custom-call | tf_op jit(solution)/shard_map/attend_forward/pallas_call | solution.py:414
  102.5 15.2 %all-gather.21.cloned.1.call-done = bf16[20,192,384]{2,1,0:T(8,128)(2,1)} async-done(((bf16[5,192,384]{2,1,0:T(8,128)(2,1)}), bf16[20,192,384]{2,1,0:T(8,128)(2,1)}) %all-gather.21.cloned.1.call-update) | async-done | bytes 2949136 | tf_op jit(solution)/shard_map/all_gather | solution.py:636
  117.7 4.1 copy.199
  126.2 11.5 %plane_gather.6 = bf16[8,256,192]{2,1,0:T(8,128)(2,1)} custom-call(bf16[256,192]{1,0:T(8,128)(2,1)} %bitcast.288), custom_call_target="tpu_custom_call" | custom-call | tf_op jit(solution)/shard_map/plane_gather/pallas_call | solution.py:313
  145.1 65.8 %plane_gather.5 = bf16[8,576,1536]{2,1,0:T(8,128)(2,1)} custom-call(bf16[576,1536]{1,0:T(8,128)(2,1)} %bitcast.254), custom_call_target="tpu_custom_call" | custom-call | tf_op jit(solution)/shard_map/plane_gather/pallas_call | solution.py:313
  211.0 4.8 fusion.81
  216.1 5.0 fusion.34
  221.1 3.0 fusion.86
  226.0 4.9 fusion.80
  233.3 32.7 %plane_gather.7 = bf16[8,256,1536]{2,1,0:T(8,128)(2,1)} custom-call(bf16[256,1536]{1,0:T(8,128)(2,1)} %bitcast.267), custom_call_target="tpu_custom_call" | custom-call | tf_op jit(solution)/shard_map/plane_gather/pallas_call | solution.py:313
  266.0 9.6 %fusion.89 = f32[2048,768]{1,0:T(8,128)} fusion(bf16[2048,1536]{1,0:T(8,128)(2,1)} %bitcast.255, bf16[1536,768]{1,0:T(8,128)(2,1)} %all-gather.11.cloned.1.call-done), kind=kOutput, calls=%fused_computation.172 | convolution fusion | flops 4831838208 | bytes 14942208 | tf_op jit(solution)/shard_map/rd,dh->rh/dot_general | solution.py:599
  275.7 22.6 %add_convert_fusion = (bf16[2048,768]{1,0:T(8,128)(2,1)S(1)}, f32[2048,768]{1,0:T(8,128)}) fusion(f32[2048,768]{1,0:T(8,128)} %fusion.89, bf16[2048,1536]{1,0:T(8,128)(2,1)} %bitcast.289, bf16[1536,768]{1,0:T(8,128)(2,1)} %all-gather.13.cloned.1.call-done), kind=kOutput, calls=%fused_computation.9 | convolution fusion | flops 4945084416 | bytes 24379392 | tf_op jit(solution)/shard_map/rd,dh->rh/dot_general | solution.py:599
  300.0 6.5 convolution_convert_fusion.4
  306.4 7.2 multiply_convert_fusion
  313.7 9.1 %convolution_convert_fusion.1 = bf16[2048,1536]{1,0:T(8,128)(2,1)} fusion(bf16[2048,768]{1,0:T(8,128)(2,1)} %multiply_convert_fusion, bf16[1536,768]{1,0:T(8,128)(2,1)} %all-gather.13.cloned.1.call-done), kind=kOutput, calls=%fused_computation.6 | convolution fusion | flops 4834983936 | bytes 11796480 | tf_op jit(solution)/shard_map/rh,dh->rd/dot_general | solution.py:599
  322.7 32.6 %plane_scatter.4 = f32[256,1536]{1,0:T(8,128)} custom-call(bf16[8,256,1536]{2,1,0:T(8,128)(2,1)} %bitcast.261), custom_call_target="tpu_custom_call" | custom-call | tf_op jit(solution)/shard_map/plane_scatter/pallas_call | solution.py:330
  355.3 9.4 %convolution_convert_fusion = bf16[2048,1536]{1,0:T(8,128)(2,1)} fusion(bf16[2048,768]{1,0:T(8,128)(2,1)} %copy-done.47, bf16[1536,768]{1,0:T(8,128)(2,1)S(1)} %copy-done.46), kind=kOutput, calls=%fused_computation.5 | convolution fusion | flops 4834983936 | bytes 11796480 | tf_op jit(solution)/shard_map/rh,dh->rd/dot_general | solution.py:599
  364.7 32.3 %plane_scatter.5 = f32[256,1536]{1,0:T(8,128)} custom-call(bf16[8,256,1536]{2,1,0:T(8,128)(2,1)} %bitcast.260), custom_call_target="tpu_custom_call" | custom-call | tf_op jit(solution)/shard_map/plane_scatter/pallas_call | solution.py:330
  397.1 4.4 multiply_reduce_fusion.4
  406.7 4.1 fusion.33
  414.6 4.7 fusion.77
  421.7 6.5 convolution_convert_fusion.3
  428.3 4.2 fusion.78
  432.5 3.8 fusion.35
  437.8 2.8 fusion.18
  445.7 5.5 copy.127
  451.2 77.7 %attend_backward.1 = (bf16[8,256,576]{2,1,0:T(8,128)(2,1)}, bf16[576,1536]{1,0:T(8,128)(2,1)}) custom-call(bf16[8,256,192]{2,1,0:T(8,128)(2,1)} %bitcast.263, bf16[8,256,576]{2,1,0:T(8,128)(2,1)} %get-tuple-element.23.qkv_ref, bf16[8,256,192]{2,1,0:T(8,128)(2,1)} %get-tuple-element.24.mix_ref, f32[6,1024]{1,0:T(8,128)} %get-tuple-element.25.log_ref, ...), custom_call_target="tpu_custom_call" | custom-call | tf_op jit(solution)/shard_map/attend_backward/pallas_call | solution.py:503
  528.9 8.6 %bitcast_convert_fusion.2 = bf16[1536,576]{0,1:T(8,128)(2,1)} fusion(bf16[8,256,1536]{2,1,0:T(8,128)(2,1)} %plane_gather.4.rows_ref, bf16[8,256,576]{2,1,0:T(8,128)(2,1)} %get-tuple-element.26), kind=kOutput, calls=%fused_computation.40 | convolution fusion | flops 3624763392 | bytes 10420224 | tf_op jit(solution)/shard_map/rd,re->de/dot_general | solution.py:599
  537.6 4.0 copy.163
  546.6 4.5 copy.160
  551.1 5.0 reshape.253.in_ref
  556.1 10.4 %plane_scatter.6 = f32[256,192]{1,0:T(8,128)} custom-call(bf16[8,256,192]{2,1,0:T(8,128)(2,1)} %reshape.253.in_ref), custom_call_target="tpu_custom_call" | custom-call | tf_op jit(solution)/shard_map/plane_scatter/pallas_call | solution.py:330
  573.8 4.1 concatenate.23
  577.8 3.1 copy.136
  581.0 4.6 maximum_bitcast_fusion
  588.6 2.8 multiply_reduce_fusion
  596.5 72.3 %reduce-scatter.7.cloned.1.call-done = bf16[1,5,192,384]{3,1,2,0:T(8,128)(2,1)} async-done(((bf16[4,5,192,384]{3,1,2,0:T(8,128)(2,1)}), bf16[1,5,192,384]{3,1,2,0:T(8,128)(2,1)}) %reduce-scatter.7.cloned.1.call-update) | async-done | bytes 737296 | tf_op jit(solution)/shard_map/reduce_scatter | solution.py:707
  668.8 3.6 pad_maximum_fusion.3
  675.1 9.7 %plane_scatter.7 = f32[16,1536]{1,0:T(8,128)} custom-call(bf16[8,16,1536]{2,1,0:T(8,128)(2,1)} %copy_bitcast_fusion.4.in_ref), custom_call_target="tpu_custom_call" | custom-call | tf_op jit(solution)/shard_map/plane_scatter/pallas_call | solution.py:330
  685.5 8.8 %convolution_convert_fusion.2 = bf16[2048,1536]{1,0:T(8,128)(2,1)} fusion(bf16[2048,576]{1,0:T(8,128)(2,1)} %bitcast.293, bf16[1536,576]{1,0:T(8,128)(2,1)S(1)} %copy-done.27), kind=kOutput, calls=%fused_computation.7 | convolution fusion | flops 3627024384 | bytes 10420224 | tf_op jit(solution)/shard_map/re,de->rd/dot_general | solution.py:599
  694.3 62.9 %last_step.1 = (f32[256,1536]{1,0:T(8,128)}, f32[8,1536]{1,0:T(8,128)}) custom-call(bf16[8,256,1536]{2,1,0:T(8,128)(2,1)} %bitcast.259, bf16[256,1536]{1,0:T(8,128)(2,1)} %bitcast.249, f32[1,1536]{1,0:T(1,128)} %get-tuple-element.96.gain_ref, f32[256,1536]{1,0:T(8,128)} %bitcast.262, f32[8,1536]{1,0:T(8,128)} %concatenate.22.stats_ref), custom_call_target="tpu_custom_call" | custom-call | tf_op jit(solution)/shard_map/last_step/pallas_call | solution.py:578
  760.9 3.0 convert_element_type.154
  763.9 3.0 convert_element_type.156
  766.8 3.8 all-gather.15.cloned.1.call-done
  770.6 3.4 slice.153
  774.0 4.3 copy.141
  (226 shorter events, 87.7 us)
Async XLA Ops:
  7.2 4.9 copy-start
  7.2 2.7 copy-start.34
  7.2 49.3 %all-gather.9.cloned.1.call-start = ((), (), s32[]{:S(2)}) async-start(), calls=%async_computation.4 | async-start | bytes 2457600 | tf_op jit(solution)/shard_map/all_gather | solution.py:636
  7.3 3.3 copy-start.38
  7.3 3.3 copy-start.39
  9.8 107.9 %all-gather.21.cloned.1.call-start = ((), (), s32[]{:S(2)}) async-start(), calls=%async_computation.13 | async-start | bytes 3686400 | tf_op jit(solution)/shard_map/all_gather | solution.py:636
  12.0 3.0 copy-start.9
  12.0 254.0 %all-gather.11.cloned.1.call-start = ((), (), s32[]{:S(2)}) async-start(), calls=%async_computation.5 | async-start | bytes 2949120 | tf_op jit(solution)/shard_map/all_gather | solution.py:636
  12.1 3.5 copy-start.43
  12.1 4.2 copy-start.42
  13.0 262.6 %all-gather.13.cloned.1.call-start = ((), (), s32[]{:S(2)}) async-start(), calls=%async_computation.6 | async-start | bytes 2949120 | tf_op jit(solution)/shard_map/all_gather | solution.py:636
  15.0 570.6 %reduce-scatter.9.cloned.1.call-start = ((), (), s32[]{:S(2)}) async-start(), calls=%async_computation.9 | async-start | bytes 2949120 | tf_op jit(solution)/shard_map/reduce_scatter | solution.py:707
  145.1 76.0 %copy-start.19 = (bf16[8,1,2,64,3,64]{5,3,4,0,2,1:T(8,128)(2,1)}, bf16[8,1,2,64,3,64]{5,3,4,0,2,1:T(8,128)(2,1)S(1)}, u32[]{:S(2)}) copy-start(bf16[8,1,2,64,3,64]{5,3,4,0,2,1:T(8,128)(2,1)S(1)} %copy.171) | copy-start | bytes 1179652
  211.0 5.1 copy-start.45
  215.8 10.3 %copy-start.6 = (f32[2,128,1536]{2,1,0:T(8,128)}, f32[2,128,1536]{2,1,0:T(8,128)S(1)}, u32[]{:S(2)}) copy-start(f32[2,128,1536]{2,1,0:T(8,128)S(1)} %get-tuple-element.74) | copy-start | bytes 4718596
  221.1 4.6 copy-start.21
  225.6 5.3 copy-start.14
  226.0 4.9 copy-start.29
  226.0 6.0 copy-start.41
  266.0 33.9 %slice-start = ((s8[6291456]{0:T(1024)(128)(4,1)}), s8[2097152]{0:T(1024)(128)(4,1)S(1)}, s32[]{:S(2)}) async-start(s8[6291456]{0:T(1024)(128)(4,1)} %bitcast.256), calls=%async_computation.15 | async-start | bytes 4194304
  275.7 24.3 %slice-start.1 = ((s8[6291456]{0:T(1024)(128)(4,1)}), s8[4194304]{0:T(1024)(128)(4,1)S(1)}, s32[]{:S(2)}) async-start(s8[6291456]{0:T(1024)(128)(4,1)} %bitcast.256), calls=%async_computation.16 | async-start | bytes 8388608
  313.6 272.7 %reduce-scatter.11.cloned.1.call-start = ((), (), s32[]{:S(2)}) async-start(), calls=%async_computation.11 | async-start | bytes 2949120 | tf_op jit(solution)/shard_map/reduce_scatter | solution.py:707
  322.7 32.6 %copy-start.46 = (bf16[1536,768]{1,0:T(8,128)(2,1)S(1)}, bf16[1536,768]{1,0:T(8,128)(2,1)}, u32[]{:S(2)}) copy-start(bf16[1536,768]{1,0:T(8,128)(2,1)} %all-gather.11.cloned.1.call-done) | copy-start | bytes 7077892
  397.1 4.4 copy-start.2
  397.1 4.4 copy-start.4
  397.1 4.4 copy-start.5
  401.5 3.5 copy-start.13
  406.7 4.1 copy-start.31
  406.7 4.1 copy-start.16
  406.7 4.1 copy-start.22
  411.7 2.9 copy-start.7
  412.8 7.6 slice-start.2
  414.6 5.8 slice-start.3
  419.3 2.5 copy-start.25
  428.2 165.9 %reduce-scatter.13.cloned.1.call-start = ((), (), s32[]{:S(2)}) async-start(), calls=%async_computation.14 | async-start | bytes 2457600
  437.7 2.9 copy-start.28
  537.6 4.1 copy-start.15
  541.6 127.2 %reduce-scatter.7.cloned.1.call-start = ((), (), s32[]{:S(2)}) async-start(), calls=%async_computation.7 | async-start | bytes 5898240 | tf_op jit(solution)/shard_map/reduce_scatter | solution.py:707
  551.1 16.4 %copy-start.37 = (bf16[2,64,1536]{2,1,0:T(8,128)(2,1)S(1)}, bf16[2,64,1536]{2,1,0:T(8,128)(2,1)}, u32[]{:S(2)}) copy-start(bf16[2,64,1536]{2,1,0:T(8,128)(2,1)} %param.12) | copy-start | bytes 1179652
  577.8 3.1 copy-start.18
  585.6 175.3 %all-gather.17.cloned.1.call-start = ((), (), s32[]{:S(2)}) async-start(), calls=%async_computation.10 | async-start | bytes 1769472 | tf_op jit(solution)/shard_map/all_gather | solution.py:772
  586.3 177.6 %all-gather.19.cloned.1.call-start = ((), (), s32[]{:S(2)}) async-start(), calls=%async_computation.12 | async-start | bytes 1769472 | tf_op jit(solution)/shard_map/all_gather | solution.py:772
  586.9 183.7 %all-gather.15.cloned.1.call-start = ((), (), s32[]{:S(2)}) async-start(), calls=%async_computation.8 | async-start | bytes 3538944 | tf_op jit(solution)/shard_map/all_gather | solution.py:772
  672.5 12.3 %copy-start.44 = (f32[1536]{0:T(1024)S(1)}, f32[1536]{0:T(1024)}, u32[]{:S(2)}) copy-start(f32[1536]{0:T(1024)} %get-tuple-element.59) | copy-start | bytes 18436
  672.5 13.1 %copy-start.27 = (bf16[1536,576]{1,0:T(8,128)(2,1)S(1)}, bf16[1536,576]{1,0:T(8,128)(2,1)}, u32[]{:S(2)}) copy-start(bf16[1536,576]{1,0:T(8,128)(2,1)} %all-gather.9.cloned.1.call-done.w_ref) | copy-start | bytes 5308420
  774.0 4.3 copy-start.10
  786.5 5.7 copy-start.1
  788.9 2.7 copy-start.35
  (15 other events, 21.8 us)
Sparse Core Ops, SparseCore 0:
  10.2 46.2 all-gather.8
  58.6 59.0 all-gather.20
  119.9 49.1 all-gather.10
  171.1 49.2 all-gather.12
  313.7 45.8 reduce-scatter.8
  428.3 45.8 reduce-scatter.10
  541.7 39.3 reduce-scatter.12
  585.7 83.0 reduce-scatter.6
  670.3 24.4 all-gather.16
  696.2 35.0 all-gather.18
  733.4 37.1 all-gather.14

commit v3 on v2

--- a/solution.py
+++ b/solution.py
@@ -149,29 +149,27 @@
 
 
 class Scatter:
-    semaphores = 10
-
     @staticmethod
     def scratch(rows, columns):
         return [
             pltpu.VMEM((4, rows, columns), BF),
-            pltpu.VMEM((4, rows, columns), BF),
-            pltpu.VMEM((3, rows, columns), BF),
             pltpu.VMEM((2, rows // 2, columns), BF),
             pltpu.VMEM((2, rows, columns), BF),
-            pltpu.SemaphoreType.DMA((4,)),
             pltpu.SemaphoreType.DMA((10,)),
             pltpu.SemaphoreType.DMA((10,)),
         ]
 
-    def __init__(self, in_ref, out_ref, mine, core, sums, relay, final, local_sem, send, recv):
-        self.in_ref, self.out_ref = in_ref, out_ref
-        self.mine, self.core, self.sums = mine, core, sums
-        self.relay, self.final = relay, final
-        self.local_sem, self.send, self.recv = local_sem, send, recv
+    def __init__(self, part_ref, core, relay, final, send, recv):
+        self.part_ref, self.core, self.relay, self.final = part_ref, core, relay, final
+        self.send, self.recv = send, recv
         self.to_x, self.to_y, self.to_c = neighbours()
-        rows = out_ref.shape[0]
+        z, x, y, c = place()
+        chips = ((1 - x, 1 - y), (1 - x, y), (x, 1 - y), (x, y))
+        self.mine = [slot(*chip, c) for chip in chips]
+        self.theirs = [slot(*chip, 1 - c) for chip in chips]
+        rows = part_ref.shape[1]
         self.low, self.high = pl.ds(0, rows // 2), pl.ds(rows // 2, rows // 2)
+        self.sends = []
 
     def forward(self, index, source, target_ref, target):
         copy = remote_copy(
@@ -180,60 +178,82 @@
         copy.start()
         self.sends.append(copy)
 
-    def pair(self, index, part):
-        return self.mine[index, part].astype(F32) + self.core[index, part].astype(F32)
+    def arrived(self, index, ref):
+        remote_copy(ref, ref, self.send.at[index], self.recv.at[index], self.to_c).wait_recv()
+
+    def pass_core(self, index):
+        source = self.part_ref.at[self.theirs[index]]
+        self.forward(index, source, self.core.at[index], self.to_c)
+
+    def add(self, index, part, more=None):
+        mine = self.mine[index]
+        total = self.part_ref[mine, part].astype(F32) + self.core[index, part].astype(F32)
+        if more is not None:
+            total += more.astype(F32)
+        self.part_ref[mine, part] = total.astype(BF)
+        return self.part_ref.at[mine, part]
+
+    def far(self):
+        self.arrived(0, self.core.at[0])
+        self.forward(4, self.add(0, self.low), self.relay.at[0], self.to_x)
+        self.forward(5, self.add(0, self.high), self.relay.at[1], self.to_y)
+
+    def near(self):
+        self.arrived(1, self.core.at[1])
+        self.forward(6, self.add(1, self.low), self.final.at[0, self.low], self.to_x)
+        self.arrived(2, self.core.at[2])
+        self.forward(7, self.add(2, self.high), self.final.at[1, self.high], self.to_y)
+
+    def second(self):
+        low, high, final, relay = self.low, self.high, self.final, self.relay
+        self.arrived(5, relay.at[1])
+        self.forward(8, self.add(1, high, relay[1]), final.at[0, high], self.to_x)
+        self.arrived(4, relay.at[0])
+        self.forward(9, self.add(2, low, relay[0]), final.at[1, low], self.to_y)
+
+    def total(self):
+        self.arrived(3, self.core.at[3])
+        self.arrived(6, self.final.at[0, self.low])
+        self.arrived(7, self.final.at[1, self.high])
+        self.arrived(8, self.final.at[0, self.high])
+        self.arrived(9, self.final.at[1, self.low])
+        total = self.part_ref[self.mine[3]].astype(F32) + self.core[3].astype(F32)
+        return total + self.final[0].astype(F32) + self.final[1].astype(F32)
+
+    def finish(self):
+        for copy in self.sends:
+            copy.wait_send()
+
+
+class LoadedScatter(Scatter):
+    @staticmethod
+    def scratch(rows, columns):
+        return [
+            pltpu.VMEM((4, rows, columns), BF),
+            pltpu.SemaphoreType.DMA((4,)),
+        ] + Scatter.scratch(rows, columns)
+
+    def __init__(self, in_ref, part_ref, local_sem, *scratch):
+        super().__init__(part_ref, *scratch)
+        self.in_ref, self.local_sem = in_ref, local_sem
 
     def start(self):
-        z, x, y, c = place()
-        self.sends, self.loads = [], []
-        chips = ((1 - x, 1 - y), (1 - x, y), (x, 1 - y), (x, y))
-        for index, (cx, cy) in enumerate(chips):
-            self.forward(
-                index, self.in_ref.at[slot(cx, cy, 1 - c)], self.core.at[index], self.to_c
-            )
+        self.loads = []
+        for index, (mine, theirs) in enumerate(zip(self.mine, self.theirs)):
+            source = self.in_ref.at[theirs]
+            self.forward(index, source, self.core.at[index], self.to_c)
             load = pltpu.make_async_copy(
-                self.in_ref.at[slot(cx, cy, c)], self.mine.at[index], self.local_sem.at[index]
+                self.in_ref.at[mine], self.part_ref.at[index], self.local_sem.at[index]
             )
             load.start()
             self.loads.append(load)
-
-    def ready(self, index):
-        self.loads[index].wait()
-        self.sends[index].wait_recv()
+        self.mine = (0, 1, 2, 3)
 
     def first(self):
-        low, high, sums = self.low, self.high, self.sums
-        self.ready(0)
-        sums[0, low] = self.pair(0, low).astype(BF)
-        self.forward(4, sums.at[0, low], self.relay.at[0], self.to_x)
-        sums[0, high] = self.pair(0, high).astype(BF)
-        self.forward(5, sums.at[0, high], self.relay.at[1], self.to_y)
-        self.ready(1)
-        sums[1, low] = self.pair(1, low).astype(BF)
-        self.forward(6, sums.at[1, low], self.final.at[0, low], self.to_x)
-        self.ready(2)
-        sums[2, high] = self.pair(2, high).astype(BF)
-        self.forward(7, sums.at[2, high], self.final.at[1, high], self.to_y)
-        self.ready(3)
-
-    def second(self):
-        low, high, sums = self.low, self.high, self.sums
-        self.sends[5].wait_recv()
-        sums[1, high] = (self.pair(1, high) + self.relay[1].astype(F32)).astype(BF)
-        self.forward(8, sums.at[1, high], self.final.at[0, high], self.to_x)
-        self.sends[4].wait_recv()
-        sums[2, low] = (self.pair(2, low) + self.relay[0].astype(F32)).astype(BF)
-        self.forward(9, sums.at[2, low], self.final.at[1, low], self.to_y)
-
-    def total(self):
-        for index in (6, 7, 8, 9):
-            self.sends[index].wait_recv()
-        everything = self.pair(3, slice(None))
-        return everything + self.final[0].astype(F32) + self.final[1].astype(F32)
-
-    def finish(self):
-        for copy in self.sends:
-            copy.wait_send()
+        for load in self.loads:
+            load.wait()
+        self.far()
+        self.near()
 
 
 class Exchange:
@@ -272,7 +292,7 @@
 IN_VMEM = pl.BlockSpec(memory_space=pltpu.VMEM)
 
 
-def call(kernel, name, outs, out_specs, in_specs, scratch, ident=None):
+def call(kernel, name, outs, out_specs, in_specs, scratch, ident, micros):
     return pl.pallas_call(
         kernel,
         out_shape=outs,
@@ -280,10 +300,11 @@
         out_specs=out_specs,
         scratch_shapes=scratch,
         name=name,
+        cost_estimate=pl.CostEstimate(
+            flops=micros * 10**9, bytes_accessed=micros * 10**6, transcendentals=0
+        ),
         compiler_params=pltpu.CompilerParams(
-            collective_id=ident,
-            has_side_effects=ident is not None,
-            vmem_limit_bytes=VMEM_LIMIT,
+            collective_id=ident, has_side_effects=True, vmem_limit_bytes=VMEM_LIMIT
         ),
     )
 
@@ -300,22 +321,37 @@
     ]
 
 
-def gather_kernel(*refs):
+def gather_kernel(count, *refs):
     enter(neighbours())
-    job = Gather(*refs)
-    job.start()
-    job.rest()
-
-
-def plane_gather(values, ident):
-    rows, columns = values.shape
-    outs = shape(8, rows, columns, dtype=values.dtype)
-    return call(gather_kernel, "plane_gather", outs, ANY, [ANY], gather_scratch(), ident)(values)
+    jobs = []
+    for index in range(count):
+        scratch = refs[2 * count + 3 * index : 2 * count + 3 * index + 3]
+        jobs.append(Gather(refs[index], refs[count + index], *scratch))
+    for job in jobs:
+        job.start()
+    for job in jobs:
+        job.relay_y()
+        job.relay_x()
+    for job in jobs:
+        job.relay_far()
+    for job in jobs:
+        job.finish()
+
+
+def plane_gather(arrays, ident, micros):
+    count = len(arrays)
+    outs = tuple(shape(8, *values.shape, dtype=values.dtype) for values in arrays)
+    kernel = partial(gather_kernel, count)
+    scratch = gather_scratch() * count
+    any_space = [ANY] * count
+    return call(kernel, "plane_gather", outs, tuple(any_space), any_space, scratch, ident, micros)(
+        *arrays
+    )
 
 
 def scatter_kernel(in_ref, out_ref, *scratch):
     enter(neighbours())
-    job = Scatter(in_ref, out_ref, *scratch)
+    job = LoadedScatter(in_ref, *scratch)
     job.start()
     job.first()
     job.second()
@@ -323,11 +359,144 @@
     job.finish()
 
 
-def plane_scatter(values, ident):
+def plane_scatter(values, ident, micros):
     _, rows, columns = values.shape
     outs = shape(rows, columns, dtype=F32)
-    scratch = Scatter.scratch(rows, columns)
-    return call(scatter_kernel, "plane_scatter", outs, IN_VMEM, [ANY], scratch, ident)(values)
+    scratch = LoadedScatter.scratch(rows, columns)
+    return call(
+        scatter_kernel, "plane_scatter", outs, IN_VMEM, [ANY], scratch, ident, micros
+    )(values)
+
+
+def feed_kernel(
+    own_ref, grad_ref, up_ref, down_ref,
+    normed_out, branch_out, up_out, down_out,
+    rows_ref, grads_ref, hidden_ref, slope_ref, part_a, part_b,
+    load_sem, g_local, g_send, g_recv, *scratch,
+):
+    enter(neighbours())
+    gather = Gather(own_ref, rows_ref, g_local, g_send, g_recv)
+    gather.start()
+    blocks, _, width = rows_ref.shape
+    loads = []
+    for block in range(blocks):
+        load = pltpu.make_async_copy(grad_ref.at[block], grads_ref.at[block], load_sem.at[block])
+        load.start()
+        loads.append(load)
+    for load in loads:
+        load.wait()
+
+    def early(block, carry):
+        slope_ref[block] = nn(grads_ref[block], down_ref[...]).astype(BF)
+        return carry
+
+    lax.fori_loop(0, blocks, early, 0)
+
+    def middle(block):
+        before = nn(rows_ref[block], up_ref[...])
+        share = 0.5 + 0.5 * lax.erf(before * (0.5**0.5))
+        hidden_ref[block] = (before * share).astype(BF)
+        slope = share + before * (jnp.exp(-0.5 * before * before) * (2.0 * jnp.pi) ** (-0.5))
+        slope = (slope_ref[block].astype(F32) * slope).astype(BF)
+        slope_ref[block] = slope
+        part_a[block] = nt(slope, up_ref[...]).astype(BF)
+
+    size = len(scratch) // 2
+    first = Scatter(part_a, *scratch[:size])
+    other = Scatter(part_b, *scratch[size:])
+    x, y, c = gather.spot
+
+    def pair(cx, cy):
+        def one(index, carry):
+            middle(slot(cx, cy, 0) + index)
+            return carry
+
+        lax.fori_loop(0, 2, one, 0)
+
+    gather.own.wait()
+    gather.arrived(2, slot(x, y, 1 - c), 0, gather.rows)
+    pair(x, y)
+    first.pass_core(3)
+    gather.relay_y()
+    gather.relay_x()
+    gather.arrived(6, slot(1 - x, y, 1 - c), 0, gather.rows)
+    pair(1 - x, y)
+    first.pass_core(1)
+    gather.arrived(5, slot(x, 1 - y, 1 - c), 0, gather.rows)
+    pair(x, 1 - y)
+    first.pass_core(2)
+    gather.relay_far()
+    first.near()
+    gather.arrived(7, slot(1 - x, 1 - y, 1 - c), 0, gather.rows // 2)
+    gather.arrived(8, slot(1 - x, 1 - y, 1 - c), gather.rows // 2, gather.rows // 2)
+    pair(1 - x, 1 - y)
+    first.pass_core(0)
+    first.far()
+    for copy in gather.sends:
+        copy.wait_send()
+
+    def branch(block, carry):
+        part_b[block] = nt(hidden_ref[block], down_ref[...]).astype(BF)
+        return carry
+
+    lax.fori_loop(0, blocks, branch, 0)
+    for index in range(4):
+        other.pass_core(index)
+    first.second()
+    other.far()
+    other.near()
+    tile = 256
+    hidden_width = hidden_ref.shape[2]
+
+    def weight(left_ref, right_ref, out_ref):
+        def one(index, carry):
+            lanes = pl.ds(pl.multiple_of(index * tile, tile), tile)
+            left = left_ref[:, :, lanes].reshape(-1, tile)
+            right = right_ref[...].reshape(-1, hidden_width)
+            out_ref[lanes, :] = lax.dot_general(
+                left, right, (((0,), (0,)), ((), ())), preferred_element_type=F32
+            ).astype(BF)
+            return carry
+
+        lax.fori_loop(0, width // tile, one, 0)
+
+    weight(grads_ref, hidden_ref, down_out)
+    normed_out[...] = first.total()
+    other.second()
+    weight(rows_ref, slope_ref, up_out)
+    branch_out[...] = other.total()
+    first.finish()
+    other.finish()
+
+
+def feed_forward(own, grads, w_up, w_down, ident):
+    rows, width = own.shape
+    hidden = w_up.shape[1]
+    outs = (
+        shape(rows, width, dtype=F32),
+        shape(rows, width, dtype=F32),
+        shape(width, hidden),
+        shape(width, hidden),
+    )
+    scratch = [
+        pltpu.VMEM((8, rows, width), BF),
+        pltpu.VMEM((8, rows, width), BF),
+        pltpu.VMEM((8, rows, hidden), BF),
+        pltpu.VMEM((8, rows, hidden), BF),
+        pltpu.VMEM((8, rows, width), BF),
+        pltpu.VMEM((8, rows, width), BF),
+        pltpu.SemaphoreType.DMA((8,)),
+    ]
+    return call(
+        feed_kernel,
+        "feed_forward",
+        outs,
+        (IN_VMEM,) * 4,
+        [ANY, ANY, IN_VMEM, IN_VMEM],
+        scratch + gather_scratch() + Scatter.scratch(rows, width) * 2,
+        ident,
+        90,
+    )(own, grads, w_up, w_down)
 
 
 SIDE = 256
@@ -430,12 +599,13 @@
         ]
         + gather_scratch(),
         ident,
+        45,
     )(rows, weights, cotangent)
 
 
 def backward_kernel(
-    grad_ref, qkv_ref, mix_ref, log_ref, side_ref,
-    out_ref, side_out,
+    grad_ref, qkv_ref, mix_ref, log_ref, side_ref, text_ref,
+    out_ref, side_out, text_out,
     grad_all, query_turned, ex_local, ex_send, ex_recv, *scratch,
 ):
     enter(plane_others())
@@ -447,7 +617,11 @@
     step = SIDE // rows
     for clip in range(2):
         exchange.start(clip, pl.ds(clip * rows, rows))
-    side = Scatter(side_ref, side_out, *scratch)
+    size = len(scratch) // 2
+    text = LoadedScatter(text_ref, *scratch[size:])
+    text.start()
+    text.first()
+    side = LoadedScatter(side_ref, *scratch[:size])
     side.start()
     side.first()
     for clip in range(2):
@@ -492,20 +666,24 @@
             grad_query = grad_query.astype(BF).reshape(blocks, rows, HEAD_DIM)
             out_ref[:, part, lanes[0]] = grad_query
         if clip == 0:
+            text.second()
             side.second()
+    text_out[...] = text.total()
     side_out[...] = side.total().astype(BF)
+    text.finish()
     side.finish()
 
 
-def attend_backward(grad_mix, qkv, mix, logs, side, ident):
+def attend_backward(grad_mix, qkv, mix, logs, side, text, ident):
     blocks, block, columns = mix.shape
     _, rows, width = side.shape
+    text_shape = text.shape[1:]
     return call(
         backward_kernel,
         "attend_backward",
-        (shape(blocks, block, 3 * columns), shape(rows, width)),
-        (IN_VMEM, IN_VMEM),
-        [ANY, IN_VMEM, IN_VMEM, IN_VMEM, ANY],
+        (shape(blocks, block, 3 * columns), shape(rows, width), shape(*text_shape, dtype=F32)),
+        (IN_VMEM, IN_VMEM, IN_VMEM),
+        [ANY, IN_VMEM, IN_VMEM, IN_VMEM, ANY, ANY],
         [
             pltpu.VMEM((blocks, block, columns), BF),
             pltpu.VMEM((HEAD_DIM, blocks * block // 2), F32),
@@ -513,14 +691,16 @@
             pltpu.SemaphoreType.DMA((2, 7)),
             pltpu.SemaphoreType.DMA((2, 7)),
         ]
-        + Scatter.scratch(rows, width),
+        + LoadedScatter.scratch(rows, width)
+        + LoadedScatter.scratch(*text_shape),
         ident,
-    )(grad_mix, qkv, mix, logs, side)
+        75,
+    )(grad_mix, qkv, mix, logs, side, text)
 
 
 def last_kernel(
-    part_ref, frames_ref, gain_ref, grad_ref, stats_ref,
-    out_ref, total_ref,
+    part_ref, frames_ref, gain_ref, grad_ref, stats_ref, text_ref,
+    out_ref, total_ref, text_out,
     mine, came, all_ref, st_send, st_recv, z_send, z_recv, *scratch,
 ):
     z = lax.axis_index("shard")
@@ -528,14 +708,20 @@
     others = [lax.rem(z + i, shards) for i in range(1, shards)]
     spot = place()[1:]
     enter(neighbours() + [device(other, *spot) for other in others])
-    job = Scatter(part_ref, out_ref, *scratch)
+    size = len(scratch) // 2
+    text = LoadedScatter(text_ref, *scratch[size:])
+    text.start()
+    job = LoadedScatter(part_ref, *scratch[:size])
     job.start()
     inputs = frames_ref[...].astype(F32)
     average = jnp.mean(inputs, axis=-1, keepdims=True)
     centred = inputs - average
     rate = lax.rsqrt(jnp.mean(centred * centred, axis=-1, keepdims=True) + EPS)
+    text.first()
     job.first()
+    text.second()
     job.second()
+    text_out[...] = text.total()
     grads = job.total()
     normed = centred * rate
     mine[0] = stats_ref[...]
@@ -570,17 +756,22 @@
     total_ref[...] = total
     for copy in sends:
         copy.wait_send()
+    text.finish()
     job.finish()
 
 
-def last_step(part, frames, gain, grad, stats, shards, ident):
+def last_step(part, frames, gain, grad, stats, text, shards, ident):
     _, rows, width = part.shape
     return call(
         last_kernel,
         "last_step",
-        (shape(rows, width, dtype=F32), shape(8, width, dtype=F32)),
-        (IN_VMEM, IN_VMEM),
-        [ANY, IN_VMEM, IN_VMEM, IN_VMEM, IN_VMEM],
+        (
+            shape(rows, width, dtype=F32),
+            shape(8, width, dtype=F32),
+            shape(*text.shape[1:], dtype=F32),
+        ),
+        (IN_VMEM, IN_VMEM, IN_VMEM),
+        [ANY, IN_VMEM, IN_VMEM, IN_VMEM, IN_VMEM, ANY],
         [
             pltpu.VMEM((4, 8, width), F32),
             pltpu.VMEM((3, 8, width), F32),
@@ -590,9 +781,11 @@
             pltpu.SemaphoreType.DMA((shards - 1,)),
             pltpu.SemaphoreType.DMA((shards - 1,)),
         ]
-        + Scatter.scratch(rows, width),
+        + LoadedScatter.scratch(rows, width)
+        + LoadedScatter.scratch(*text.shape[1:]),
         ident,
-    )(part, frames, gain, grad, stats)
+        50,
+    )(part, frames, gain, grad, stats, text)
 
 
 def dots(spec, *operands):
@@ -648,13 +841,21 @@
 
     stream_zero = frames.astype(F32)
     norm_one = layer_norm(stream_zero, norm_gain[0], norm_bias[0])
-    all_one = plane_gather(norm_one.astype(BF).reshape(block, width), 0)
+    (all_one,) = plane_gather([norm_one.astype(BF).reshape(block, width)], 0, 33)
     flat_one = all_one.reshape(8 * block, width)
     qkv, self_log, mix, my_mix, all_grad = attend_forward(
         all_one, w_qkv, cotangent.reshape(block, width), 1
     )
 
-    plane_w = plane_gather(w_side[:3].reshape(3 * columns, width), 2)
+    text_part = dots("cnd,ted->tcne", text_states, w_side[3:]).astype(BF)
+    plane_w, text_all = plane_gather(
+        [
+            w_side[:3].reshape(3 * columns, width),
+            text_part.reshape(2 * clips * texts, columns),
+        ],
+        2,
+        65,
+    )
     plane_w = plane_w.reshape(8, 3, columns, width)
     w_out, w_query, w_cross = plane_w[:, 0], plane_w[:, 1], plane_w[:, 2]
     branch_one = dots("bre,bed->rd", my_mix, w_out).reshape(clips, rows, width)
@@ -662,8 +863,6 @@
     norm_two, norm_two_back = jax.vjp(layer_norm, stream_one, norm_gain[1], norm_bias[1])
     low_two = norm_two.astype(BF)
     cross_q = dots("cfd,bed->cfbe", low_two, w_query).astype(BF)
-    text_part = dots("cnd,ted->tcne", text_states, w_side[3:]).astype(BF)
-    text_all = plane_gather(text_part.reshape(2 * clips * texts, columns), 3)
     text_all = text_all.reshape(8, 2, clips, texts, heads, HEAD_DIM)
     text_k, text_v = text_all[:, 0], text_all[:, 1]
     cross_q = cross_q.reshape(clips, rows, 8, heads, HEAD_DIM)
@@ -679,13 +878,9 @@
     stream_two = stream_one + branch_two
 
     norm_three, norm_three_back = jax.vjp(layer_norm, stream_two, norm_gain[2], norm_bias[2])
-    all_three = plane_gather(norm_three.astype(BF).reshape(block, width), 4)
-    flat_three = all_three.reshape(8 * block, width)
-    pre_act = dots("rd,dh->rh", flat_three, w_up)
-    hidden, gelu_back = jax.vjp(partial(jax.nn.gelu, approximate=False), pre_act)
-    hidden_low = hidden.astype(BF)
-    part_three = dots("rh,dh->rd", hidden_low, w_down).astype(BF)
-    branch_three = plane_scatter(part_three.reshape(8, block, width), 5)
+    grad_normed, branch_three, grad_up, grad_down = feed_forward(
+        norm_three.astype(BF).reshape(block, width), all_grad, w_up, w_down, 4
+    )
     branch_three = branch_three.reshape(clips, rows, width)
     stream_out = stream_two + branch_three
     squares = jnp.stack(
@@ -697,17 +892,10 @@
         ]
     )
 
-    flat_grad = all_grad.reshape(8 * block, width)
-    grad_hidden = dots("rd,dh->rh", flat_grad, w_down)
-    grad_pre = gelu_back(grad_hidden)[0].astype(BF)
-    part_norm = dots("rh,dh->rd", grad_pre, w_up).astype(BF)
-    grad_normed = plane_scatter(part_norm.reshape(8, block, width), 7)
-
     def to_shard(part):
         return lax.psum_scatter(part.astype(BF), "shard", scatter_dimension=0, tiled=True)
 
-    grad_down = to_shard(dots("rd,rh->dh", flat_grad, hidden_low))
-    grad_up = to_shard(dots("rd,rh->dh", flat_three, grad_pre))
+    grad_down, grad_up = to_shard(grad_down), to_shard(grad_up)
     grad_inner, gain_three, shift_three = norm_three_back(grad_normed.reshape(clips, rows, width))
     grad_two = cotangent.astype(F32) + grad_inner
 
@@ -731,19 +919,21 @@
     grad_mix = dots("rd,bed->bre", grad_low, w_out).astype(BF)
     w_grad_out = dots("rd,bre->bed", grad_low, my_mix)
 
-    text_grads = jnp.stack([grad_text_k, grad_text_v], axis=1).astype(BF)
-    text_grads = plane_scatter(text_grads.reshape(8, 2 * clips * texts, columns), 9)
-    text_grads = text_grads.reshape(2, clips, texts, columns)
-    text_grads_low = text_grads.astype(BF)
-    w_grad_text = dots("cnd,tcne->ted", text_states, text_grads_low)
-    grad_text = dots("tcne,ted->cnd", text_grads_low, w_side[3:])
-    grad_text = grad_text.reshape(clips, 8, texts // 8, width).transpose(1, 0, 2, 3).astype(BF)
-    grad_text = plane_scatter(grad_text.reshape(8, clips * texts // 8, width), 10)
-    grad_text = grad_text.reshape(clips, texts // 8, width)
-
     part_side = jnp.stack([w_grad_out, w_grad_query, w_grad_cross], axis=1).astype(BF)
     part_side = part_side.reshape(8, 3 * columns, width)
-    grad_qkv, part_side = attend_backward(grad_mix, qkv, mix, self_log, part_side, 8)
+    text_grads = jnp.stack([grad_text_k, grad_text_v], axis=1).astype(BF)
+    text_grads = text_grads.reshape(8, 2 * clips * texts, columns)
+    grad_qkv, part_side, text_grads = attend_backward(
+        grad_mix, qkv, mix, self_log, part_side, text_grads, 8
+    )
+    text_grads = text_grads.reshape(2, clips, texts, columns).astype(BF)
+    w_grad_text = dots("cnd,tcne->ted", text_states, text_grads).astype(BF)
+    part_side = jnp.concatenate([part_side, w_grad_text.reshape(2 * columns, width)], axis=0)
+    part_side = part_side.reshape(5 * columns, slices, depth).transpose(1, 0, 2)
+    grad_side = to_shard(part_side)
+    grad_text = dots("tcne,ted->cnd", text_grads, w_side[3:])
+    grad_text = grad_text.reshape(clips, 8, texts // 8, width).transpose(1, 0, 2, 3).astype(BF)
+    grad_text = grad_text.reshape(8, clips * texts // 8, width)
     grad_qkv = grad_qkv.reshape(8 * block, 3 * columns)
     part_norm = dots("re,de->rd", grad_qkv, w_qkv).astype(BF)
     grad_w_qkv = to_shard(dots("rd,re->de", flat_one, grad_qkv))
@@ -752,28 +942,27 @@
         v[None] for v in (gain_two, shift_two, gain_three, shift_three)
     ]
     stats.append(jnp.pad(squares, (0, width - 4))[None])
-    grad_frames, totals = last_step(
+    grad_frames, totals, grad_text = last_step(
         part_norm.reshape(8, block, width),
         frames.reshape(block, width),
         norm_gain[0][None],
         grad_one.reshape(block, width),
         jnp.concatenate(stats + [nothing], axis=0),
+        grad_text,
         lax.axis_size("shard"),
         11,
     )
     grad_frames = grad_frames.reshape(clips, rows, width)
-
-    part_side = part_side.reshape(3, columns, width)
-    part_side = jnp.concatenate([part_side, w_grad_text.astype(BF)], axis=0)
-    part_side = part_side.reshape(5, columns, slices, depth).transpose(2, 0, 1, 3)
-    grad_side = to_shard(part_side)[0]
+    grad_text = grad_text.reshape(clips, texts // 8, width)
+
+    grad_w_qkv, grad_side, totals = lax.optimization_barrier((grad_w_qkv, grad_side, totals))
 
     def whole(values):
         return lax.all_gather(values, "context", axis=values.ndim - 1, tiled=True).astype(F32)
 
     grad_up, grad_down = whole(grad_up), whole(grad_down)
     grad_self = jnp.stack([grad_w_qkv[:, j * columns : (j + 1) * columns] for j in range(3)])
-    grad_side = grad_side.transpose(0, 2, 1)
+    grad_side = grad_side.reshape(5, columns, depth).transpose(0, 2, 1)
     grad_all = whole(jnp.concatenate([grad_self, grad_side], axis=0))
 
     gains = jnp.stack([totals[0], totals[2], totals[4]])

time: 804 us -> 682 us (0.85)
  matrix products: 126 us -> 56.8 us
  Pallas kernels: 416 us -> 376 us
  waiting for transfers between devices: 96.6 us -> 117 us
  other arithmetic: 56.7 us -> 38.4 us
  local copies, waits for them, and re-layouts: 87.6 us -> 72.7 us
    all_gather x3, waiting for transfers between devices: 3.76 us -> 76.7 us  [whole(): lax.all_gather(values, 'context', axis=values.ndim - 1, tiled=True)]
    dot_general x25 -> x19, matrix products: 123 us -> 54.8 us  [dots(): return jnp.einsum(spec, *operands, preferred_element_type=F32)]
    reduce_scatter x3, waiting for transfers between devices: 72.4 us -> 21.2 us  [to_shard(): lax.psum_scatter(part.astype(BF), 'shard', scatter_dimension=0, tiled=True)]
    pallas_call x8 -> x3, Pallas kernels: 230 us -> 196 us  [the longest x2 103 us: plane_gather(): call(kernel, 'plane_gather', outs, tuple(any_space), any_space, scratch,...]
    pallas_call x1, Pallas kernels: 62.9 us -> 52.2 us  [last_step(): call(last_kernel, 'last_step', (shape(rows, width, dtype=F32), shape(8, w...]
    concatenate x4 -> x3, local copies, waits for them, and re-layouts: 11.9 us -> 2.84 us  [on_device(): jnp.concatenate([part_side, w_grad_text.reshape(2 * columns, width)], axi...]
    convert_element_type x4 -> x3, other arithmetic: 10.6 us -> 2.48 us  [the longest x1 1.25 us: on_device(): all_one, = plane_gather([norm_one.astype(BF).reshape(block, width)], 0, 33)]
    unnamed x118 -> x121, local copies, waits for them, and re-layouts: 30.1 us -> 28.5 us
  transfers between devices with their start and end apart: 11 -> 11, of which waited for: 4 -> 6; matrix products, arithmetic and copies ran while one was open for 25% -> 18% of each run, Pallas kernels for 52% -> 42%
where the time goes in v3:
time: 682 us; the launch traced here: 677 us
  Pallas kernels  376 us (55%)
  waiting for transfers between devices  117 us (17%)
  local copies, waits for them, and re-layouts  72.7 us (11%)
  matrix products  56.8 us (8%)
  other arithmetic  38.4 us (6%)
  between operations  14.9 us (2%)
    pallas_call x2, Pallas kernels, plane_gather(): call(kernel, 'plane_gather', outs, tuple(any_space), any_space, scratch,...  103 us
    pallas_call x1, Pallas kernels, feed_forward(): call(feed_kernel, 'feed_forward', outs, (IN_VMEM,) * 4, [ANY, ANY, IN_VME...  93.1 us
    pallas_call x1, Pallas kernels, attend_backward(): call(backward_kernel, 'attend_backward', (shape(blocks, block, 3 * column...  81.9 us
    all_gather x3, waiting for transfers between devices, whole(): lax.all_gather(values, 'context', axis=values.ndim - 1, tiled=True)  76.7 us
    dot_general x19, matrix products, dots(): return jnp.einsum(spec, *operands, preferred_element_type=F32)  54.8 us
    pallas_call x1, Pallas kernels, last_step(): call(last_kernel, 'last_step', (shape(rows, width, dtype=F32), shape(8, w...  52.2 us
    pallas_call x1, Pallas kernels, attend_forward(): call(forward_kernel, 'attend_forward', (shape(blocks, block, 3 * columns)...  46 us
    unnamed x121, local copies, waits for them, and re-layouts  28.5 us
  transfers between devices with their start and end apart: 11, of which 6 were waited for; matrix products, arithmetic and copies ran while one was open for 18% of the time, Pallas kernels for 42%

profile of v3, /device:TPU:0, one launch (start us, length us, event | category | flops | bytes accessed | tf_op | source)
XLA Modules:
  0.0 677.0 jit_solution(15690820015786086963)
XLA Ops:
  18.1 34.4 %plane_gather.2.rows_ref = bf16[8,256,1536]{2,1,0:T(8,128)(2,1)} custom-call(bf16[256,1536]{1,0:T(8,128)(2,1)} %bitcast.251), custom_call_target="tpu_custom_call" | custom-call | flops 32999999488 | bytes 33000000 | tf_op jit(solution)/shard_map/plane_gather/pallas_call | solution.py:347
  52.5 4.0 all-gather.9.cloned.1.call-done.w_ref
  56.5 46.0 %attend_forward.1 = (bf16[8,256,576]{2,1,0:T(8,128)(2,1)}, f32[6,1024]{1,0:T(8,128)}, bf16[8,256,192]{2,1,0:T(8,128)(2,1)}, bf16[8,256,192]{2,1,0:T(8,128)(2,1)}, bf16[8,256,1536]{2,1,0:T(8,128)(2,1)}) custom-call(bf16[8,256,1536]{2,1,0:T(8,128)(2,1)} %plane_gather.2.rows_ref, bf16[1536,576]{1,0:T(8,128)(2,1)} %all-gather.9.cloned.1.call-done.w_ref, ...), custom_call_target="tpu_custom_call" | custom-call | flops 44999999488 | bytes 45000000 | tf_op jit(solution)/shard_map/attend_forward/pallas_call | solution.py:583
  102.4 15.3 %all-gather.21.cloned.1.call-done = bf16[20,192,384]{2,1,0:T(8,128)(2,1)} async-done(((bf16[5,192,384]{2,1,0:T(8,128)(2,1)}), bf16[20,192,384]{2,1,0:T(8,128)(2,1)}) %all-gather.21.cloned.1.call-update) | async-done | bytes 2949136 | tf_op jit(solution)/shard_map/all_gather | solution.py:829
  117.7 4.1 copy.189
  122.9 1.7 copy.166
  126.8 68.2 %plane_gather.3 = (bf16[8,576,1536]{2,1,0:T(8,128)(2,1)}, bf16[8,256,192]{2,1,0:T(8,128)(2,1)}) custom-call(bf16[576,1536]{1,0:T(8,128)(2,1)} %bitcast.246, bf16[256,192]{1,0:T(8,128)(2,1)} %bitcast.275), custom_call_target="tpu_custom_call" | custom-call | flops 65000001536 | bytes 65000000 | tf_op jit(solution)/shard_map/plane_gather/pallas_call | solution.py:347
  195.0 4.5 fusion.74
  199.5 2.7 copy.114
  202.3 3.3 reshape.205
  205.5 2.8 fusion.75
  209.5 1.8 copy.162
  211.4 4.7 fusion.28
  216.1 2.0 fusion.77
  220.2 4.9 fusion.73
  227.1 93.1 %feed_forward.1 = (f32[256,1536]{1,0:T(8,128)}, f32[256,1536]{1,0:T(8,128)}, bf16[1536,768]{1,0:T(8,128)(2,1)}, bf16[1536,768]{1,0:T(8,128)(2,1)}) custom-call(bf16[256,1536]{1,0:T(8,128)(2,1)} %bitcast.258, bf16[8,256,1536]{2,1,0:T(8,128)(2,1)} %get-tuple-element.35.grad_ref, bf16[1536,768]{1,0:T(8,128)(2,1)} %all-gather.11.cloned.1.call-done.up_ref, ...), custom_call_target="tpu_custom_call" | custom-call | flops 89999998976 | bytes 90000000 | tf_op jit(solution)/shard_map/feed_forward/pallas_call | solution.py:490
  320.1 3.9 multiply_reduce_fusion.4
  324.0 2.8 add_add_fusion.1
  328.4 4.1 fusion.27
  336.2 5.0 fusion.71
  341.3 2.7 multiply_reduce_fusion.5
  344.1 3.0 fusion.72
  348.0 3.8 fusion.29
  353.1 2.9 fusion.12
  357.6 1.8 fusion.11
  359.4 1.7 pad_maximum_fusion
  361.1 5.5 copy.123
  368.9 2.5 copy.153
  371.4 4.9 reshape.241.text_ref
  376.8 81.9 %attend_backward.1 = (bf16[8,256,576]{2,1,0:T(8,128)(2,1)}, bf16[576,1536]{1,0:T(8,128)(2,1)}, f32[256,192]{1,0:T(8,128)}) custom-call(bf16[8,256,192]{2,1,0:T(8,128)(2,1)} %bitcast.250, bf16[8,256,576]{2,1,0:T(8,128)(2,1)} %get-tuple-element.38.qkv_ref, bf16[8,256,192]{2,1,0:T(8,128)(2,1)} %get-tuple-element.39.mix_ref, ...), custom_call_target="tpu_custom_call" | custom-call | flops 74999996416 | bytes 75000000 | tf_op jit(solution)/shard_map/attend_backward/pallas_call | solution.py:681
  458.7 7.4 %bitcast_convert_fusion.2 = bf16[1536,576]{0,1:T(8,128)(2,1)S(1)} fusion(bf16[8,256,1536]{2,1,0:T(8,128)(2,1)} %plane_gather.2.rows_ref, bf16[8,256,576]{2,1,0:T(8,128)(2,1)} %get-tuple-element.41), kind=kOutput, calls=%fused_computation.20 | convolution fusion | flops 3624763392 | bytes 10420224 | tf_op jit(solution)/shard_map/rd,re->de/dot_general | solution.py:792
  466.2 2.3 copy.154
  471.0 2.5 concatenate.24
  475.2 1.9 maximum_bitcast_fusion
  481.2 2.7 select_maximum_fusion
  485.9 9.0 %convolution_convert_fusion = bf16[2048,1536]{1,0:T(8,128)(2,1)} fusion(bf16[2048,576]{1,0:T(8,128)(2,1)} %bitcast.272, bf16[1536,576]{1,0:T(8,128)(2,1)} %all-gather.9.cloned.1.call-done.w_ref), kind=kOutput, calls=%fused_computation.4 | convolution fusion | flops 3627024384 | bytes 10420224 | tf_op jit(solution)/shard_map/re,de->rd/dot_general | solution.py:792
  495.2 52.2 %last_step.1 = (f32[256,1536]{1,0:T(8,128)}, f32[8,1536]{1,0:T(8,128)}, f32[16,1536]{1,0:T(8,128)}) custom-call(bf16[8,256,1536]{2,1,0:T(8,128)(2,1)} %bitcast.271, bf16[256,1536]{1,0:T(8,128)(2,1)} %bitcast.240, f32[1,1536]{1,0:T(1,128)} %get-tuple-element.127.gain_ref, f32[256,1536]{1,0:T(8,128)} %bitcast.248, f32[8,1536]{1,0:T(8,128)} %concatenate.22.stats_ref, ...), custom_call_target="tpu_custom_call" | custom-call | flops 49999998976 | bytes 50000000 | tf_op jit(solution)/shard_map/last_step/pallas_call | solution.py:765
  548.7 21.2 %reduce-scatter.7.cloned.1.call-done = bf16[1,960,384]{2,1,0:T(8,128)(2,1)} async-done(((bf16[4,960,384]{2,1,0:T(8,128)(2,1)}), bf16[1,960,384]{2,1,0:T(8,128)(2,1)}) %reduce-scatter.7.cloned.1.call-update) | async-done | bytes 737296 | tf_op jit(solution)/shard_map/reduce_scatter | solution.py:896
  569.9 2.3 pad_maximum_fusion.3
  572.2 22.0 %all-gather.17.cloned.1.call-done = bf16[384,1536]{1,0:T(8,128)(2,1)} async-done(((bf16[384,768]{1,0:T(8,128)(2,1)}), bf16[384,1536]{1,0:T(8,128)(2,1)}) %all-gather.17.cloned.1.call-update) | async-done | bytes 1179664 | tf_op jit(solution)/shard_map/all_gather | solution.py:961
  594.2 3.0 convert_element_type.131
  597.1 21.3 %all-gather.19.cloned.1.call-done = bf16[384,1536]{1,0:T(8,128)(2,1)} async-done(((bf16[384,768]{1,0:T(8,128)(2,1)}), bf16[384,1536]{1,0:T(8,128)(2,1)}) %all-gather.19.cloned.1.call-update) | async-done | bytes 1179664 | tf_op jit(solution)/shard_map/all_gather | solution.py:961
  618.4 3.0 convert_element_type.132
  623.3 33.4 %all-gather.15.cloned.1.call-done = bf16[8,384,384]{1,2,0:T(8,128)(2,1)} async-done(((bf16[8,384,192]{1,2,0:T(8,128)(2,1)}), bf16[8,384,384]{1,2,0:T(8,128)(2,1)}) %all-gather.15.cloned.1.call-update) | async-done | bytes 2359312 | tf_op jit(solution)/shard_map/all_gather | solution.py:961
  656.7 2.5 slice.150
  659.2 3.0 copy.134
  663.9 1.8 copy.136
  666.8 2.8 copy.193
  (214 shorter events, 48.1 us)
Async XLA Ops:
  7.2 4.9 copy-start
  7.2 2.6 copy-start.39
  7.2 49.3 %all-gather.9.cloned.1.call-start = ((), (), s32[]{:S(2)}) async-start(), calls=%async_computation.4 | async-start | bytes 2457600 | tf_op jit(solution)/shard_map/all_gather | solution.py:829
  9.8 108.0 %all-gather.21.cloned.1.call-start = ((), (), s32[]{:S(2)}) async-start(), calls=%async_computation.13 | async-start | bytes 3686400 | tf_op jit(solution)/shard_map/all_gather | solution.py:829
  12.0 1.5 copy-start.42
  12.0 215.0 %all-gather.11.cloned.1.call-start = ((), (), s32[]{:S(2)}) async-start(), calls=%async_computation.5 | async-start | bytes 2949120 | tf_op jit(solution)/shard_map/all_gather | solution.py:829
  12.1 2.3 copy-start.52
  12.1 3.0 copy-start.51
  12.1 4.2 copy-start.13
  13.0 214.0 %all-gather.13.cloned.1.call-start = ((), (), s32[]{:S(2)}) async-start(), calls=%async_computation.6 | async-start | bytes 2949120 | tf_op jit(solution)/shard_map/all_gather | solution.py:829
  14.4 470.7 %reduce-scatter.9.cloned.1.call-start = ((), (), s32[]{:S(2)}) async-start(), calls=%async_computation.9 | async-start | bytes 2949120 | tf_op jit(solution)/shard_map/reduce_scatter | solution.py:896
  122.9 1.7 copy-start.11
  126.8 68.2 %copy-start.14 = (bf16[2,128,1536]{2,1,0:T(8,128)(2,1)S(1)}, bf16[2,128,1536]{2,1,0:T(8,128)(2,1)}, u32[]{:S(2)}) copy-start(bf16[2,128,1536]{2,1,0:T(8,128)(2,1)} %param.11) | copy-start | bytes 2359300
  126.8 68.2 %copy-start.30 = (bf16[8,256,192]{2,1,0:T(8,128)(2,1)S(1)}, bf16[8,256,192]{2,1,0:T(8,128)(2,1)}, u32[]{:S(2)}) copy-start(bf16[8,256,192]{2,1,0:T(8,128)(2,1)} %get-tuple-element.32) | copy-start | bytes 2359300
  199.5 20.7 %copy-start.7 = (f32[2,128,1536]{2,1,0:T(8,128)}, f32[2,128,1536]{2,1,0:T(8,128)S(1)}, u32[]{:S(2)}) copy-start(f32[2,128,1536]{2,1,0:T(8,128)S(1)} %get-tuple-element.106) | copy-start | bytes 4718596
  208.4 3.0 copy-start.48
  208.4 3.0 copy-start.53
  218.1 2.1 copy-start.17
  218.1 1.7 copy-start.24
  218.3 1.8 copy-start.15
  220.2 4.9 copy-start.32
  225.1 95.1 %copy-start.3 = (f32[2,128,1536]{2,1,0:T(8,128)}, f32[2,128,1536]{2,1,0:T(8,128)S(1)}, u32[]{:S(2)}) copy-start(f32[2,128,1536]{2,1,0:T(8,128)S(1)} %get-tuple-element.104) | copy-start | bytes 4718596
  320.1 3.9 copy-start.2
  320.1 3.9 copy-start.5
  328.4 4.1 copy-start.36
  328.4 4.1 copy-start.18
  328.4 4.1 copy-start.25
  334.5 1.7 copy-start.8
  335.4 5.7 copy-start.37
  341.2 153.7 %reduce-scatter.11.cloned.1.call-start = ((), (), s32[]{:S(2)}) async-start(), calls=%async_computation.11 | async-start | bytes 2949120 | tf_op jit(solution)/shard_map/reduce_scatter | solution.py:896
  341.3 2.7 copy-start.9
  341.3 2.8 copy-start.19
  353.1 2.9 copy-start.21
  353.1 2.9 copy-start.31
  356.0 1.6 copy-start.38
  361.1 5.5 copy-start.16
  361.1 5.5 copy-start.35
  376.3 171.1 %reduce-scatter.13.cloned.1.call-start = ((), (), s32[]{:S(2)}) async-start(), calls=%async_computation.14 | async-start | bytes 2457600
  468.5 101.4 %reduce-scatter.7.cloned.1.call-start = ((), (), s32[]{:S(2)}) async-start(), calls=%async_computation.7 | async-start | bytes 3686400 | tf_op jit(solution)/shard_map/reduce_scatter | solution.py:896
  477.1 117.0 %all-gather.17.cloned.1.call-start = ((), (), s32[]{:S(2)}) async-start(), calls=%async_computation.10 | async-start | bytes 1769472 | tf_op jit(solution)/shard_map/all_gather | solution.py:961
  478.4 1.9 copy-start.6
  479.7 5.0 copy-start.29
  485.1 133.3 %all-gather.19.cloned.1.call-start = ((), (), s32[]{:S(2)}) async-start(), calls=%async_computation.12 | async-start | bytes 1769472 | tf_op jit(solution)/shard_map/all_gather | solution.py:961
  494.9 161.8 %all-gather.15.cloned.1.call-start = ((), (), s32[]{:S(2)}) async-start(), calls=%async_computation.8 | async-start | bytes 3538944 | tf_op jit(solution)/shard_map/all_gather | solution.py:961
  597.1 24.3 %copy-start.50 = (f32[8,1536]{1,0:T(8,128)S(1)}, f32[8,1536]{1,0:T(8,128)}, u32[]{:S(2)}) copy-start(f32[8,1536]{1,0:T(8,128)} %get-tuple-element.47) | copy-start | bytes 147460
  659.2 3.0 copy-start.4
  666.8 3.4 copy-start.1
  666.8 2.8 copy-start.47
  (18 other events, 20.4 us)
Sparse Core Ops, SparseCore 0:
  10.2 46.2 all-gather.8
  58.6 59.0 all-gather.20
  119.9 49.2 all-gather.10
  171.2 49.2 all-gather.12
  341.3 45.9 reduce-scatter.8
  389.5 47.5 reduce-scatter.10
  468.6 39.2 reduce-scatter.12
  510.2 59.5 reduce-scatter.6
  571.5 22.6 all-gather.16
  595.6 22.7 all-gather.18
  620.6 36.0 all-gather.14

commit v4 on v3

--- a/solution.py
+++ b/solution.py
@@ -699,20 +699,30 @@
 
 
 def last_kernel(
-    part_ref, frames_ref, gain_ref, grad_ref, stats_ref, text_ref,
-    out_ref, total_ref, text_out,
-    mine, came, all_ref, st_send, st_recv, z_send, z_recv, *scratch,
+    part_ref, frames_ref, gain_ref, grad_ref, stats_ref, text_ref, qkv_ref, up_ref, down_ref,
+    out_ref, total_ref, text_out, qkv_out, up_out, down_out,
+    mine, came, all_ref, st_send, st_recv, z_send, z_recv,
+    qkv_came, qkv_pair, up_pair, down_pair, q_send, q_recv, x_send, x_recv, *scratch,
 ):
     z = lax.axis_index("shard")
     shards = lax.axis_size("shard")
     others = [lax.rem(z + i, shards) for i in range(1, shards)]
     spot = place()[1:]
+    context = spot[0]
     enter(neighbours() + [device(other, *spot) for other in others])
     size = len(scratch) // 2
     text = LoadedScatter(text_ref, *scratch[size:])
     text.start()
     job = LoadedScatter(part_ref, *scratch[:size])
     job.start()
+    sends, moves = [], []
+    for index, other in enumerate(others):
+        copy = remote_copy(
+            qkv_ref.at[other], qkv_came.at[index], q_send.at[index], q_recv.at[index],
+            device(other, *spot),
+        )
+        copy.start()
+        moves.append(copy)
     inputs = frames_ref[...].astype(F32)
     average = jnp.mean(inputs, axis=-1, keepdims=True)
     centred = inputs - average
@@ -721,13 +731,18 @@
     job.first()
     text.second()
     job.second()
+    to_x = neighbours()[0]
+    pairs = []
+    for index, (source, pair_ref) in enumerate(((up_ref, up_pair), (down_ref, down_pair))):
+        copy = remote_copy(source, pair_ref, x_send.at[index], x_recv.at[index], to_x)
+        copy.start()
+        pairs.append(copy)
     text_out[...] = text.total()
     grads = job.total()
     normed = centred * rate
     mine[0] = stats_ref[...]
     mine[0, 0:1] = jnp.sum(grads * normed, axis=0, keepdims=True)
     mine[0, 1:2] = jnp.sum(grads, axis=0, keepdims=True)
-    sends = []
     for index, target in enumerate(reversed(neighbours())):
         copy = remote_copy(
             mine.at[index], came.at[index], st_send.at[index], st_recv.at[index], target
@@ -748,20 +763,48 @@
         copy.start()
         sends.append(copy)
     all_ref[z] = mine[3]
+    total = qkv_ref[z].astype(F32)
+    for index, copy in enumerate(moves):
+        copy.wait_recv()
+        total += qkv_came[index].astype(F32)
+    qkv_pair[0] = total.astype(BF)
+    copy = remote_copy(qkv_pair.at[0], qkv_pair.at[1], x_send.at[2], x_recv.at[2], to_x)
+    copy.start()
+    pairs.append(copy)
     for copy in sends[3:]:
         copy.wait_recv()
     total = all_ref[0]
     for index in range(1, shards):
         total += all_ref[index]
     total_ref[...] = total
-    for copy in sends:
+    half = up_ref.shape[1]
+    ours = pl.ds(pl.multiple_of(context * half, half), half)
+    theirs = pl.ds(pl.multiple_of((1 - context) * half, half), half)
+    for copy, source, pair_ref, target in (
+        (pairs[0], up_ref, up_pair, up_out),
+        (pairs[1], down_ref, down_pair, down_out),
+    ):
+        target[:, ours] = source[...].astype(F32)
+        copy.wait_recv()
+        target[:, theirs] = pair_ref[...].astype(F32)
+    pairs[2].wait_recv()
+    lead = jnp.where(context == 0, qkv_pair[0], qkv_pair[1]).astype(F32)
+    trail = jnp.where(context == 0, qkv_pair[1], qkv_pair[0]).astype(F32)
+    width = lead.shape[1] // 3
+    for index in range(3):
+        lanes = slice(index * width, (index + 1) * width)
+        qkv_out[index, :, :width] = lead[:, lanes]
+        qkv_out[index, :, width:] = trail[:, lanes]
+    for copy in sends + moves + pairs:
         copy.wait_send()
     text.finish()
     job.finish()
 
 
-def last_step(part, frames, gain, grad, stats, text, shards, ident):
+def last_step(part, frames, gain, grad, stats, text, qkv, up, down, shards, ident):
     _, rows, width = part.shape
+    depth, half = up.shape
+    columns = qkv.shape[2]
     return call(
         last_kernel,
         "last_step",
@@ -769,9 +812,12 @@
             shape(rows, width, dtype=F32),
             shape(8, width, dtype=F32),
             shape(*text.shape[1:], dtype=F32),
+            shape(3, depth, 2 * columns // 3, dtype=F32),
+            shape(depth, 2 * half, dtype=F32),
+            shape(depth, 2 * half, dtype=F32),
         ),
-        (IN_VMEM, IN_VMEM, IN_VMEM),
-        [ANY, IN_VMEM, IN_VMEM, IN_VMEM, IN_VMEM, ANY],
+        (IN_VMEM,) * 6,
+        [ANY] + [IN_VMEM] * 4 + [ANY] + [IN_VMEM] * 3,
         [
             pltpu.VMEM((4, 8, width), F32),
             pltpu.VMEM((3, 8, width), F32),
@@ -780,12 +826,20 @@
             pltpu.SemaphoreType.DMA((3,)),
             pltpu.SemaphoreType.DMA((shards - 1,)),
             pltpu.SemaphoreType.DMA((shards - 1,)),
+            pltpu.VMEM((shards - 1, depth, columns), BF),
+            pltpu.VMEM((2, depth, columns), BF),
+            pltpu.VMEM((depth, half), BF),
+            pltpu.VMEM((depth, half), BF),
+            pltpu.SemaphoreType.DMA((shards - 1,)),
+            pltpu.SemaphoreType.DMA((shards - 1,)),
+            pltpu.SemaphoreType.DMA((3,)),
+            pltpu.SemaphoreType.DMA((3,)),
         ]
         + LoadedScatter.scratch(rows, width)
         + LoadedScatter.scratch(*text.shape[1:]),
         ident,
-        50,
-    )(part, frames, gain, grad, stats, text)
+        65,
+    )(part, frames, gain, grad, stats, text, qkv, up, down)
 
 
 def dots(spec, *operands):
@@ -926,6 +980,9 @@
     grad_qkv, part_side, text_grads = attend_backward(
         grad_mix, qkv, mix, self_log, part_side, text_grads, 8
     )
+    grad_qkv, part_side, text_grads, grad_down, grad_up = lax.optimization_barrier(
+        (grad_qkv, part_side, text_grads, grad_down, grad_up)
+    )
     text_grads = text_grads.reshape(2, clips, texts, columns).astype(BF)
     w_grad_text = dots("cnd,tcne->ted", text_states, text_grads).astype(BF)
     part_side = jnp.concatenate([part_side, w_grad_text.reshape(2 * columns, width)], axis=0)
@@ -936,35 +993,34 @@
     grad_text = grad_text.reshape(8, clips * texts // 8, width)
     grad_qkv = grad_qkv.reshape(8 * block, 3 * columns)
     part_norm = dots("re,de->rd", grad_qkv, w_qkv).astype(BF)
-    grad_w_qkv = to_shard(dots("rd,re->de", flat_one, grad_qkv))
+    grad_w_qkv = dots("rd,re->de", flat_one, grad_qkv).astype(BF)
     nothing = jnp.zeros((1, width), F32)
     stats = [nothing, nothing] + [
         v[None] for v in (gain_two, shift_two, gain_three, shift_three)
     ]
     stats.append(jnp.pad(squares, (0, width - 4))[None])
-    grad_frames, totals, grad_text = last_step(
+    grad_frames, totals, grad_text, grad_w_qkv, grad_up, grad_down = last_step(
         part_norm.reshape(8, block, width),
         frames.reshape(block, width),
         norm_gain[0][None],
         grad_one.reshape(block, width),
         jnp.concatenate(stats + [nothing], axis=0),
         grad_text,
-        lax.axis_size("shard"),
+        grad_w_qkv.reshape(slices, depth, 3 * columns),
+        grad_up,
+        grad_down,
+        slices,
         11,
     )
     grad_frames = grad_frames.reshape(clips, rows, width)
     grad_text = grad_text.reshape(clips, texts // 8, width)
 
-    grad_w_qkv, grad_side, totals = lax.optimization_barrier((grad_w_qkv, grad_side, totals))
+    grad_side, totals = lax.optimization_barrier((grad_side, totals))
 
     def whole(values):
-        return lax.all_gather(values, "context", axis=values.ndim - 1, tiled=True).astype(F32)
-
-    grad_up, grad_down = whole(grad_up), whole(grad_down)
-    grad_self = jnp.stack([grad_w_qkv[:, j * columns : (j + 1) * columns] for j in range(3)])
-    grad_side = grad_side.reshape(5, columns, depth).transpose(0, 2, 1)
-    grad_all = whole(jnp.concatenate([grad_self, grad_side], axis=0))
-
+        return lax.all_gather(values, "context", axis=1, tiled=True)
+
+    grad_side = whole(grad_side.reshape(5, columns, depth)).astype(F32).transpose(0, 2, 1)
     gains = jnp.stack([totals[0], totals[2], totals[4]])
     shifts = jnp.stack([totals[1], totals[3], totals[5]])
     squares = totals[6, :4]
@@ -978,10 +1034,10 @@
         grad_text,
         grad_gain,
         grad_shift,
-        grad_all[:3],
-        grad_all[3],
-        jnp.stack([grad_all[4], grad_all[6], grad_all[7]]),
-        grad_all[5],
+        grad_w_qkv,
+        grad_side[0],
+        jnp.stack([grad_side[1], grad_side[3], grad_side[4]]),
+        grad_side[2],
         grad_up,
         grad_down,
         jnp.sqrt(squares / entries),

time: 682 us -> 647 us (0.949)
  waiting for transfers between devices: 117 us -> 51.5 us
  Pallas kernels: 376 us -> 418 us
  other arithmetic: 38.4 us -> 30.4 us
    all_gather x3 -> x1, waiting for transfers between devices: 76.7 us -> 32 us  [whole(): return lax.all_gather(values, 'context', axis=1, tiled=True)]
    pallas_call x1, Pallas kernels: 52.2 us -> 94.1 us  [last_step(): call(last_kernel, 'last_step', (shape(rows, width, dtype=F32), shape(8, w...]
    reduce_scatter x3, waiting for transfers between devices: 21.2 us -> 0.06 us  [to_shard(): lax.psum_scatter(part.astype(BF), 'shard', scatter_dimension=0, tiled=True)]
    unnamed x121 -> x122, local copies, waits for them, and re-layouts: 28.5 us -> 29.6 us
  transfers between devices with their start and end apart: 11 -> 8, of which waited for: 6 -> 3; matrix products, arithmetic and copies ran while one was open for 18% -> 15% of each run, Pallas kernels for 42% -> 51%
where the time goes in v4:
time: 647 us; the launch traced here: 642 us
  Pallas kernels  418 us (65%)
  local copies, waits for them, and re-layouts  71.4 us (11%)
  matrix products  55.3 us (9%)
  waiting for transfers between devices  51.5 us (8%)
  other arithmetic  30.4 us (5%)
  between operations  15.3 us (2%)
    pallas_call x2, Pallas kernels, plane_gather(): call(kernel, 'plane_gather', outs, tuple(any_space), any_space, scratch,...  103 us
    pallas_call x1, Pallas kernels, last_step(): call(last_kernel, 'last_step', (shape(rows, width, dtype=F32), shape(8, w...  94.1 us
    pallas_call x1, Pallas kernels, feed_forward(): call(feed_kernel, 'feed_forward', outs, (IN_VMEM,) * 4, [ANY, ANY, IN_VME...  92.9 us
    pallas_call x1, Pallas kernels, attend_backward(): call(backward_kernel, 'attend_backward', (shape(blocks, block, 3 * column...  82 us
    dot_general x19, matrix products, dots(): return jnp.einsum(spec, *operands, preferred_element_type=F32)  53.3 us
    pallas_call x1, Pallas kernels, attend_forward(): call(forward_kernel, 'attend_forward', (shape(blocks, block, 3 * columns)...  46 us
    all_gather x1, waiting for transfers between devices, whole(): return lax.all_gather(values, 'context', axis=1, tiled=True)  32 us
    unnamed x122, local copies, waits for them, and re-layouts  29.6 us
  transfers between devices with their start and end apart: 8, of which 3 were waited for; matrix products, arithmetic and copies ran while one was open for 15% of the time, Pallas kernels for 51%

profile of v4, /device:TPU:0, one launch (start us, length us, event | category | flops | bytes accessed | tf_op | source)
XLA Modules:
  0.0 642.2 jit_solution(170115369448668968)
XLA Ops:
  7.3 1.5 dynamic-slice_bitcast_fusion.2
  18.1 34.4 %plane_gather.2.rows_ref = bf16[8,256,1536]{2,1,0:T(8,128)(2,1)} custom-call(bf16[256,1536]{1,0:T(8,128)(2,1)} %bitcast.246), custom_call_target="tpu_custom_call" | custom-call | flops 32999999488 | bytes 33000000 | tf_op jit(solution)/shard_map/plane_gather/pallas_call | solution.py:347
  52.5 4.0 all-gather.7.cloned.1.call-done.w_ref
  56.5 46.0 %attend_forward.1 = (bf16[8,256,576]{2,1,0:T(8,128)(2,1)}, f32[6,1024]{1,0:T(8,128)}, bf16[8,256,192]{2,1,0:T(8,128)(2,1)}, bf16[8,256,192]{2,1,0:T(8,128)(2,1)}, bf16[8,256,1536]{2,1,0:T(8,128)(2,1)}) custom-call(bf16[8,256,1536]{2,1,0:T(8,128)(2,1)} %plane_gather.2.rows_ref, bf16[1536,576]{1,0:T(8,128)(2,1)} %all-gather.7.cloned.1.call-done.w_ref, ...), custom_call_target="tpu_custom_call" | custom-call | flops 44999999488 | bytes 45000000 | tf_op jit(solution)/shard_map/attend_forward/pallas_call | solution.py:583
  102.4 15.3 %all-gather.15.cloned.1.call-done = bf16[20,192,384]{2,1,0:T(8,128)(2,1)} async-done(((bf16[5,192,384]{2,1,0:T(8,128)(2,1)}), bf16[20,192,384]{2,1,0:T(8,128)(2,1)}) %all-gather.15.cloned.1.call-update) | async-done | bytes 2949136 | tf_op jit(solution)/shard_map/all_gather | solution.py:883
  117.7 4.1 copy.185
  122.9 1.7 copy.162
  126.7 68.2 %plane_gather.3 = (bf16[8,576,1536]{2,1,0:T(8,128)(2,1)}, bf16[8,256,192]{2,1,0:T(8,128)(2,1)}) custom-call(bf16[576,1536]{1,0:T(8,128)(2,1)} %bitcast.241, bf16[256,192]{1,0:T(8,128)(2,1)} %bitcast.270), custom_call_target="tpu_custom_call" | custom-call | flops 65000001536 | bytes 65000000 | tf_op jit(solution)/shard_map/plane_gather/pallas_call | solution.py:347
  195.0 4.8 fusion.74
  199.8 2.0 copy.112
  201.8 1.6 reshape.208
  203.4 3.9 fusion.75
  208.9 1.8 copy.158
  210.7 4.7 fusion.28
  215.4 2.0 fusion.77
  217.7 1.5 copy-done.20
  219.5 4.9 fusion.73
  226.3 92.9 %feed_forward.1 = (f32[256,1536]{1,0:T(8,128)}, f32[256,1536]{1,0:T(8,128)}, bf16[1536,768]{1,0:T(8,128)(2,1)}, bf16[1536,768]{1,0:T(8,128)(2,1)}) custom-call(bf16[256,1536]{1,0:T(8,128)(2,1)} %bitcast.253, bf16[8,256,1536]{2,1,0:T(8,128)(2,1)} %get-tuple-element.42.grad_ref, bf16[1536,768]{1,0:T(8,128)(2,1)} %all-gather.9.cloned.1.call-done.up_ref, ...), custom_call_target="tpu_custom_call" | custom-call | flops 89999998976 | bytes 90000000 | tf_op jit(solution)/shard_map/feed_forward/pallas_call | solution.py:490
  319.3 3.9 multiply_reduce_fusion.4
  323.1 1.4 add_add_fusion.1
  324.6 1.6 reduce_sum.227
  326.6 4.1 fusion.27
  334.4 4.9 fusion.71
  339.5 2.2 multiply_reduce_fusion.5
  341.7 1.8 fusion.72
  344.5 3.8 fusion.29
  348.2 1.8 copy.119
  350.0 2.9 fusion.12
  352.9 1.4 convert_bitcast_fusion
  354.4 1.8 fusion.11
  356.2 1.7 pad_maximum_fusion
  357.9 5.6 copy.121
  365.8 2.5 copy.151
  368.3 5.1 reshape.245.text_ref
  374.4 2.7 select_maximum_fusion
  378.0 82.0 %attend_backward.1 = (bf16[8,256,576]{2,1,0:T(8,128)(2,1)}, bf16[576,1536]{1,0:T(8,128)(2,1)}, f32[256,192]{1,0:T(8,128)}) custom-call(bf16[8,256,192]{2,1,0:T(8,128)(2,1)} %bitcast.245, bf16[8,256,576]{2,1,0:T(8,128)(2,1)} %get-tuple-element.45.qkv_ref, bf16[8,256,192]{2,1,0:T(8,128)(2,1)} %get-tuple-element.46.mix_ref, ...), custom_call_target="tpu_custom_call" | custom-call | flops 74999996416 | bytes 75000000 | tf_op jit(solution)/shard_map/attend_backward/pallas_call | solution.py:681
  463.0 6.8 %bitcast_convert_fusion.2 = bf16[1536,576]{0,1:T(8,128)(2,1)S(1)} fusion(bf16[8,256,1536]{2,1,0:T(8,128)(2,1)} %plane_gather.2.rows_ref, bf16[8,256,576]{2,1,0:T(8,128)(2,1)S(1)} %copy-done.53), kind=kOutput, calls=%fused_computation.20 | convolution fusion | flops 3624763392 | bytes 10420224 | tf_op jit(solution)/shard_map/rd,re->de/dot_general | solution.py:846
  469.8 2.3 copy.130
  474.5 1.9 maximum_bitcast_fusion
  478.0 8.8 %convolution_convert_fusion = bf16[2048,1536]{1,0:T(8,128)(2,1)} fusion(bf16[2048,576]{1,0:T(8,128)(2,1)} %bitcast.267, bf16[1536,576]{1,0:T(8,128)(2,1)S(1)} %copy-done.52), kind=kOutput, calls=%fused_computation.4 | convolution fusion | flops 3627024384 | bytes 10420224 | tf_op jit(solution)/shard_map/re,de->rd/dot_general | solution.py:846
  486.7 94.1 %last_step.1 = (f32[256,1536]{1,0:T(8,128)}, f32[8,1536]{1,0:T(8,128)}, f32[16,1536]{1,0:T(8,128)}, f32[3,384,384]{2,1,0:T(8,128)}, f32[384,1536]{1,0:T(8,128)}, /*index=5*/f32[384,1536]{1,0:T(8,128)}) custom-call(bf16[8,256,1536]{2,1,0:T(8,128)(2,1)} %bitcast.266, bf16[256,1536]{1,0:T(8,128)(2,1)} %bitcast.234, f32[1,1536]{1,0:T(1,128)} %get-tuple-element.139.gain_ref, ...), custom_call_target="tpu_custom_call" | custom-call | flops 65000001536 | bytes 65000000 | tf_op jit(solution)/shard_map/last_step/pallas_call | solution.py:808
  584.6 32.0 %all-gather.13.cloned.1.call-done = bf16[5,384,384]{2,1,0:T(8,128)(2,1)} async-done(((bf16[5,192,384]{2,1,0:T(8,128)(2,1)}), bf16[5,384,384]{2,1,0:T(8,128)(2,1)}) %all-gather.13.cloned.1.call-update) | async-done | bytes 1474576 | tf_op jit(solution)/shard_map/all_gather | solution.py:1021
  616.6 1.6 convert_bitcast_fusion.1
  620.2 2.2 copy.133
  622.5 1.8 copy.134
  625.4 2.8 copy.192
  631.2 1.4 copy.195
  633.7 1.4 copy.196
  (201 shorter events, 43.6 us)
Async XLA Ops:
  7.2 4.9 copy-start
  7.2 2.6 copy-start.38
  7.2 49.3 %all-gather.7.cloned.1.call-start = ((), (), s32[]{:S(2)}) async-start(), calls=%async_computation.3 | async-start | bytes 2457600 | tf_op jit(solution)/shard_map/all_gather | solution.py:883
  9.8 108.0 %all-gather.15.cloned.1.call-start = ((), (), s32[]{:S(2)}) async-start(), calls=%async_computation.10 | async-start | bytes 3686400 | tf_op jit(solution)/shard_map/all_gather | solution.py:883
  12.0 214.3 %all-gather.9.cloned.1.call-start = ((), (), s32[]{:S(2)}) async-start(), calls=%async_computation.4 | async-start | bytes 2949120 | tf_op jit(solution)/shard_map/all_gather | solution.py:883
  12.1 2.3 copy-start.49
  12.1 3.0 copy-start.48
  12.1 4.2 copy-start.8
  13.0 213.3 %all-gather.11.cloned.1.call-start = ((), (), s32[]{:S(2)}) async-start(), calls=%async_computation.5 | async-start | bytes 2949120 | tf_op jit(solution)/shard_map/all_gather | solution.py:883
  14.4 445.7 %reduce-scatter.4.cloned.1.call-start = ((), (), s32[]{:S(2)}) async-start(), calls=%async_computation.6 | async-start | bytes 2949120 | tf_op jit(solution)/shard_map/reduce_scatter | solution.py:950
  126.7 68.2 %copy-start.9 = (bf16[2,128,1536]{2,1,0:T(8,128)(2,1)S(1)}, bf16[2,128,1536]{2,1,0:T(8,128)(2,1)}, u32[]{:S(2)}) copy-start(bf16[2,128,1536]{2,1,0:T(8,128)(2,1)} %param.11) | copy-start | bytes 2359300
  199.8 19.7 %copy-start.3 = (f32[2,128,1536]{2,1,0:T(8,128)}, f32[2,128,1536]{2,1,0:T(8,128)S(1)}, u32[]{:S(2)}) copy-start(f32[2,128,1536]{2,1,0:T(8,128)S(1)} %get-tuple-element.120) | copy-start | bytes 4718596
  207.6 3.1 copy-start.46
  208.9 1.8 copy-start.50
  217.4 2.1 copy-start.12
  217.4 1.7 copy-start.20
  217.7 1.8 copy-start.10
  219.5 4.9 copy-start.31
  319.2 3.9 copy-start.2
  319.3 3.9 copy-start.5
  324.6 1.8 copy-start.17
  326.6 4.1 copy-start.35
  326.6 4.1 copy-start.13
  326.6 4.1 copy-start.21
  332.7 1.7 copy-start.4
  333.6 5.7 copy-start.36
  339.4 120.7 %reduce-scatter.6.cloned.1.call-start = ((), (), s32[]{:S(2)}) async-start(), calls=%async_computation.7 | async-start | bytes 2949120 | tf_op jit(solution)/shard_map/reduce_scatter | solution.py:950
  339.4 2.2 copy-start.14
  339.5 2.2 copy-start.18
  348.2 1.8 copy-start.32
  350.0 2.9 copy-start.16
  350.0 2.9 copy-start.30
  357.9 5.6 copy-start.11
  357.9 5.6 copy-start.34
  368.3 5.1 copy-start.6
  377.1 203.8 %reduce-scatter.8.cloned.1.call-start = ((), (), s32[]{:S(2)}) async-start(), calls=%async_computation.8 | async-start | bytes 3686400 | tf_op jit(solution)/shard_map/reduce_scatter | solution.py:950
  378.0 83.1 %copy-start.29 = (bf16[2,192,1536,1,1]{2,1,0,3,4:T(8,128)(2,1)S(1)}, bf16[2,192,1536,1,1]{2,1,0,3,4:T(8,128)(2,1)}, u32[]{:S(2)}) copy-start(bf16[2,192,1536,1,1]{2,1,0,3,4:T(8,128)(2,1)} %reshape.240) | copy-start | bytes 3538948
  461.1 1.9 copy-start.53
  469.7 2.3 copy-start.40
  476.4 140.2 %all-gather.13.cloned.1.call-start = ((), (), s32[]{:S(2)}) async-start(), calls=%async_computation.9 | async-start | bytes 2211840 | tf_op jit(solution)/shard_map/all_gather | solution.py:1021
  618.2 2.0 copy-start.7
  620.2 2.2 slice-start
  622.5 1.8 copy-start.24
  625.4 2.8 copy-start.45
  625.4 3.4 copy-start.27
  628.8 2.3 copy-start.26
  631.1 2.5 copy-start.25
  631.1 3.9 copy-start.1
  (16 other events, 19.1 us)
Sparse Core Ops, SparseCore 0:
  10.2 46.2 all-gather.6
  58.6 59.0 all-gather.14
  119.9 49.1 all-gather.8
  171.1 49.2 all-gather.10
  339.5 45.9 reduce-scatter.3
  387.6 47.5 reduce-scatter.5
  476.6 89.6 reduce-scatter.7
  581.0 35.5 all-gather.12

commit v5 on v4

--- a/solution.py
+++ b/solution.py
@@ -211,14 +211,20 @@
         self.arrived(4, relay.at[0])
         self.forward(9, self.add(2, low, relay[0]), final.at[1, low], self.to_y)
 
-    def total(self):
+    def wait(self):
         self.arrived(3, self.core.at[3])
         self.arrived(6, self.final.at[0, self.low])
         self.arrived(7, self.final.at[1, self.high])
         self.arrived(8, self.final.at[0, self.high])
         self.arrived(9, self.final.at[1, self.low])
-        total = self.part_ref[self.mine[3]].astype(F32) + self.core[3].astype(F32)
-        return total + self.final[0].astype(F32) + self.final[1].astype(F32)
+
+    def value(self, part=slice(None)):
+        total = self.part_ref[self.mine[3], part].astype(F32) + self.core[3, part].astype(F32)
+        return total + self.final[0, part].astype(F32) + self.final[1, part].astype(F32)
+
+    def total(self):
+        self.wait()
+        return self.value()
 
     def finish(self):
         for copy in self.sends:
@@ -372,7 +378,7 @@
     own_ref, grad_ref, up_ref, down_ref,
     normed_out, branch_out, up_out, down_out,
     rows_ref, grads_ref, hidden_ref, slope_ref, part_a, part_b,
-    load_sem, g_local, g_send, g_recv, *scratch,
+    load_sem, store_sem, g_local, g_send, g_recv, *scratch,
 ):
     enter(neighbours())
     gather = Gather(own_ref, rows_ref, g_local, g_send, g_recv)
@@ -401,9 +407,7 @@
         slope_ref[block] = slope
         part_a[block] = nt(slope, up_ref[...]).astype(BF)
 
-    size = len(scratch) // 2
-    first = Scatter(part_a, *scratch[:size])
-    other = Scatter(part_b, *scratch[size:])
+    first = Scatter(part_a, *scratch)
     x, y, c = gather.spot
 
     def pair(cx, cy):
@@ -435,38 +439,35 @@
     for copy in gather.sends:
         copy.wait_send()
 
+    def store(block):
+        return pltpu.make_async_copy(part_b.at[block], branch_out.at[block], store_sem.at[block])
+
     def branch(block, carry):
         part_b[block] = nt(hidden_ref[block], down_ref[...]).astype(BF)
+        store(block).start()
         return carry
 
     lax.fori_loop(0, blocks, branch, 0)
-    for index in range(4):
-        other.pass_core(index)
     first.second()
-    other.far()
-    other.near()
     tile = 256
-    hidden_width = hidden_ref.shape[2]
 
     def weight(left_ref, right_ref, out_ref):
+        right = right_ref[...].reshape(-1, right_ref.shape[2])
+
         def one(index, carry):
             lanes = pl.ds(pl.multiple_of(index * tile, tile), tile)
             left = left_ref[:, :, lanes].reshape(-1, tile)
-            right = right_ref[...].reshape(-1, hidden_width)
-            out_ref[lanes, :] = lax.dot_general(
-                left, right, (((0,), (0,)), ((), ())), preferred_element_type=F32
-            ).astype(BF)
+            out_ref[lanes, :] = tn(left, right).astype(BF)
             return carry
 
         lax.fori_loop(0, width // tile, one, 0)
 
     weight(grads_ref, hidden_ref, down_out)
+    weight(rows_ref, slope_ref, up_out)
     normed_out[...] = first.total()
-    other.second()
-    weight(rows_ref, slope_ref, up_out)
-    branch_out[...] = other.total()
     first.finish()
-    other.finish()
+    for block in range(blocks):
+        store(block).wait()
 
 
 def feed_forward(own, grads, w_up, w_down, ident):
@@ -474,7 +475,7 @@
     hidden = w_up.shape[1]
     outs = (
         shape(rows, width, dtype=F32),
-        shape(rows, width, dtype=F32),
+        shape(8, rows, width),
         shape(width, hidden),
         shape(width, hidden),
     )
@@ -486,16 +487,17 @@
         pltpu.VMEM((8, rows, width), BF),
         pltpu.VMEM((8, rows, width), BF),
         pltpu.SemaphoreType.DMA((8,)),
+        pltpu.SemaphoreType.DMA((8,)),
     ]
     return call(
         feed_kernel,
         "feed_forward",
         outs,
-        (IN_VMEM,) * 4,
+        (IN_VMEM, ANY, IN_VMEM, IN_VMEM),
         [ANY, ANY, IN_VMEM, IN_VMEM],
-        scratch + gather_scratch() + Scatter.scratch(rows, width) * 2,
+        scratch + gather_scratch() + Scatter.scratch(rows, width),
         ident,
-        90,
+        70,
     )(own, grads, w_up, w_down)
 
 
@@ -508,6 +510,10 @@
 
 def nn(left, right):
     return lax.dot_general(left, right, (((1,), (0,)), ((), ())), preferred_element_type=F32)
+
+
+def tn(left, right):
+    return lax.dot_general(left, right, (((0,), (0,)), ((), ())), preferred_element_type=F32)
 
 
 def turn(values):
@@ -604,9 +610,9 @@
 
 
 def backward_kernel(
-    grad_ref, qkv_ref, mix_ref, log_ref, side_ref, text_ref,
-    out_ref, side_out, text_out,
-    grad_all, query_turned, ex_local, ex_send, ex_recv, *scratch,
+    grad_ref, qkv_ref, mix_ref, log_ref, rows_ref, w_ref, side_ref, text_ref,
+    part_out, w_out, side_out, text_out,
+    out_ref, part_ref, store_sem, grad_all, query_turned, ex_local, ex_send, ex_recv, *scratch,
 ):
     enter(plane_others())
     exchange = Exchange(grad_ref, grad_all, ex_local, ex_send, ex_recv)
@@ -668,34 +674,254 @@
         if clip == 0:
             text.second()
             side.second()
+    def store(block):
+        return pltpu.make_async_copy(part_ref.at[block], part_out.at[block], store_sem.at[block])
+
+    def project(block, carry):
+        part_ref[block] = nt(out_ref[block], w_ref[...]).astype(BF)
+        store(block).start()
+        return carry
+
+    lax.fori_loop(0, blocks, project, 0)
+    tile = 256
+    right = out_ref[...].reshape(blocks * both, 3 * width)
+
+    def weight(index, carry):
+        lanes = pl.ds(pl.multiple_of(index * tile, tile), tile)
+        left = rows_ref[:, :, lanes].reshape(blocks * both, tile)
+        w_out[lanes, :] = tn(left, right).astype(BF)
+        return carry
+
+    lax.fori_loop(0, w_out.shape[0] // tile, weight, 0)
     text_out[...] = text.total()
     side_out[...] = side.total().astype(BF)
     text.finish()
     side.finish()
-
-
-def attend_backward(grad_mix, qkv, mix, logs, side, text, ident):
+    for block in range(blocks):
+        store(block).wait()
+
+
+def attend_backward(grad_mix, qkv, mix, logs, rows, weights, side, text, ident):
     blocks, block, columns = mix.shape
-    _, rows, width = side.shape
+    _, side_rows, width = side.shape
     text_shape = text.shape[1:]
     return call(
         backward_kernel,
         "attend_backward",
-        (shape(blocks, block, 3 * columns), shape(rows, width), shape(*text_shape, dtype=F32)),
-        (IN_VMEM, IN_VMEM, IN_VMEM),
-        [ANY, IN_VMEM, IN_VMEM, IN_VMEM, ANY, ANY],
+        (
+            shape(blocks, block, width),
+            shape(width, 3 * columns),
+            shape(side_rows, width),
+            shape(*text_shape, dtype=F32),
+        ),
+        (ANY, IN_VMEM, IN_VMEM, IN_VMEM),
+        [ANY] + [IN_VMEM] * 5 + [ANY, ANY],
         [
+            pltpu.VMEM((blocks, block, 3 * columns), BF),
+            pltpu.VMEM((blocks, block, width), BF),
+            pltpu.SemaphoreType.DMA((8,)),
             pltpu.VMEM((blocks, block, columns), BF),
             pltpu.VMEM((HEAD_DIM, blocks * block // 2), F32),
             pltpu.SemaphoreType.DMA((2,)),
             pltpu.SemaphoreType.DMA((2, 7)),
             pltpu.SemaphoreType.DMA((2, 7)),
         ]
-        + LoadedScatter.scratch(rows, width)
+        + LoadedScatter.scratch(side_rows, width)
         + LoadedScatter.scratch(*text_shape),
         ident,
-        75,
-    )(grad_mix, qkv, mix, logs, side, text)
+        45,
+    )(grad_mix, qkv, mix, logs, rows, weights, side, text)
+
+
+CHUNK = 64
+
+
+def chunks(rows, body, carry=None):
+    def one(index, carry):
+        return body(pl.ds(pl.multiple_of(index * CHUNK, CHUNK), CHUNK), carry)
+
+    return lax.fori_loop(0, rows // CHUNK, one, 0 if carry is None else carry)
+
+
+def normalise(inputs):
+    average = jnp.mean(inputs, axis=-1, keepdims=True)
+    centred = inputs - average
+    rate = lax.rsqrt(jnp.mean(centred * centred, axis=-1, keepdims=True) + EPS)
+    return centred * rate, rate
+
+
+def norm_back(grads, inputs, gain):
+    normed, rate = normalise(inputs)
+    scaled = grads * gain
+    inner = jnp.mean(scaled * normed, axis=-1, keepdims=True)
+    result = rate * (scaled - jnp.mean(scaled, axis=-1, keepdims=True) - normed * inner)
+    sums = (
+        jnp.sum(grads * normed, axis=0, keepdims=True),
+        jnp.sum(grads, axis=0, keepdims=True),
+    )
+    return result, sums
+
+
+def rows_back_kernel(
+    normed_ref, cot_ref, one_ref, two_ref, query_ref, mix_ref, text_ref, my_mix_ref,
+    gain_ref, bias_ref, w_ref, branch_ref,
+    grad_ref, layer_ref, stats_ref, grad_mix_ref, out_ref, side_ref, text_out,
+    w_cross, w_query, w_out, low_ref, two_low_ref, back_ref, grad_cm, grad_cq, w_sem,
+    *scratch,
+):
+    enter(neighbours())
+    cross_job = Scatter(w_cross, *scratch[:5])
+    query_job = Scatter(w_query, *scratch[5:10])
+    branch_job = LoadedScatter(branch_ref, *scratch[10:])
+    branch_job.start()
+    blocks, columns, width = w_out.shape
+    rows = low_ref.shape[0]
+    heads = columns // HEAD_DIM
+    loads = []
+    for index, buffer in ((2, w_cross), (1, w_query), (0, w_out)):
+        load = pltpu.make_async_copy(
+            w_ref.at[:, index], buffer, w_sem.at[index]
+        )
+        load.start()
+        loads.append(load)
+    nothing = (jnp.zeros((1, width), F32),) * 2
+
+    def third(part, sums):
+        back, more = norm_back(normed_ref[part], two_ref[part], gain_ref[2:3])
+        total = cot_ref[part].astype(F32) + back
+        grad_ref[part] = total
+        low_ref[part] = total.astype(BF)
+        normed, _ = normalise(one_ref[part])
+        two_low_ref[part] = (normed * gain_ref[1:2] + bias_ref[1:2]).astype(BF)
+        return sums[0] + more[0], sums[1] + more[1]
+
+    gain_three, shift_three = chunks(rows, third, nothing)
+    branch_job.first()
+    loads[0].wait()
+
+    def cross_weight(block, carry):
+        grad_cm[block] = nt(low_ref[...], w_cross[block]).astype(BF)
+        w_cross[block] = tn(mix_ref[block], low_ref[...]).astype(BF)
+        return carry
+
+    lax.fori_loop(0, blocks, cross_weight, 0)
+    for index in range(4):
+        cross_job.pass_core(index)
+    half = rows // 2
+    texts = text_ref.shape[1] // 4
+    loads[1].wait()
+
+    def cross(block, carry):
+        for clip in range(2):
+            part = pl.ds(clip * half, half)
+            keys = pl.ds(clip * texts, texts)
+            values = pl.ds((2 + clip) * texts, texts)
+            for head in range(heads):
+                here = pl.ds(head * HEAD_DIM, HEAD_DIM)
+                query = query_ref[block, part, here] * jnp.asarray(HEAD_DIM ** (-0.5), BF)
+                key, value = text_ref[block, keys, here], text_ref[block, values, here]
+                grad = grad_cm[block, part, here]
+                scores = nt(key, query)
+                weights = jnp.exp(scores - jnp.max(scores, axis=0, keepdims=True))
+                weights = weights / jnp.sum(weights, axis=0, keepdims=True)
+                slopes = nt(value, grad)
+                inner = jnp.sum(weights * slopes, axis=0, keepdims=True)
+                slopes = (weights * (slopes - inner)).astype(BF)
+                grad_query = jnp.transpose(nn(turn(key).astype(BF), slopes))
+                grad_cq[block, part, here] = (grad_query * HEAD_DIM ** (-0.5)).astype(BF)
+                text_out[block, keys, here] = nn(slopes, query).astype(BF)
+                text_out[block, values, here] = nn(weights.astype(BF), grad).astype(BF)
+        back = nn(grad_cq[block], w_query[block])
+        back_ref[...] += back
+        w_query[block] = tn(grad_cq[block], two_low_ref[...]).astype(BF)
+        return carry
+
+    back_ref[...] = jnp.zeros_like(back_ref)
+    lax.fori_loop(0, blocks // 2, cross, 0)
+    branch_job.second()
+    cross_job.far()
+    cross_job.near()
+    lax.fori_loop(blocks // 2, blocks, cross, 0)
+    for index in range(4):
+        query_job.pass_core(index)
+
+    def second(part, sums):
+        back, more = norm_back(back_ref[part], one_ref[part], gain_ref[1:2])
+        total = grad_ref[part] + back
+        grad_ref[part] = total
+        low_ref[part] = total.astype(BF)
+        return sums[0] + more[0], sums[1] + more[1]
+
+    gain_two, shift_two = chunks(rows, second, nothing)
+    cross_job.second()
+    query_job.far()
+    query_job.near()
+    loads[2].wait()
+
+    def out_weight(block, carry):
+        grad_mix_ref[block] = nt(low_ref[...], w_out[block]).astype(BF)
+        out_ref[block] = tn(my_mix_ref[block], low_ref[...]).astype(BF)
+        return carry
+
+    lax.fori_loop(0, blocks, out_weight, 0)
+    branch_job.wait()
+
+    def last(part, sums):
+        branch = branch_job.value(part)
+        total = two_ref[part] + branch
+        layer_ref[part] = total.astype(BF)
+        return (
+            sums[0] + jnp.sum(total * total, axis=0, keepdims=True),
+            sums[1] + jnp.sum(branch * branch, axis=0, keepdims=True),
+        )
+
+    square_out, square_three = chunks(rows, last, nothing)
+    rest = jnp.zeros((1, width), F32)
+    for index, row in enumerate(
+        (rest, rest, gain_two, shift_two, gain_three, shift_three, square_out, square_three)
+    ):
+        stats_ref[index : index + 1] = row
+    query_job.second()
+    side_ref[1] = cross_job.total().astype(BF)
+    side_ref[0] = query_job.total().astype(BF)
+    branch_job.finish()
+    cross_job.finish()
+    query_job.finish()
+
+
+def rows_back(
+    normed, cot, one, two, query, mix, text, my_mix, gain, bias, weights, branch, ident
+):
+    rows, width = cot.shape
+    blocks, _, columns = my_mix.shape
+    return call(
+        rows_back_kernel,
+        "rows_back",
+        (
+            shape(rows, width, dtype=F32),
+            shape(rows, width),
+            shape(8, width, dtype=F32),
+            shape(*my_mix.shape),
+            shape(blocks, columns, width),
+            shape(2, columns, width),
+            shape(*text.shape),
+        ),
+        (IN_VMEM,) * 7,
+        [IN_VMEM] * 10 + [ANY, ANY],
+        [pltpu.VMEM((blocks, columns, width), BF)] * 3
+        + [
+            pltpu.VMEM((rows, width), BF),
+            pltpu.VMEM((rows, width), BF),
+            pltpu.VMEM((rows, width), F32),
+            pltpu.VMEM(my_mix.shape, BF),
+            pltpu.VMEM(my_mix.shape, BF),
+            pltpu.SemaphoreType.DMA((3,)),
+        ]
+        + Scatter.scratch(columns, width) * 2
+        + LoadedScatter.scratch(rows, width),
+        ident,
+        65,
+    )(normed, cot, one, two, query, mix, text, my_mix, gain, bias, weights, branch)
 
 
 def last_kernel(
@@ -810,7 +1036,7 @@
         "last_step",
         (
             shape(rows, width, dtype=F32),
-            shape(8, width, dtype=F32),
+            shape(16, width, dtype=F32),
             shape(*text.shape[1:], dtype=F32),
             shape(3, depth, 2 * columns // 3, dtype=F32),
             shape(depth, 2 * half, dtype=F32),
@@ -819,9 +1045,9 @@
         (IN_VMEM,) * 6,
         [ANY] + [IN_VMEM] * 4 + [ANY] + [IN_VMEM] * 3,
         [
-            pltpu.VMEM((4, 8, width), F32),
-            pltpu.VMEM((3, 8, width), F32),
-            pltpu.VMEM((shards, 8, width), F32),
+            pltpu.VMEM((4, 16, width), F32),
+            pltpu.VMEM((3, 16, width), F32),
+            pltpu.VMEM((shards, 16, width), F32),
             pltpu.SemaphoreType.DMA((3,)),
             pltpu.SemaphoreType.DMA((3,)),
             pltpu.SemaphoreType.DMA((shards - 1,)),
@@ -893,10 +1119,9 @@
     w_up = over_shard(half(mlp_up))
     w_down = over_shard(half(mlp_down))
 
-    stream_zero = frames.astype(F32)
+    stream_zero = frames.astype(F32).reshape(block, width)
     norm_one = layer_norm(stream_zero, norm_gain[0], norm_bias[0])
-    (all_one,) = plane_gather([norm_one.astype(BF).reshape(block, width)], 0, 33)
-    flat_one = all_one.reshape(8 * block, width)
+    (all_one,) = plane_gather([norm_one.astype(BF)], 0, 33)
     qkv, self_log, mix, my_mix, all_grad = attend_forward(
         all_one, w_qkv, cotangent.reshape(block, width), 1
     )
@@ -912,99 +1137,70 @@
     )
     plane_w = plane_w.reshape(8, 3, columns, width)
     w_out, w_query, w_cross = plane_w[:, 0], plane_w[:, 1], plane_w[:, 2]
-    branch_one = dots("bre,bed->rd", my_mix, w_out).reshape(clips, rows, width)
+    branch_one = dots("bre,bed->rd", my_mix, w_out)
     stream_one = stream_zero + branch_one
-    norm_two, norm_two_back = jax.vjp(layer_norm, stream_one, norm_gain[1], norm_bias[1])
-    low_two = norm_two.astype(BF)
-    cross_q = dots("cfd,bed->cfbe", low_two, w_query).astype(BF)
-    text_all = text_all.reshape(8, 2, clips, texts, heads, HEAD_DIM)
-    text_k, text_v = text_all[:, 0], text_all[:, 1]
-    cross_q = cross_q.reshape(clips, rows, 8, heads, HEAD_DIM)
+    norm_two = layer_norm(stream_one, norm_gain[1], norm_bias[1]).astype(BF)
+    cross_q = dots("rd,bed->bre", norm_two, w_query).astype(BF)
+    text_heads = text_all.reshape(8, 2, clips, texts, heads, HEAD_DIM)
     scale = HEAD_DIM ** (-0.5)
-    scores = dots("cfbhd,bcnhd->cbhfn", cross_q, text_k) * scale
-    top = jnp.max(scores, axis=-1, keepdims=True)
-    cross_full = jnp.exp(scores - top)
-    cross_full = cross_full / jnp.sum(cross_full, axis=-1, keepdims=True)
-    cross_probs = cross_full.astype(BF)
-    cross_mix = dots("cbhfn,bcnhd->cfbhd", cross_probs, text_v).astype(BF)
-    cross_mix = cross_mix.reshape(clips, rows, 8, columns)
-    branch_two = dots("cfbe,bed->cfd", cross_mix, w_cross)
+    queries = cross_q.reshape(8, clips, rows, heads, HEAD_DIM)
+    scores = dots("bcfhd,bcnhd->cbhfn", queries, text_heads[:, 0]) * scale
+    weights = jnp.exp(scores - jnp.max(scores, axis=-1, keepdims=True))
+    weights = weights / jnp.sum(weights, axis=-1, keepdims=True)
+    cross_mix = dots("cbhfn,bcnhd->bcfhd", weights.astype(BF), text_heads[:, 1]).astype(BF)
+    cross_mix = cross_mix.reshape(8, block, columns)
+    branch_two = dots("bre,bed->rd", cross_mix, w_cross)
     stream_two = stream_one + branch_two
 
-    norm_three, norm_three_back = jax.vjp(layer_norm, stream_two, norm_gain[2], norm_bias[2])
-    grad_normed, branch_three, grad_up, grad_down = feed_forward(
-        norm_three.astype(BF).reshape(block, width), all_grad, w_up, w_down, 4
-    )
-    branch_three = branch_three.reshape(clips, rows, width)
-    stream_out = stream_two + branch_three
-    squares = jnp.stack(
-        [
-            jnp.sum(stream_out * stream_out),
-            jnp.sum(branch_one * branch_one),
-            jnp.sum(branch_two * branch_two),
-            jnp.sum(branch_three * branch_three),
-        ]
+    norm_three = layer_norm(stream_two, norm_gain[2], norm_bias[2]).astype(BF)
+    grad_normed, part_three, grad_up, grad_down = feed_forward(
+        norm_three, all_grad, w_up, w_down, 4
     )
 
     def to_shard(part):
         return lax.psum_scatter(part.astype(BF), "shard", scatter_dimension=0, tiled=True)
 
     grad_down, grad_up = to_shard(grad_down), to_shard(grad_up)
-    grad_inner, gain_three, shift_three = norm_three_back(grad_normed.reshape(clips, rows, width))
-    grad_two = cotangent.astype(F32) + grad_inner
-
-    grad_low = grad_two.astype(BF)
-    grad_cross_mix = dots("cfd,bed->cfbe", grad_low, w_cross).astype(BF)
-    w_grad_cross = dots("cfd,cfbe->bed", grad_low, cross_mix)
-    grad_heads = grad_cross_mix.reshape(clips, rows, 8, heads, HEAD_DIM)
-    cross_dp = dots("cfbhd,bcnhd->cbhfn", grad_heads, text_v)
-    inner = jnp.sum(cross_full * cross_dp, axis=-1, keepdims=True)
-    grad_scores = (cross_full * (cross_dp - inner)).astype(BF)
-    grad_cq = (dots("cbhfn,bcnhd->cfbhd", grad_scores, text_k) * scale).astype(BF)
-    grad_text_k = dots("cbhfn,cfbhd->bcnhd", grad_scores, cross_q) * scale
-    grad_text_v = dots("cbhfn,cfbhd->bcnhd", cross_probs, grad_heads)
-    grad_cq = grad_cq.reshape(clips, rows, 8, columns)
-    w_grad_query = dots("cfd,cfbe->bed", low_two, grad_cq)
-    grad_normed = dots("cfbe,bed->cfd", grad_cq, w_query)
-    grad_inner, gain_two, shift_two = norm_two_back(grad_normed)
-    grad_one = grad_two + grad_inner
-
-    grad_low = grad_one.astype(BF).reshape(block, width)
-    grad_mix = dots("rd,bed->bre", grad_low, w_out).astype(BF)
-    w_grad_out = dots("rd,bre->bed", grad_low, my_mix)
-
-    part_side = jnp.stack([w_grad_out, w_grad_query, w_grad_cross], axis=1).astype(BF)
-    part_side = part_side.reshape(8, 3 * columns, width)
-    text_grads = jnp.stack([grad_text_k, grad_text_v], axis=1).astype(BF)
-    text_grads = text_grads.reshape(8, 2 * clips * texts, columns)
-    grad_qkv, part_side, text_grads = attend_backward(
-        grad_mix, qkv, mix, self_log, part_side, text_grads, 8
-    )
-    grad_qkv, part_side, text_grads, grad_down, grad_up = lax.optimization_barrier(
-        (grad_qkv, part_side, text_grads, grad_down, grad_up)
+    grad_one, layer_out, stats, grad_mix, part_out, side, text_grads = rows_back(
+        grad_normed,
+        cotangent.reshape(block, width),
+        stream_one,
+        stream_two,
+        cross_q,
+        cross_mix,
+        text_all,
+        my_mix,
+        norm_gain,
+        norm_bias,
+        plane_w,
+        part_three,
+        3,
+    )
+
+    def slice_shards(part):
+        return part.reshape(-1, slices, depth).transpose(1, 0, 2)
+
+    grad_cross = to_shard(slice_shards(side))
+    part_norm, grad_w_qkv, grad_out, text_grads = attend_backward(
+        grad_mix, qkv, mix, self_log, all_one, w_qkv, part_out, text_grads, 8
+    )
+    part_norm, grad_w_qkv, grad_out, text_grads, grad_down, grad_up = lax.optimization_barrier(
+        (part_norm, grad_w_qkv, grad_out, text_grads, grad_down, grad_up)
     )
     text_grads = text_grads.reshape(2, clips, texts, columns).astype(BF)
     w_grad_text = dots("cnd,tcne->ted", text_states, text_grads).astype(BF)
-    part_side = jnp.concatenate([part_side, w_grad_text.reshape(2 * columns, width)], axis=0)
-    part_side = part_side.reshape(5 * columns, slices, depth).transpose(1, 0, 2)
-    grad_side = to_shard(part_side)
+    rest = jnp.concatenate([grad_out, w_grad_text.reshape(2 * columns, width)], axis=0)
+    grad_rest = to_shard(slice_shards(rest))
     grad_text = dots("tcne,ted->cnd", text_grads, w_side[3:])
     grad_text = grad_text.reshape(clips, 8, texts // 8, width).transpose(1, 0, 2, 3).astype(BF)
     grad_text = grad_text.reshape(8, clips * texts // 8, width)
-    grad_qkv = grad_qkv.reshape(8 * block, 3 * columns)
-    part_norm = dots("re,de->rd", grad_qkv, w_qkv).astype(BF)
-    grad_w_qkv = dots("rd,re->de", flat_one, grad_qkv).astype(BF)
-    nothing = jnp.zeros((1, width), F32)
-    stats = [nothing, nothing] + [
-        v[None] for v in (gain_two, shift_two, gain_three, shift_three)
-    ]
-    stats.append(jnp.pad(squares, (0, width - 4))[None])
+    squares = [jnp.sum(v * v, axis=0)[None] for v in (branch_one, branch_two)]
     grad_frames, totals, grad_text, grad_w_qkv, grad_up, grad_down = last_step(
-        part_norm.reshape(8, block, width),
+        part_norm,
         frames.reshape(block, width),
         norm_gain[0][None],
-        grad_one.reshape(block, width),
-        jnp.concatenate(stats + [nothing], axis=0),
+        grad_one,
+        jnp.concatenate([stats] + squares + [jnp.zeros((6, width), F32)], axis=0),
         grad_text,
         grad_w_qkv.reshape(slices, depth, 3 * columns),
         grad_up,
@@ -1015,7 +1211,8 @@
     grad_frames = grad_frames.reshape(clips, rows, width)
     grad_text = grad_text.reshape(clips, texts // 8, width)
 
-    grad_side, totals = lax.optimization_barrier((grad_side, totals))
+    grad_cross, grad_rest, totals = lax.optimization_barrier((grad_cross, grad_rest, totals))
+    grad_side = jnp.concatenate([grad_cross, grad_rest], axis=1)
 
     def whole(values):
         return lax.all_gather(values, "context", axis=1, tiled=True)
@@ -1023,21 +1220,21 @@
     grad_side = whole(grad_side.reshape(5, columns, depth)).astype(F32).transpose(0, 2, 1)
     gains = jnp.stack([totals[0], totals[2], totals[4]])
     shifts = jnp.stack([totals[1], totals[3], totals[5]])
-    squares = totals[6, :4]
+    squares = jnp.stack([totals[j].sum() for j in (6, 8, 9, 7)])
     start = lax.axis_index("shard") * depth
     grad_gain = lax.dynamic_slice_in_dim(gains, start, depth, 1)
     grad_shift = lax.dynamic_slice_in_dim(shifts, start, depth, 1)
     entries = float(clips * rows * width * lax.axis_size(("shard",) + PLANE))
     return (
-        stream_out.astype(BF),
+        layer_out.reshape(clips, rows, width),
         grad_frames,
         grad_text,
         grad_gain,
         grad_shift,
         grad_w_qkv,
-        grad_side[0],
-        jnp.stack([grad_side[1], grad_side[3], grad_side[4]]),
         grad_side[2],
+        jnp.stack([grad_side[0], grad_side[3], grad_side[4]]),
+        grad_side[1],
         grad_up,
         grad_down,
         jnp.sqrt(squares / entries),

time: 647 us -> 586 us (0.906)
  matrix products: 55.3 us -> 19 us
  local copies, waits for them, and re-layouts: 71.4 us -> 47 us
  Pallas kernels: 418 us -> 437 us
  other arithmetic: 30.4 us -> 16.5 us
    dot_general x19 -> x7, matrix products: 53.3 us -> 17.2 us  [dots(): return jnp.einsum(spec, *operands, preferred_element_type=F32)]
    pallas_call x3 -> x4, Pallas kernels: 269 us -> 289 us  [the longest x1 87.9 us: last_step(): call(last_kernel, 'last_step', (shape(rows, width, dtype=F32), shape(16,...]
    convert_element_type x4 -> x2, local copies, waits for them, and re-layouts: 11.6 us -> 2.1 us  [the longest x1 1.28 us: on_device(): cross_q = dots('rd,bed->bre', norm_two, w_query).astype(BF)]
    unnamed x122 -> x91, local copies, waits for them, and re-layouts: 29.6 us -> 20.7 us
    reduce_sum x5 -> x1, other arithmetic: 8.81 us -> 0.64 us  [on_device(): squares = jnp.stack([totals[j].sum() for j in (6, 8, 9, 7)])]
  transfers between devices with their start and end apart: 8 -> 9, of which waited for: 3 -> 3; matrix products, arithmetic and copies ran while one was open for 15% -> 10% of each run, Pallas kernels for 51% -> 63%
where the time goes in v5:
time: 586 us; the launch traced here: 582 us
  Pallas kernels  437 us (75%)
  local copies, waits for them, and re-layouts  47 us (8%)
  waiting for transfers between devices  47 us (8%)
  matrix products  19 us (3%)
  other arithmetic  16.5 us (3%)
  between operations  14.7 us (3%)
    pallas_call x2, Pallas kernels, plane_gather(): call(kernel, 'plane_gather', outs, tuple(any_space), any_space, scratch,...  103 us
    pallas_call x1, Pallas kernels, last_step(): call(last_kernel, 'last_step', (shape(rows, width, dtype=F32), shape(16,...  87.9 us
    pallas_call x1, Pallas kernels, rows_back(): call(rows_back_kernel, 'rows_back', (shape(rows, width, dtype=F32), shape...  79.7 us
    pallas_call x1, Pallas kernels, feed_forward(): call(feed_kernel, 'feed_forward', outs, (IN_VMEM, ANY, IN_VMEM, IN_VMEM),...  70.2 us
    pallas_call x1, Pallas kernels, attend_backward(): call(backward_kernel, 'attend_backward', (shape(blocks, block, width), sh...  50.9 us
    pallas_call x1, Pallas kernels, attend_forward(): call(forward_kernel, 'attend_forward', (shape(blocks, block, 3 * columns)...  45.9 us
    all_gather x1, waiting for transfers between devices, whole(): return lax.all_gather(values, 'context', axis=1, tiled=True)  26.9 us
    unnamed x91, local copies, waits for them, and re-layouts  20.7 us
  transfers between devices with their start and end apart: 9, of which 3 were waited for; matrix products, arithmetic and copies ran while one was open for 10% of the time, Pallas kernels for 63%

profile of v5, /device:TPU:0, one launch (start us, length us, event | category | flops | bytes accessed | tf_op | source)
XLA Modules:
  0.0 582.0 jit_solution(664986257756056191)
XLA Ops:
  7.3 1.5 dynamic-slice_bitcast_fusion.2
  8.8 0.9 pad_maximum_fusion.2
  11.0 1.0 maximum_bitcast_fusion.1
  12.1 0.9 constant_dynamic-slice_fusion.1
  13.5 0.9 constant_dynamic-slice_fusion.2
  15.0 1.2 slice_reduce_fusion.4
  16.2 1.2 fusion.13.refs_0_
  17.5 34.4 %plane_gather.2.rows_ref = bf16[8,256,1536]{2,1,0:T(8,128)(2,1)} custom-call(bf16[256,1536]{1,0:T(8,128)(2,1)} %fusion.13.refs_0_), custom_call_target="tpu_custom_call" | custom-call | flops 32999999488 | bytes 33000000 | tf_op jit(solution)/shard_map/plane_gather/pallas_call | solution.py:353
  51.9 4.6 all-gather.7.cloned.1.call-done.w_ref
  56.5 45.9 %attend_forward.1 = (bf16[8,256,576]{2,1,0:T(8,128)(2,1)}, f32[6,1024]{1,0:T(8,128)}, bf16[8,256,192]{2,1,0:T(8,128)(2,1)}, bf16[8,256,192]{2,1,0:T(8,128)(2,1)}, bf16[8,256,1536]{2,1,0:T(8,128)(2,1)}) custom-call(bf16[8,256,1536]{2,1,0:T(8,128)(2,1)} %plane_gather.2.rows_ref, bf16[1536,576]{1,0:T(8,128)(2,1)} %all-gather.7.cloned.1.call-done.w_ref, ...), custom_call_target="tpu_custom_call" | custom-call | flops 44999999488 | bytes 45000000 | tf_op jit(solution)/shard_map/attend_forward/pallas_call | solution.py:589
  102.4 15.3 %all-gather.15.cloned.1.call-done = bf16[20,192,384]{2,1,0:T(8,128)(2,1)} async-done(((bf16[5,192,384]{2,1,0:T(8,128)(2,1)}), bf16[20,192,384]{2,1,0:T(8,128)(2,1)}) %all-gather.15.cloned.1.call-update) | async-done | bytes 2949136 | tf_op jit(solution)/shard_map/all_gather | solution.py:1109
  117.7 4.1 copy.131
  123.3 1.5 reshape.161
  124.8 1.5 copy.108
  126.8 1.2 fusion.21
  128.0 68.2 %plane_gather.3 = (bf16[8,576,1536]{2,1,0:T(8,128)(2,1)}, bf16[8,256,192]{2,1,0:T(8,128)(2,1)}) custom-call(bf16[576,1536]{1,0:T(8,128)(2,1)} %bitcast.156, bf16[256,192]{1,0:T(8,128)(2,1)} %bitcast.173), custom_call_target="tpu_custom_call" | custom-call | flops 65000001536 | bytes 65000000 | tf_op jit(solution)/shard_map/plane_gather/pallas_call | solution.py:353
  196.1 4.5 fusion.54
  201.4 3.9 fusion.15
  205.4 1.1 reshape.150
  208.1 2.6 fusion.55
  211.8 1.8 fusion.56
  213.6 1.8 fusion.16
  216.7 4.9 fusion.53
  222.4 1.2 add_convert_fusion.own_ref
  223.6 70.2 %feed_forward.1 = (f32[256,1536]{1,0:T(8,128)}, bf16[8,256,1536]{2,1,0:T(8,128)(2,1)}, bf16[1536,768]{1,0:T(8,128)(2,1)}, bf16[1536,768]{1,0:T(8,128)(2,1)}) custom-call(bf16[256,1536]{1,0:T(8,128)(2,1)} %add_convert_fusion.own_ref, bf16[8,256,1536]{2,1,0:T(8,128)(2,1)} %get-tuple-element.52.grad_ref, bf16[1536,768]{1,0:T(8,128)(2,1)} %all-gather.9.cloned.1.call-done.up_ref, ...), custom_call_target="tpu_custom_call" | custom-call | flops 70000001024 | bytes 70000000 | tf_op jit(solution)/shard_map/feed_forward/pallas_call | solution.py:492
  294.0 1.3 copy.87.mix_ref
  295.3 1.3 copy.81
  296.6 79.7 %rows_back.1 = (f32[256,1536]{1,0:T(8,128)}, bf16[256,1536]{1,0:T(8,128)(2,1)}, f32[8,1536]{1,0:T(8,128)}, bf16[8,256,192]{2,1,0:T(8,128)(2,1)}, bf16[8,192,1536...) custom-call(f32[256,1536]{1,0:T(8,128)} %get-tuple-element.53.normed_ref, ...), custom_call_target="tpu_custom_call" | custom-call | flops 65000001536 | bytes 65000000 | tf_op jit(solution)/shard_map/rows_back/pallas_call | solution.py:897
  376.3 2.5 reshape.158
  378.8 1.2 copy.132
  380.3 50.9 %attend_backward.1 = (bf16[8,256,1536]{2,1,0:T(8,128)(2,1)}, bf16[1536,576]{1,0:T(8,128)(2,1)}, bf16[192,1536]{1,0:T(8,128)(2,1)}, f32[256,192]{1,0:T(8,128)}) custom-call(bf16[8,256,192]{2,1,0:T(8,128)(2,1)} %get-tuple-element.56.grad_ref, bf16[8,256,576]{2,1,0:T(8,128)(2,1)} %get-tuple-element.57.qkv_ref, bf16[8,256,192]{2,1,0:T(8,128)(2,1)} %get-tuple-element.58.mix_ref, ...), custom_call_target="tpu_custom_call" | custom-call | flops 44999999488 | bytes 45000000 | tf_op jit(solution)/shard_map/attend_backward/pallas_call | solution.py:708
  434.4 0.9 copy-done.17
  435.4 1.4 maximum_bitcast_fusion
  438.1 87.9 %last_step.1 = (f32[256,1536]{1,0:T(8,128)}, f32[16,1536]{1,0:T(8,128)}, f32[16,1536]{1,0:T(8,128)}, f32[3,384,384]{2,1,0:T(8,128)}, f32[384,1536]{1,0:T(8,128)}, /*index=5*/f32[384,1536]{1,0:T(8,128)}) custom-call(bf16[8,256,1536]{2,1,0:T(8,128)(2,1)} %get-tuple-element.68.part_ref, bf16[256,1536]{1,0:T(8,128)(2,1)} %bitcast.150, ...), custom_call_target="tpu_custom_call" | custom-call | flops 65000001536 | bytes 65000000 | tf_op jit(solution)/shard_map/last_step/pallas_call | solution.py:1034
  526.1 2.0 pad_maximum_fusion.1
  528.8 3.2 fusion.41
  533.3 26.9 %all-gather.13.cloned.1.call-done = bf16[5,384,384]{2,1,0:T(8,128)(2,1)} async-done(((bf16[5,192,384]{2,1,0:T(8,128)(2,1)}), bf16[5,384,384]{2,1,0:T(8,128)(2,1)}) %all-gather.13.cloned.1.call-update) | async-done | bytes 1474576 | tf_op jit(solution)/shard_map/all_gather | solution.py:1218
  560.2 1.6 convert_bitcast_fusion
  562.1 1.8 copy.93
  563.9 1.0 copy.92
  564.9 1.0 copy.94
  566.0 0.9 copy.140
  566.9 1.1 copy.141
  569.0 1.2 copy.143
  570.2 1.1 copy-done.8
  571.3 1.4 copy.144
  572.7 1.1 copy-done.7
  573.8 1.4 copy.145
  (143 shorter events, 18.1 us)
Async XLA Ops:
  7.2 4.9 copy-start
  7.2 2.6 copy-start.20
  7.2 49.3 %all-gather.7.cloned.1.call-start = ((), (), s32[]{:S(2)}) async-start(), calls=%async_computation.4 | async-start | bytes 2457600 | tf_op jit(solution)/shard_map/all_gather | solution.py:1109
  8.8 1.4 copy-start.25
  8.8 1.4 copy-start.26
  9.8 108.0 %all-gather.15.cloned.1.call-start = ((), (), s32[]{:S(2)}) async-start(), calls=%async_computation.12 | async-start | bytes 3686400 | tf_op jit(solution)/shard_map/all_gather | solution.py:1109
  12.0 1.5 copy-start.23
  12.0 211.6 %all-gather.11.cloned.1.call-start = ((), (), s32[]{:S(2)}) async-start(), calls=%async_computation.6 | async-start | bytes 2949120 | tf_op jit(solution)/shard_map/all_gather | solution.py:1109
  12.1 2.3 copy-start.4
  13.0 2.0 copy-start.32
  13.0 2.0 copy-start.33
  13.0 210.6 %all-gather.9.cloned.1.call-start = ((), (), s32[]{:S(2)}) async-start(), calls=%async_computation.5 | async-start | bytes 2949120 | tf_op jit(solution)/shard_map/all_gather | solution.py:1109
  14.4 418.4 %reduce-scatter.5.cloned.1.call-start = ((), (), s32[]{:S(2)}) async-start(), calls=%async_computation.7 | async-start | bytes 2949120 | tf_op jit(solution)/shard_map/reduce_scatter | solution.py:1161
  122.3 1.0 copy-start.2
  124.8 1.6 copy-start.12
  124.8 2.0 copy-start.21
  127.9 68.2 %copy-start.5 = (bf16[2,128,1536]{2,1,0:T(8,128)(2,1)S(1)}, bf16[2,128,1536]{2,1,0:T(8,128)(2,1)}, u32[]{:S(2)}) copy-start(bf16[2,128,1536]{2,1,0:T(8,128)(2,1)} %param.11) | copy-start | bytes 2359300
  127.9 68.2 %copy-start.38 = (bf16[8,256,192]{2,1,0:T(8,128)(2,1)S(1)}, bf16[8,256,192]{2,1,0:T(8,128)(2,1)}, u32[]{:S(2)}) copy-start(bf16[8,256,192]{2,1,0:T(8,128)(2,1)} %get-tuple-element.49.my_mix_ref) | copy-start | bytes 2359300
  200.7 4.7 copy-start.10
  200.7 0.7 copy-start.34
  200.7 0.8 copy-start.35
  205.4 1.5 copy-start.13
  210.7 1.1 copy-start.15
  211.8 1.8 copy-start.16
  221.7 2.0 copy-start.6
  221.7 0.7 copy-start.30
  221.7 0.8 copy-start.31
  293.9 138.9 %reduce-scatter.7.cloned.1.call-start = ((), (), s32[]{:S(2)}) async-start(), calls=%async_computation.8 | async-start | bytes 2949120 | tf_op jit(solution)/shard_map/reduce_scatter | solution.py:1161
  296.6 229.5 %reduce-scatter.9.cloned.1.call-start = ((), (), s32[]{:S(2)}) async-start(), calls=%async_computation.9 | async-start | bytes 1474560 | tf_op jit(solution)/shard_map/reduce_scatter | solution.py:1161
  380.0 146.0 %reduce-scatter.11.cloned.1.call-start = ((), (), s32[]{:S(2)}) async-start(), calls=%async_computation.10 | async-start | bytes 2211840 | tf_op jit(solution)/shard_map/reduce_scatter | solution.py:1161
  380.3 50.9 %copy-start.3 = (bf16[2,192,4,384]{3,2,1,0:T(4,128)(2,1)S(1)}, bf16[2,192,4,384]{3,2,1,0:T(4,128)(2,1)}, u32[]{:S(2)}) copy-start(bf16[2,192,4,384]{3,2,1,0:T(4,128)(2,1)} %copy-done.2) | copy-start | bytes 3538948
  431.2 0.7 copy-start.37
  431.2 0.7 copy-start.36
  431.3 0.8 copy-start.28
  431.3 1.5 copy-start.24
  431.3 2.2 copy-start.22
  432.8 0.7 copy-start.18
  434.3 1.1 copy-start.17
  435.4 1.4 copy-start.19
  438.0 122.1 %all-gather.13.cloned.1.call-start = ((), (), s32[]{:S(2)}) async-start(), calls=%async_computation.11 | async-start | bytes 2211840 | tf_op jit(solution)/shard_map/all_gather | solution.py:1218
  526.0 2.1 copy-start.29
  563.9 2.1 copy-start.14
  564.9 1.9 copy-start.11
  566.9 1.1 copy-start.27
  566.9 2.1 copy-start.9
  569.0 2.3 copy-start.8
  571.3 2.5 copy-start.7
  571.3 3.9 copy-start.1
Sparse Core Ops, SparseCore 0:
  10.2 46.2 all-gather.6
  58.6 59.0 all-gather.14
  119.9 49.0 all-gather.10
  171.0 49.3 all-gather.8
  294.0 45.6 reduce-scatter.4
  341.8 47.5 reduce-scatter.6
  392.3 28.6 reduce-scatter.8
  438.1 66.0 reduce-scatter.10
  528.2 31.8 all-gather.12

commit v6 on v5

--- a/solution.py
+++ b/solution.py
@@ -327,51 +327,67 @@
     ]
 
 
-def gather_kernel(count, *refs):
-    enter(neighbours())
-    jobs = []
-    for index in range(count):
-        scratch = refs[2 * count + 3 * index : 2 * count + 3 * index + 3]
-        jobs.append(Gather(refs[index], refs[count + index], *scratch))
-    for job in jobs:
-        job.start()
-    for job in jobs:
-        job.relay_y()
-        job.relay_x()
-    for job in jobs:
-        job.relay_far()
-    for job in jobs:
-        job.finish()
-
-
-def plane_gather(arrays, ident, micros):
-    count = len(arrays)
-    outs = tuple(shape(8, *values.shape, dtype=values.dtype) for values in arrays)
-    kernel = partial(gather_kernel, count)
-    scratch = gather_scratch() * count
-    any_space = [ANY] * count
-    return call(kernel, "plane_gather", outs, tuple(any_space), any_space, scratch, ident, micros)(
-        *arrays
-    )
-
-
-def scatter_kernel(in_ref, out_ref, *scratch):
-    enter(neighbours())
-    job = LoadedScatter(in_ref, *scratch)
-    job.start()
-    job.first()
-    job.second()
-    out_ref[...] = job.total()
-    job.finish()
-
-
-def plane_scatter(values, ident, micros):
-    _, rows, columns = values.shape
-    outs = shape(rows, columns, dtype=F32)
-    scratch = LoadedScatter.scratch(rows, columns)
+def shard_others():
+    z, shards = lax.axis_index("shard"), lax.axis_size("shard")
+    return [lax.rem(z + i, shards) for i in range(1, shards)]
+
+
+def first_kernel(
+    frames_ref, gain_ref, bias_ref, cot_ref, w_ref,
+    rows_out, cot_out, w_out,
+    normed_ref, w_sem, w_send, w_recv, *scratch,
+):
+    z = lax.axis_index("shard")
+    spot = place()[1:]
+    others = shard_others()
+    enter(neighbours() + [device(other, *spot) for other in others])
+    own = pltpu.make_async_copy(w_ref, w_out.at[z], w_sem)
+    own.start()
+    copies = []
+    for index, other in enumerate(others):
+        copy = remote_copy(
+            w_ref, w_out.at[z], w_send.at[index], w_recv.at[index], device(other, *spot)
+        )
+        copy.start()
+        copies.append(copy)
+
+    def norm(part, carry):
+        normed, _ = normalise(frames_ref[part].astype(F32))
+        normed_ref[part] = (normed * gain_ref[0:1] + bias_ref[0:1]).astype(BF)
+        return carry
+
+    chunks(frames_ref.shape[0], norm)
+    rows, grads = Gather(normed_ref, rows_out, *scratch[:3]), Gather(cot_ref, cot_out, *scratch[3:])
+    rows.start()
+    rows.relay_y()
+    rows.relay_x()
+    grads.start()
+    rows.relay_far()
+    rows.finish()
+    grads.rest()
+    own.wait()
+    for copy in copies:
+        copy.wait()
+
+
+def first_step(frames, gain, bias, cotangent, w_qkv, shards, ident):
+    rows, width = frames.shape
     return call(
-        scatter_kernel, "plane_scatter", outs, IN_VMEM, [ANY], scratch, ident, micros
-    )(values)
+        first_kernel,
+        "first_step",
+        (shape(8, rows, width), shape(8, rows, width), shape(shards, *w_qkv.shape)),
+        (ANY, ANY, ANY),
+        [IN_VMEM, IN_VMEM, IN_VMEM, ANY, ANY],
+        [
+            pltpu.VMEM((rows, width), BF),
+            pltpu.SemaphoreType.DMA,
+            pltpu.SemaphoreType.DMA((shards - 1,)),
+            pltpu.SemaphoreType.DMA((shards - 1,)),
+        ]
+        + gather_scratch() * 2,
+        ident,
+        60,
+    )(frames, gain, bias, cotangent, w_qkv)
 
 
 def feed_kernel(
@@ -527,19 +543,36 @@
 
 
 def forward_kernel(
-    rows_ref, w_ref, cot_ref,
-    qkv_ref, log_ref, mix_ref, mine_ref, cot_out,
-    ex_local, ex_send, ex_recv, g_local, g_send, g_recv,
+    rows_ref, w_ref, side_ref, text_in, frames_ref, gain_ref, bias_ref,
+    qkv_ref, log_ref, mix_ref, mine_ref, one_ref, two_ref, query_ref, cross_ref, low_ref,
+    text_ref, square_ref, plane_out,
+    w_own, w_out, w_query, w_cross, sum_ref, two_low_ref, store_sem,
+    ex_local, ex_send, ex_recv, *scratch,
 ):
     enter(plane_others())
-    side = Gather(cot_ref, cot_out, g_local, g_send, g_recv)
-    side.start()
     blocks, both, _ = rows_ref.shape
     rows = both // 2
     width = mix_ref.shape[2]
+    features = two_low_ref.shape[1]
     heads = width // HEAD_DIM
     length = blocks * rows
     step = SIDE // rows
+    depth = side_ref.shape[2]
+    for index in range(side_ref.shape[0]):
+        lanes = slice(index * depth, (index + 1) * depth)
+        for kind in range(3):
+            w_own[kind, :, lanes] = side_ref[index, kind * width : (kind + 1) * width]
+    weights = (w_out, w_query, w_cross)
+    jobs = [Gather(w_own.at[k], weights[k], *scratch[3 * k : 3 * k + 3]) for k in range(3)]
+    text_job = Gather(text_in, text_ref, *scratch[9:])
+    text_job.start()
+    jobs[0].start()
+    stores = []
+
+    def keep(kind):
+        copy = pltpu.make_async_copy(weights[kind], plane_out.at[kind], store_sem.at[kind])
+        copy.start()
+        stores.append(copy)
 
     def project(block, carry):
         qkv_ref[block] = nn(rows_ref[block], w_ref[...]).astype(BF)
@@ -575,38 +608,132 @@
                 log_ref[pl.ds(clip * heads + head, 1), pl.ds(start, SIDE)] = top + jnp.log(total)
         exchange.start(clip, part)
         if clip == 0:
-            side.relay_y()
-            side.relay_x()
-    side.relay_far()
+            jobs[0].relay_y()
+            jobs[0].relay_x()
+            jobs[1].start()
+    text_job.relay_y()
+    text_job.relay_x()
+    jobs[0].relay_far()
+    jobs[0].finish()
+    keep(0)
     exchange.finish()
-    side.finish()
-
-
-def attend_forward(rows, weights, cotangent, ident):
+
+    def apply(values_ref, kind):
+        sum_ref[...] = jnp.zeros_like(sum_ref)
+
+        def one(block, carry):
+            sum_ref[...] += nn(values_ref[block], weights[kind][block])
+            return carry
+
+        lax.fori_loop(0, blocks, one, 0)
+
+    apply(mine_ref, 0)
+    jobs[1].relay_y()
+    jobs[1].relay_x()
+    jobs[2].start()
+    nothing = jnp.zeros((1, features), F32)
+
+    def first(part, sums):
+        branch = sum_ref[part]
+        total = frames_ref[part].astype(F32) + branch
+        one_ref[part] = total
+        normed, _ = normalise(total)
+        two_low_ref[part] = (normed * gain_ref[1:2] + bias_ref[1:2]).astype(BF)
+        return sums + jnp.sum(branch * branch, axis=0, keepdims=True)
+
+    square_one = chunks(both, first, nothing)
+    text_job.relay_far()
+    text_job.finish()
+    jobs[1].relay_far()
+    jobs[1].finish()
+    keep(1)
+
+    def ask(block, carry):
+        query_ref[block] = nt(two_low_ref[...], w_query[block]).astype(BF)
+        return carry
+
+    lax.fori_loop(0, blocks, ask, 0)
+    texts = text_ref.shape[1] // 4
+
+    def cross(block, carry):
+        for clip in range(2):
+            part = pl.ds(clip * rows, rows)
+            keys = pl.ds(clip * texts, texts)
+            values = pl.ds((2 + clip) * texts, texts)
+            for head in range(heads):
+                here = pl.ds(head * HEAD_DIM, HEAD_DIM)
+                query = query_ref[block, part, here] * jnp.asarray(HEAD_DIM ** (-0.5), BF)
+                scores = nt(text_ref[block, keys, here], query)
+                probs = jnp.exp(scores - jnp.max(scores, axis=0, keepdims=True))
+                probs = probs / jnp.sum(probs, axis=0, keepdims=True)
+                mix = nn(turn(text_ref[block, values, here]).astype(BF), probs.astype(BF))
+                cross_ref[block, part, here] = jnp.transpose(mix).astype(BF)
+        return carry
+
+    lax.fori_loop(0, blocks // 2, cross, 0)
+    jobs[2].relay_y()
+    jobs[2].relay_x()
+    lax.fori_loop(blocks // 2, blocks, cross, 0)
+    jobs[2].relay_far()
+    jobs[2].finish()
+    keep(2)
+    apply(cross_ref, 2)
+
+    def second(part, sums):
+        branch = sum_ref[part]
+        total = one_ref[part] + branch
+        two_ref[part] = total
+        normed, _ = normalise(total)
+        low_ref[part] = (normed * gain_ref[2:3] + bias_ref[2:3]).astype(BF)
+        return sums + jnp.sum(branch * branch, axis=0, keepdims=True)
+
+    square_two = chunks(both, second, nothing)
+    square_ref[...] = jnp.zeros_like(square_ref)
+    square_ref[0:1] = square_one
+    square_ref[1:2] = square_two
+    for copy in stores:
+        copy.wait()
+
+
+def attend_forward(rows, w_qkv, side, text, frames, gain, bias, ident):
     blocks, block, width = rows.shape
-    columns = weights.shape[1] // 3
+    columns = w_qkv.shape[1] // 3
     heads = columns // HEAD_DIM
+    heads_shape = shape(blocks, block, columns)
+    stream = shape(block, width, dtype=F32)
     return call(
         forward_kernel,
         "attend_forward",
         (
             shape(blocks, block, 3 * columns),
             shape(2 * heads, blocks * block // 2, dtype=F32),
-            shape(blocks, block, columns),
-            shape(blocks, block, columns),
-            shape(blocks, block, width),
+            heads_shape,
+            heads_shape,
+            stream,
+            stream,
+            heads_shape,
+            heads_shape,
+            shape(block, width),
+            shape(blocks, *text.shape),
+            shape(8, width, dtype=F32),
+            shape(3, blocks, columns, width),
         ),
-        (IN_VMEM, IN_VMEM, IN_VMEM, ANY, ANY),
-        [IN_VMEM, IN_VMEM, ANY],
-        [
+        (IN_VMEM,) * 11 + (ANY,),
+        [IN_VMEM] * 3 + [ANY] + [IN_VMEM] * 3,
+        [pltpu.VMEM((3, columns, width), BF)]
+        + [pltpu.VMEM((blocks, columns, width), BF)] * 3
+        + [
+            pltpu.VMEM((block, width), F32),
+            pltpu.VMEM((block, width), BF),
+            pltpu.SemaphoreType.DMA((3,)),
             pltpu.SemaphoreType.DMA((2,)),
             pltpu.SemaphoreType.DMA((2, 7)),
             pltpu.SemaphoreType.DMA((2, 7)),
         ]
-        + gather_scratch(),
+        + gather_scratch() * 4,
         ident,
-        45,
-    )(rows, weights, cotangent)
+        80,
+    )(rows, w_qkv, side, text, frames, gain, bias)
 
 
 def backward_kernel(
@@ -780,7 +907,7 @@
     loads = []
     for index, buffer in ((2, w_cross), (1, w_query), (0, w_out)):
         load = pltpu.make_async_copy(
-            w_ref.at[:, index], buffer, w_sem.at[index]
+            w_ref.at[index], buffer, w_sem.at[index]
         )
         load.start()
         loads.append(load)
@@ -1108,51 +1235,40 @@
     def over_shard(weight, tiled=True):
         return lax.all_gather(weight, "shard", axis=0, tiled=tiled)
 
+    cross_part = half(cross_qkv)
+    side = jnp.concatenate([half(self_out), cross_part[0], half(cross_out)], axis=1)
+    w_side = over_shard(side.transpose(1, 0), tiled=False)
+    w_text = over_shard(jnp.concatenate([cross_part[1], cross_part[2]], axis=1))
+    w_down = over_shard(half(mlp_down))
+    w_up = over_shard(half(mlp_up))
+
     qkv_part = half(self_qkv)
-    w_qkv = over_shard(jnp.concatenate([qkv_part[0], qkv_part[1], qkv_part[2]], axis=-1))
-    cross_part = half(cross_qkv)
-    side = jnp.stack(
-        [half(self_out), cross_part[0], half(cross_out), cross_part[1], cross_part[2]]
-    )
-    w_side = over_shard(side.transpose(0, 2, 1), tiled=False).transpose(1, 2, 0, 3)
-    w_side = w_side.reshape(5, columns, width)
-    w_up = over_shard(half(mlp_up))
-    w_down = over_shard(half(mlp_down))
-
-    stream_zero = frames.astype(F32).reshape(block, width)
-    norm_one = layer_norm(stream_zero, norm_gain[0], norm_bias[0])
-    (all_one,) = plane_gather([norm_one.astype(BF)], 0, 33)
-    qkv, self_log, mix, my_mix, all_grad = attend_forward(
-        all_one, w_qkv, cotangent.reshape(block, width), 1
-    )
-
-    text_part = dots("cnd,ted->tcne", text_states, w_side[3:]).astype(BF)
-    plane_w, text_all = plane_gather(
-        [
-            w_side[:3].reshape(3 * columns, width),
-            text_part.reshape(2 * clips * texts, columns),
-        ],
-        2,
-        65,
-    )
-    plane_w = plane_w.reshape(8, 3, columns, width)
-    w_out, w_query, w_cross = plane_w[:, 0], plane_w[:, 1], plane_w[:, 2]
-    branch_one = dots("bre,bed->rd", my_mix, w_out)
-    stream_one = stream_zero + branch_one
-    norm_two = layer_norm(stream_one, norm_gain[1], norm_bias[1]).astype(BF)
-    cross_q = dots("rd,bed->bre", norm_two, w_query).astype(BF)
-    text_heads = text_all.reshape(8, 2, clips, texts, heads, HEAD_DIM)
-    scale = HEAD_DIM ** (-0.5)
-    queries = cross_q.reshape(8, clips, rows, heads, HEAD_DIM)
-    scores = dots("bcfhd,bcnhd->cbhfn", queries, text_heads[:, 0]) * scale
-    weights = jnp.exp(scores - jnp.max(scores, axis=-1, keepdims=True))
-    weights = weights / jnp.sum(weights, axis=-1, keepdims=True)
-    cross_mix = dots("cbhfn,bcnhd->bcfhd", weights.astype(BF), text_heads[:, 1]).astype(BF)
-    cross_mix = cross_mix.reshape(8, block, columns)
-    branch_two = dots("bre,bed->rd", cross_mix, w_cross)
-    stream_two = stream_one + branch_two
-
-    norm_three = layer_norm(stream_two, norm_gain[2], norm_bias[2]).astype(BF)
+    all_one, all_grad, w_qkv = first_step(
+        frames.reshape(block, width),
+        norm_gain,
+        norm_bias,
+        cotangent.reshape(block, width),
+        jnp.concatenate([qkv_part[0], qkv_part[1], qkv_part[2]], axis=-1),
+        slices,
+        0,
+    )
+    w_qkv = w_qkv.reshape(width, 3 * columns)
+    text_part = dots("cnd,de->cne", text_states, w_text).astype(BF)
+    text_part = text_part.reshape(clips * texts, 2, columns).transpose(1, 0, 2)
+    (
+        qkv, self_log, mix, my_mix, stream_one, stream_two, cross_q, cross_mix, norm_three,
+        text_all, squares, plane_w,
+    ) = attend_forward(
+        all_one,
+        w_qkv,
+        w_side,
+        text_part.reshape(2 * clips * texts, columns),
+        frames.reshape(block, width),
+        norm_gain,
+        norm_bias,
+        1,
+    )
+
     grad_normed, part_three, grad_up, grad_down = feed_forward(
         norm_three, all_grad, w_up, w_down, 4
     )
@@ -1184,23 +1300,24 @@
     part_norm, grad_w_qkv, grad_out, text_grads = attend_backward(
         grad_mix, qkv, mix, self_log, all_one, w_qkv, part_out, text_grads, 8
     )
-    part_norm, grad_w_qkv, grad_out, text_grads, grad_down, grad_up = lax.optimization_barrier(
-        (part_norm, grad_w_qkv, grad_out, text_grads, grad_down, grad_up)
+    (
+        part_norm, grad_w_qkv, grad_out, text_grads, grad_down, grad_up, grad_cross
+    ) = lax.optimization_barrier(
+        (part_norm, grad_w_qkv, grad_out, text_grads, grad_down, grad_up, grad_cross)
     )
     text_grads = text_grads.reshape(2, clips, texts, columns).astype(BF)
-    w_grad_text = dots("cnd,tcne->ted", text_states, text_grads).astype(BF)
-    rest = jnp.concatenate([grad_out, w_grad_text.reshape(2 * columns, width)], axis=0)
-    grad_rest = to_shard(slice_shards(rest))
-    grad_text = dots("tcne,ted->cnd", text_grads, w_side[3:])
+    text_grads = text_grads.transpose(1, 2, 0, 3).reshape(clips, texts, 2 * columns)
+    grad_w_text = to_shard(dots("cnd,cne->de", text_states, text_grads))
+    grad_out = to_shard(slice_shards(grad_out))
+    grad_text = dots("cne,de->cnd", text_grads, w_text)
     grad_text = grad_text.reshape(clips, 8, texts // 8, width).transpose(1, 0, 2, 3).astype(BF)
     grad_text = grad_text.reshape(8, clips * texts // 8, width)
-    squares = [jnp.sum(v * v, axis=0)[None] for v in (branch_one, branch_two)]
     grad_frames, totals, grad_text, grad_w_qkv, grad_up, grad_down = last_step(
         part_norm,
         frames.reshape(block, width),
         norm_gain[0][None],
         grad_one,
-        jnp.concatenate([stats] + squares + [jnp.zeros((6, width), F32)], axis=0),
+        jnp.concatenate([stats, squares], axis=0),
         grad_text,
         grad_w_qkv.reshape(slices, depth, 3 * columns),
         grad_up,
@@ -1211,13 +1328,13 @@
     grad_frames = grad_frames.reshape(clips, rows, width)
     grad_text = grad_text.reshape(clips, texts // 8, width)
 
-    grad_cross, grad_rest, totals = lax.optimization_barrier((grad_cross, grad_rest, totals))
-    grad_side = jnp.concatenate([grad_cross, grad_rest], axis=1)
-
-    def whole(values):
-        return lax.all_gather(values, "context", axis=1, tiled=True)
-
-    grad_side = whole(grad_side.reshape(5, columns, depth)).astype(F32).transpose(0, 2, 1)
+    grad_cross, grad_out, grad_w_text, totals = lax.optimization_barrier(
+        (grad_cross, grad_out, grad_w_text, totals)
+    )
+    grad_text_pair = [grad_w_text[None, :, k * columns : (k + 1) * columns] for k in range(2)]
+    grad_side = jnp.concatenate([grad_cross, grad_out], axis=1).reshape(3, columns, depth)
+    grad_side = jnp.concatenate([grad_side.transpose(0, 2, 1)] + grad_text_pair, axis=0)
+    grad_side = lax.all_gather(grad_side, "context", axis=2, tiled=True).astype(F32)
     gains = jnp.stack([totals[0], totals[2], totals[4]])
     shifts = jnp.stack([totals[1], totals[3], totals[5]])
     squares = jnp.stack([totals[j].sum() for j in (6, 8, 9, 7)])

time: 586 us -> 653 us (1.11)
  waiting for transfers between devices: 47 us -> 138 us
  matrix products: 19 us -> 2.64 us
  local copies, waits for them, and re-layouts: 47 us -> 31.3 us
  Pallas kernels: 437 us -> 444 us
    reduce_scatter x4, waiting for transfers between devices: 0.04 us -> 77.2 us  [to_shard(): lax.psum_scatter(part.astype(BF), 'shard', scatter_dimension=0, tiled=True)]
    pallas_call x1, Pallas kernels: 45.9 us -> 98.5 us  [attend_forward(): call(forward_kernel, 'attend_forward', (shape(blocks, block, 3 * columns)...]
    pallas_call x2 -> x1, Pallas kernels: 103 us -> 64.1 us  [first_step(): call(first_kernel, 'first_step', (shape(8, rows, width), shape(8, rows, w...]
    all_gather x4, waiting for transfers between devices: 19.9 us -> 39.5 us  [over_shard(): return lax.all_gather(weight, 'shard', axis=0, tiled=tiled)]
    dot_general x7 -> x3, matrix products: 17.2 us -> 2.64 us  [dots(): return jnp.einsum(spec, *operands, preferred_element_type=F32)]
    all_gather x1, waiting for transfers between devices: 26.9 us -> 19.6 us  [on_device(): lax.all_gather(grad_side, 'context', axis=2, tiled=True).astype(F32)]
    pallas_call x1, Pallas kernels: 87.9 us -> 80.7 us  [last_step(): call(last_kernel, 'last_step', (shape(rows, width, dtype=F32), shape(16,...]
    unnamed x91 -> x50, local copies, waits for them, and re-layouts: 20.7 us -> 15.9 us
  transfers between devices with their start and end apart: 9 -> 10, of which waited for: 3 -> 6; matrix products, arithmetic and copies ran while one was open for 10% -> 3% of each run, Pallas kernels for 63% -> 46%
where the time goes in v6:
time: 653 us; the launch traced here: 643 us
  Pallas kernels  444 us (68%)
  waiting for transfers between devices  138 us (21%)
  local copies, waits for them, and re-layouts  31.3 us (5%)
  between operations  14.9 us (2%)
  other arithmetic  12.2 us (2%)
    pallas_call x1, Pallas kernels, attend_forward(): call(forward_kernel, 'attend_forward', (shape(blocks, block, 3 * columns)...  98.5 us
    pallas_call x1, Pallas kernels, last_step(): call(last_kernel, 'last_step', (shape(rows, width, dtype=F32), shape(16,...  80.7 us
    pallas_call x1, Pallas kernels, rows_back(): call(rows_back_kernel, 'rows_back', (shape(rows, width, dtype=F32), shape...  79.6 us
    reduce_scatter x4, waiting for transfers between devices, to_shard(): lax.psum_scatter(part.astype(BF), 'shard', scatter_dimension=0, tiled=True)  77.2 us
    pallas_call x1, Pallas kernels, feed_forward(): call(feed_kernel, 'feed_forward', outs, (IN_VMEM, ANY, IN_VMEM, IN_VMEM),...  69.1 us
    pallas_call x1, Pallas kernels, first_step(): call(first_kernel, 'first_step', (shape(8, rows, width), shape(8, rows, w...  64.1 us
    pallas_call x1, Pallas kernels, attend_backward(): call(backward_kernel, 'attend_backward', (shape(blocks, block, width), sh...  51.5 us
    all_gather x4, waiting for transfers between devices, over_shard(): return lax.all_gather(weight, 'shard', axis=0, tiled=tiled)  39.5 us
  transfers between devices with their start and end apart: 10, of which 6 were waited for; matrix products, arithmetic and copies ran while one was open for 3% of the time, Pallas kernels for 46%

profile of v6, /device:TPU:0, one launch (start us, length us, event | category | flops | bytes accessed | tf_op | source)
XLA Modules:
  0.0 642.9 jit_solution(17975561383539528025)
XLA Ops:
  7.3 2.1 dynamic-slice_bitcast_fusion.1
  9.3 0.8 pad_maximum_fusion.4
  10.6 1.0 copy.40
  11.7 0.9 constant_dynamic-slice_fusion
  12.6 0.9 constant_dynamic-slice_fusion.1
  13.5 0.9 pad_maximum_fusion.2.w_ref
  14.5 64.1 %first_step.1 = (bf16[8,256,1536]{2,1,0:T(8,128)(2,1)}, bf16[8,256,1536]{2,1,0:T(8,128)(2,1)}, bf16[4,384,576]{2,1,0:T(8,128)(2,1)}) custom-call(bf16[256,1536]{1,0:T(8,128)(2,1)} %bitcast.98, f32[3,1536]{1,0:T(4,128)} %gain_ref.5, f32[3,1536]{1,0:T(4,128)} %bias_ref.5, bf16[256,1536]{1,0:T(8,128)(2,1)} %bitcast.96, bf16[384,576]{1,0:T(8,128)(2,1)} %pad_maximum_fusion.2.w_ref), custom_call_target="tpu_custom_call" | custom-call | flops 60000002048 | bytes 60000000 | tf_op jit(solution)/shard_map/first_step/pallas_call | solution.py:375
  78.7 1.6 fusion.9
  80.4 0.7 copy.41
  81.1 35.2 %all-gather.15.cloned.1.call-done = bf16[2304,384]{1,0:T(8,128)(2,1)} async-done(((bf16[576,384]{1,0:T(8,128)(2,1)}), bf16[2304,384]{1,0:T(8,128)(2,1)}) %all-gather.15.cloned.1.call-update) | async-done | bytes 1769488 | tf_op jit(solution)/shard_map/all_gather | solution.py:1236
  116.3 98.5 %attend_forward.1 = (bf16[8,256,576]{2,1,0:T(8,128)(2,1)}, f32[6,1024]{1,0:T(8,128)}, bf16[8,256,192]{2,1,0:T(8,128)(2,1)}, bf16[8,256,192]{2,1,0:T(8,128)(2,1)}...) custom-call(bf16[8,256,1536]{2,1,0:T(8,128)(2,1)} %get-tuple-element, ...), custom_call_target="tpu_custom_call" | custom-call | flops 80000000000 | bytes 80000000 | tf_op jit(solution)/shard_map/attend_forward/pallas_call | solution.py:704
  214.8 4.3 all-gather.9.cloned.1.call-done.up_ref
  219.1 69.1 %feed_forward.1 = (f32[256,1536]{1,0:T(8,128)}, bf16[8,256,1536]{2,1,0:T(8,128)(2,1)}, bf16[1536,768]{1,0:T(8,128)(2,1)}, bf16[1536,768]{1,0:T(8,128)(2,1)}) custom-call(bf16[256,1536]{1,0:T(8,128)(2,1)} %get-tuple-element.61.own_ref, bf16[8,256,1536]{2,1,0:T(8,128)(2,1)} %get-tuple-element.62.grad_ref, ...), custom_call_target="tpu_custom_call" | custom-call | flops 70000001024 | bytes 70000000 | tf_op jit(solution)/shard_map/feed_forward/pallas_call | solution.py:508
  288.2 79.6 %rows_back.1 = (f32[256,1536]{1,0:T(8,128)}, bf16[256,1536]{1,0:T(8,128)(2,1)}, f32[8,1536]{1,0:T(8,128)}, bf16[8,256,192]{2,1,0:T(8,128)(2,1)}, bf16[8,192,1536...) custom-call(f32[256,1536]{1,0:T(8,128)} %get-tuple-element.63.normed_ref, ...), custom_call_target="tpu_custom_call" | custom-call | flops 65000001536 | bytes 65000000 | tf_op jit(solution)/shard_map/rows_back/pallas_call | solution.py:1024
  367.9 2.5 reshape.80
  370.4 1.2 copy.57
  372.2 0.7 reduce-scatter.8.cloned.1.call-update
  373.1 51.5 %attend_backward.1 = (bf16[8,256,1536]{2,1,0:T(8,128)(2,1)}, bf16[1536,576]{1,0:T(8,128)(2,1)}, bf16[192,1536]{1,0:T(8,128)(2,1)}, f32[256,192]{1,0:T(8,128)}) custom-call(bf16[8,256,192]{2,1,0:T(8,128)(2,1)} %get-tuple-element.73.grad_ref, bf16[8,256,576]{2,1,0:T(8,128)(2,1)} %get-tuple-element.74.qkv_ref, bf16[8,256,192]{2,1,0:T(8,128)(2,1)} %get-tuple-element.75.mix_ref, ...), custom_call_target="tpu_custom_call" | custom-call | flops 44999999488 | bytes 45000000 | tf_op jit(solution)/shard_map/attend_backward/pallas_call | solution.py:835
  424.6 23.4 %reduce-scatter.10.cloned.1.call-done.up_ref = bf16[384,768]{1,0:T(8,128)(2,1)} async-done(((bf16[1536,768]{1,0:T(8,128)(2,1)}), bf16[384,768]{1,0:T(8,128)(2,1)}) %reduce-scatter.10.cloned.1.call-update) | async-done | bytes 589840 | tf_op jit(solution)/shard_map/reduce_scatter | solution.py:1277
  448.0 49.9 %reduce-scatter.8.cloned.1.call-done.down_ref = bf16[384,768]{1,0:T(8,128)(2,1)} async-done(((bf16[1536,768]{1,0:T(8,128)(2,1)}), bf16[384,768]{1,0:T(8,128)(2,1)}) %reduce-scatter.8.cloned.1.call-update) | async-done | bytes 589840 | tf_op jit(solution)/shard_map/reduce_scatter | solution.py:1277
  497.9 1.0 convert_element_type.29
  499.6 1.4 copy.51
  501.1 1.4 slice.77.gain_ref
  502.5 0.6 pad_maximum_fusion.5.stats_ref
  503.8 0.8 copy.59
  504.6 0.9 copy.58
  505.6 80.7 %last_step.1 = (f32[256,1536]{1,0:T(8,128)}, f32[16,1536]{1,0:T(8,128)}, f32[16,1536]{1,0:T(8,128)}, f32[3,384,384]{2,1,0:T(8,128)}, f32[384,1536]{1,0:T(8,128)}, /*index=5*/f32[384,1536]{1,0:T(8,128)}) custom-call(bf16[8,256,1536]{2,1,0:T(8,128)(2,1)} %get-tuple-element.86.part_ref, bf16[256,1536]{1,0:T(8,128)(2,1)} %bitcast.100, ...), custom_call_target="tpu_custom_call" | custom-call | flops 65000001536 | bytes 65000000 | tf_op jit(solution)/shard_map/last_step/pallas_call | solution.py:1161
  586.3 1.2 copy.52
  587.5 4.0 reduce-scatter.14.cloned.1.call-done
  591.5 1.0 pad_maximum_fusion.3
  592.5 1.0 pad_maximum_fusion.1
  594.2 3.2 fusion.16
  597.3 0.7 fusion.13
  598.0 0.7 fusion.15
  598.7 19.6 %all-gather.13.cloned.1.call-done = bf16[5,384,384]{1,2,0:T(8,128)(2,1)} async-done(((bf16[5,384,192]{1,2,0:T(8,128)(2,1)}), bf16[5,384,384]{1,2,0:T(8,128)(2,1)}) %all-gather.13.cloned.1.call-update) | async-done | bytes 1474576 | tf_op jit(solution)/shard_map/all_gather | solution.py:1337
  618.2 1.3 slice.96
  619.8 1.3 pad_maximum_fusion
  621.2 2.8 copy.48
  624.3 1.1 copy.47
  625.4 1.0 copy.49
  626.4 0.9 copy.66
  627.3 1.1 copy.67
  628.5 0.6 copy.68
  629.4 1.2 copy.69
  630.6 1.1 copy-done.5
  631.7 1.4 copy.70
  633.1 1.1 copy-done.4
  634.2 1.4 copy.71
  (74 shorter events, 4.8 us)
Async XLA Ops:
  7.2 4.5 copy-start
  7.2 3.0 copy-start.15
  7.2 3.0 copy-start.14
  7.2 71.4 %all-gather.7.cloned.1.call-start = ((), (), s32[]{:S(2)}) async-start(), calls=%async_computation.5 | async-start | bytes 1474560 | tf_op jit(solution)/shard_map/all_gather | solution.py:1236
  10.2 106.1 %all-gather.15.cloned.1.call-start = ((), (), s32[]{:S(2)}) async-start(), calls=%async_computation.13 | async-start | bytes 2211840 | tf_op jit(solution)/shard_map/all_gather | solution.py:1236
  10.6 2.0 copy-start.13
  11.6 203.2 %all-gather.11.cloned.1.call-start = ((), (), s32[]{:S(2)}) async-start(), calls=%async_computation.7 | async-start | bytes 2949120 | tf_op jit(solution)/shard_map/all_gather | solution.py:1236
  12.6 206.6 %all-gather.9.cloned.1.call-start = ((), (), s32[]{:S(2)}) async-start(), calls=%async_computation.6 | async-start | bytes 2949120 | tf_op jit(solution)/shard_map/all_gather | solution.py:1236
  13.5 411.1 %reduce-scatter.12.cloned.1.call-start = ((), (), s32[]{:S(2)}) async-start(), calls=%async_computation.10 | async-start | bytes 1474560 | tf_op jit(solution)/shard_map/reduce_scatter | solution.py:1277
  14.5 64.2 %copy-start.8 = (bf16[2,64,1536]{2,1,0:T(8,128)(2,1)S(1)}, bf16[2,64,1536]{2,1,0:T(8,128)(2,1)}, u32[]{:S(2)}) copy-start(bf16[2,64,1536]{2,1,0:T(8,128)(2,1)} %param.12) | copy-start | bytes 1179652
  371.6 76.4 %reduce-scatter.10.cloned.1.call-start = ((), (), s32[]{:S(2)}) async-start(), calls=%async_computation.9 | async-start | bytes 2949120 | tf_op jit(solution)/shard_map/reduce_scatter | solution.py:1277
  372.2 125.7 %reduce-scatter.8.cloned.1.call-start = ((), (), s32[]{:S(2)}) async-start(), calls=%async_computation.8 | async-start | bytes 2949120 | tf_op jit(solution)/shard_map/reduce_scatter | solution.py:1277
  372.9 213.4 %reduce-scatter.16.cloned.1.call-start = ((), (), s32[]{:S(2)}) async-start(), calls=%async_computation.14 | async-start | bytes 1474560
  373.1 126.0 %copy-start.9 = (bf16[2,64,1536]{2,1,0:T(8,128)(2,1)S(1)}, bf16[2,64,1536]{2,1,0:T(8,128)(2,1)}, u32[]{:S(2)}) copy-start(bf16[2,64,1536]{2,1,0:T(8,128)(2,1)} %param.12) | copy-start | bytes 1179652
  499.6 2.9 copy-start.17
  499.6 2.9 copy-start.18
  499.6 3.7 copy-start.3
  501.0 3.5 copy-start.11
  501.1 90.4 %reduce-scatter.14.cloned.1.call-start = ((), (), s32[]{:S(2)}) async-start(), calls=%async_computation.11 | async-start | bytes 737280 | tf_op jit(solution)/shard_map/reduce_scatter | solution.py:1277
  505.5 112.7 %all-gather.13.cloned.1.call-start = ((), (), s32[]{:S(2)}) async-start(), calls=%async_computation.12 | async-start | bytes 2211840 | tf_op jit(solution)/shard_map/all_gather | solution.py:1337
  505.5 86.0 %copy-start.12 = (bf16[1,384,384]{2,1,0:T(8,128)(2,1)S(1)}, bf16[1,384,384]{2,1,0:T(8,128)(2,1)}, u32[]{:S(2)}) copy-start(bf16[1,384,384]{2,1,0:T(8,128)(2,1)} %reduce-scatter.12.cloned.1.call-done) | copy-start | bytes 884740
  591.5 2.0 copy-start.19
  618.2 1.6 copy-start.2
  624.3 2.1 copy-start.10
  624.3 3.0 copy-start.7
  627.3 1.1 copy-start.16
  627.3 2.1 copy-start.6
  629.4 2.3 copy-start.5
  631.7 2.5 copy-start.4
  631.7 3.9 copy-start.1
Sparse Core Ops, SparseCore 0:
  10.3 62.5 all-gather.6
  75.0 41.1 all-gather.14
  118.4 49.3 all-gather.10
  169.8 49.2 all-gather.8
  371.7 27.3 reduce-scatter.11
  401.2 46.7 reduce-scatter.9
  450.3 47.5 reduce-scatter.7
  501.2 55.2 reduce-scatter.15
  559.4 32.0 reduce-scatter.13
  593.6 24.5 all-gather.12

commit v7 on v6

--- a/solution.py
+++ b/solution.py
@@ -332,24 +332,33 @@
     return [lax.rem(z + i, shards) for i in range(1, shards)]
 
 
+def spread(source_of, target_ref, send, recv, others, spot):
+    z = lax.axis_index("shard")
+    copies = []
+    for index, other in enumerate(others):
+        copy = remote_copy(
+            source_of(other), target_ref.at[z], send.at[index], recv.at[index],
+            device(other, *spot),
+        )
+        copy.start()
+        copies.append(copy)
+    return copies
+
+
 def first_kernel(
-    frames_ref, gain_ref, bias_ref, cot_ref, w_ref,
-    rows_out, cot_out, w_out,
-    normed_ref, w_sem, w_send, w_recv, *scratch,
+    frames_ref, gain_ref, bias_ref, cot_ref, w_ref, text_ref, w_text_ref,
+    rows_out, cot_out, w_out, text_all, text_out,
+    normed_ref, part_ref, came_ref, sems, sends, recvs, *scratch,
 ):
     z = lax.axis_index("shard")
     spot = place()[1:]
     others = shard_others()
     enter(neighbours() + [device(other, *spot) for other in others])
-    own = pltpu.make_async_copy(w_ref, w_out.at[z], w_sem)
+    own = pltpu.make_async_copy(w_ref, w_out.at[z], sems.at[0])
     own.start()
-    copies = []
-    for index, other in enumerate(others):
-        copy = remote_copy(
-            w_ref, w_out.at[z], w_send.at[index], w_recv.at[index], device(other, *spot)
-        )
-        copy.start()
-        copies.append(copy)
+    texts = spread(lambda other: text_ref.at[other], text_all, sends.at[0], recvs.at[0], others, spot)
+    copies = spread(lambda other: w_ref, w_out, sends.at[1], recvs.at[1], others, spot)
+    text_all[z] = text_ref[z]
 
     def norm(part, carry):
         normed, _ = normalise(frames_ref[part].astype(F32))
@@ -359,35 +368,62 @@
     chunks(frames_ref.shape[0], norm)
     rows, grads = Gather(normed_ref, rows_out, *scratch[:3]), Gather(cot_ref, cot_out, *scratch[3:])
     rows.start()
+    for copy in texts:
+        copy.wait_recv()
+
+    def share(index, carry):
+        part_ref[index] = nn(text_all[index], w_text_ref[...]).astype(BF)
+        return carry
+
+    lax.fori_loop(0, text_all.shape[0], share, 0)
+    parts = spread(lambda other: part_ref.at[other], came_ref, sends.at[2], recvs.at[2], others, spot)
+    came_ref[z] = part_ref[z]
     rows.relay_y()
     rows.relay_x()
     grads.start()
+    for copy in parts:
+        copy.wait_recv()
+    total = came_ref[0].astype(F32)
+    for index in range(1, came_ref.shape[0]):
+        total += came_ref[index].astype(F32)
+    text_out[...] = total.astype(BF)
     rows.relay_far()
     rows.finish()
     grads.rest()
     own.wait()
     for copy in copies:
-        copy.wait()
-
-
-def first_step(frames, gain, bias, cotangent, w_qkv, shards, ident):
+        copy.wait_recv()
+    for copy in texts + copies + parts:
+        copy.wait_send()
+
+
+def first_step(frames, gain, bias, cotangent, w_qkv, text, w_text, ident):
     rows, width = frames.shape
+    shards, texts, depth = text.shape
     return call(
         first_kernel,
         "first_step",
-        (shape(8, rows, width), shape(8, rows, width), shape(shards, *w_qkv.shape)),
-        (ANY, ANY, ANY),
-        [IN_VMEM, IN_VMEM, IN_VMEM, ANY, ANY],
+        (
+            shape(8, rows, width),
+            shape(8, rows, width),
+            shape(shards, *w_qkv.shape),
+            shape(shards, texts, depth),
+            shape(texts, w_text.shape[1]),
+        ),
+        (ANY, ANY, ANY, IN_VMEM, IN_VMEM),
+        [IN_VMEM, IN_VMEM, IN_VMEM, ANY, ANY, IN_VMEM, IN_VMEM],
         [
             pltpu.VMEM((rows, width), BF),
-            pltpu.SemaphoreType.DMA,
-            pltpu.SemaphoreType.DMA((shards - 1,)),
-            pltpu.SemaphoreType.DMA((shards - 1,)),
+            pltpu.VMEM((shards, texts, w_text.shape[1]), BF),
+            pltpu.VMEM((shards, texts, w_text.shape[1]), BF),
+            pltpu.SemaphoreType.DMA((1,)),
+            pltpu.SemaphoreType.DMA((3, shards - 1)),
+            pltpu.SemaphoreType.DMA((3, shards - 1)),
         ]
         + gather_scratch() * 2,
         ident,
         60,
-    )(frames, gain, bias, cotangent, w_qkv)
+    )(frames, gain, bias, cotangent, w_qkv, text, w_text)
 
 
 def feed_kernel(
@@ -610,11 +646,13 @@
         if clip == 0:
             jobs[0].relay_y()
             jobs[0].relay_x()
-            jobs[1].start()
-    text_job.relay_y()
-    text_job.relay_x()
+            text_job.relay_y()
+            text_job.relay_x()
+    jobs[1].start()
     jobs[0].relay_far()
+    text_job.relay_far()
     jobs[0].finish()
+    text_job.finish()
     keep(0)
     exchange.finish()
 
@@ -628,9 +666,6 @@
         lax.fori_loop(0, blocks, one, 0)
 
     apply(mine_ref, 0)
-    jobs[1].relay_y()
-    jobs[1].relay_x()
-    jobs[2].start()
     nothing = jnp.zeros((1, features), F32)
 
     def first(part, sums):
@@ -642,8 +677,9 @@
         return sums + jnp.sum(branch * branch, axis=0, keepdims=True)
 
     square_one = chunks(both, first, nothing)
-    text_job.relay_far()
-    text_job.finish()
+    jobs[1].relay_y()
+    jobs[1].relay_x()
+    jobs[2].start()
     jobs[1].relay_far()
     jobs[1].finish()
     keep(1)
@@ -653,20 +689,20 @@
         return carry
 
     lax.fori_loop(0, blocks, ask, 0)
-    texts = text_ref.shape[1] // 4
+    texts = text_ref.shape[1] // 2
 
     def cross(block, carry):
         for clip in range(2):
             part = pl.ds(clip * rows, rows)
             keys = pl.ds(clip * texts, texts)
-            values = pl.ds((2 + clip) * texts, texts)
             for head in range(heads):
                 here = pl.ds(head * HEAD_DIM, HEAD_DIM)
                 query = query_ref[block, part, here] * jnp.asarray(HEAD_DIM ** (-0.5), BF)
+                there = pl.ds(width + head * HEAD_DIM, HEAD_DIM)
                 scores = nt(text_ref[block, keys, here], query)
                 probs = jnp.exp(scores - jnp.max(scores, axis=0, keepdims=True))
                 probs = probs / jnp.sum(probs, axis=0, keepdims=True)
-                mix = nn(turn(text_ref[block, values, here]).astype(BF), probs.astype(BF))
+                mix = nn(turn(text_ref[block, keys, there]).astype(BF), probs.astype(BF))
                 cross_ref[block, part, here] = jnp.transpose(mix).astype(BF)
         return carry
 
@@ -736,10 +772,19 @@
     )(rows, w_qkv, side, text, frames, gain, bias)
 
 
+def beside(own_ref, copy, other_ref, out_ref):
+    half = own_ref.shape[1]
+    context = lax.axis_index("context")
+    out_ref[:, pl.ds(pl.multiple_of(context * half, half), half)] = own_ref[...].astype(F32)
+    copy.wait_recv()
+    there = pl.ds(pl.multiple_of((1 - context) * half, half), half)
+    out_ref[:, there] = other_ref[...].astype(F32)
+
+
 def backward_kernel(
-    grad_ref, qkv_ref, mix_ref, log_ref, rows_ref, w_ref, side_ref, text_ref,
-    part_out, w_out, side_out, text_out,
-    out_ref, part_ref, store_sem, grad_all, query_turned, ex_local, ex_send, ex_recv, *scratch,
+    grad_ref, qkv_ref, mix_ref, log_ref, rows_ref, w_ref, side_ref, text_ref, down_ref,
+    part_out, w_out, side_out, text_out, down_out,
+    out_ref, part_ref, store_sem, down_pair, pair_sem, grad_all, query_turned, ex_local, ex_send, ex_recv, *scratch,
 ):
     enter(plane_others())
     exchange = Exchange(grad_ref, grad_all, ex_local, ex_send, ex_recv)
@@ -801,6 +846,10 @@
         if clip == 0:
             text.second()
             side.second()
+            to_x = neighbours()[0]
+            pair = remote_copy(down_ref, down_pair, pair_sem.at[0], pair_sem.at[1], to_x)
+            pair.start()
+
     def store(block):
         return pltpu.make_async_copy(part_ref.at[block], part_out.at[block], store_sem.at[block])
 
@@ -820,15 +869,17 @@
         return carry
 
     lax.fori_loop(0, w_out.shape[0] // tile, weight, 0)
-    text_out[...] = text.total()
+    text_out[...] = text.total().astype(BF)
     side_out[...] = side.total().astype(BF)
     text.finish()
     side.finish()
+    beside(down_ref, pair, down_pair, down_out)
+    pair.wait_send()
     for block in range(blocks):
         store(block).wait()
 
 
-def attend_backward(grad_mix, qkv, mix, logs, rows, weights, side, text, ident):
+def attend_backward(grad_mix, qkv, mix, logs, rows, weights, side, text, down, ident):
     blocks, block, columns = mix.shape
     _, side_rows, width = side.shape
     text_shape = text.shape[1:]
@@ -839,14 +890,17 @@
             shape(blocks, block, width),
             shape(width, 3 * columns),
             shape(side_rows, width),
-            shape(*text_shape, dtype=F32),
+            shape(*text_shape),
+            shape(down.shape[0], 2 * down.shape[1], dtype=F32),
         ),
-        (ANY, IN_VMEM, IN_VMEM, IN_VMEM),
-        [ANY] + [IN_VMEM] * 5 + [ANY, ANY],
+        (ANY, IN_VMEM, IN_VMEM, IN_VMEM, IN_VMEM),
+        [ANY] + [IN_VMEM] * 5 + [ANY, ANY, IN_VMEM],
         [
             pltpu.VMEM((blocks, block, 3 * columns), BF),
             pltpu.VMEM((blocks, block, width), BF),
             pltpu.SemaphoreType.DMA((8,)),
+            pltpu.VMEM(down.shape, BF),
+            pltpu.SemaphoreType.DMA((2,)),
             pltpu.VMEM((blocks, block, columns), BF),
             pltpu.VMEM((HEAD_DIM, blocks * block // 2), F32),
             pltpu.SemaphoreType.DMA((2,)),
@@ -856,8 +910,8 @@
         + LoadedScatter.scratch(side_rows, width)
         + LoadedScatter.scratch(*text_shape),
         ident,
-        45,
-    )(grad_mix, qkv, mix, logs, rows, weights, side, text)
+        1,
+    )(grad_mix, qkv, mix, logs, rows, weights, side, text, down)
 
 
 CHUNK = 64
@@ -891,12 +945,18 @@
 
 def rows_back_kernel(
     normed_ref, cot_ref, one_ref, two_ref, query_ref, mix_ref, text_ref, my_mix_ref,
-    gain_ref, bias_ref, w_ref, branch_ref,
-    grad_ref, layer_ref, stats_ref, grad_mix_ref, out_ref, side_ref, text_out,
+    gain_ref, bias_ref, w_ref, branch_ref, up_ref,
+    grad_ref, layer_ref, stats_ref, grad_mix_ref, out_ref, side_ref, text_out, up_came,
     w_cross, w_query, w_out, low_ref, two_low_ref, back_ref, grad_cm, grad_cq, w_sem,
-    *scratch,
+    up_send, up_recv, *scratch,
 ):
-    enter(neighbours())
+    z = lax.axis_index("shard")
+    spot = place()[1:]
+    others = shard_others()
+    enter(neighbours() + [device(other, *spot) for other in others])
+    up_moves = spread(lambda other: up_ref.at[other], up_came, up_send, up_recv, others, spot)
+    up_own = pltpu.make_async_copy(up_ref.at[z], up_came.at[z], w_sem.at[3])
+    up_own.start()
     cross_job = Scatter(w_cross, *scratch[:5])
     query_job = Scatter(w_query, *scratch[5:10])
     branch_job = LoadedScatter(branch_ref, *scratch[10:])
@@ -935,18 +995,18 @@
     for index in range(4):
         cross_job.pass_core(index)
     half = rows // 2
-    texts = text_ref.shape[1] // 4
+    texts = text_ref.shape[1] // 2
     loads[1].wait()
 
     def cross(block, carry):
         for clip in range(2):
             part = pl.ds(clip * half, half)
             keys = pl.ds(clip * texts, texts)
-            values = pl.ds((2 + clip) * texts, texts)
             for head in range(heads):
                 here = pl.ds(head * HEAD_DIM, HEAD_DIM)
                 query = query_ref[block, part, here] * jnp.asarray(HEAD_DIM ** (-0.5), BF)
-                key, value = text_ref[block, keys, here], text_ref[block, values, here]
+                there = pl.ds(columns + head * HEAD_DIM, HEAD_DIM)
+                key, value = text_ref[block, keys, here], text_ref[block, keys, there]
                 grad = grad_cm[block, part, here]
                 scores = nt(key, query)
                 weights = jnp.exp(scores - jnp.max(scores, axis=0, keepdims=True))
@@ -957,7 +1017,7 @@
                 grad_query = jnp.transpose(nn(turn(key).astype(BF), slopes))
                 grad_cq[block, part, here] = (grad_query * HEAD_DIM ** (-0.5)).astype(BF)
                 text_out[block, keys, here] = nn(slopes, query).astype(BF)
-                text_out[block, values, here] = nn(weights.astype(BF), grad).astype(BF)
+                text_out[block, keys, there] = nn(weights.astype(BF), grad).astype(BF)
         back = nn(grad_cq[block], w_query[block])
         back_ref[...] += back
         w_query[block] = tn(grad_cq[block], two_low_ref[...]).astype(BF)
@@ -1014,10 +1074,13 @@
     branch_job.finish()
     cross_job.finish()
     query_job.finish()
+    up_own.wait()
+    for copy in up_moves:
+        copy.wait()
 
 
 def rows_back(
-    normed, cot, one, two, query, mix, text, my_mix, gain, bias, weights, branch, ident
+    normed, cot, one, two, query, mix, text, my_mix, gain, bias, weights, branch, up, ident
 ):
     rows, width = cot.shape
     blocks, _, columns = my_mix.shape
@@ -1032,9 +1095,10 @@
             shape(blocks, columns, width),
             shape(2, columns, width),
             shape(*text.shape),
+            shape(*up.shape),
         ),
-        (IN_VMEM,) * 7,
-        [IN_VMEM] * 10 + [ANY, ANY],
+        (IN_VMEM,) * 7 + (ANY,),
+        [IN_VMEM] * 10 + [ANY, ANY, ANY],
         [pltpu.VMEM((blocks, columns, width), BF)] * 3
         + [
             pltpu.VMEM((rows, width), BF),
@@ -1042,60 +1106,97 @@
             pltpu.VMEM((rows, width), F32),
             pltpu.VMEM(my_mix.shape, BF),
             pltpu.VMEM(my_mix.shape, BF),
-            pltpu.SemaphoreType.DMA((3,)),
+            pltpu.SemaphoreType.DMA((4,)),
+            pltpu.SemaphoreType.DMA((up.shape[0] - 1,)),
+            pltpu.SemaphoreType.DMA((up.shape[0] - 1,)),
         ]
         + Scatter.scratch(columns, width) * 2
         + LoadedScatter.scratch(rows, width),
         ident,
-        65,
-    )(normed, cot, one, two, query, mix, text, my_mix, gain, bias, weights, branch)
+        60,
+    )(normed, cot, one, two, query, mix, text, my_mix, gain, bias, weights, branch, up)
 
 
 def last_kernel(
-    part_ref, frames_ref, gain_ref, grad_ref, stats_ref, text_ref, qkv_ref, up_ref, down_ref,
-    out_ref, total_ref, text_out, qkv_out, up_out, down_out,
+    part_ref, frames_ref, gain_ref, grad_ref, stats_ref, qkv_ref, up_ref, cross_ref, out_w_ref,
+    text_ref, text_in, w_text_ref,
+    out_ref, total_ref, text_out, qkv_out, up_out, query_out, cross_out, self_out, key_out,
     mine, came, all_ref, st_send, st_recv, z_send, z_recv,
-    qkv_came, qkv_pair, up_pair, down_pair, q_send, q_recv, x_send, x_recv, *scratch,
+    qkv_came, out_came, text_came, text_part, text_mine, text_all,
+    qkv_pair, up_mine, up_pair, cross_pair, out_pair, key_pair, x_send, x_recv, *scratch,
 ):
     z = lax.axis_index("shard")
     shards = lax.axis_size("shard")
-    others = [lax.rem(z + i, shards) for i in range(1, shards)]
+    others = shard_others()
     spot = place()[1:]
     context = spot[0]
     enter(neighbours() + [device(other, *spot) for other in others])
-    size = len(scratch) // 2
-    text = LoadedScatter(text_ref, *scratch[size:])
-    text.start()
+
+    def over(index, source_of, target_ref):
+        return spread(source_of, target_ref, z_send.at[index], z_recv.at[index], others, spot)
+
+    text_moves = over(0, lambda other: text_ref, text_came)
+    qkv_moves = over(1, lambda other: qkv_ref.at[other], qkv_came)
+    out_moves = over(2, lambda other: out_w_ref.at[other], out_came)
+    size = len(scratch) - 5
+    text = Scatter(text_part, *scratch[size:])
     job = LoadedScatter(part_ref, *scratch[:size])
     job.start()
-    sends, moves = [], []
-    for index, other in enumerate(others):
-        copy = remote_copy(
-            qkv_ref.at[other], qkv_came.at[index], q_send.at[index], q_recv.at[index],
-            device(other, *spot),
-        )
-        copy.start()
-        moves.append(copy)
     inputs = frames_ref[...].astype(F32)
     average = jnp.mean(inputs, axis=-1, keepdims=True)
     centred = inputs - average
     rate = lax.rsqrt(jnp.mean(centred * centred, axis=-1, keepdims=True) + EPS)
-    text.first()
+    total = up_ref[0].astype(F32)
+    for index in range(1, shards):
+        total += up_ref[index].astype(F32)
+    up_mine[...] = total.astype(BF)
+    text_came[z] = text_ref[...]
+    for copy in text_moves:
+        copy.wait_recv()
     job.first()
-    text.second()
+    texts = text_ref.shape[0] // 2
+    own = texts // 8
+
+    def text_back(index, carry):
+        grads = nt(text_came[index], w_text_ref[...])
+        rows = pl.ds(pl.multiple_of(index * 2 * own, 2 * own), 2 * own)
+        for block in range(8):
+            pair = [grads[k * texts + block * own : k * texts + block * own + own] for k in range(2)]
+            text_part[block, rows] = jnp.concatenate(pair, axis=0).astype(BF)
+        return carry
+
+    lax.fori_loop(0, shards, text_back, 0)
+    for index in range(4):
+        text.pass_core(index)
+    key_grad = tn(text_in[0], text_came[0])
+    for index in range(1, shards):
+        key_grad += tn(text_in[index], text_came[index])
+    key_pair[0] = key_grad.astype(BF)
+    text.far()
+    text.near()
     job.second()
     to_x = neighbours()[0]
-    pairs = []
-    for index, (source, pair_ref) in enumerate(((up_ref, up_pair), (down_ref, down_pair))):
-        copy = remote_copy(source, pair_ref, x_send.at[index], x_recv.at[index], to_x)
+
+    def swap(index, source, target_ref):
+        copy = remote_copy(source, target_ref, x_send.at[index], x_recv.at[index], to_x)
         copy.start()
-        pairs.append(copy)
-    text_out[...] = text.total()
+        return copy
+
+    text.second()
+    pairs = [swap(0, up_mine, up_pair), swap(1, cross_ref, cross_pair)]
+    pairs.append(swap(2, key_pair.at[0], key_pair.at[1]))
+    text.wait()
+    for index in range(shards):
+        rows = slice(index * 2 * own, (index + 1) * 2 * own)
+        text_mine[index] = text.value(rows).astype(BF)
+    text_moves += over(3, lambda other: text_mine.at[other], text_all)
+    text_all[z] = text_mine[z]
     grads = job.total()
     normed = centred * rate
     mine[0] = stats_ref[...]
     mine[0, 0:1] = jnp.sum(grads * normed, axis=0, keepdims=True)
     mine[0, 1:2] = jnp.sum(grads, axis=0, keepdims=True)
+    sends = []
     for index, target in enumerate(reversed(neighbours())):
         copy = remote_copy(
             mine.at[index], came.at[index], st_send.at[index], st_recv.at[index], target
@@ -1109,90 +1210,115 @@
             out_ref[...] = grad_ref[...] + rate * scaled
         copy.wait_recv()
         mine[index + 1] = mine[index] + came[index]
-    for index, other in enumerate(others):
-        copy = remote_copy(
-            mine.at[3], all_ref.at[z], z_send.at[index], z_recv.at[index], device(other, *spot)
-        )
-        copy.start()
-        sends.append(copy)
+    stat_moves = over(4, lambda other: mine.at[3], all_ref)
     all_ref[z] = mine[3]
-    total = qkv_ref[z].astype(F32)
-    for index, copy in enumerate(moves):
+
+    def collect(moves, source_ref, came_ref):
+        came_ref[z] = source_ref[z]
+        for copy in moves:
+            copy.wait_recv()
+        total = came_ref[0].astype(F32)
+        for index in range(1, shards):
+            total += came_ref[index].astype(F32)
+        return total.astype(BF)
+
+    qkv_pair[0] = collect(qkv_moves, qkv_ref, qkv_came)
+    pairs.append(swap(3, qkv_pair.at[0], qkv_pair.at[1]))
+    out_pair[0] = collect(out_moves, out_w_ref, out_came)
+    pairs.append(swap(4, out_pair.at[0], out_pair.at[1]))
+    for copy in text_moves[shards - 1 :] + stat_moves:
         copy.wait_recv()
-        total += qkv_came[index].astype(F32)
-    qkv_pair[0] = total.astype(BF)
-    copy = remote_copy(qkv_pair.at[0], qkv_pair.at[1], x_send.at[2], x_recv.at[2], to_x)
-    copy.start()
-    pairs.append(copy)
-    for copy in sends[3:]:
-        copy.wait_recv()
+    text_out[...] = text_all[...].astype(F32)
     total = all_ref[0]
     for index in range(1, shards):
         total += all_ref[index]
     total_ref[...] = total
-    half = up_ref.shape[1]
-    ours = pl.ds(pl.multiple_of(context * half, half), half)
-    theirs = pl.ds(pl.multiple_of((1 - context) * half, half), half)
-    for copy, source, pair_ref, target in (
-        (pairs[0], up_ref, up_pair, up_out),
-        (pairs[1], down_ref, down_pair, down_out),
-    ):
-        target[:, ours] = source[...].astype(F32)
-        copy.wait_recv()
-        target[:, theirs] = pair_ref[...].astype(F32)
+    beside(up_mine, pairs[0], up_pair, up_out)
+
+    def ordered(first, second):
+        first, second = first.astype(F32), second.astype(F32)
+        return jnp.where(context == 0, first, second), jnp.where(context == 0, second, first)
+
+    pairs[1].wait_recv()
+    lead, trail = ordered(cross_ref[...], cross_pair[...])
+    width = lead.shape[0] // 2
+    query_out[:, :width] = jnp.transpose(lead[:width])
+    query_out[:, width:] = jnp.transpose(trail[:width])
+    cross_out[:, :width] = jnp.transpose(lead[width:])
+    cross_out[:, width:] = jnp.transpose(trail[width:])
     pairs[2].wait_recv()
-    lead = jnp.where(context == 0, qkv_pair[0], qkv_pair[1]).astype(F32)
-    trail = jnp.where(context == 0, qkv_pair[1], qkv_pair[0]).astype(F32)
-    width = lead.shape[1] // 3
+    lead, trail = ordered(key_pair[0], key_pair[1])
+    for index in range(2):
+        lanes = slice(index * width, (index + 1) * width)
+        key_out[index, :, :width] = lead[:, lanes]
+        key_out[index, :, width:] = trail[:, lanes]
+    pairs[3].wait_recv()
+    lead, trail = ordered(qkv_pair[0], qkv_pair[1])
     for index in range(3):
         lanes = slice(index * width, (index + 1) * width)
         qkv_out[index, :, :width] = lead[:, lanes]
         qkv_out[index, :, width:] = trail[:, lanes]
-    for copy in sends + moves + pairs:
+    pairs[4].wait_recv()
+    lead, trail = ordered(out_pair[0], out_pair[1])
+    self_out[:, :width] = jnp.transpose(lead)
+    self_out[:, width:] = jnp.transpose(trail)
+    for copy in sends + text_moves + qkv_moves + out_moves + stat_moves + pairs:
         copy.wait_send()
     text.finish()
     job.finish()
 
 
-def last_step(part, frames, gain, grad, stats, text, qkv, up, down, shards, ident):
+def last_step(part, frames, gain, grad, stats, qkv, up, cross, out, text, text_in, w_text, ident):
     _, rows, width = part.shape
-    depth, half = up.shape
-    columns = qkv.shape[2]
+    shards, texts, depth = text_in.shape
+    half = up.shape[2]
+    columns = out.shape[1]
+    own = texts // 8
+    square = shape(depth, 2 * columns, dtype=F32)
     return call(
         last_kernel,
         "last_step",
         (
             shape(rows, width, dtype=F32),
             shape(16, width, dtype=F32),
-            shape(*text.shape[1:], dtype=F32),
-            shape(3, depth, 2 * columns // 3, dtype=F32),
+            shape(shards, own, depth, dtype=F32),
+            shape(3, depth, 2 * columns, dtype=F32),
             shape(depth, 2 * half, dtype=F32),
-            shape(depth, 2 * half, dtype=F32),
+            square,
+            square,
+            square,
+            shape(2, depth, 2 * columns, dtype=F32),
         ),
-        (IN_VMEM,) * 6,
-        [ANY] + [IN_VMEM] * 4 + [ANY] + [IN_VMEM] * 3,
+        (IN_VMEM,) * 9,
+        [ANY] + [IN_VMEM] * 11,
         [
             pltpu.VMEM((4, 16, width), F32),
             pltpu.VMEM((3, 16, width), F32),
             pltpu.VMEM((shards, 16, width), F32),
             pltpu.SemaphoreType.DMA((3,)),
             pltpu.SemaphoreType.DMA((3,)),
-            pltpu.SemaphoreType.DMA((shards - 1,)),
-            pltpu.SemaphoreType.DMA((shards - 1,)),
-            pltpu.VMEM((shards - 1, depth, columns), BF),
-            pltpu.VMEM((2, depth, columns), BF),
+            pltpu.SemaphoreType.DMA((5, shards - 1)),
+            pltpu.SemaphoreType.DMA((5, shards - 1)),
+            pltpu.VMEM((shards, depth, 3 * columns), BF),
+            pltpu.VMEM((shards, columns, depth), BF),
+            pltpu.VMEM((shards, texts, 2 * columns), BF),
+            pltpu.VMEM((8, shards * own, depth), BF),
+            pltpu.VMEM((shards, own, depth), BF),
+            pltpu.VMEM((shards, own, depth), BF),
+            pltpu.VMEM((2, depth, 3 * columns), BF),
             pltpu.VMEM((depth, half), BF),
             pltpu.VMEM((depth, half), BF),
-            pltpu.SemaphoreType.DMA((shards - 1,)),
-            pltpu.SemaphoreType.DMA((shards - 1,)),
-            pltpu.SemaphoreType.DMA((3,)),
-            pltpu.SemaphoreType.DMA((3,)),
+            pltpu.VMEM((2 * columns, depth), BF),
+            pltpu.VMEM((2, columns, depth), BF),
+            pltpu.VMEM((2, depth, 2 * columns), BF),
+            pltpu.SemaphoreType.DMA((5,)),
+            pltpu.SemaphoreType.DMA((5,)),
         ]
         + LoadedScatter.scratch(rows, width)
-        + LoadedScatter.scratch(*text.shape[1:]),
+        + Scatter.scratch(shards * own, depth),
         ident,
         65,
-    )(part, frames, gain, grad, stats, text, qkv, up, down)
+    )(part, frames, gain, grad, stats, qkv, up, cross, out, text, text_in, w_text)
 
 
 def dots(spec, *operands):
@@ -1238,23 +1364,23 @@
     cross_part = half(cross_qkv)
     side = jnp.concatenate([half(self_out), cross_part[0], half(cross_out)], axis=1)
     w_side = over_shard(side.transpose(1, 0), tiled=False)
-    w_text = over_shard(jnp.concatenate([cross_part[1], cross_part[2]], axis=1))
+    w_text = jnp.concatenate([cross_part[1], cross_part[2]], axis=1)
+    text_slices = text_states.reshape(clips * texts, slices, depth).transpose(1, 0, 2)
     w_down = over_shard(half(mlp_down))
     w_up = over_shard(half(mlp_up))
 
     qkv_part = half(self_qkv)
-    all_one, all_grad, w_qkv = first_step(
+    all_one, all_grad, w_qkv, text_in, text_part = first_step(
         frames.reshape(block, width),
         norm_gain,
         norm_bias,
         cotangent.reshape(block, width),
         jnp.concatenate([qkv_part[0], qkv_part[1], qkv_part[2]], axis=-1),
-        slices,
+        text_slices,
+        w_text,
         0,
     )
     w_qkv = w_qkv.reshape(width, 3 * columns)
-    text_part = dots("cnd,de->cne", text_states, w_text).astype(BF)
-    text_part = text_part.reshape(clips * texts, 2, columns).transpose(1, 0, 2)
     (
         qkv, self_log, mix, my_mix, stream_one, stream_two, cross_q, cross_mix, norm_three,
         text_all, squares, plane_w,
@@ -1262,7 +1388,7 @@
         all_one,
         w_qkv,
         w_side,
-        text_part.reshape(2 * clips * texts, columns),
+        text_part,
         frames.reshape(block, width),
         norm_gain,
         norm_bias,
@@ -1276,8 +1402,8 @@
     def to_shard(part):
         return lax.psum_scatter(part.astype(BF), "shard", scatter_dimension=0, tiled=True)
 
-    grad_down, grad_up = to_shard(grad_down), to_shard(grad_up)
-    grad_one, layer_out, stats, grad_mix, part_out, side, text_grads = rows_back(
+    grad_down = to_shard(grad_down)
+    grad_one, layer_out, stats, grad_mix, part_out, side, text_grads, grad_up = rows_back(
         grad_normed,
         cotangent.reshape(block, width),
         stream_one,
@@ -1290,51 +1416,38 @@
         norm_bias,
         plane_w,
         part_three,
+        grad_up.reshape(slices, depth, -1),
         3,
     )
 
     def slice_shards(part):
         return part.reshape(-1, slices, depth).transpose(1, 0, 2)
 
-    grad_cross = to_shard(slice_shards(side))
-    part_norm, grad_w_qkv, grad_out, text_grads = attend_backward(
-        grad_mix, qkv, mix, self_log, all_one, w_qkv, part_out, text_grads, 8
+    grad_cross = to_shard(slice_shards(side))[0]
+    part_norm, grad_w_qkv, grad_out, text_grads, grad_down = attend_backward(
+        grad_mix, qkv, mix, self_log, all_one, w_qkv, part_out, text_grads, grad_down, 8
     )
     (
-        part_norm, grad_w_qkv, grad_out, text_grads, grad_down, grad_up, grad_cross
-    ) = lax.optimization_barrier(
-        (part_norm, grad_w_qkv, grad_out, text_grads, grad_down, grad_up, grad_cross)
-    )
-    text_grads = text_grads.reshape(2, clips, texts, columns).astype(BF)
-    text_grads = text_grads.transpose(1, 2, 0, 3).reshape(clips, texts, 2 * columns)
-    grad_w_text = to_shard(dots("cnd,cne->de", text_states, text_grads))
-    grad_out = to_shard(slice_shards(grad_out))
-    grad_text = dots("cne,de->cnd", text_grads, w_text)
-    grad_text = grad_text.reshape(clips, 8, texts // 8, width).transpose(1, 0, 2, 3).astype(BF)
-    grad_text = grad_text.reshape(8, clips * texts // 8, width)
-    grad_frames, totals, grad_text, grad_w_qkv, grad_up, grad_down = last_step(
+        grad_frames, totals, grad_text, grad_w_qkv, grad_up, grad_query, grad_cross, grad_out,
+        grad_keys,
+    ) = last_step(
         part_norm,
         frames.reshape(block, width),
         norm_gain[0][None],
         grad_one,
         jnp.concatenate([stats, squares], axis=0),
-        grad_text,
         grad_w_qkv.reshape(slices, depth, 3 * columns),
         grad_up,
-        grad_down,
-        slices,
+        grad_cross,
+        slice_shards(grad_out),
+        text_grads,
+        text_in,
+        w_text,
         11,
     )
     grad_frames = grad_frames.reshape(clips, rows, width)
-    grad_text = grad_text.reshape(clips, texts // 8, width)
-
-    grad_cross, grad_out, grad_w_text, totals = lax.optimization_barrier(
-        (grad_cross, grad_out, grad_w_text, totals)
-    )
-    grad_text_pair = [grad_w_text[None, :, k * columns : (k + 1) * columns] for k in range(2)]
-    grad_side = jnp.concatenate([grad_cross, grad_out], axis=1).reshape(3, columns, depth)
-    grad_side = jnp.concatenate([grad_side.transpose(0, 2, 1)] + grad_text_pair, axis=0)
-    grad_side = lax.all_gather(grad_side, "context", axis=2, tiled=True).astype(F32)
+    grad_text = grad_text.transpose(1, 0, 2).reshape(clips, texts // 8, width)
+
     gains = jnp.stack([totals[0], totals[2], totals[4]])
     shifts = jnp.stack([totals[1], totals[3], totals[5]])
     squares = jnp.stack([totals[j].sum() for j in (6, 8, 9, 7)])
@@ -1349,9 +1462,9 @@
         grad_gain,
         grad_shift,
         grad_w_qkv,
-        grad_side[2],
-        jnp.stack([grad_side[0], grad_side[3], grad_side[4]]),
-        grad_side[1],
+        grad_out,
+        jnp.concatenate([grad_query[None], grad_keys]),
+        grad_cross,
         grad_up,
         grad_down,
         jnp.sqrt(squares / entries),

time: 653 us -> 616 us (0.943)
  the two profiles are of different devices: /device:TPU:0 before, /device:TPU:8 now
where the time goes in v7:
time: 616 us; the launch traced here: 605 us
  Pallas kernels  552 us (90%)
  local copies, waits for them, and re-layouts  26.6 us (4%)
  between operations  14.3 us (2%)
  other arithmetic  11.9 us (2%)
    pallas_call x1, Pallas kernels, first_step(): call(first_kernel, 'first_step', (shape(8, rows, width), shape(8, rows, w...  119 us
    pallas_call x1, Pallas kernels, last_step(): call(last_kernel, 'last_step', (shape(rows, width, dtype=F32), shape(16,...  110 us
    pallas_call x1, Pallas kernels, rows_back(): call(rows_back_kernel, 'rows_back', (shape(rows, width, dtype=F32), shape...  102 us
    pallas_call x1, Pallas kernels, attend_forward(): call(forward_kernel, 'attend_forward', (shape(blocks, block, 3 * columns)...  93.1 us
    pallas_call x1, Pallas kernels, feed_forward(): call(feed_kernel, 'feed_forward', outs, (IN_VMEM, ANY, IN_VMEM, IN_VMEM),...  70.3 us
    pallas_call x1, Pallas kernels, attend_backward(): call(backward_kernel, 'attend_backward', (shape(blocks, block, width), sh...  58 us
  transfers between devices with their start and end apart: 5, of which 0 were waited for; matrix products, arithmetic and copies ran while one was open for 2% of the time, Pallas kernels for 61%

profile of v7, /device:TPU:8, one launch (start us, length us, event | category | flops | bytes accessed | tf_op | source)
XLA Modules:
  0.0 605.5 jit_solution(10555720797658085141)
XLA Ops:
  7.2 0.0 all-gather.9.cloned.1.call-start
  7.2 1.3 constant_dynamic-slice_fusion.2
  8.6 1.9 dynamic-slice_bitcast_fusion
  10.5 0.2 maximum_bitcast_fusion
  10.7 1.0 copy.30
  11.6 0.0 all-gather.9.cloned.1.call-update
  11.7 0.0 all-gather.5.cloned.1.call-start
  11.7 0.9 constant_dynamic-slice_fusion.1
  12.6 0.0 all-gather.7.cloned.1.call-start
  12.7 1.9 constant_dynamic-slice_fusion
  14.6 0.0 reduce-scatter.3.cloned.1.call-start
  14.7 0.1 reshape.62
  14.8 0.8 copy.40
  15.6 0.8 pad_maximum_fusion.2.w_text_ref
  16.4 0.9 pad_maximum_fusion.1.w_ref
  17.3 119.0 %first_step.1 = (bf16[8,256,1536]{2,1,0:T(8,128)(2,1)}, bf16[8,256,1536]{2,1,0:T(8,128)(2,1)}, bf16[4,384,576]{2,1,0:T(8,128)(2,1)}, bf16[4,128,384]{2,1,0:T(8,128)(2,1)}, bf16[128,384]{1,0:T(8,128)(2,1)}) custom-call(bf16[256,1536]{1,0:T(8,128)(2,1)} %bitcast.56, f32[3,1536]{1,0:T(4,128)} %gain_ref.5, f32[3,1536]{1,0:T(4,128)} %bias_ref.5, ...), custom_call_target="tpu_custom_call" | custom-call | flops 60000002048 | bytes 60000000 | tf_op jit(solution)/shard_map/first_step/pallas_call | solution.py:403
  136.4 0.0 all-gather.9.cloned.1.call-done
  136.4 93.1 %attend_forward.1 = (bf16[8,256,576]{2,1,0:T(8,128)(2,1)}, f32[6,1024]{1,0:T(8,128)}, bf16[8,256,192]{2,1,0:T(8,128)(2,1)}, bf16[8,256,192]{2,1,0:T(8,128)(2,1)}...) custom-call(bf16[8,256,1536]{2,1,0:T(8,128)(2,1)} %get-tuple-element, ...), custom_call_target="tpu_custom_call" | custom-call | flops 80000000000 | bytes 80000000 | tf_op jit(solution)/shard_map/attend_forward/pallas_call | solution.py:740
  229.5 0.0 all-gather.5.cloned.1.call-done.up_ref
  229.5 0.0 all-gather.7.cloned.1.call-done.down_ref
  229.5 70.3 %feed_forward.1 = (f32[256,1536]{1,0:T(8,128)}, bf16[8,256,1536]{2,1,0:T(8,128)(2,1)}, bf16[1536,768]{1,0:T(8,128)(2,1)}, bf16[1536,768]{1,0:T(8,128)(2,1)}) custom-call(bf16[256,1536]{1,0:T(8,128)(2,1)} %get-tuple-element.58.own_ref, bf16[8,256,1536]{2,1,0:T(8,128)(2,1)} %get-tuple-element.59.grad_ref, ...), custom_call_target="tpu_custom_call" | custom-call | flops 70000001024 | bytes 70000000 | tf_op jit(solution)/shard_map/feed_forward/pallas_call | solution.py:544
  299.9 0.0 reduce-scatter.3.cloned.1.call-update
  299.9 0.0 reduce-scatter.5.cloned.1.call-start
  300.0 101.9 %rows_back.1 = (f32[256,1536]{1,0:T(8,128)}, bf16[256,1536]{1,0:T(8,128)(2,1)}, f32[8,1536]{1,0:T(8,128)}, bf16[8,256,192]{2,1,0:T(8,128)(2,1)}, bf16[8,192,1536...) custom-call(f32[256,1536]{1,0:T(8,128)} %get-tuple-element.60.normed, ...), custom_call_target="tpu_custom_call" | custom-call | flops 60000002048 | bytes 60000000 | tf_op jit(solution)/shard_map/rows_back/pallas_call | solution.py:1087
  401.8 2.7 reshape.67
  404.6 1.2 copy.38
  405.7 1.3 slice.57.gain_ref
  407.1 0.6 pad_maximum_fusion.3.stats_ref
  407.7 58.0 %attend_backward.1 = (bf16[8,256,1536]{2,1,0:T(8,128)(2,1)}, bf16[1536,576]{1,0:T(8,128)(2,1)}, bf16[192,1536]{1,0:T(8,128)(2,1)}, bf16[128,384]{1,0:T(8,128)(2,1)}, f32[384,1536]{1,0:T(8,128)}) custom-call(bf16[8,256,192]{2,1,0:T(8,128)(2,1)} %get-tuple-element.71.grad_ref, bf16[8,256,576]{2,1,0:T(8,128)(2,1)} %get-tuple-element.72.qkv_ref, ...), custom_call_target="tpu_custom_call" | custom-call | flops 1000000000 | bytes 1000000 | tf_op jit(solution)/shard_map/attend_backward/pallas_call | solution.py:886
  465.7 1.9 copy.39
  467.7 110.0 %last_step.1 = (f32[256,1536]{1,0:T(8,128)}, f32[16,1536]{1,0:T(8,128)}, f32[4,16,384]{2,1,0:T(8,128)}, f32[3,384,384]{2,1,0:T(8,128)}, f32[384,1536]{1,0:T(8,12...) custom-call(bf16[8,256,1536]{2,1,0:T(8,128)(2,1)} %get-tuple-element.78.part_ref, ...), custom_call_target="tpu_custom_call" | custom-call | flops 65000001536 | bytes 65000000 | tf_op jit(solution)/shard_map/last_step/pallas_call | solution.py:1278
  577.6 1.9 slice_reduce_fusion.3
  579.6 0.9 copy.33
  580.5 0.7 reshape.70
  581.2 2.9 pad_maximum_fusion
  584.1 0.7 fusion.1
  584.8 0.7 fusion.3
  585.4 3.2 fusion.4
  588.6 0.9 copy.48
  589.5 1.1 copy.49
  590.7 0.9 copy-done.4
  591.6 1.2 copy.50
  592.8 0.2 copy-done.8
  593.0 0.8 copy.51
  593.8 0.8 copy.52
  594.6 1.4 copy.53
  596.0 1.1 copy-done.2
  597.2 1.4 copy.54
  (26 shorter events, 0.1 us)
Async XLA Ops:
  7.2 4.5 copy-start
  7.2 129.2 %all-gather.9.cloned.1.call-start = ((), (), s32[]{:S(2)}) async-start(), calls=%async_computation.6 | async-start | bytes 2211840 | tf_op jit(solution)/shard_map/all_gather | solution.py:1362
  11.7 217.8 %all-gather.5.cloned.1.call-start = ((), (), s32[]{:S(2)}) async-start(), calls=%async_computation.2 | async-start | bytes 2949120 | tf_op jit(solution)/shard_map/all_gather | solution.py:1362
  11.7 2.9 copy-start.9
  12.6 216.9 %all-gather.7.cloned.1.call-start = ((), (), s32[]{:S(2)}) async-start(), calls=%async_computation.3 | async-start | bytes 2949120 | tf_op jit(solution)/shard_map/all_gather | solution.py:1362
  14.6 393.1 %reduce-scatter.3.cloned.1.call-start = ((), (), s32[]{:S(2)}) async-start(), calls=%async_computation.4 | async-start | bytes 2949120 | tf_op jit(solution)/shard_map/reduce_scatter | solution.py:1403
  299.9 167.8 %reduce-scatter.5.cloned.1.call-start = ((), (), s32[]{:S(2)}) async-start(), calls=%async_computation.5 | async-start | bytes 1474560 | tf_op jit(solution)/shard_map/reduce_scatter | solution.py:1403
  404.5 2.5 copy-start.10
  404.5 2.5 copy-start.11
  581.2 7.4 %copy-start.6 = (bf16[256,1536]{1,0:T(8,128)(2,1)S(1)}, bf16[256,1536]{1,0:T(8,128)(2,1)}, u32[]{:S(2)}) copy-start(bf16[256,1536]{1,0:T(8,128)(2,1)} %get-tuple-element.70) | copy-start | bytes 2359300
  581.2 8.3 %copy-start.5 = (f32[256,1536]{1,0:T(8,128)S(1)}, f32[256,1536]{1,0:T(8,128)}, u32[]{:S(2)}) copy-start(f32[256,1536]{1,0:T(8,128)} %get-tuple-element.88) | copy-start | bytes 4718596
  589.5 2.0 copy-start.4
  591.6 1.4 copy-start.8
  591.6 2.3 copy-start.7
  591.6 3.1 copy-start.3
  594.6 2.5 copy-start.2
  594.6 3.9 copy-start.1
Sparse Core Ops, SparseCore 0:
  11.8 78.1 all-gather.8
  92.2 54.6 all-gather.4
  149.0 51.1 all-gather.6
  300.0 95.9 reduce-scatter.2
  405.9 27.0 reduce-scatter.4

commit v8 on v7

--- a/solution.py
+++ b/solution.py
@@ -346,18 +346,15 @@
 
 
 def first_kernel(
-    frames_ref, gain_ref, bias_ref, cot_ref, w_ref, text_ref, w_text_ref,
-    rows_out, cot_out, w_out, text_all, text_out,
-    normed_ref, part_ref, came_ref, sems, sends, recvs, *scratch,
+    frames_ref, gain_ref, bias_ref, cot_ref, text_ref, w_text_ref,
+    rows_out, cot_out, text_all, text_out,
+    normed_ref, part_ref, came_ref, sends, recvs, *scratch,
 ):
     z = lax.axis_index("shard")
     spot = place()[1:]
     others = shard_others()
     enter(neighbours() + [device(other, *spot) for other in others])
-    own = pltpu.make_async_copy(w_ref, w_out.at[z], sems.at[0])
-    own.start()
     texts = spread(lambda other: text_ref.at[other], text_all, sends.at[0], recvs.at[0], others, spot)
-    copies = spread(lambda other: w_ref, w_out, sends.at[1], recvs.at[1], others, spot)
     text_all[z] = text_ref[z]
 
     def norm(part, carry):
@@ -376,28 +373,25 @@
         return carry
 
     lax.fori_loop(0, text_all.shape[0], share, 0)
-    parts = spread(lambda other: part_ref.at[other], came_ref, sends.at[2], recvs.at[2], others, spot)
+    parts = spread(lambda other: part_ref.at[other], came_ref, sends.at[1], recvs.at[1], others, spot)
     came_ref[z] = part_ref[z]
     rows.relay_y()
     rows.relay_x()
     grads.start()
+    rows.relay_far()
+    rows.finish()
+    grads.rest()
     for copy in parts:
         copy.wait_recv()
     total = came_ref[0].astype(F32)
     for index in range(1, came_ref.shape[0]):
         total += came_ref[index].astype(F32)
     text_out[...] = total.astype(BF)
-    rows.relay_far()
-    rows.finish()
-    grads.rest()
-    own.wait()
-    for copy in copies:
-        copy.wait_recv()
-    for copy in texts + copies + parts:
+    for copy in texts + parts:
         copy.wait_send()
 
 
-def first_step(frames, gain, bias, cotangent, w_qkv, text, w_text, ident):
+def first_step(frames, gain, bias, cotangent, text, w_text, ident):
     rows, width = frames.shape
     shards, texts, depth = text.shape
     return call(
@@ -406,28 +400,26 @@
         (
             shape(8, rows, width),
             shape(8, rows, width),
-            shape(shards, *w_qkv.shape),
             shape(shards, texts, depth),
             shape(texts, w_text.shape[1]),
         ),
-        (ANY, ANY, ANY, IN_VMEM, IN_VMEM),
-        [IN_VMEM, IN_VMEM, IN_VMEM, ANY, ANY, IN_VMEM, IN_VMEM],
+        (ANY, ANY, IN_VMEM, IN_VMEM),
+        [IN_VMEM, IN_VMEM, IN_VMEM, ANY, IN_VMEM, IN_VMEM],
         [
             pltpu.VMEM((rows, width), BF),
             pltpu.VMEM((shards, texts, w_text.shape[1]), BF),
             pltpu.VMEM((shards, texts, w_text.shape[1]), BF),
-            pltpu.SemaphoreType.DMA((1,)),
-            pltpu.SemaphoreType.DMA((3, shards - 1)),
-            pltpu.SemaphoreType.DMA((3, shards - 1)),
+            pltpu.SemaphoreType.DMA((2, shards - 1)),
+            pltpu.SemaphoreType.DMA((2, shards - 1)),
         ]
         + gather_scratch() * 2,
         ident,
         60,
-    )(frames, gain, bias, cotangent, w_qkv, text, w_text)
+    )(frames, gain, bias, cotangent, text, w_text)
 
 
 def feed_kernel(
-    own_ref, grad_ref, up_ref, down_ref,
+    own_ref, grad_ref, w_ref,
     normed_out, branch_out, up_out, down_out,
     rows_ref, grads_ref, hidden_ref, slope_ref, part_a, part_b,
     load_sem, store_sem, g_local, g_send, g_recv, *scratch,
@@ -435,6 +427,8 @@
     enter(neighbours())
     gather = Gather(own_ref, rows_ref, g_local, g_send, g_recv)
     gather.start()
+    hidden = hidden_ref.shape[2]
+    up_ref, down_ref = w_ref.at[:, pl.ds(0, hidden)], w_ref.at[:, pl.ds(hidden, hidden)]
     blocks, _, width = rows_ref.shape
     loads = []
     for block in range(blocks):
@@ -522,9 +516,9 @@
         store(block).wait()
 
 
-def feed_forward(own, grads, w_up, w_down, ident):
+def feed_forward(own, grads, weights, ident):
     rows, width = own.shape
-    hidden = w_up.shape[1]
+    hidden = weights.shape[1] // 2
     outs = (
         shape(rows, width, dtype=F32),
         shape(8, rows, width),
@@ -546,11 +540,11 @@
         "feed_forward",
         outs,
         (IN_VMEM, ANY, IN_VMEM, IN_VMEM),
-        [ANY, ANY, IN_VMEM, IN_VMEM],
+        [ANY, ANY, IN_VMEM],
         scratch + gather_scratch() + Scatter.scratch(rows, width),
         ident,
         70,
-    )(own, grads, w_up, w_down)
+    )(own, grads, weights)
 
 
 SIDE = 256
@@ -579,7 +573,7 @@
 
 
 def forward_kernel(
-    rows_ref, w_ref, side_ref, text_in, frames_ref, gain_ref, bias_ref,
+    rows_ref, side_ref, text_in, frames_ref, gain_ref, bias_ref,
     qkv_ref, log_ref, mix_ref, mine_ref, one_ref, two_ref, query_ref, cross_ref, low_ref,
     text_ref, square_ref, plane_out,
     w_own, w_out, w_query, w_cross, sum_ref, two_low_ref, store_sem,
@@ -593,12 +587,12 @@
     heads = width // HEAD_DIM
     length = blocks * rows
     step = SIDE // rows
-    depth = side_ref.shape[2]
-    for index in range(side_ref.shape[0]):
-        lanes = slice(index * depth, (index + 1) * depth)
-        for kind in range(3):
-            w_own[kind, :, lanes] = side_ref[index, kind * width : (kind + 1) * width]
     weights = (w_out, w_query, w_cross)
+
+    def turn_own(kind):
+        w_own[kind] = turn(side_ref[:, (3 + kind) * width : (4 + kind) * width]).astype(BF)
+
+    turn_own(0)
     jobs = [Gather(w_own.at[k], weights[k], *scratch[3 * k : 3 * k + 3]) for k in range(3)]
     text_job = Gather(text_in, text_ref, *scratch[9:])
     text_job.start()
@@ -611,10 +605,12 @@
         stores.append(copy)
 
     def project(block, carry):
-        qkv_ref[block] = nn(rows_ref[block], w_ref[...]).astype(BF)
+        qkv_ref[block] = nn(rows_ref[block], side_ref[:, : 3 * width]).astype(BF)
         return carry
 
     lax.fori_loop(0, blocks, project, 0)
+    turn_own(1)
+    turn_own(2)
     exchange = Exchange(mix_ref, mine_ref, ex_local, ex_send, ex_recv)
     for clip in range(2):
         part = pl.ds(clip * rows, rows)
@@ -731,9 +727,9 @@
         copy.wait()
 
 
-def attend_forward(rows, w_qkv, side, text, frames, gain, bias, ident):
+def attend_forward(rows, side, text, frames, gain, bias, ident):
     blocks, block, width = rows.shape
-    columns = w_qkv.shape[1] // 3
+    columns = side.shape[1] // 6
     heads = columns // HEAD_DIM
     heads_shape = shape(blocks, block, columns)
     stream = shape(block, width, dtype=F32)
@@ -755,13 +751,13 @@
             shape(3, blocks, columns, width),
         ),
         (IN_VMEM,) * 11 + (ANY,),
-        [IN_VMEM] * 3 + [ANY] + [IN_VMEM] * 3,
+        [IN_VMEM] * 2 + [ANY] + [IN_VMEM] * 3,
         [pltpu.VMEM((3, columns, width), BF)]
         + [pltpu.VMEM((blocks, columns, width), BF)] * 3
         + [
             pltpu.VMEM((block, width), F32),
             pltpu.VMEM((block, width), BF),
-            pltpu.SemaphoreType.DMA((3,)),
+            pltpu.SemaphoreType.DMA((4,)),
             pltpu.SemaphoreType.DMA((2,)),
             pltpu.SemaphoreType.DMA((2, 7)),
             pltpu.SemaphoreType.DMA((2, 7)),
@@ -769,24 +765,27 @@
         + gather_scratch() * 4,
         ident,
         80,
-    )(rows, w_qkv, side, text, frames, gain, bias)
+    )(rows, side, text, frames, gain, bias)
 
 
 def beside(own_ref, copy, other_ref, out_ref):
     half = own_ref.shape[1]
     context = lax.axis_index("context")
-    out_ref[:, pl.ds(pl.multiple_of(context * half, half), half)] = own_ref[...].astype(F32)
+    out_ref[:, pl.ds(pl.multiple_of(context * half, half), half)] = own_ref[...]
     copy.wait_recv()
     there = pl.ds(pl.multiple_of((1 - context) * half, half), half)
-    out_ref[:, there] = other_ref[...].astype(F32)
+    out_ref[:, there] = other_ref[...]
 
 
 def backward_kernel(
-    grad_ref, qkv_ref, mix_ref, log_ref, rows_ref, w_ref, side_ref, text_ref, down_ref,
-    part_out, w_out, side_out, text_out, down_out,
-    out_ref, part_ref, store_sem, down_pair, pair_sem, grad_all, query_turned, ex_local, ex_send, ex_recv, *scratch,
+    grad_ref, qkv_ref, mix_ref, log_ref, rows_ref, w_ref, side_ref, text_ref, down_ref, up_ref,
+    part_out, w_out, side_out, text_out, down_out, up_came,
+    up_send, up_recv, out_ref, part_ref, store_sem, down_pair, pair_sem, grad_all, query_turned, ex_local, ex_send, ex_recv, *scratch,
 ):
-    enter(plane_others())
+    z = lax.axis_index("shard")
+    spot = place()[1:]
+    others = shard_others()
+    enter(plane_others() + [device(other, *spot) for other in others])
     exchange = Exchange(grad_ref, grad_all, ex_local, ex_send, ex_recv)
     blocks, both, width = mix_ref.shape
     rows = both // 2
@@ -795,6 +794,12 @@
     step = SIDE // rows
     for clip in range(2):
         exchange.start(clip, pl.ds(clip * rows, rows))
+    some = pl.ds(up_came.shape[2], up_came.shape[2])
+    up_moves = spread(
+        lambda other: up_ref.at[other, :, some], up_came, up_send, up_recv, others, spot
+    )
+    up_own = pltpu.make_async_copy(up_ref.at[z, :, some], up_came.at[z], pair_sem.at[2])
+    up_own.start()
     size = len(scratch) // 2
     text = LoadedScatter(text_ref, *scratch[size:])
     text.start()
@@ -854,7 +859,7 @@
         return pltpu.make_async_copy(part_ref.at[block], part_out.at[block], store_sem.at[block])
 
     def project(block, carry):
-        part_ref[block] = nt(out_ref[block], w_ref[...]).astype(BF)
+        part_ref[block] = nt(out_ref[block], w_ref[:, : 3 * width]).astype(BF)
         store(block).start()
         return carry
 
@@ -875,11 +880,14 @@
     side.finish()
     beside(down_ref, pair, down_pair, down_out)
     pair.wait_send()
+    up_own.wait()
+    for copy in up_moves:
+        copy.wait()
     for block in range(blocks):
         store(block).wait()
 
 
-def attend_backward(grad_mix, qkv, mix, logs, rows, weights, side, text, down, ident):
+def attend_backward(grad_mix, qkv, mix, logs, rows, weights, side, text, down, up, ident):
     blocks, block, columns = mix.shape
     _, side_rows, width = side.shape
     text_shape = text.shape[1:]
@@ -891,16 +899,19 @@
             shape(width, 3 * columns),
             shape(side_rows, width),
             shape(*text_shape),
-            shape(down.shape[0], 2 * down.shape[1], dtype=F32),
+            shape(down.shape[0], 2 * down.shape[1]),
+            shape(*up.shape[:2], up.shape[2] // 2),
         ),
-        (ANY, IN_VMEM, IN_VMEM, IN_VMEM, IN_VMEM),
-        [ANY] + [IN_VMEM] * 5 + [ANY, ANY, IN_VMEM],
+        (ANY, IN_VMEM, IN_VMEM, IN_VMEM, IN_VMEM, ANY),
+        [ANY] + [IN_VMEM] * 5 + [ANY, ANY, IN_VMEM, ANY],
         [
+            pltpu.SemaphoreType.DMA((up.shape[0] - 1,)),
+            pltpu.SemaphoreType.DMA((up.shape[0] - 1,)),
             pltpu.VMEM((blocks, block, 3 * columns), BF),
             pltpu.VMEM((blocks, block, width), BF),
             pltpu.SemaphoreType.DMA((8,)),
             pltpu.VMEM(down.shape, BF),
-            pltpu.SemaphoreType.DMA((2,)),
+            pltpu.SemaphoreType.DMA((3,)),
             pltpu.VMEM((blocks, block, columns), BF),
             pltpu.VMEM((HEAD_DIM, blocks * block // 2), F32),
             pltpu.SemaphoreType.DMA((2,)),
@@ -911,7 +922,7 @@
         + LoadedScatter.scratch(*text_shape),
         ident,
         1,
-    )(grad_mix, qkv, mix, logs, rows, weights, side, text, down)
+    )(grad_mix, qkv, mix, logs, rows, weights, side, text, down, up)
 
 
 CHUNK = 64
@@ -954,8 +965,11 @@
     spot = place()[1:]
     others = shard_others()
     enter(neighbours() + [device(other, *spot) for other in others])
-    up_moves = spread(lambda other: up_ref.at[other], up_came, up_send, up_recv, others, spot)
-    up_own = pltpu.make_async_copy(up_ref.at[z], up_came.at[z], w_sem.at[3])
+    some = pl.ds(0, up_came.shape[2])
+    up_moves = spread(
+        lambda other: up_ref.at[other, :, some], up_came, up_send, up_recv, others, spot
+    )
+    up_own = pltpu.make_async_copy(up_ref.at[z, :, some], up_came.at[z], w_sem.at[3])
     up_own.start()
     cross_job = Scatter(w_cross, *scratch[:5])
     query_job = Scatter(w_query, *scratch[5:10])
@@ -1024,8 +1038,8 @@
         return carry
 
     back_ref[...] = jnp.zeros_like(back_ref)
+    branch_job.second()
     lax.fori_loop(0, blocks // 2, cross, 0)
-    branch_job.second()
     cross_job.far()
     cross_job.near()
     lax.fori_loop(blocks // 2, blocks, cross, 0)
@@ -1065,7 +1079,7 @@
     square_out, square_three = chunks(rows, last, nothing)
     rest = jnp.zeros((1, width), F32)
     for index, row in enumerate(
-        (rest, rest, gain_two, shift_two, gain_three, shift_three, square_out, square_three)
+        (rest, gain_two, gain_three, rest, shift_two, shift_three, square_out, square_three)
     ):
         stats_ref[index : index + 1] = row
     query_job.second()
@@ -1095,7 +1109,7 @@
             shape(blocks, columns, width),
             shape(2, columns, width),
             shape(*text.shape),
-            shape(*up.shape),
+            shape(*up.shape[:2], up.shape[2] // 2),
         ),
         (IN_VMEM,) * 7 + (ANY,),
         [IN_VMEM] * 10 + [ANY, ANY, ANY],
@@ -1118,9 +1132,9 @@
 
 
 def last_kernel(
-    part_ref, frames_ref, gain_ref, grad_ref, stats_ref, qkv_ref, up_ref, cross_ref, out_w_ref,
+    part_ref, frames_ref, gain_ref, grad_ref, stats_ref, qkv_ref, up_a, up_b, cross_ref, out_w_ref,
     text_ref, text_in, w_text_ref,
-    out_ref, total_ref, text_out, qkv_out, up_out, query_out, cross_out, self_out, key_out,
+    out_ref, total_ref, text_out, qkv_out, up_out, cross_out, self_out, key_out,
     mine, came, all_ref, st_send, st_recv, z_send, z_recv,
     qkv_came, out_came, text_came, text_part, text_mine, text_all,
     qkv_pair, up_mine, up_pair, cross_pair, out_pair, key_pair, x_send, x_recv, *scratch,
@@ -1146,10 +1160,11 @@
     average = jnp.mean(inputs, axis=-1, keepdims=True)
     centred = inputs - average
     rate = lax.rsqrt(jnp.mean(centred * centred, axis=-1, keepdims=True) + EPS)
-    total = up_ref[0].astype(F32)
-    for index in range(1, shards):
-        total += up_ref[index].astype(F32)
-    up_mine[...] = total.astype(BF)
+    for start, up_ref in ((0, up_a), (up_a.shape[2], up_b)):
+        total = up_ref[0].astype(F32)
+        for index in range(1, shards):
+            total += up_ref[index].astype(F32)
+        up_mine[:, start : start + up_ref.shape[2]] = total.astype(BF)
     text_came[z] = text_ref[...]
     for copy in text_moves:
         copy.wait_recv()
@@ -1183,27 +1198,27 @@
         return copy
 
     text.second()
-    pairs = [swap(0, up_mine, up_pair), swap(1, cross_ref, cross_pair)]
-    pairs.append(swap(2, key_pair.at[0], key_pair.at[1]))
-    text.wait()
-    for index in range(shards):
-        rows = slice(index * 2 * own, (index + 1) * 2 * own)
-        text_mine[index] = text.value(rows).astype(BF)
-    text_moves += over(3, lambda other: text_mine.at[other], text_all)
-    text_all[z] = text_mine[z]
     grads = job.total()
     normed = centred * rate
     mine[0] = stats_ref[...]
     mine[0, 0:1] = jnp.sum(grads * normed, axis=0, keepdims=True)
-    mine[0, 1:2] = jnp.sum(grads, axis=0, keepdims=True)
+    mine[0, 3:4] = jnp.sum(grads, axis=0, keepdims=True)
     sends = []
-    for index, target in enumerate(reversed(neighbours())):
+    for index, target in enumerate(neighbours()):
         copy = remote_copy(
             mine.at[index], came.at[index], st_send.at[index], st_recv.at[index], target
         )
         copy.start()
         sends.append(copy)
         if index == 0:
+            pairs = [swap(0, up_mine, up_pair), swap(1, cross_ref, cross_pair)]
+            pairs.append(swap(2, key_pair.at[0], key_pair.at[1]))
+            text.wait()
+            for block in range(shards):
+                rows = slice(block * 2 * own, (block + 1) * 2 * own)
+                text_mine[block] = text.value(rows).astype(BF)
+            text_moves += over(3, lambda other: text_mine.at[other], text_all)
+            text_all[z] = text_mine[z]
             scaled = grads * gain_ref[...]
             inner = jnp.mean(scaled * normed, axis=-1, keepdims=True)
             scaled = scaled - jnp.mean(scaled, axis=-1, keepdims=True) - normed * inner
@@ -1236,16 +1251,15 @@
     beside(up_mine, pairs[0], up_pair, up_out)
 
     def ordered(first, second):
-        first, second = first.astype(F32), second.astype(F32)
         return jnp.where(context == 0, first, second), jnp.where(context == 0, second, first)
 
     pairs[1].wait_recv()
     lead, trail = ordered(cross_ref[...], cross_pair[...])
     width = lead.shape[0] // 2
-    query_out[:, :width] = jnp.transpose(lead[:width])
-    query_out[:, width:] = jnp.transpose(trail[:width])
-    cross_out[:, :width] = jnp.transpose(lead[width:])
-    cross_out[:, width:] = jnp.transpose(trail[width:])
+    for index in range(2):
+        part = slice(index * width, (index + 1) * width)
+        cross_out[index, :width] = lead[part]
+        cross_out[index, width:] = trail[part]
     pairs[2].wait_recv()
     lead, trail = ordered(key_pair[0], key_pair[1])
     for index in range(2):
@@ -1260,21 +1274,22 @@
         qkv_out[index, :, width:] = trail[:, lanes]
     pairs[4].wait_recv()
     lead, trail = ordered(out_pair[0], out_pair[1])
-    self_out[:, :width] = jnp.transpose(lead)
-    self_out[:, width:] = jnp.transpose(trail)
+    self_out[:width] = lead
+    self_out[width:] = trail
     for copy in sends + text_moves + qkv_moves + out_moves + stat_moves + pairs:
         copy.wait_send()
     text.finish()
     job.finish()
 
 
-def last_step(part, frames, gain, grad, stats, qkv, up, cross, out, text, text_in, w_text, ident):
+def last_step(
+    part, frames, gain, grad, stats, qkv, up_a, up_b, cross, out, text, text_in, w_text, ident
+):
     _, rows, width = part.shape
     shards, texts, depth = text_in.shape
-    half = up.shape[2]
+    half = 2 * up_a.shape[2]
     columns = out.shape[1]
     own = texts // 8
-    square = shape(depth, 2 * columns, dtype=F32)
     return call(
         last_kernel,
         "last_step",
@@ -1282,15 +1297,14 @@
             shape(rows, width, dtype=F32),
             shape(16, width, dtype=F32),
             shape(shards, own, depth, dtype=F32),
-            shape(3, depth, 2 * columns, dtype=F32),
-            shape(depth, 2 * half, dtype=F32),
-            square,
-            square,
-            square,
-            shape(2, depth, 2 * columns, dtype=F32),
+            shape(3, depth, 2 * columns),
+            shape(depth, 2 * half),
+            shape(2, 2 * columns, depth),
+            shape(2 * columns, depth),
+            shape(2, depth, 2 * columns),
         ),
-        (IN_VMEM,) * 9,
-        [ANY] + [IN_VMEM] * 11,
+        (IN_VMEM,) * 8,
+        [ANY] + [IN_VMEM] * 12,
         [
             pltpu.VMEM((4, 16, width), F32),
             pltpu.VMEM((3, 16, width), F32),
@@ -1318,7 +1332,7 @@
         + Scatter.scratch(shards * own, depth),
         ident,
         65,
-    )(part, frames, gain, grad, stats, qkv, up, cross, out, text, text_in, w_text)
+    )(part, frames, gain, grad, stats, qkv, up_a, up_b, cross, out, text, text_in, w_text)
 
 
 def dots(spec, *operands):
@@ -1362,32 +1376,29 @@
         return lax.all_gather(weight, "shard", axis=0, tiled=tiled)
 
     cross_part = half(cross_qkv)
-    side = jnp.concatenate([half(self_out), cross_part[0], half(cross_out)], axis=1)
-    w_side = over_shard(side.transpose(1, 0), tiled=False)
+    qkv_part = half(self_qkv)
+    early = [qkv_part[0], qkv_part[1], qkv_part[2], half(self_out), cross_part[0], half(cross_out)]
+    w_early = over_shard(jnp.concatenate(early, axis=1))
+    w_late = over_shard(jnp.concatenate([half(mlp_up), half(mlp_down)], axis=1))
     w_text = jnp.concatenate([cross_part[1], cross_part[2]], axis=1)
     text_slices = text_states.reshape(clips * texts, slices, depth).transpose(1, 0, 2)
     w_down = over_shard(half(mlp_down))
-    w_up = over_shard(half(mlp_up))
-
-    qkv_part = half(self_qkv)
-    all_one, all_grad, w_qkv, text_in, text_part = first_step(
+
+    all_one, all_grad, text_in, text_part = first_step(
         frames.reshape(block, width),
         norm_gain,
         norm_bias,
         cotangent.reshape(block, width),
-        jnp.concatenate([qkv_part[0], qkv_part[1], qkv_part[2]], axis=-1),
         text_slices,
         w_text,
         0,
     )
-    w_qkv = w_qkv.reshape(width, 3 * columns)
     (
         qkv, self_log, mix, my_mix, stream_one, stream_two, cross_q, cross_mix, norm_three,
         text_all, squares, plane_w,
     ) = attend_forward(
         all_one,
-        w_qkv,
-        w_side,
+        w_early,
         text_part,
         frames.reshape(block, width),
         norm_gain,
@@ -1396,14 +1407,15 @@
     )
 
     grad_normed, part_three, grad_up, grad_down = feed_forward(
-        norm_three, all_grad, w_up, w_down, 4
+        norm_three, all_grad, w_late, 4
     )
 
     def to_shard(part):
         return lax.psum_scatter(part.astype(BF), "shard", scatter_dimension=0, tiled=True)
 
     grad_down = to_shard(grad_down)
-    grad_one, layer_out, stats, grad_mix, part_out, side, text_grads, grad_up = rows_back(
+    grad_up = grad_up.reshape(slices, depth, -1)
+    grad_one, layer_out, stats, grad_mix, part_out, side, text_grads, up_a = rows_back(
         grad_normed,
         cotangent.reshape(block, width),
         stream_one,
@@ -1416,7 +1428,7 @@
         norm_bias,
         plane_w,
         part_three,
-        grad_up.reshape(slices, depth, -1),
+        grad_up,
         3,
     )
 
@@ -1424,12 +1436,11 @@
         return part.reshape(-1, slices, depth).transpose(1, 0, 2)
 
     grad_cross = to_shard(slice_shards(side))[0]
-    part_norm, grad_w_qkv, grad_out, text_grads, grad_down = attend_backward(
-        grad_mix, qkv, mix, self_log, all_one, w_qkv, part_out, text_grads, grad_down, 8
+    part_norm, grad_w_qkv, grad_out, text_grads, grad_down, up_b = attend_backward(
+        grad_mix, qkv, mix, self_log, all_one, w_early, part_out, text_grads, grad_down, grad_up, 8
     )
     (
-        grad_frames, totals, grad_text, grad_w_qkv, grad_up, grad_query, grad_cross, grad_out,
-        grad_keys,
+        grad_frames, totals, grad_text, grad_w_qkv, grad_up, grad_cross, grad_out, grad_keys,
     ) = last_step(
         part_norm,
         frames.reshape(block, width),
@@ -1437,7 +1448,8 @@
         grad_one,
         jnp.concatenate([stats, squares], axis=0),
         grad_w_qkv.reshape(slices, depth, 3 * columns),
-        grad_up,
+        up_a,
+        up_b,
         grad_cross,
         slice_shards(grad_out),
         text_grads,
@@ -1448,12 +1460,10 @@
     grad_frames = grad_frames.reshape(clips, rows, width)
     grad_text = grad_text.transpose(1, 0, 2).reshape(clips, texts // 8, width)
 
-    gains = jnp.stack([totals[0], totals[2], totals[4]])
-    shifts = jnp.stack([totals[1], totals[3], totals[5]])
-    squares = jnp.stack([totals[j].sum() for j in (6, 8, 9, 7)])
+    squares = totals[6:10].sum(axis=1)[jnp.array([0, 2, 3, 1])]
     start = lax.axis_index("shard") * depth
-    grad_gain = lax.dynamic_slice_in_dim(gains, start, depth, 1)
-    grad_shift = lax.dynamic_slice_in_dim(shifts, start, depth, 1)
+    grad_gain = lax.dynamic_slice_in_dim(totals[:3], start, depth, 1)
+    grad_shift = lax.dynamic_slice_in_dim(totals[3:6], start, depth, 1)
     entries = float(clips * rows * width * lax.axis_size(("shard",) + PLANE))
     return (
         layer_out.reshape(clips, rows, width),
@@ -1461,12 +1471,12 @@
         grad_text,
         grad_gain,
         grad_shift,
-        grad_w_qkv,
-        grad_out,
-        jnp.concatenate([grad_query[None], grad_keys]),
-        grad_cross,
-        grad_up,
-        grad_down,
+        grad_w_qkv.astype(F32),
+        grad_out.transpose(1, 0).astype(F32),
+        jnp.concatenate([grad_cross[:1].transpose(0, 2, 1), grad_keys]).astype(F32),
+        grad_cross[1].transpose(1, 0).astype(F32),
+        grad_up.astype(F32),
+        grad_down.astype(F32),
         jnp.sqrt(squares / entries),
     )
 

time: 616 us -> 545 us (0.88)
  the two profiles are of different devices: /device:TPU:8 before, /device:TPU:12 now
where the time goes in v8:
time: 545 us; the launch traced here: 535 us
  Pallas kernels  475 us (87%)
  local copies, waits for them, and re-layouts  22 us (4%)
  between operations  14.4 us (3%)
  waiting for transfers between devices  13.7 us (3%)
  other arithmetic  10.3 us (2%)
    pallas_call x1, Pallas kernels, last_step(): call(last_kernel, 'last_step', (shape(rows, width, dtype=F32), shape(16,...  108 us
    pallas_call x1, Pallas kernels, attend_forward(): call(forward_kernel, 'attend_forward', (shape(blocks, block, 3 * columns)...  93.8 us
    pallas_call x1, Pallas kernels, rows_back(): call(rows_back_kernel, 'rows_back', (shape(rows, width, dtype=F32), shape...  82.1 us
    pallas_call x1, Pallas kernels, feed_forward(): call(feed_kernel, 'feed_forward', outs, (IN_VMEM, ANY, IN_VMEM, IN_VMEM),...  69.6 us
    pallas_call x1, Pallas kernels, first_step(): call(first_kernel, 'first_step', (shape(8, rows, width), shape(8, rows, w...  64.3 us
    pallas_call x1, Pallas kernels, attend_backward(): call(backward_kernel, 'attend_backward', (shape(blocks, block, width), sh...  57.4 us
    all_gather x2, waiting for transfers between devices, over_shard(): return lax.all_gather(weight, 'shard', axis=0, tiled=tiled)  13.6 us
  transfers between devices with their start and end apart: 4, of which 1 were waited for; matrix products, arithmetic and copies ran while one was open for 2% of the time, Pallas kernels for 56%

profile of v8, /device:TPU:12, one launch (start us, length us, event | category | flops | bytes accessed | tf_op | source)
XLA Modules:
  0.0 535.4 jit_solution(14308095853338671285)
XLA Ops:
  7.2 0.0 all-gather.3.cloned.1.call-start
  7.2 1.2 constant_dynamic-slice_fusion.4
  8.5 1.9 dynamic-slice_bitcast_fusion
  10.4 1.3 concatenate.16
  11.7 0.0 all-gather.3.cloned.1.call-update
  11.8 0.0 all-gather.5.cloned.1.call-start
  11.8 1.1 constant_dynamic-slice_fusion.2
  13.0 1.1 pad_maximum_fusion
  14.1 0.0 all-gather.5.cloned.1.call-update
  14.1 0.0 reduce-scatter.3.cloned.1.call-start
  14.2 0.1 reshape.61
  14.3 0.8 copy.40
  15.1 0.8 pad_maximum_fusion.1.w_text_ref
  15.9 64.3 %first_step.1 = (bf16[8,256,1536]{2,1,0:T(8,128)(2,1)}, bf16[8,256,1536]{2,1,0:T(8,128)(2,1)}, bf16[4,128,384]{2,1,0:T(8,128)(2,1)}, bf16[128,384]{1,0:T(8,128)(2,1)}) custom-call(bf16[256,1536]{1,0:T(8,128)(2,1)} %bitcast.54, f32[3,1536]{1,0:T(4,128)} %gain_ref.5, f32[3,1536]{1,0:T(4,128)} %bias_ref.5, bf16[256,1536]{1,0:T(8,128)(2,1)} %bitcast.52, ...), custom_call_target="tpu_custom_call" | custom-call | flops 60000002048 | bytes 60000000 | tf_op jit(solution)/shard_map/first_step/pallas_call | solution.py:397
  80.2 13.6 %all-gather.3.cloned.1.call-done.side_ref.w_ref = bf16[1536,1152]{1,0:T(8,128)(2,1)} async-done(((bf16[384,1152]{1,0:T(8,128)(2,1)}), bf16[1536,1152]{1,0:T(8,128)(2,1)}) %all-gather.3.cloned.1.call-update) | async-done | bytes 3538960 | tf_op jit(solution)/shard_map/all_gather | solution.py:1376
  93.8 93.8 %attend_forward.1 = (bf16[8,256,576]{2,1,0:T(8,128)(2,1)}, f32[6,1024]{1,0:T(8,128)}, bf16[8,256,192]{2,1,0:T(8,128)(2,1)}, bf16[8,256,192]{2,1,0:T(8,128)(2,1)}...) custom-call(bf16[8,256,1536]{2,1,0:T(8,128)(2,1)} %get-tuple-element, ...), custom_call_target="tpu_custom_call" | custom-call | flops 80000000000 | bytes 80000000 | tf_op jit(solution)/shard_map/attend_forward/pallas_call | solution.py:736
  187.6 0.0 all-gather.5.cloned.1.call-done.w_ref
  187.7 69.6 %feed_forward.1 = (f32[256,1536]{1,0:T(8,128)}, bf16[8,256,1536]{2,1,0:T(8,128)(2,1)}, bf16[1536,768]{1,0:T(8,128)(2,1)}, bf16[1536,768]{1,0:T(8,128)(2,1)}) custom-call(bf16[256,1536]{1,0:T(8,128)(2,1)} %get-tuple-element.56.own_ref, bf16[8,256,1536]{2,1,0:T(8,128)(2,1)} %get-tuple-element.57.grad_ref, bf16[1536,1536]{1,0:T(8,128)(2,1)} %all-gather.5.cloned.1.call-done.w_ref), custom_call_target="tpu_custom_call" | custom-call | flops 70000001024 | bytes 70000000 | tf_op jit(solution)/shard_map/feed_forward/pallas_call | solution.py:538
  257.2 0.0 reduce-scatter.3.cloned.1.call-update
  257.3 0.0 reduce-scatter.5.cloned.1.call-start
  257.3 82.1 %rows_back.1 = (f32[256,1536]{1,0:T(8,128)}, bf16[256,1536]{1,0:T(8,128)(2,1)}, f32[8,1536]{1,0:T(8,128)}, bf16[8,256,192]{2,1,0:T(8,128)(2,1)}, bf16[8,192,1536...) custom-call(f32[256,1536]{1,0:T(8,128)} %get-tuple-element.58.normed, ...), custom_call_target="tpu_custom_call" | custom-call | flops 60000002048 | bytes 60000000 | tf_op jit(solution)/shard_map/rows_back/pallas_call | solution.py:1101
  339.5 2.7 reshape.65
  342.2 0.0 copy-start.13
  342.2 1.2 copy.38
  343.4 0.0 reduce-scatter.5.cloned.1.call-update
  343.4 1.3 slice.42.gain_ref
  344.7 0.6 pad_maximum_fusion.2.stats_ref
  345.4 57.4 %attend_backward.1 = (bf16[8,256,1536]{2,1,0:T(8,128)(2,1)}, bf16[1536,576]{1,0:T(8,128)(2,1)}, bf16[192,1536]{1,0:T(8,128)(2,1)}, bf16[128,384]{1,0:T(8,128)(2,...) custom-call(bf16[8,256,192]{2,1,0:T(8,128)(2,1)} %get-tuple-element.69.grad_ref, ...), custom_call_target="tpu_custom_call" | custom-call | flops 1000000000 | bytes 1000000 | tf_op jit(solution)/shard_map/attend_backward/pallas_call | solution.py:894
  402.8 1.9 copy.39
  404.7 107.6 %last_step.1 = (f32[256,1536]{1,0:T(8,128)}, f32[16,1536]{1,0:T(8,128)}, f32[4,16,384]{2,1,0:T(8,128)}, bf16[3,384,384]{2,1,0:T(8,128)(2,1)}, bf16[384,1536]{1,0...) custom-call(bf16[8,256,1536]{2,1,0:T(8,128)(2,1)} %get-tuple-element.76.part_re, ...), custom_call_target="tpu_custom_call" | custom-call | flops 65000001536 | bytes 65000000 | tf_op jit(solution)/shard_map/last_step/pallas_call | solution.py:1293
  512.4 1.5 copy.31
  513.8 1.0 convert_bitcast_fusion
  514.9 0.1 slice_reduce_fusion
  515.1 1.7 convert_element_type.34
  516.8 1.3 convert_element_type.27
  518.1 1.1 copy.32
  519.2 1.0 copy.33
  520.3 0.7 reshape.68
  521.0 0.6 constant_dynamic-slice_fusion
  521.6 0.6 constant_dynamic-slice_fusion.1
  522.2 0.6 gather_fusion
  522.8 0.5 multiply_sqrt_fusion
  523.3 1.7 convert_element_type.35
  525.0 1.3 maximum_convert_fusion
  526.4 0.0 copy-done.4
  526.4 0.9 copy.43
  527.3 0.0 copy-done
  527.3 1.1 copy.44
  (32 shorter events, 0.2 us)
Async XLA Ops:
  7.2 86.6 %all-gather.3.cloned.1.call-start = ((), (), s32[]{:S(2)}) async-start(), calls=%async_computation.2 | async-start | bytes 4423680 | tf_op jit(solution)/shard_map/all_gather | solution.py:1376
  10.4 1.4 copy-start.7
  11.8 175.9 %all-gather.5.cloned.1.call-start = ((), (), s32[]{:S(2)}) async-start(), calls=%async_computation.3 | async-start | bytes 5898240 | tf_op jit(solution)/shard_map/all_gather | solution.py:1376
  13.0 1.2 copy-start.6
  14.1 331.3 %reduce-scatter.3.cloned.1.call-start = ((), (), s32[]{:S(2)}) async-start(), calls=%async_computation.4 | async-start | bytes 2949120 | tf_op jit(solution)/shard_map/reduce_scatter | solution.py:1414
  257.3 147.4 %reduce-scatter.5.cloned.1.call-start = ((), (), s32[]{:S(2)}) async-start(), calls=%async_computation.5 | async-start | bytes 1474560 | tf_op jit(solution)/shard_map/reduce_scatter | solution.py:1414
  342.2 2.6 copy-start.13
  342.2 2.6 copy-start.11
  342.2 2.6 copy-start.12
  512.4 2.5 copy-start.10
  512.4 2.7 copy-start.2
  515.1 1.7 copy-start.3
  516.8 1.3 copy-start.8
  518.1 2.2 copy-start.9
  518.1 5.2 copy-start.1
  523.3 1.7 copy-start.5
  525.0 1.4 copy-start.4
  525.0 2.3 copy-start
Sparse Core Ops, SparseCore 0:
  11.9 81.8 all-gather.2
  95.9 88.9 all-gather.4
  257.4 72.4 reduce-scatter.2
  343.5 47.6 reduce-scatter.4

commit v9 on v8

--- a/solution.py
+++ b/solution.py
@@ -232,6 +232,8 @@
 
 
 class LoadedScatter(Scatter):
+    steep = False
+
     @staticmethod
     def scratch(rows, columns):
         return [
@@ -243,23 +245,49 @@
         super().__init__(part_ref, *scratch)
         self.in_ref, self.local_sem = in_ref, local_sem
 
+    def bring(self, index):
+        source = self.in_ref.at[self.theirs[index]]
+        self.forward(index, source, self.core.at[index], self.to_c)
+        load = pltpu.make_async_copy(
+            self.in_ref.at[self.blocks[index]], self.part_ref.at[index], self.local_sem.at[index]
+        )
+        load.start()
+        self.loads.append(load)
+
     def start(self):
         self.loads = []
-        for index, (mine, theirs) in enumerate(zip(self.mine, self.theirs)):
-            source = self.in_ref.at[theirs]
-            self.forward(index, source, self.core.at[index], self.to_c)
-            load = pltpu.make_async_copy(
-                self.in_ref.at[mine], self.part_ref.at[index], self.local_sem.at[index]
-            )
-            load.start()
-            self.loads.append(load)
-        self.mine = (0, 1, 2, 3)
+        self.blocks, self.mine = self.mine, (0, 1, 2, 3)
+        for index in range(4):
+            self.bring(index)
 
     def first(self):
         for load in self.loads:
             load.wait()
-        self.far()
-        self.near()
+        if not self.steep:
+            self.far()
+            self.near()
+            return
+        self.arrived(0, self.core.at[0])
+        self.forward(4, self.add(0, self.low), self.relay.at[0], self.to_y)
+        self.forward(5, self.add(0, self.high), self.relay.at[1], self.to_y)
+        self.arrived(2, self.core.at[2])
+        self.forward(7, self.add(2, self.high), self.final.at[1, self.high], self.to_y)
+        self.forward(9, self.add(2, self.low), self.final.at[1, self.low], self.to_y)
+
+    def second(self):
+        if not self.steep:
+            super().second()
+            return
+        final, relay = self.final, self.relay
+        self.arrived(1, self.core.at[1])
+        self.arrived(4, relay.at[0])
+        self.forward(6, self.add(1, self.low, relay[0]), final.at[0, self.low], self.to_x)
+        self.arrived(5, relay.at[1])
+        self.forward(8, self.add(1, self.high, relay[1]), final.at[0, self.high], self.to_x)
+
+
+class SteepScatter(LoadedScatter):
+    steep = True
 
 
 class Exchange:
@@ -564,6 +592,20 @@
 
 def turn(values):
     return jnp.transpose(values.astype(F32))
+
+
+def side_by_side(ref):
+    return jnp.concatenate([ref[block] for block in range(ref.shape[0])], axis=1)
+
+
+def all_rows(ref):
+    return ref[...].reshape(-1, ref.shape[2])
+
+
+def split_columns(values, ref):
+    columns = ref.shape[2]
+    for block in range(ref.shape[0]):
+        ref[block] = values[:, block * columns : (block + 1) * columns].astype(BF)
 
 
 def causal(scores):
@@ -653,13 +695,7 @@
     exchange.finish()
 
     def apply(values_ref, kind):
-        sum_ref[...] = jnp.zeros_like(sum_ref)
-
-        def one(block, carry):
-            sum_ref[...] += nn(values_ref[block], weights[kind][block])
-            return carry
-
-        lax.fori_loop(0, blocks, one, 0)
+        sum_ref[...] = nn(side_by_side(values_ref), all_rows(weights[kind]))
 
     apply(mine_ref, 0)
     nothing = jnp.zeros((1, features), F32)
@@ -680,11 +716,7 @@
     jobs[1].finish()
     keep(1)
 
-    def ask(block, carry):
-        query_ref[block] = nt(two_low_ref[...], w_query[block]).astype(BF)
-        return carry
-
-    lax.fori_loop(0, blocks, ask, 0)
+    split_columns(nt(two_low_ref[...], all_rows(w_query)), query_ref)
     texts = text_ref.shape[1] // 2
 
     def cross(block, carry):
@@ -1000,8 +1032,9 @@
     branch_job.first()
     loads[0].wait()
 
+    split_columns(nt(low_ref[...], all_rows(w_cross)), grad_cm)
+
     def cross_weight(block, carry):
-        grad_cm[block] = nt(low_ref[...], w_cross[block]).astype(BF)
         w_cross[block] = tn(mix_ref[block], low_ref[...]).astype(BF)
         return carry
 
@@ -1032,17 +1065,19 @@
                 grad_cq[block, part, here] = (grad_query * HEAD_DIM ** (-0.5)).astype(BF)
                 text_out[block, keys, here] = nn(slopes, query).astype(BF)
                 text_out[block, keys, there] = nn(weights.astype(BF), grad).astype(BF)
-        back = nn(grad_cq[block], w_query[block])
-        back_ref[...] += back
+        return carry
+
+    def query_weight(block, carry):
         w_query[block] = tn(grad_cq[block], two_low_ref[...]).astype(BF)
         return carry
 
-    back_ref[...] = jnp.zeros_like(back_ref)
     branch_job.second()
     lax.fori_loop(0, blocks // 2, cross, 0)
     cross_job.far()
     cross_job.near()
     lax.fori_loop(blocks // 2, blocks, cross, 0)
+    back_ref[...] = nn(side_by_side(grad_cq), all_rows(w_query))
+    lax.fori_loop(0, blocks, query_weight, 0)
     for index in range(4):
         query_job.pass_core(index)
 
@@ -1059,8 +1094,9 @@
     query_job.near()
     loads[2].wait()
 
+    split_columns(nt(low_ref[...], all_rows(w_out)), grad_mix_ref)
+
     def out_weight(block, carry):
-        grad_mix_ref[block] = nt(low_ref[...], w_out[block]).astype(BF)
         out_ref[block] = tn(my_mix_ref[block], low_ref[...]).astype(BF)
         return carry
 
@@ -1137,7 +1173,8 @@
     out_ref, total_ref, text_out, qkv_out, up_out, cross_out, self_out, key_out,
     mine, came, all_ref, st_send, st_recv, z_send, z_recv,
     qkv_came, out_came, text_came, text_part, text_mine, text_all,
-    qkv_pair, up_mine, up_pair, cross_pair, out_pair, key_pair, x_send, x_recv, *scratch,
+    qkv_pair, up_mine, up_pair, cross_pair, out_pair, key_pair, x_send, x_recv, q_send, q_recv,
+    *scratch,
 ):
     z = lax.axis_index("shard")
     shards = lax.axis_size("shard")
@@ -1146,29 +1183,61 @@
     context = spot[0]
     enter(neighbours() + [device(other, *spot) for other in others])
 
+    def collect(moves, source_ref, came_ref, rows=slice(None)):
+        for copy in moves:
+            copy.wait_recv()
+        total = source_ref[z, rows].astype(F32)
+        for other in others:
+            total += came_ref[other, rows].astype(F32)
+        return total.astype(BF)
+
     def over(index, source_of, target_ref):
         return spread(source_of, target_ref, z_send.at[index], z_recv.at[index], others, spot)
 
     text_moves = over(0, lambda other: text_ref, text_came)
-    qkv_moves = over(1, lambda other: qkv_ref.at[other], qkv_came)
-    out_moves = over(2, lambda other: out_w_ref.at[other], out_came)
     size = len(scratch) - 5
     text = Scatter(text_part, *scratch[size:])
-    job = LoadedScatter(part_ref, *scratch[:size])
+    job = SteepScatter(part_ref, *scratch[:size])
     job.start()
-    inputs = frames_ref[...].astype(F32)
-    average = jnp.mean(inputs, axis=-1, keepdims=True)
-    centred = inputs - average
-    rate = lax.rsqrt(jnp.mean(centred * centred, axis=-1, keepdims=True) + EPS)
+    out_moves = over(2, lambda other: out_w_ref.at[other], out_came)
+    third = qkv_ref.shape[1] // 3
+    thirds = [pl.ds(index * third, third) for index in range(3)]
+    qkv_moves = []
+
+    def send_third(index):
+        for step, other in enumerate(others):
+            copy = remote_copy(
+                qkv_ref.at[other, thirds[index]], qkv_came.at[z, thirds[index]],
+                q_send.at[index, step], q_recv.at[index, step], device(other, *spot),
+            )
+            copy.start()
+            qkv_moves.append(copy)
+
+    def sum_third(index):
+        moves = qkv_moves[index * len(others) : (index + 1) * len(others)]
+        rows = thirds[index]
+        qkv_pair[0, rows] = collect(moves, qkv_ref, qkv_came, rows)
+        pairs.append(swap(4 + index, qkv_pair.at[0, rows], qkv_pair.at[1, rows]))
+
+    send_third(0)
+    to_x = neighbours()[0]
+
+    def swap(index, source, target_ref):
+        copy = remote_copy(source, target_ref, x_send.at[index], x_recv.at[index], to_x)
+        copy.start()
+        return copy
+
+    cross_move = swap(1, cross_ref, cross_pair)
+    job.first()
     for start, up_ref in ((0, up_a), (up_a.shape[2], up_b)):
         total = up_ref[0].astype(F32)
         for index in range(1, shards):
             total += up_ref[index].astype(F32)
         up_mine[:, start : start + up_ref.shape[2]] = total.astype(BF)
+    pairs = [swap(0, up_mine, up_pair), cross_move]
     text_came[z] = text_ref[...]
     for copy in text_moves:
         copy.wait_recv()
-    job.first()
     texts = text_ref.shape[0] // 2
     own = texts // 8
 
@@ -1187,22 +1256,28 @@
     for index in range(1, shards):
         key_grad += tn(text_in[index], text_came[index])
     key_pair[0] = key_grad.astype(BF)
+    pairs.append(swap(2, key_pair.at[0], key_pair.at[1]))
+    job.second()
     text.far()
     text.near()
-    job.second()
-    to_x = neighbours()[0]
-
-    def swap(index, source, target_ref):
-        copy = remote_copy(source, target_ref, x_send.at[index], x_recv.at[index], to_x)
-        copy.start()
-        return copy
-
+    out_pair[0] = collect(out_moves, out_w_ref, out_came)
+    pairs.append(swap(3, out_pair.at[0], out_pair.at[1]))
+    send_third(1)
     text.second()
-    grads = job.total()
-    normed = centred * rate
+    job.wait()
+    sum_third(0)
+    send_third(2)
+
+    def norm(part, sums):
+        back, more = norm_back(job.value(part), frames_ref[part].astype(F32), gain_ref[...])
+        out_ref[part] = grad_ref[part] + back
+        return sums[0] + more[0], sums[1] + more[1]
+
+    nothing = (jnp.zeros((1, frames_ref.shape[1]), F32),) * 2
+    gain_one, shift_one = chunks(frames_ref.shape[0], norm, nothing)
     mine[0] = stats_ref[...]
-    mine[0, 0:1] = jnp.sum(grads * normed, axis=0, keepdims=True)
-    mine[0, 3:4] = jnp.sum(grads, axis=0, keepdims=True)
+    mine[0, 0:1] = gain_one
+    mine[0, 3:4] = shift_one
     sends = []
     for index, target in enumerate(neighbours()):
         copy = remote_copy(
@@ -1211,36 +1286,19 @@
         copy.start()
         sends.append(copy)
         if index == 0:
-            pairs = [swap(0, up_mine, up_pair), swap(1, cross_ref, cross_pair)]
-            pairs.append(swap(2, key_pair.at[0], key_pair.at[1]))
             text.wait()
             for block in range(shards):
                 rows = slice(block * 2 * own, (block + 1) * 2 * own)
                 text_mine[block] = text.value(rows).astype(BF)
             text_moves += over(3, lambda other: text_mine.at[other], text_all)
             text_all[z] = text_mine[z]
-            scaled = grads * gain_ref[...]
-            inner = jnp.mean(scaled * normed, axis=-1, keepdims=True)
-            scaled = scaled - jnp.mean(scaled, axis=-1, keepdims=True) - normed * inner
-            out_ref[...] = grad_ref[...] + rate * scaled
         copy.wait_recv()
         mine[index + 1] = mine[index] + came[index]
     stat_moves = over(4, lambda other: mine.at[3], all_ref)
     all_ref[z] = mine[3]
 
-    def collect(moves, source_ref, came_ref):
-        came_ref[z] = source_ref[z]
-        for copy in moves:
-            copy.wait_recv()
-        total = came_ref[0].astype(F32)
-        for index in range(1, shards):
-            total += came_ref[index].astype(F32)
-        return total.astype(BF)
-
-    qkv_pair[0] = collect(qkv_moves, qkv_ref, qkv_came)
-    pairs.append(swap(3, qkv_pair.at[0], qkv_pair.at[1]))
-    out_pair[0] = collect(out_moves, out_w_ref, out_came)
-    pairs.append(swap(4, out_pair.at[0], out_pair.at[1]))
+    sum_third(1)
+    sum_third(2)
     for copy in text_moves[shards - 1 :] + stat_moves:
         copy.wait_recv()
     text_out[...] = text_all[...].astype(F32)
@@ -1267,15 +1325,16 @@
         key_out[index, :, :width] = lead[:, lanes]
         key_out[index, :, width:] = trail[:, lanes]
     pairs[3].wait_recv()
+    lead, trail = ordered(out_pair[0], out_pair[1])
+    self_out[:width] = lead
+    self_out[width:] = trail
+    for copy in pairs[4:]:
+        copy.wait_recv()
     lead, trail = ordered(qkv_pair[0], qkv_pair[1])
     for index in range(3):
         lanes = slice(index * width, (index + 1) * width)
         qkv_out[index, :, :width] = lead[:, lanes]
         qkv_out[index, :, width:] = trail[:, lanes]
-    pairs[4].wait_recv()
-    lead, trail = ordered(out_pair[0], out_pair[1])
-    self_out[:width] = lead
-    self_out[width:] = trail
     for copy in sends + text_moves + qkv_moves + out_moves + stat_moves + pairs:
         copy.wait_send()
     text.finish()
@@ -1325,8 +1384,10 @@
             pltpu.VMEM((2 * columns, depth), BF),
             pltpu.VMEM((2, columns, depth), BF),
             pltpu.VMEM((2, depth, 2 * columns), BF),
-            pltpu.SemaphoreType.DMA((5,)),
-            pltpu.SemaphoreType.DMA((5,)),
+            pltpu.SemaphoreType.DMA((7,)),
+            pltpu.SemaphoreType.DMA((7,)),
+            pltpu.SemaphoreType.DMA((3, shards - 1)),
+            pltpu.SemaphoreType.DMA((3, shards - 1)),
         ]
         + LoadedScatter.scratch(rows, width)
         + Scatter.scratch(shards * own, depth),

time: 545 us -> 522 us (0.958)
  the two profiles are of different devices: /device:TPU:12 before, /device:TPU:0 now
where the time goes in v9:
time: 522 us; the launch traced here: 512 us
  Pallas kernels  449 us (86%)
  local copies, waits for them, and re-layouts  22 us (4%)
  waiting for transfers between devices  16.6 us (3%)
  between operations  14.5 us (3%)
  other arithmetic  10.3 us (2%)
    pallas_call x1, Pallas kernels, attend_forward(): call(forward_kernel, 'attend_forward', (shape(blocks, block, 3 * columns)...  92.4 us
    pallas_call x1, Pallas kernels, last_step(): call(last_kernel, 'last_step', (shape(rows, width, dtype=F32), shape(16,...  82.6 us
    pallas_call x1, Pallas kernels, rows_back(): call(rows_back_kernel, 'rows_back', (shape(rows, width, dtype=F32), shape...  79.9 us
    pallas_call x1, Pallas kernels, feed_forward(): call(feed_kernel, 'feed_forward', outs, (IN_VMEM, ANY, IN_VMEM, IN_VMEM),...  70.6 us
    pallas_call x1, Pallas kernels, first_step(): call(first_kernel, 'first_step', (shape(8, rows, width), shape(8, rows, w...  65.2 us
    pallas_call x1, Pallas kernels, attend_backward(): call(backward_kernel, 'attend_backward', (shape(blocks, block, width), sh...  58.1 us
    all_gather x2, waiting for transfers between devices, over_shard(): return lax.all_gather(weight, 'shard', axis=0, tiled=tiled)  16.5 us
  transfers between devices with their start and end apart: 4, of which 1 were waited for; matrix products, arithmetic and copies ran while one was open for 2% of the time, Pallas kernels for 58%

profile of v9, /device:TPU:0, one launch (start us, length us, event | category | flops | bytes accessed | tf_op | source)
XLA Modules:
  0.0 512.3 jit_solution(617097917883304374)
XLA Ops:
  7.2 0.0 all-gather.3.cloned.1.call-start
  7.2 1.2 constant_dynamic-slice_fusion.4
  8.5 1.9 dynamic-slice_bitcast_fusion
  10.4 1.3 concatenate.16
  11.7 0.0 all-gather.3.cloned.1.call-update
  11.8 0.0 all-gather.5.cloned.1.call-start
  11.8 1.1 constant_dynamic-slice_fusion.2
  13.0 1.1 pad_maximum_fusion
  14.1 0.0 all-gather.5.cloned.1.call-update
  14.1 0.0 reduce-scatter.3.cloned.1.call-start
  14.2 0.1 reshape.61
  14.3 0.8 copy.40
  15.1 0.8 pad_maximum_fusion.1.w_text_ref
  15.9 65.2 %first_step.1 = (bf16[8,256,1536]{2,1,0:T(8,128)(2,1)}, bf16[8,256,1536]{2,1,0:T(8,128)(2,1)}, bf16[4,128,384]{2,1,0:T(8,128)(2,1)}, bf16[128,384]{1,0:T(8,128)(2,1)}) custom-call(bf16[256,1536]{1,0:T(8,128)(2,1)} %bitcast.54, f32[3,1536]{1,0:T(4,128)} %gain_ref.5, f32[3,1536]{1,0:T(4,128)} %bias_ref.5, bf16[256,1536]{1,0:T(8,128)(2,1)} %bitcast.52, ...), custom_call_target="tpu_custom_call" | custom-call | flops 60000002048 | bytes 60000000 | tf_op jit(solution)/shard_map/first_step/pallas_call | solution.py:425
  81.1 16.5 %all-gather.3.cloned.1.call-done.side_ref.w_ref = bf16[1536,1152]{1,0:T(8,128)(2,1)} async-done(((bf16[384,1152]{1,0:T(8,128)(2,1)}), bf16[1536,1152]{1,0:T(8,128)(2,1)}) %all-gather.3.cloned.1.call-update) | async-done | bytes 3538960 | tf_op jit(solution)/shard_map/all_gather | solution.py:1437
  97.6 92.4 %attend_forward.1 = (bf16[8,256,576]{2,1,0:T(8,128)(2,1)}, f32[6,1024]{1,0:T(8,128)}, bf16[8,256,192]{2,1,0:T(8,128)(2,1)}, bf16[8,256,192]{2,1,0:T(8,128)(2,1)}...) custom-call(bf16[8,256,1536]{2,1,0:T(8,128)(2,1)} %get-tuple-element, ...), custom_call_target="tpu_custom_call" | custom-call | flops 80000000000 | bytes 80000000 | tf_op jit(solution)/shard_map/attend_forward/pallas_call | solution.py:768
  190.0 0.0 all-gather.5.cloned.1.call-done.w_ref
  190.0 70.6 %feed_forward.1 = (f32[256,1536]{1,0:T(8,128)}, bf16[8,256,1536]{2,1,0:T(8,128)(2,1)}, bf16[1536,768]{1,0:T(8,128)(2,1)}, bf16[1536,768]{1,0:T(8,128)(2,1)}) custom-call(bf16[256,1536]{1,0:T(8,128)(2,1)} %get-tuple-element.56.own_ref, bf16[8,256,1536]{2,1,0:T(8,128)(2,1)} %get-tuple-element.57.grad_ref, bf16[1536,1536]{1,0:T(8,128)(2,1)} %all-gather.5.cloned.1.call-done.w_ref), custom_call_target="tpu_custom_call" | custom-call | flops 70000001024 | bytes 70000000 | tf_op jit(solution)/shard_map/feed_forward/pallas_call | solution.py:566
  260.6 0.0 reduce-scatter.3.cloned.1.call-update
  260.6 0.0 reduce-scatter.5.cloned.1.call-start
  260.7 79.9 %rows_back.1 = (f32[256,1536]{1,0:T(8,128)}, bf16[256,1536]{1,0:T(8,128)(2,1)}, f32[8,1536]{1,0:T(8,128)}, bf16[8,256,192]{2,1,0:T(8,128)(2,1)}, bf16[8,192,1536...) custom-call(f32[256,1536]{1,0:T(8,128)} %get-tuple-element.58.normed, ...), custom_call_target="tpu_custom_call" | custom-call | flops 60000002048 | bytes 60000000 | tf_op jit(solution)/shard_map/rows_back/pallas_call | solution.py:1137
  340.6 2.7 reshape.65
  343.4 0.0 copy-start.13
  343.4 1.2 copy.38
  344.6 0.0 reduce-scatter.5.cloned.1.call-update
  344.6 1.3 slice.42.gain_ref
  346.0 0.6 pad_maximum_fusion.2.stats_ref
  346.6 58.1 %attend_backward.1 = (bf16[8,256,1536]{2,1,0:T(8,128)(2,1)}, bf16[1536,576]{1,0:T(8,128)(2,1)}, bf16[192,1536]{1,0:T(8,128)(2,1)}, bf16[128,384]{1,0:T(8,128)(2,...) custom-call(bf16[8,256,192]{2,1,0:T(8,128)(2,1)} %get-tuple-element.69.grad_ref, ...), custom_call_target="tpu_custom_call" | custom-call | flops 1000000000 | bytes 1000000 | tf_op jit(solution)/shard_map/attend_backward/pallas_call | solution.py:926
  404.7 1.9 copy.39
  406.6 82.6 %last_step.1 = (f32[256,1536]{1,0:T(8,128)}, f32[16,1536]{1,0:T(8,128)}, f32[4,16,384]{2,1,0:T(8,128)}, bf16[3,384,384]{2,1,0:T(8,128)(2,1)}, bf16[384,1536]{1,0...) custom-call(bf16[8,256,1536]{2,1,0:T(8,128)(2,1)} %get-tuple-element.76.part_re, ...), custom_call_target="tpu_custom_call" | custom-call | flops 65000001536 | bytes 65000000 | tf_op jit(solution)/shard_map/last_step/pallas_call | solution.py:1352
  489.3 1.5 copy.31
  490.8 1.0 convert_bitcast_fusion
  491.8 0.1 slice_reduce_fusion
  492.0 1.7 convert_element_type.34
  493.7 1.3 convert_element_type.27
  495.1 1.1 copy.32
  496.1 1.0 copy.33
  497.2 0.7 reshape.68
  497.9 0.6 constant_dynamic-slice_fusion
  498.5 0.6 constant_dynamic-slice_fusion.1
  499.1 0.6 gather_fusion
  499.7 0.5 multiply_sqrt_fusion
  500.2 1.7 convert_element_type.35
  501.9 1.3 maximum_convert_fusion
  503.3 0.0 copy-done.4
  503.3 0.9 copy.43
  504.2 0.0 copy-done
  504.2 1.1 copy.44
  (32 shorter events, 0.2 us)
Async XLA Ops:
  7.2 90.4 %all-gather.3.cloned.1.call-start = ((), (), s32[]{:S(2)}) async-start(), calls=%async_computation.2 | async-start | bytes 4423680 | tf_op jit(solution)/shard_map/all_gather | solution.py:1437
  10.4 1.4 copy-start.7
  11.8 178.3 %all-gather.5.cloned.1.call-start = ((), (), s32[]{:S(2)}) async-start(), calls=%async_computation.3 | async-start | bytes 5898240 | tf_op jit(solution)/shard_map/all_gather | solution.py:1437
  13.0 1.2 copy-start.6
  14.1 332.5 %reduce-scatter.3.cloned.1.call-start = ((), (), s32[]{:S(2)}) async-start(), calls=%async_computation.4 | async-start | bytes 2949120 | tf_op jit(solution)/shard_map/reduce_scatter | solution.py:1475
  260.6 146.0 %reduce-scatter.5.cloned.1.call-start = ((), (), s32[]{:S(2)}) async-start(), calls=%async_computation.5 | async-start | bytes 1474560 | tf_op jit(solution)/shard_map/reduce_scatter | solution.py:1475
  343.4 2.6 copy-start.13
  343.4 2.6 copy-start.11
  343.4 2.6 copy-start.12
  489.3 2.5 copy-start.10
  489.3 2.7 copy-start.2
  492.0 1.7 copy-start.3
  493.7 1.3 copy-start.8
  495.0 2.2 copy-start.9
  495.0 5.2 %copy-start.1 = (bf16[384,1536]{1,0:T(8,128)(2,1)S(1)}, bf16[384,1536]{1,0:T(8,128)(2,1)}, u32[]{:S(2)}) copy-start(bf16[384,1536]{1,0:T(8,128)(2,1)} %get-tuple-element.95) | copy-start | bytes 3538948
  500.2 1.7 copy-start.5
  501.9 1.4 copy-start.4
  501.9 2.3 copy-start
Sparse Core Ops, SparseCore 0:
  11.9 85.6 all-gather.2
  99.8 89.2 all-gather.4
  260.8 68.0 reduce-scatter.2
  344.7 44.9 reduce-scatter.4

commit v10 on v9

--- a/solution.py
+++ b/solution.py
@@ -326,21 +326,79 @@
 IN_VMEM = pl.BlockSpec(memory_space=pltpu.VMEM)
 
 
+class Moves:
+    def __init__(self, loads, stores):
+        self.loads, self.stores = loads, stores
+        for _, copy in loads:
+            copy.start()
+        self.begun = []
+
+    def ready(self, *refs):
+        rest = []
+        for ref, copy in self.loads:
+            if not refs or any(ref is wanted for wanted in refs):
+                copy.wait()
+            else:
+                rest.append((ref, copy))
+        self.loads = rest
+
+    def store(self, *refs):
+        rest = []
+        for ref, copy in self.stores:
+            if not refs or any(ref is wanted for wanted in refs):
+                copy.start()
+                self.begun.append(copy)
+            else:
+                rest.append((ref, copy))
+        self.stores = rest
+
+    def finish(self):
+        self.ready()
+        self.store()
+        for copy in self.begun:
+            copy.wait()
+
+
 def call(kernel, name, outs, out_specs, in_specs, scratch, ident, micros):
-    return pl.pallas_call(
-        kernel,
-        out_shape=outs,
-        in_specs=in_specs,
-        out_specs=out_specs,
-        scratch_shapes=scratch,
-        name=name,
-        cost_estimate=pl.CostEstimate(
-            flops=micros * 10**9, bytes_accessed=micros * 10**6, transcendentals=0
-        ),
-        compiler_params=pltpu.CompilerParams(
-            collective_id=ident, has_side_effects=True, vmem_limit_bytes=VMEM_LIMIT
-        ),
-    )
+    def run(*args):
+        loaded = [i for i, spec in enumerate(in_specs) if spec is IN_VMEM]
+        stored = [i for i, spec in enumerate(out_specs) if spec is IN_VMEM]
+        buffers = [pltpu.VMEM(args[i].shape, args[i].dtype) for i in loaded]
+        buffers += [pltpu.VMEM(outs[i].shape, outs[i].dtype) for i in stored]
+
+        def wrapped(*refs):
+            ends = len(in_specs), len(in_specs) + len(outs)
+            given, made, rest = list(refs[: ends[0]]), list(refs[ends[0] : ends[1]]), refs[ends[1] :]
+            sems, rest = rest[len(buffers)], (rest[: len(buffers)], rest[len(buffers) + 1 :])
+            loads, stores = [], []
+            for k, i in enumerate(loaded):
+                copy = pltpu.make_async_copy(given[i], rest[0][k], sems.at[k])
+                loads.append((rest[0][k], copy))
+                given[i] = rest[0][k]
+            for k, i in enumerate(stored, len(loaded)):
+                copy = pltpu.make_async_copy(rest[0][k], made[i], sems.at[k])
+                stores.append((rest[0][k], copy))
+                made[i] = rest[0][k]
+            moves = Moves(loads, stores)
+            kernel(moves, *given, *made, *rest[1])
+            moves.finish()
+
+        return pl.pallas_call(
+            wrapped,
+            out_shape=outs,
+            in_specs=[ANY] * len(in_specs),
+            out_specs=(ANY,) * len(outs),
+            scratch_shapes=buffers + [pltpu.SemaphoreType.DMA((len(buffers),))] + scratch,
+            name=name,
+            cost_estimate=pl.CostEstimate(
+                flops=micros * 10**9, bytes_accessed=micros * 10**6, transcendentals=0
+            ),
+            compiler_params=pltpu.CompilerParams(
+                collective_id=ident, has_side_effects=True, vmem_limit_bytes=VMEM_LIMIT
+            ),
+        )(*args)
+
+    return run
 
 
 def shape(*dims, dtype=BF):
@@ -374,7 +432,7 @@
 
 
 def first_kernel(
-    frames_ref, gain_ref, bias_ref, cot_ref, text_ref, w_text_ref,
+    moves, frames_ref, gain_ref, bias_ref, cot_ref, text_ref, w_text_ref,
     rows_out, cot_out, text_all, text_out,
     normed_ref, part_ref, came_ref, sends, recvs, *scratch,
 ):
@@ -382,6 +440,7 @@
     spot = place()[1:]
     others = shard_others()
     enter(neighbours() + [device(other, *spot) for other in others])
+    moves.ready()
     texts = spread(lambda other: text_ref.at[other], text_all, sends.at[0], recvs.at[0], others, spot)
     text_all[z] = text_ref[z]
 
@@ -447,7 +506,7 @@
 
 
 def feed_kernel(
-    own_ref, grad_ref, w_ref,
+    moves, own_ref, grad_ref, w_ref,
     normed_out, branch_out, up_out, down_out,
     rows_ref, grads_ref, hidden_ref, slope_ref, part_a, part_b,
     load_sem, store_sem, g_local, g_send, g_recv, *scratch,
@@ -470,6 +529,7 @@
         slope_ref[block] = nn(grads_ref[block], down_ref[...]).astype(BF)
         return carry
 
+    moves.ready()
     lax.fori_loop(0, blocks, early, 0)
 
     def middle(block):
@@ -537,7 +597,9 @@
         lax.fori_loop(0, width // tile, one, 0)
 
     weight(grads_ref, hidden_ref, down_out)
+    moves.store(down_out)
     weight(rows_ref, slope_ref, up_out)
+    moves.store(up_out)
     normed_out[...] = first.total()
     first.finish()
     for block in range(blocks):
@@ -615,7 +677,7 @@
 
 
 def forward_kernel(
-    rows_ref, side_ref, text_in, frames_ref, gain_ref, bias_ref,
+    moves, rows_ref, side_ref, text_in, frames_ref, gain_ref, bias_ref,
     qkv_ref, log_ref, mix_ref, mine_ref, one_ref, two_ref, query_ref, cross_ref, low_ref,
     text_ref, square_ref, plane_out,
     w_own, w_out, w_query, w_cross, sum_ref, two_low_ref, store_sem,
@@ -634,6 +696,7 @@
     def turn_own(kind):
         w_own[kind] = turn(side_ref[:, (3 + kind) * width : (4 + kind) * width]).astype(BF)
 
+    moves.ready(side_ref)
     turn_own(0)
     jobs = [Gather(w_own.at[k], weights[k], *scratch[3 * k : 3 * k + 3]) for k in range(3)]
     text_job = Gather(text_in, text_ref, *scratch[9:])
@@ -650,7 +713,9 @@
         qkv_ref[block] = nn(rows_ref[block], side_ref[:, : 3 * width]).astype(BF)
         return carry
 
+    moves.ready()
     lax.fori_loop(0, blocks, project, 0)
+    moves.store(qkv_ref)
     turn_own(1)
     turn_own(2)
     exchange = Exchange(mix_ref, mine_ref, ex_local, ex_send, ex_recv)
@@ -687,12 +752,14 @@
             text_job.relay_y()
             text_job.relay_x()
     jobs[1].start()
+    moves.store(mix_ref, log_ref)
     jobs[0].relay_far()
     text_job.relay_far()
     jobs[0].finish()
     text_job.finish()
     keep(0)
     exchange.finish()
+    moves.store(mine_ref, text_ref)
 
     def apply(values_ref, kind):
         sum_ref[...] = nn(side_by_side(values_ref), all_rows(weights[kind]))
@@ -709,6 +776,7 @@
         return sums + jnp.sum(branch * branch, axis=0, keepdims=True)
 
     square_one = chunks(both, first, nothing)
+    moves.store(one_ref)
     jobs[1].relay_y()
     jobs[1].relay_x()
     jobs[2].start()
@@ -738,6 +806,7 @@
     jobs[2].relay_y()
     jobs[2].relay_x()
     lax.fori_loop(blocks // 2, blocks, cross, 0)
+    moves.store(query_ref, cross_ref)
     jobs[2].relay_far()
     jobs[2].finish()
     keep(2)
@@ -810,7 +879,7 @@
 
 
 def backward_kernel(
-    grad_ref, qkv_ref, mix_ref, log_ref, rows_ref, w_ref, side_ref, text_ref, down_ref, up_ref,
+    moves, grad_ref, qkv_ref, mix_ref, log_ref, rows_ref, w_ref, side_ref, text_ref, down_ref, up_ref,
     part_out, w_out, side_out, text_out, down_out, up_came,
     up_send, up_recv, out_ref, part_ref, store_sem, down_pair, pair_sem, grad_all, query_turned, ex_local, ex_send, ex_recv, *scratch,
 ):
@@ -839,6 +908,7 @@
     side = LoadedScatter(side_ref, *scratch[:size])
     side.start()
     side.first()
+    moves.ready()
     for clip in range(2):
         exchange.finish(clip)
         part = pl.ds(clip * rows, rows)
@@ -906,6 +976,7 @@
         return carry
 
     lax.fori_loop(0, w_out.shape[0] // tile, weight, 0)
+    moves.store(w_out)
     text_out[...] = text.total().astype(BF)
     side_out[...] = side.total().astype(BF)
     text.finish()
@@ -987,7 +1058,7 @@
 
 
 def rows_back_kernel(
-    normed_ref, cot_ref, one_ref, two_ref, query_ref, mix_ref, text_ref, my_mix_ref,
+    moves, normed_ref, cot_ref, one_ref, two_ref, query_ref, mix_ref, text_ref, my_mix_ref,
     gain_ref, bias_ref, w_ref, branch_ref, up_ref,
     grad_ref, layer_ref, stats_ref, grad_mix_ref, out_ref, side_ref, text_out, up_came,
     w_cross, w_query, w_out, low_ref, two_low_ref, back_ref, grad_cm, grad_cq, w_sem,
@@ -1028,6 +1099,7 @@
         two_low_ref[part] = (normed * gain_ref[1:2] + bias_ref[1:2]).astype(BF)
         return sums[0] + more[0], sums[1] + more[1]
 
+    moves.ready()
     gain_three, shift_three = chunks(rows, third, nothing)
     branch_job.first()
     loads[0].wait()
@@ -1076,6 +1148,7 @@
     cross_job.far()
     cross_job.near()
     lax.fori_loop(blocks // 2, blocks, cross, 0)
+    moves.store(text_out)
     back_ref[...] = nn(side_by_side(grad_cq), all_rows(w_query))
     lax.fori_loop(0, blocks, query_weight, 0)
     for index in range(4):
@@ -1089,6 +1162,7 @@
         return sums[0] + more[0], sums[1] + more[1]
 
     gain_two, shift_two = chunks(rows, second, nothing)
+    moves.store(grad_ref)
     cross_job.second()
     query_job.far()
     query_job.near()
@@ -1101,6 +1175,7 @@
         return carry
 
     lax.fori_loop(0, blocks, out_weight, 0)
+    moves.store(grad_mix_ref, out_ref)
     branch_job.wait()
 
     def last(part, sums):
@@ -1118,6 +1193,7 @@
         (rest, gain_two, gain_three, rest, shift_two, shift_three, square_out, square_three)
     ):
         stats_ref[index : index + 1] = row
+    moves.store(layer_ref, stats_ref)
     query_job.second()
     side_ref[1] = cross_job.total().astype(BF)
     side_ref[0] = query_job.total().astype(BF)
@@ -1168,7 +1244,7 @@
 
 
 def last_kernel(
-    part_ref, frames_ref, gain_ref, grad_ref, stats_ref, qkv_ref, up_a, up_b, cross_ref, out_w_ref,
+    moves, part_ref, frames_ref, gain_ref, grad_ref, stats_ref, qkv_ref, up_a, up_b, cross_ref, out_w_ref,
     text_ref, text_in, w_text_ref,
     out_ref, total_ref, text_out, qkv_out, up_out, cross_out, self_out, key_out,
     mine, came, all_ref, st_send, st_recv, z_send, z_recv,
@@ -1183,8 +1259,8 @@
     context = spot[0]
     enter(neighbours() + [device(other, *spot) for other in others])
 
-    def collect(moves, source_ref, came_ref, rows=slice(None)):
-        for copy in moves:
+    def collect(copies, source_ref, came_ref, rows=slice(None)):
+        for copy in copies:
             copy.wait_recv()
         total = source_ref[z, rows].astype(F32)
         for other in others:
@@ -1194,11 +1270,12 @@
     def over(index, source_of, target_ref):
         return spread(source_of, target_ref, z_send.at[index], z_recv.at[index], others, spot)
 
-    text_moves = over(0, lambda other: text_ref, text_came)
     size = len(scratch) - 5
     text = Scatter(text_part, *scratch[size:])
     job = SteepScatter(part_ref, *scratch[:size])
     job.start()
+    moves.ready()
+    text_moves = over(0, lambda other: text_ref, text_came)
     out_moves = over(2, lambda other: out_w_ref.at[other], out_came)
     third = qkv_ref.shape[1] // 3
     thirds = [pl.ds(index * third, third) for index in range(3)]
@@ -1275,6 +1352,7 @@
 
     nothing = (jnp.zeros((1, frames_ref.shape[1]), F32),) * 2
     gain_one, shift_one = chunks(frames_ref.shape[0], norm, nothing)
+    moves.store(out_ref)
     mine[0] = stats_ref[...]
     mine[0, 0:1] = gain_one
     mine[0, 3:4] = shift_one

time: 522 us -> 501 us (0.960)
  Pallas kernels: 449 us -> 424 us
    pallas_call x6, Pallas kernels: 449 us -> 424 us  [run(): pl.pallas_call(wrapped, out_shape=outs, in_specs=[ANY] * len(in_specs), o...]
  transfers between devices with their start and end apart: 4 -> 4, of which waited for: 1 -> 2; matrix products, arithmetic and copies ran while one was open for 2% -> 2% of each run, Pallas kernels for 58% -> 57%
where the time goes in v10:
time: 501 us; the launch traced here: 492 us
  Pallas kernels  424 us (85%)
  local copies, waits for them, and re-layouts  22 us (4%)
  waiting for transfers between devices  20.6 us (4%)
  between operations  14.5 us (3%)
  other arithmetic  10.3 us (2%)
    pallas_call x6, Pallas kernels, run(): pl.pallas_call(wrapped, out_shape=outs, in_specs=[ANY] * len(in_specs), o...  424 us
    all_gather x2, waiting for transfers between devices, over_shard(): return lax.all_gather(weight, 'shard', axis=0, tiled=tiled)  20.5 us
  transfers between devices with their start and end apart: 4, of which 2 were waited for; matrix products, arithmetic and copies ran while one was open for 2% of the time, Pallas kernels for 57%

profile of v10, /device:TPU:0, one launch (start us, length us, event | category | flops | bytes accessed | tf_op | source)
XLA Modules:
  0.0 491.5 jit_solution(17546881968274691777)
XLA Ops:
  7.2 0.0 all-gather.3.cloned.1.call-start
  7.2 1.2 constant_dynamic-slice_fusion.4
  8.5 1.9 dynamic-slice_bitcast_fusion
  10.4 1.3 concatenate.16
  11.7 0.0 all-gather.3.cloned.1.call-update
  11.8 0.0 all-gather.5.cloned.1.call-start
  11.8 1.1 constant_dynamic-slice_fusion.2
  13.0 1.1 pad_maximum_fusion
  14.1 0.0 all-gather.5.cloned.1.call-update
  14.1 0.0 reduce-scatter.3.cloned.1.call-start
  14.2 0.1 reshape.61
  14.3 0.8 copy.40
  15.1 0.8 pad_maximum_fusion.1.refs_5_.refs_12_
  15.9 63.9 %first_step.1 = (bf16[8,256,1536]{2,1,0:T(8,128)(2,1)}, bf16[8,256,1536]{2,1,0:T(8,128)(2,1)}, bf16[4,128,384]{2,1,0:T(8,128)(2,1)}, bf16[128,384]{1,0:T(8,128)(2,1)}) custom-call(bf16[256,1536]{1,0:T(8,128)(2,1)} %bitcast.54, f32[3,1536]{1,0:T(4,128)} %refs_8_.1, f32[3,1536]{1,0:T(4,128)} %refs_9_.1, bf16[256,1536]{1,0:T(8,128)(2,1)} %bitcast.52, ...), custom_call_target="tpu_custom_call" | custom-call | flops 60000002048 | bytes 60000000 | tf_op jit(solution)/shard_map/first_step/pallas_call | solution.py:386
  79.8 16.5 %all-gather.3.cloned.1.call-done.refs_1_.refs_5_ = bf16[1536,1152]{1,0:T(8,128)(2,1)} async-done(((bf16[384,1152]{1,0:T(8,128)(2,1)}), bf16[1536,1152]{1,0:T(8,128)(2,1)}) %all-gather.3.cloned.1.call-update) | async-done | bytes 3538960 | tf_op jit(solution)/shard_map/all_gather | solution.py:1515
  96.3 87.5 %attend_forward.1 = (bf16[8,256,576]{2,1,0:T(8,128)(2,1)}, f32[6,1024]{1,0:T(8,128)}, bf16[8,256,192]{2,1,0:T(8,128)(2,1)}, bf16[8,256,192]{2,1,0:T(8,128)(2,1)}...) custom-call(bf16[8,256,1536]{2,1,0:T(8,128)(2,1)} %get-tuple-element, ...), custom_call_target="tpu_custom_call" | custom-call | flops 80000000000 | bytes 80000000 | tf_op jit(solution)/shard_map/attend_forward/pallas_call | solution.py:386
  183.9 4.0 all-gather.5.cloned.1.call-done.refs_2_
  187.9 65.8 %feed_forward.1 = (f32[256,1536]{1,0:T(8,128)}, bf16[8,256,1536]{2,1,0:T(8,128)(2,1)}, bf16[1536,768]{1,0:T(8,128)(2,1)}, bf16[1536,768]{1,0:T(8,128)(2,1)}) custom-call(bf16[256,1536]{1,0:T(8,128)(2,1)} %get-tuple-element.56.refs_0_, bf16[8,256,1536]{2,1,0:T(8,128)(2,1)} %get-tuple-element.57.refs_1_, bf16[1536,1536]{1,0:T(8,128)(2,1)} %all-gather.5.cloned.1.call-done.refs_2_), custom_call_target="tpu_custom_call" | custom-call | flops 70000001024 | bytes 70000000 | tf_op jit(solution)/shard_map/feed_forward/pallas_call | solution.py:386
  253.7 0.0 reduce-scatter.3.cloned.1.call-update
  253.7 0.0 reduce-scatter.5.cloned.1.call-start
  253.8 75.7 %rows_back.1 = (f32[256,1536]{1,0:T(8,128)}, bf16[256,1536]{1,0:T(8,128)(2,1)}, f32[8,1536]{1,0:T(8,128)}, bf16[8,256,192]{2,1,0:T(8,128)(2,1)}, bf16[8,192,1536...) custom-call(f32[256,1536]{1,0:T(8,128)} %get-tuple-element.58.refs_0, ...), custom_call_target="tpu_custom_call" | custom-call | flops 60000002048 | bytes 60000000 | tf_op jit(solution)/shard_map/rows_back/pallas_call | solution.py:386
  329.5 2.7 reshape.65
  332.3 0.0 copy-start.13
  332.3 1.2 copy.38
  333.5 0.0 reduce-scatter.5.cloned.1.call-update
  333.5 1.3 slice.42.refs_2_
  334.9 0.6 pad_maximum_fusion.2.refs_4_
  335.5 52.0 %attend_backward.1 = (bf16[8,256,1536]{2,1,0:T(8,128)(2,1)}, bf16[1536,576]{1,0:T(8,128)(2,1)}, bf16[192,1536]{1,0:T(8,128)(2,1)}, bf16[128,384]{1,0:T(8,128)(2,...) custom-call(bf16[8,256,192]{2,1,0:T(8,128)(2,1)} %get-tuple-element.69.refs_0_, ...), custom_call_target="tpu_custom_call" | custom-call | flops 1000000000 | bytes 1000000 | tf_op jit(solution)/shard_map/attend_backward/pallas_call | solution.py:386
  387.5 1.9 copy.39
  389.4 79.0 %last_step.1 = (f32[256,1536]{1,0:T(8,128)}, f32[16,1536]{1,0:T(8,128)}, f32[4,16,384]{2,1,0:T(8,128)}, bf16[3,384,384]{2,1,0:T(8,128)(2,1)}, bf16[384,1536]{1,0...) custom-call(bf16[8,256,1536]{2,1,0:T(8,128)(2,1)} %get-tuple-element.76.refs_0_, ...), custom_call_target="tpu_custom_call" | custom-call | flops 65000001536 | bytes 65000000 | tf_op jit(solution)/shard_map/last_step/pallas_call | solution.py:386
  468.5 1.5 copy.31
  469.9 1.0 convert_bitcast_fusion
  471.0 0.1 slice_reduce_fusion
  471.1 1.7 convert_element_type.34
  472.8 1.3 convert_element_type.27
  474.2 1.1 copy.32
  475.3 1.0 copy.33
  476.4 0.7 reshape.68
  477.0 0.6 constant_dynamic-slice_fusion
  477.6 0.6 constant_dynamic-slice_fusion.1
  478.2 0.6 gather_fusion
  478.9 0.5 multiply_sqrt_fusion
  479.4 1.7 convert_element_type.35
  481.1 1.3 maximum_convert_fusion
  482.4 0.0 copy-done.4
  482.5 0.9 copy.43
  483.4 0.0 copy-done
  483.4 1.1 copy.44
  (32 shorter events, 0.2 us)
Async XLA Ops:
  7.2 89.2 %all-gather.3.cloned.1.call-start = ((), (), s32[]{:S(2)}) async-start(), calls=%async_computation.2 | async-start | bytes 4423680 | tf_op jit(solution)/shard_map/all_gather | solution.py:1515
  10.4 1.4 copy-start.7
  11.8 176.1 %all-gather.5.cloned.1.call-start = ((), (), s32[]{:S(2)}) async-start(), calls=%async_computation.3 | async-start | bytes 5898240 | tf_op jit(solution)/shard_map/all_gather | solution.py:1515
  13.0 1.2 copy-start.6
  14.1 321.4 %reduce-scatter.3.cloned.1.call-start = ((), (), s32[]{:S(2)}) async-start(), calls=%async_computation.4 | async-start | bytes 2949120 | tf_op jit(solution)/shard_map/reduce_scatter | solution.py:1553
  253.7 135.7 %reduce-scatter.5.cloned.1.call-start = ((), (), s32[]{:S(2)}) async-start(), calls=%async_computation.5 | async-start | bytes 1474560 | tf_op jit(solution)/shard_map/reduce_scatter | solution.py:1553
  332.3 2.6 copy-start.13
  332.3 2.6 copy-start.11
  332.3 2.6 copy-start.12
  468.4 2.5 copy-start.10
  468.4 2.7 copy-start.2
  471.1 1.7 copy-start.3
  472.8 1.3 copy-start.8
  474.2 2.2 copy-start.9
  474.2 5.2 %copy-start.1 = (bf16[384,1536]{1,0:T(8,128)(2,1)S(1)}, bf16[384,1536]{1,0:T(8,128)(2,1)}, u32[]{:S(2)}) copy-start(bf16[384,1536]{1,0:T(8,128)(2,1)} %get-tuple-element.95) | copy-start | bytes 3538948
  479.4 1.7 copy-start.5
  481.1 1.4 copy-start.4
  481.1 2.3 copy-start
Sparse Core Ops, SparseCore 0:
  11.9 84.4 all-gather.2
  98.5 89.3 all-gather.4
  253.8 65.0 reduce-scatter.2
  333.6 43.7 reduce-scatter.4

commit v11 on v10

--- a/solution.py
+++ b/solution.py
@@ -434,15 +434,19 @@
 def first_kernel(
     moves, frames_ref, gain_ref, bias_ref, cot_ref, text_ref, w_text_ref,
     rows_out, cot_out, text_all, text_out,
-    normed_ref, part_ref, came_ref, sends, recvs, *scratch,
+    normed_ref, part_ref, came_ref, some_ref, some_flat, text_plane, sends, recvs, *scratch,
 ):
     z = lax.axis_index("shard")
     spot = place()[1:]
     others = shard_others()
     enter(neighbours() + [device(other, *spot) for other in others])
     moves.ready()
-    texts = spread(lambda other: text_ref.at[other], text_all, sends.at[0], recvs.at[0], others, spot)
-    text_all[z] = text_ref[z]
+    few = some_ref.shape[1]
+    some = pl.ds(pl.multiple_of(slot(*spot) * few, few), few)
+    texts = spread(
+        lambda other: text_ref.at[other, some], some_ref, sends.at[0], recvs.at[0], others, spot
+    )
+    some_ref[z] = text_ref[z, some]
 
     def norm(part, carry):
         normed, _ = normalise(frames_ref[part].astype(F32))
@@ -450,12 +454,19 @@
         return carry
 
     chunks(frames_ref.shape[0], norm)
-    rows, grads = Gather(normed_ref, rows_out, *scratch[:3]), Gather(cot_ref, cot_out, *scratch[3:])
+    rows, grads = Gather(normed_ref, rows_out, *scratch[:3]), Gather(cot_ref, cot_out, *scratch[3:6])
     rows.start()
     for copy in texts:
         copy.wait_recv()
+    shards, _, depth = some_ref.shape
+    some_flat[...] = some_ref[...].reshape(shards * few, depth)
+    meet = Gather(some_flat, text_plane, *scratch[6:])
+    meet.start()
+    meet.rest()
 
     def share(index, carry):
+        rows_here = pl.ds(pl.multiple_of(index * few, few), few)
+        text_all[index] = text_plane[:, rows_here].reshape(8 * few, depth)
         part_ref[index] = nn(text_all[index], w_text_ref[...]).astype(BF)
         return carry
 
@@ -496,10 +507,13 @@
             pltpu.VMEM((rows, width), BF),
             pltpu.VMEM((shards, texts, w_text.shape[1]), BF),
             pltpu.VMEM((shards, texts, w_text.shape[1]), BF),
+            pltpu.VMEM((shards, texts // 8, depth), BF),
+            pltpu.VMEM((shards * texts // 8, depth), BF),
+            pltpu.VMEM((8, shards * texts // 8, depth), BF),
             pltpu.SemaphoreType.DMA((2, shards - 1)),
             pltpu.SemaphoreType.DMA((2, shards - 1)),
         ]
-        + gather_scratch() * 2,
+        + gather_scratch() * 3,
         ident,
         60,
     )(frames, gain, bias, cotangent, text, w_text)
@@ -978,7 +992,7 @@
     lax.fori_loop(0, w_out.shape[0] // tile, weight, 0)
     moves.store(w_out)
     text_out[...] = text.total().astype(BF)
-    side_out[...] = side.total().astype(BF)
+    into_slices(side.total().astype(BF), side_out, 0)
     text.finish()
     side.finish()
     beside(down_ref, pair, down_pair, down_out)
@@ -1000,7 +1014,7 @@
         (
             shape(blocks, block, width),
             shape(width, 3 * columns),
-            shape(side_rows, width),
+            shape(up.shape[0], side_rows, up.shape[1]),
             shape(*text_shape),
             shape(down.shape[0], 2 * down.shape[1]),
             shape(*up.shape[:2], up.shape[2] // 2),
@@ -1055,6 +1069,13 @@
         jnp.sum(grads, axis=0, keepdims=True),
     )
     return result, sums
+
+
+def into_slices(values, ref, start):
+    shards, _, depth = ref.shape
+    for index in range(shards):
+        part = values[:, index * depth : (index + 1) * depth]
+        ref[index, start : start + values.shape[0]] = part
 
 
 def rows_back_kernel(
@@ -1195,8 +1216,8 @@
         stats_ref[index : index + 1] = row
     moves.store(layer_ref, stats_ref)
     query_job.second()
-    side_ref[1] = cross_job.total().astype(BF)
-    side_ref[0] = query_job.total().astype(BF)
+    for kind, job in ((1, cross_job), (0, query_job)):
+        into_slices(job.total().astype(BF), side_ref, kind * columns)
     branch_job.finish()
     cross_job.finish()
     query_job.finish()
@@ -1219,7 +1240,7 @@
             shape(8, width, dtype=F32),
             shape(*my_mix.shape),
             shape(blocks, columns, width),
-            shape(2, columns, width),
+            shape(up.shape[0], 2 * columns, up.shape[1]),
             shape(*text.shape),
             shape(*up.shape[:2], up.shape[2] // 2),
         ),
@@ -1244,7 +1265,7 @@
 
 
 def last_kernel(
-    moves, part_ref, frames_ref, gain_ref, grad_ref, stats_ref, qkv_ref, up_a, up_b, cross_ref, out_w_ref,
+    moves, part_ref, frames_ref, gain_ref, grad_ref, stats_ref, squares_ref, qkv_ref, up_a, up_b, cross_ref, out_w_ref,
     text_ref, text_in, w_text_ref,
     out_ref, total_ref, text_out, qkv_out, up_out, cross_out, self_out, key_out,
     mine, came, all_ref, st_send, st_recv, z_send, z_recv,
@@ -1346,14 +1367,15 @@
     send_third(2)
 
     def norm(part, sums):
-        back, more = norm_back(job.value(part), frames_ref[part].astype(F32), gain_ref[...])
+        back, more = norm_back(job.value(part), frames_ref[part].astype(F32), gain_ref[0:1])
         out_ref[part] = grad_ref[part] + back
         return sums[0] + more[0], sums[1] + more[1]
 
     nothing = (jnp.zeros((1, frames_ref.shape[1]), F32),) * 2
     gain_one, shift_one = chunks(frames_ref.shape[0], norm, nothing)
     moves.store(out_ref)
-    mine[0] = stats_ref[...]
+    mine[0, :8] = stats_ref[...]
+    mine[0, 8:] = squares_ref[...]
     mine[0, 0:1] = gain_one
     mine[0, 3:4] = shift_one
     sends = []
@@ -1420,7 +1442,8 @@
 
 
 def last_step(
-    part, frames, gain, grad, stats, qkv, up_a, up_b, cross, out, text, text_in, w_text, ident
+    part, frames, gain, grad, stats, squares, qkv, up_a, up_b, cross, out, text, text_in, w_text,
+    ident,
 ):
     _, rows, width = part.shape
     shards, texts, depth = text_in.shape
@@ -1441,7 +1464,7 @@
             shape(2, depth, 2 * columns),
         ),
         (IN_VMEM,) * 8,
-        [ANY] + [IN_VMEM] * 12,
+        [ANY] + [IN_VMEM] * 13,
         [
             pltpu.VMEM((4, 16, width), F32),
             pltpu.VMEM((3, 16, width), F32),
@@ -1471,7 +1494,7 @@
         + Scatter.scratch(shards * own, depth),
         ident,
         65,
-    )(part, frames, gain, grad, stats, qkv, up_a, up_b, cross, out, text, text_in, w_text)
+    )(part, frames, gain, grad, stats, squares, qkv, up_a, up_b, cross, out, text, text_in, w_text)
 
 
 def dots(spec, *operands):
@@ -1571,10 +1594,7 @@
         3,
     )
 
-    def slice_shards(part):
-        return part.reshape(-1, slices, depth).transpose(1, 0, 2)
-
-    grad_cross = to_shard(slice_shards(side))[0]
+    grad_cross = to_shard(side)[0]
     part_norm, grad_w_qkv, grad_out, text_grads, grad_down, up_b = attend_backward(
         grad_mix, qkv, mix, self_log, all_one, w_early, part_out, text_grads, grad_down, grad_up, 8
     )
@@ -1583,14 +1603,15 @@
     ) = last_step(
         part_norm,
         frames.reshape(block, width),
-        norm_gain[0][None],
+        norm_gain,
         grad_one,
-        jnp.concatenate([stats, squares], axis=0),
+        stats,
+        squares,
         grad_w_qkv.reshape(slices, depth, 3 * columns),
         up_a,
         up_b,
         grad_cross,
-        slice_shards(grad_out),
+        grad_out,
         text_grads,
         text_in,
         w_text,

time: 501 us -> 489 us (0.976)
  waiting for transfers between devices: 20.6 us -> 7.69 us
  Pallas kernels: 424 us -> 432 us
  local copies, waits for them, and re-layouts: 22 us -> 14.8 us
    all_gather x2, waiting for transfers between devices: 20.5 us -> 7.58 us  [over_shard(): return lax.all_gather(weight, 'shard', axis=0, tiled=tiled)]
    pallas_call x6, Pallas kernels: 424 us -> 432 us  [run(): pl.pallas_call(wrapped, out_shape=outs, in_specs=[ANY] * len(in_specs), o...]
    reshape x3 -> x0, local copies, waits for them, and re-layouts: 5.83 us -> none  [slice_shards(): return part.reshape(-1, slices, depth).transpose(1, 0, 2)]
  transfers between devices with their start and end apart: 4 -> 4, of which waited for: 2 -> 2; matrix products, arithmetic and copies ran while one was open for 2% -> 1% of each run, Pallas kernels for 57% -> 60%
where the time goes in v11:
time: 489 us; the launch traced here: 479 us
  Pallas kernels  432 us (88%)
  local copies, waits for them, and re-layouts  14.8 us (3%)
  between operations  14.5 us (3%)
  other arithmetic  9.67 us (2%)
  waiting for transfers between devices  7.69 us (2%)
    pallas_call x6, Pallas kernels, run(): pl.pallas_call(wrapped, out_shape=outs, in_specs=[ANY] * len(in_specs), o...  432 us
  transfers between devices with their start and end apart: 4, of which 2 were waited for; matrix products, arithmetic and copies ran while one was open for 1% of the time, Pallas kernels for 60%

profile of v11, /device:TPU:0, one launch (start us, length us, event | category | flops | bytes accessed | tf_op | source)
XLA Modules:
  0.0 479.0 jit_solution(16565140471785873218)
XLA Ops:
  7.2 0.0 all-gather.3.cloned.1.call-start
  7.2 1.2 constant_dynamic-slice_fusion.4
  8.5 1.9 dynamic-slice_bitcast_fusion
  10.4 0.0 copy-start.7
  10.4 1.3 concatenate.13
  11.7 0.0 all-gather.3.cloned.1.call-update
  11.8 0.0 all-gather.5.cloned.1.call-start
  11.8 1.1 constant_dynamic-slice_fusion.2
  13.0 0.0 copy-start.6
  13.0 1.1 pad_maximum_fusion
  14.1 0.0 all-gather.5.cloned.1.call-update
  14.1 0.0 reduce-scatter.3.cloned.1.call-start
  14.2 0.1 reshape.55
  14.3 0.8 copy.33
  15.1 0.8 pad_maximum_fusion.1.refs_5_.refs_13_
  15.9 72.8 %first_step.1 = (bf16[8,256,1536]{2,1,0:T(8,128)(2,1)}, bf16[8,256,1536]{2,1,0:T(8,128)(2,1)}, bf16[4,128,384]{2,1,0:T(8,128)(2,1)}, bf16[128,384]{1,0:T(8,128)(2,1)}) custom-call(bf16[256,1536]{1,0:T(8,128)(2,1)} %bitcast.41, f32[3,1536]{1,0:T(4,128)} %refs_2_.3, f32[3,1536]{1,0:T(4,128)} %refs_9_.1, bf16[256,1536]{1,0:T(8,128)(2,1)} %bitcast.39, ...), custom_call_target="tpu_custom_call" | custom-call | flops 60000002048 | bytes 60000000 | tf_op jit(solution)/shard_map/first_step/pallas_call | solution.py:386
  88.8 4.0 all-gather.3.cloned.1.call-done.refs_1_.refs_5_
  92.8 86.6 %attend_forward.1 = (bf16[8,256,576]{2,1,0:T(8,128)(2,1)}, f32[6,1024]{1,0:T(8,128)}, bf16[8,256,192]{2,1,0:T(8,128)(2,1)}, bf16[8,256,192]{2,1,0:T(8,128)(2,1)}...) custom-call(bf16[8,256,1536]{2,1,0:T(8,128)(2,1)} %get-tuple-element, ...), custom_call_target="tpu_custom_call" | custom-call | flops 80000000000 | bytes 80000000 | tf_op jit(solution)/shard_map/attend_forward/pallas_call | solution.py:386
  179.3 3.6 all-gather.5.cloned.1.call-done.refs_2_
  182.9 65.8 %feed_forward.1 = (f32[256,1536]{1,0:T(8,128)}, bf16[8,256,1536]{2,1,0:T(8,128)(2,1)}, bf16[1536,768]{1,0:T(8,128)(2,1)}, bf16[1536,768]{1,0:T(8,128)(2,1)}) custom-call(bf16[256,1536]{1,0:T(8,128)(2,1)} %get-tuple-element.56.refs_0_, bf16[8,256,1536]{2,1,0:T(8,128)(2,1)} %get-tuple-element.57.refs_1_, bf16[1536,1536]{1,0:T(8,128)(2,1)} %all-gather.5.cloned.1.call-done.refs_2_), custom_call_target="tpu_custom_call" | custom-call | flops 70000001024 | bytes 70000000 | tf_op jit(solution)/shard_map/feed_forward/pallas_call | solution.py:386
  248.7 0.0 reduce-scatter.3.cloned.1.call-update
  248.8 0.0 reduce-scatter.5.cloned.1.call-start
  248.8 0.0 copy-start.11
  248.8 75.8 %rows_back.1 = (f32[256,1536]{1,0:T(8,128)}, bf16[256,1536]{1,0:T(8,128)(2,1)}, f32[8,1536]{1,0:T(8,128)}, bf16[8,256,192]{2,1,0:T(8,128)(2,1)}, bf16[8,192,1536...) custom-call(f32[256,1536]{1,0:T(8,128)} %get-tuple-element.58.refs_0, ...), custom_call_target="tpu_custom_call" | custom-call | flops 60000002048 | bytes 60000000 | tf_op jit(solution)/shard_map/rows_back/pallas_call | solution.py:386
  324.6 0.0 reduce-scatter.5.cloned.1.call-update
  324.6 0.0 copy-done.11
  324.6 0.0 reduce-scatter.3.cloned.1.call-done.refs_8_
  324.7 52.1 %attend_backward.1 = (bf16[8,256,1536]{2,1,0:T(8,128)(2,1)}, bf16[1536,576]{1,0:T(8,128)(2,1)}, bf16[4,192,384]{2,1,0:T(8,128)(2,1)}, bf16[128,384]{1,0:T(8,128)...) custom-call(bf16[8,256,192]{2,1,0:T(8,128)(2,1)} %get-tuple-element.69.refs_0_, ...), custom_call_target="tpu_custom_call" | custom-call | flops 1000000000 | bytes 1000000 | tf_op jit(solution)/shard_map/attend_backward/pallas_call | solution.py:386
  376.8 0.0 reduce-scatter.5.cloned.1.call-done
  376.8 79.1 %last_step.1 = (f32[256,1536]{1,0:T(8,128)}, f32[16,1536]{1,0:T(8,128)}, f32[4,16,384]{2,1,0:T(8,128)}, bf16[3,384,384]{2,1,0:T(8,128)(2,1)}, bf16[384,1536]{1,0...) custom-call(bf16[8,256,1536]{2,1,0:T(8,128)(2,1)} %get-tuple-element.76.refs_0_, ...), custom_call_target="tpu_custom_call" | custom-call | flops 65000001536 | bytes 65000000 | tf_op jit(solution)/shard_map/last_step/pallas_call | solution.py:386
  456.0 1.5 copy.29
  457.4 1.0 convert_bitcast_fusion
  458.5 0.1 slice_reduce_fusion
  458.6 1.7 convert_element_type.34
  460.3 1.3 convert_element_type.27
  461.7 1.1 copy.30
  462.8 1.0 copy.31
  463.9 0.7 reshape.60
  464.5 0.6 constant_dynamic-slice_fusion
  465.1 0.6 constant_dynamic-slice_fusion.1
  465.7 0.6 gather_fusion
  466.4 0.5 multiply_sqrt_fusion
  466.9 1.7 convert_element_type.35
  468.6 1.3 maximum_convert_fusion
  469.9 0.0 copy-done.4
  470.0 0.9 copy.36
  470.8 0.0 copy-done
  470.9 1.1 copy.37
  (23 shorter events, 0.2 us)
Async XLA Ops:
  7.2 85.6 %all-gather.3.cloned.1.call-start = ((), (), s32[]{:S(2)}) async-start(), calls=%async_computation.2 | async-start | bytes 4423680 | tf_op jit(solution)/shard_map/all_gather | solution.py:1538
  10.4 1.4 copy-start.7
  11.8 171.1 %all-gather.5.cloned.1.call-start = ((), (), s32[]{:S(2)}) async-start(), calls=%async_computation.3 | async-start | bytes 5898240 | tf_op jit(solution)/shard_map/all_gather | solution.py:1538
  13.0 1.2 copy-start.6
  14.1 310.6 %reduce-scatter.3.cloned.1.call-start = ((), (), s32[]{:S(2)}) async-start(), calls=%async_computation.4 | async-start | bytes 2949120 | tf_op jit(solution)/shard_map/reduce_scatter | solution.py:1576
  248.8 128.1 %reduce-scatter.5.cloned.1.call-start = ((), (), s32[]{:S(2)}) async-start(), calls=%async_computation.5 | async-start | bytes 1474560 | tf_op jit(solution)/shard_map/reduce_scatter | solution.py:1576
  248.8 75.8 %copy-start.11 = (s32[4]{0:T(128)S(1)}, s32[4]{0:T(128)}, u32[]{:S(2)}) copy-start(s32[4]{0:T(128)} %constant.38) | copy-start | bytes 52
  455.9 2.5 copy-start.10
  455.9 2.7 copy-start.2
  458.6 1.7 copy-start.3
  460.3 1.3 copy-start.8
  461.7 2.2 copy-start.9
  461.7 5.2 %copy-start.1 = (bf16[384,1536]{1,0:T(8,128)(2,1)S(1)}, bf16[384,1536]{1,0:T(8,128)(2,1)}, u32[]{:S(2)}) copy-start(bf16[384,1536]{1,0:T(8,128)(2,1)} %get-tuple-element.95) | copy-start | bytes 3538948
  466.9 1.7 copy-start.5
  468.6 1.4 copy-start.4
  468.6 2.3 copy-start
Sparse Core Ops, SparseCore 0:
  11.9 80.8 all-gather.2
  94.9 87.9 all-gather.4
  248.9 65.0 reduce-scatter.2
  324.7 43.3 reduce-scatter.4
